TPU v7x, 32 devices: a whole 2x2x4 slice. The times are simulated.
32 devices in a mesh: sub: 4 (over y, x), mem: 8 (over z, core).
Axes of the slice: x: 2, y: 2, z: 4, core: 2. Of those that a mesh axis runs over, the one named last changes fastest.
Arguments:
- member_state: bfloat16 [2, 512, 32, 1024], P(None, 'mem', 'sub'), may hold values from -6 to 6
- hx_values: bfloat16 [2, 512, 4, 16, 512], P(None, 'mem', 'sub'), may hold values from -6 to 6
- obs_value: bfloat16 [2, 4, 16, 512], P(None, 'sub', 'mem'), may hold values from -6 to 6
- obs_var: bfloat16 [2, 4, 16, 512], P(None, 'sub', 'mem'), may hold values from 0.25 to 4
- courant: float32 [2, 1024], replicated, may hold values from -0.95 to 0.95
Outputs:
- forecast: bfloat16 [2, 512, 32, 1024], P(None, 'mem', 'sub')
All inputs are finite; a program needn't handle non-finite values. Where the computation divides by a largest or mean magnitude, that divisor is 1e-20 or more.
Results may differ from a plain program's by a relative error of at most 0.011.
Values may be sent and summed in bfloat16 or wider, within the bound.
No kernel may reach another device: no remote copies, remote signals or barrier semaphores. Data moves between devices by JAX's collectives and lax.ppermute only.
A program may use at most 128 MiB of HBM per device.

v0:
```python
import jax
import jax.numpy as jnp
from jax import lax
from jax.sharding import PartitionSpec as P

ITERS = 4
STEPS = 4


def extended(block, sides, width):
    for axis, dim in sides:
        count = lax.axis_size(axis)
        forward = [(i, i + 1) for i in range(count - 1)]
        forward.append((count - 1, 0))
        backward = [(target, source) for source, target in forward]
        low = lax.ppermute(
            lax.slice_in_dim(block, block.shape[dim] - width, None, axis=dim), axis, forward
        )
        high = lax.ppermute(lax.slice_in_dim(block, 0, width, axis=dim), axis, backward)
        block = jnp.concatenate([low, block, high], axis=dim)
    return block


def patch_update(hx_rows, obs_rows, var_rows, members):
    total = hx_rows.shape[0]
    obs_count = hx_rows.shape[1]
    half_rows = obs_count // 4
    taper_rows = (jnp.arange(half_rows, dtype=jnp.float32) + 1.0) / (half_rows + 1.0)
    local_weight = jnp.concatenate(
        [taper_rows, jnp.ones((2 * half_rows,), jnp.float32), taper_rows[::-1]]
    )
    hx_float = hx_rows.astype(jnp.float32)
    obs_mean = jnp.mean(hx_float, axis=0)
    centred = hx_float - obs_mean
    y_pert = centred.astype(jnp.bfloat16)
    weighted = (centred * (local_weight / var_rows)).astype(jnp.bfloat16)
    identity = jnp.eye(total, dtype=jnp.float32)
    gram_matrix = lax.dot_general(
        weighted, y_pert, (((1,), (1,)), ((), ())), preferred_element_type=jnp.float32
    )
    system = (total - 1.0) * identity + gram_matrix
    row_bound = jnp.max(jnp.sum(jnp.abs(system), axis=1))
    sqrt_iterate = system / row_bound
    inv_iterate = identity
    for iteration in range(ITERS):
        product = jnp.dot(
            inv_iterate.astype(jnp.bfloat16),
            sqrt_iterate.astype(jnp.bfloat16),
            preferred_element_type=jnp.float32,
        )
        correction = 1.5 * identity - 0.5 * product
        correction_half = correction.astype(jnp.bfloat16)
        sqrt_iterate = jnp.dot(
            sqrt_iterate.astype(jnp.bfloat16), correction_half, preferred_element_type=jnp.float32
        )
        inv_iterate = jnp.dot(
            correction_half, inv_iterate.astype(jnp.bfloat16), preferred_element_type=jnp.float32
        )
    innovation = obs_rows - obs_mean
    projected = jnp.sum(weighted.astype(jnp.float32) * innovation, axis=1)
    halfway = jnp.dot(inv_iterate, projected, precision=lax.Precision.HIGHEST)
    mean_weight = jnp.dot(inv_iterate, halfway, precision=lax.Precision.HIGHEST) / row_bound
    transform = (jnp.sqrt((total - 1.0) / row_bound) * inv_iterate + mean_weight[:, None]).astype(
        jnp.bfloat16
    )
    member_vals = members.reshape(total, -1).astype(jnp.float32)
    state_mean = jnp.mean(member_vals, axis=0)
    state_pert = (member_vals - state_mean).astype(jnp.bfloat16)
    update = lax.dot_general(
        transform, state_pert, (((0,), (0,)), ((), ())), preferred_element_type=jnp.float32
    )
    analysis = state_mean + update
    return analysis.astype(jnp.bfloat16).reshape(members.shape)


def advect(u_west, u_here, u_east, speed):
    return (
        u_here
        - 0.5 * speed * (u_east - u_west)
        + 0.5 * speed * speed * (u_east - 2.0 * u_here + u_west)
    )


def advance(member_state, hx_values, obs_value, obs_var, courant):
    slab_count, local_members, cells_a, cells_b = member_state.shape
    patches_line = hx_values.shape[3]
    grid_view = member_state.reshape(
        slab_count, local_members, cells_a, patches_line, cells_b // patches_line
    )
    patch_members, patch_hx = (
        lax.all_to_all(grid_view, "mem", split_axis=3, concat_axis=1, tiled=True),
        lax.all_to_all(hx_values, "mem", split_axis=3, concat_axis=1, tiled=True),
    )
    obs_stats = jnp.stack([obs_value, obs_var], axis=1)
    packed = jnp.concatenate([patch_hx, obs_stats], axis=1)
    half_rows = packed.shape[4] // 2
    widened = extended(packed, (("sub", 2),), 1)
    before_rows = widened[:, :, 0:1, :, half_rows:]
    after_rows = widened[:, :, 2:3, :, :half_rows]
    joined = jnp.concatenate([before_rows, packed, after_rows], axis=4)[:, :, 0]
    members_total = patch_members.shape[1]
    hx_extended = joined[:, :members_total]
    obs_extended = joined[:, members_total].astype(jnp.float32)
    var_extended = joined[:, members_total + 1].astype(jnp.float32)
    per_patch = jax.vmap(patch_update, in_axes=(1, 0, 0, 2), out_axes=2)
    analysis = jax.vmap(per_patch)(hx_extended, obs_extended, var_extended, patch_members)
    returned = lax.all_to_all(analysis, "mem", split_axis=1, concat_axis=3, tiled=True)
    analysis_view = returned.reshape(slab_count, local_members, cells_a, cells_b)
    speed = courant[:, None, None, :]
    padded = extended(analysis_view, (("sub", 2),), STEPS).astype(jnp.float32)
    for step_index in range(STEPS):
        padded = advect(padded[:, :, :-2], padded[:, :, 1:-1], padded[:, :, 2:], speed)
    return padded.astype(jnp.bfloat16)


def body(member_state, hx_values, obs_value, obs_var, courant):
    return advance(member_state, hx_values, obs_value, obs_var, courant)


def solution(mesh):
    in_specs = (
        P(None, "mem", "sub", None),
        P(None, "mem", "sub", None, None),
        P(None, "sub", "mem", None),
        P(None, "sub", "mem", None),
        P(),
    )
    out_specs = P(None, "mem", "sub", None)
    return jax.shard_map(body, mesh=mesh, in_specs=in_specs, out_specs=out_specs, check_vma=False)
```

profile of v0, /device:TPU:0, one launch (start us, length us, event | category | flops | bytes accessed | tf_op | source)
XLA Modules:
  0.0 367.8 jit_solution(16963422138206765030)
XLA Ops:
  0.0 4.1 %copy.107 = bf16[2,64,1,16,512]{4,1,2,0,3:T(8,128)(2,1)} copy(bf16[2,64,1,16,512]{4,3,2,1,0:T(8,128)(2,1)} %param.6) | data formatting | bytes 4194304 | tf_op args[1]
  4.1 6.3 %all-to-all-start.1 = ((bf16[2,64,1,16,512]{4,1,2,0,3:T(8,128)(2,1)}), bf16[2,64,1,16,512]{4,1,2,0,3:T(8,128)(2,1)S(1)}, u32[]{:S(2)}, u32[]{:S(2)}) async-start(bf16[2,64,1,16,512]{4,1,2,0,3:T(8,128)(2,1)} %copy.107), calls=%async_computation.1 | async-start | bytes 4194304 | tf_op jit(solution)/shard_map/all_to_all | solution.py:92
  10.4 6.3 %reshape.71 = bf16[2,64,8,16,64]{4,3,2,1,0:T(8,128)(2,1)} reshape(bf16[2,64,8,1024]{3,2,1,0:T(8,128)(2,1)} %param.5) | data formatting | bytes 4194304 | tf_op jit(solution)/shard_map/reshape | solution.py:87
  16.8 5.3 %copy.143 = bf16[2,64,8,16,64]{4,2,1,0,3:T(8,128)(2,1)} copy(bf16[2,64,8,16,64]{4,3,2,1,0:T(8,128)(2,1)} %reshape.71) | data formatting | bytes 4194304 | tf_op jit(solution)/shard_map/reshape | solution.py:87
  22.0 7.6 %reshape.86 = bf16[8,2,65536]{2,1,0:T(2,128)(2,1)} reshape(bf16[16,2,64,8,64]{4,3,2,1,0:T(8,128)(2,1)} %bitcast.108) | data formatting | bytes 4194304
  29.6 29.9 %all-to-all-done.1 = bf16[2,64,1,16,512]{4,1,2,0,3:T(8,128)(2,1)S(1)} async-done(((bf16[2,64,1,16,512]{4,1,2,0,3:T(8,128)(2,1)}), bf16[2,64,1,16,512]{4,1,2,0,3:T(8,128)(2,1)S(1)}, u32[]{:S(2)}, u32[]{:S(2)}) %all-to-all-start.1) | async-done | bytes 2097184 | tf_op jit(solution)/shard_map/all_to_all | solution.py:92
  59.5 4.3 %all-to-all-start = ((bf16[8,2,65536]{2,1,0:T(2,128)(2,1)}), bf16[8,2,65536]{2,1,0:T(2,128)(2,1)}, u32[]{:S(2)}, u32[]{:S(2)}) async-start(bf16[8,2,65536]{2,1,0:T(2,128)(2,1)} %reshape.86), calls=%async_computation | async-start | bytes 4194304 | tf_op jit(solution)/shard_map/all_to_all | solution.py:91
  63.9 0.2 copy.108
  64.1 0.2 copy.109
  64.4 0.2 pad_maximum_fusion
  64.6 3.0 copy.112
  67.5 2.5 collective-permute-start.1
  70.0 0.5 collective-permute-start
  70.5 0.1 fusion.28
  70.6 1.3 copy.106
  72.2 40.7 %all-to-all-done = bf16[8,2,65536]{2,1,0:T(2,128)(2,1)} async-done(((bf16[8,2,65536]{2,1,0:T(2,128)(2,1)}), bf16[8,2,65536]{2,1,0:T(2,128)(2,1)}, u32[]{:S(2)}, u32[]{:S(2)}) %all-to-all-start) | async-done | bytes 2097184 | tf_op jit(solution)/shard_map/all_to_all | solution.py:91
  112.9 7.4 %reshape.87 = bf16[16,2,64,8,64]{4,3,2,1,0:T(8,128)(2,1)} reshape(bf16[8,2,65536]{2,1,0:T(2,128)(2,1)} %all-to-all-done) | data formatting | bytes 4194304
  120.3 6.4 %bitcast_convert_fusion = f32[2,64,8,16,64]{4,2,1,0,3:T(8,128)} fusion(bf16[16,2,64,8,64]{4,3,2,1,0:T(8,128)(2,1)} %reshape.87), kind=kLoop, calls=%fused_computation.67 | loop fusion | flops 1048576 | bytes 6291456 | tf_op jit(solution)/shard_map/vmap(vmap())/convert_element_type | solution.py:66
  126.7 8.2 %copy.118 = f32[2,8,64,8,2,64]{2,1,5,3,4,0:T(8,128)} copy(f32[2,8,64,8,2,64]{5,3,2,0,4,1:T(8,128)} %bitcast.105) | data formatting | bytes 8388608 | tf_op jit(solution)/shard_map/vmap(vmap())/convert_element_type | solution.py:66
  134.9 7.5 %reshape.77 = f32[2,512,8,2,64]{1,4,2,3,0:T(8,128)} reshape(f32[2,8,64,8,2,64]{2,1,5,3,4,0:T(8,128)} %copy.118) | data formatting | bytes 8388608 | tf_op jit(solution)/shard_map/vmap(vmap())/convert_element_type | solution.py:66
  142.4 3.0 convert_reduce_fusion.1
  145.6 3.8 %fusion.7 = bf16[2,2,512,512]{2,3,1,0:T(8,128)(2,1)} fusion(f32[2,512,8,2,64]{1,4,2,3,0:T(8,128)} %reshape.77, f32[2,2,512]{2,1,0:T(2,128)S(1)} %copy.105), kind=kLoop, calls=%fused_computation.15 | loop fusion | flops 2097152 | bytes 6299648 | tf_op jit(solution)/shard_map/vmap(vmap())/convert_element_type | solution.py:68
  149.4 1.9 slice.77
  151.4 0.2 copy.132
  151.5 10.4 %collective-permute-done = bf16[2,514,1,2,512]{4,3,2,1,0:T(2,128)(2,1)} collective-permute-done((bf16[2,514,1,2,512]{4,3,2,1,0:T(2,128)(2,1)}, bf16[2,514,1,2,512]{4,3,2,1,0:T(2,128)(2,1)}, u32[]{:S(2)}, u32[]{:S(2)}) %collective-permute-start) | collective-permute-done | bytes 2105376 | tf_op jit(solution)/shard_map/ppermute | solution.py:16
  162.0 1.9 slice.76
  163.9 0.2 copy.131
  164.1 0.9 maximum_bitcast_fusion
  165.1 0.9 convert_reduce_fusion
  166.0 1.0 copy-done.3
  167.0 4.2 %abs_reduce_fusion = (f32[2,2,512]{2,1,0:T(2,128)S(1)}, f32[2,2,512,512]{2,3,1,0:T(8,128)}) fusion(f32[512,512]{0,1:T(8,128)S(1)} %copy-done.3, f32[2,2,1024]{2,1,0:T(2,128)S(1)} %get-tuple-element.10, bf16[2,514,2,1024]{3,1,2,0:T(8,128)(2,1)S(1)} %maximum_bitcast_fusion, f32[2,2,1024]{2,1,0:T(2,128)S(1)} %get-tuple-element.15), kind=kOutput, calls=%fused_computation.24 | convolution fusion | flops 2165307392 | bytes 13688832 | tf_op jit(solution)/shard_map/vmap(vmap())/dot_general | solution.py:38
  171.3 3.6 subtract_convert_fusion.3
  174.9 1.2 fusion.21
  176.1 0.9 copy-done.7
  177.1 1.5 fusion.18
  178.5 1.3 subtract_convert_fusion.2
  179.8 1.3 convolution_convert_fusion.2
  181.1 1.3 convolution_convert_fusion.1
  182.4 1.3 subtract_convert_fusion.1
  183.7 2.6 convolution_convert_fusion
  186.3 2.6 fusion.39
  188.9 1.4 multiply_reduce_fusion
  190.4 7.4 %fusion.25 = f32[2,2,512,512]{3,2,1,0:T(8,128)} fusion(bf16[2,2,512,512]{3,2,1,0:T(8,128)(2,1)} %convolution_convert_fusion, bf16[2,2,512,512]{3,2,1,0:T(8,128)(2,1)} %fusion.39, f32[512,512]{1,0:T(8,128)S(1)} %fusion.27), kind=kOutput, calls=%fused_computation.41 | convolution fusion | flops 2150629376 | bytes 9437184 | tf_op jit(solution)/shard_map/vmap(vmap())/dot_general | solution.py:56
  197.7 5.9 %fusion.34 = f32[2,2,1,512]{3,2,1,0:T(1,128)S(1)} fusion(f32[2,2,512,512]{3,2,1,0:T(8,128)} %fusion.25, f32[2,2,512,1]{2,1,0,3:T(2,128)S(1)} %bitcast.113), kind=kOutput, calls=%fused_computation.56 | convolution fusion | flops 12582912 | bytes 4210688 | tf_op jit(solution)/shard_map/vmap(vmap())/dot_general | solution.py:61
  203.7 3.6 fusion.32
  207.4 1.7 add_convert_fusion.1
  209.1 6.6 %copy.119 = bf16[2,2,512,8,64]{4,3,1,0,2:T(8,128)(2,1)} copy(bf16[2,2,512,8,64]{2,4,3,1,0:T(8,128)(2,1)S(1)} %bitcast.111) | data formatting | bytes 4194304 | tf_op jit(solution)/shard_map/vmap(vmap())/reshape | solution.py:73
  215.7 4.8 %bitcast_bitcast_fusion = bf16[512,2,2,8,64]{4,3,2,1,0:T(8,128)(2,1)} fusion(bf16[2,2,512,8,64]{4,3,1,0,2:T(8,128)(2,1)} %copy.119), kind=kLoop, calls=%fused_computation.68 | loop fusion | bytes 4194304
  220.6 6.4 %reshape.88 = bf16[8,2,65536]{2,1,0:T(2,128)(2,1)S(1)} reshape(bf16[512,2,2,8,64]{4,3,2,1,0:T(8,128)(2,1)} %bitcast_bitcast_fusion) | data formatting | bytes 4194304
  226.9 54.0 %all_to_all.45 = bf16[8,2,65536]{2,1,0:T(2,128)(2,1)} all-to-all(bf16[8,2,65536]{2,1,0:T(2,128)(2,1)S(1)} %reshape.88), channel_id=1, replica_groups=mesh['sub'=4,'mem'=8] {'mem'}, dimensions={0} | all-to-all | bytes 4194304 | tf_op jit(solution)/shard_map/all_to_all | solution.py:107
  280.9 7.4 %reshape.89 = bf16[512,2,2,8,64]{4,3,2,1,0:T(8,128)(2,1)} reshape(bf16[8,2,65536]{2,1,0:T(2,128)(2,1)} %all_to_all.45) | data formatting | bytes 4194304
  288.3 8.2 %copy.120 = bf16[2,64,8,8,2,64]{5,4,3,1,2,0:T(2,128)(2,1)} copy(bf16[2,64,8,8,2,64]{5,2,4,0,1,3:T(8,128)(2,1)} %bitcast.109) | data formatting | bytes 4194304 | tf_op jit(solution)/shard_map/all_to_all | solution.py:107
  296.5 9.4 %reshape.73 = bf16[2,64,8,1024]{3,1,2,0:T(8,128)(2,1)S(1)} reshape(bf16[2,64,8,8,2,64]{5,4,3,1,2,0:T(2,128)(2,1)} %copy.120) | data formatting | bytes 4194304 | tf_op jit(solution)/shard_map/reshape | solution.py:108
  306.0 0.2 fusion.38
  306.2 1.5 collective-permute-start.3
  307.6 0.6 collective-permute-start.2
  308.2 24.1 %collective-permute-done.3 = bf16[2,64,4,1024]{3,1,2,0:T(8,128)(2,1)S(1)} collective-permute-done((bf16[2,64,4,1024]{3,1,2,0:T(8,128)(2,1)S(1)}, bf16[2,64,4,1024]{3,1,2,0:T(8,128)(2,1)S(1)}, u32[]{:S(2)}, u32[]{:S(2)}) %collective-permute-start.3) | collective-permute-done | bytes 1048608 | tf_op jit(solution)/shard_map/ppermute | solution.py:19
  332.3 20.9 %collective-permute-done.2 = bf16[2,64,4,1024]{3,1,2,0:T(8,128)(2,1)S(1)} collective-permute-done((bf16[2,64,4,1024]{3,1,2,0:T(8,128)(2,1)S(1)}, bf16[2,64,4,1024]{3,1,2,0:T(8,128)(2,1)S(1)}, u32[]{:S(2)}, u32[]{:S(2)}) %collective-permute-start.2) | collective-permute-done | bytes 1048608 | tf_op jit(solution)/shard_map/ppermute | solution.py:16
  353.2 0.9 maximum_convert_fusion
  354.1 3.7 %multiply_add_fusion = f32[2,64,14,1024]{3,1,2,0:T(8,128)S(1)} fusion(f32[2,64,16,1024]{3,1,2,0:T(8,128)S(1)} %maximum_convert_fusion, f32[2,1024]{1,0:T(2,128)S(1)} %get-tuple-element.12, f32[2,1024]{1,0:T(2,128)S(1)} %get-tuple-element.11), kind=kLoop, calls=%fused_computation.6 | loop fusion | flops 14680064 | bytes 29376512 | tf_op jit(solution)/shard_map/add | solution.py:78
  357.9 2.5 multiply_add_fusion.1
  360.3 2.7 multiply_add_fusion.2
  363.0 1.8 add_convert_fusion
  364.8 2.5 copy.121
  (40 shorter events, 0.6 us)
Async XLA Ops:
  4.1 55.4 %all-to-all-start.1 = ((bf16[2,64,1,16,512]{4,1,2,0,3:T(8,128)(2,1)}), bf16[2,64,1,16,512]{4,1,2,0,3:T(8,128)(2,1)S(1)}, u32[]{:S(2)}, u32[]{:S(2)}) async-start(bf16[2,64,1,16,512]{4,1,2,0,3:T(8,128)(2,1)} %copy.107), calls=%async_computation.1 | async-start | bytes 4194304 | tf_op jit(solution)/shard_map/all_to_all | solution.py:92
  22.0 41.8 %copy-start.5 = (bf16[2,1,2,512]{3,2,1,0:T(2,128)(2,1)S(1)}, bf16[2,1,2,512]{3,2,1,0:T(2,128)(2,1)}, u32[]{:S(2)}) copy-start(bf16[2,1,2,512]{3,2,1,0:T(2,128)(2,1)} %param.8) | copy-start | bytes 12292
  22.0 41.8 %copy-start.6 = (bf16[2,1,2,512]{3,2,1,0:T(2,128)(2,1)S(1)}, bf16[2,1,2,512]{3,2,1,0:T(2,128)(2,1)}, u32[]{:S(2)}) copy-start(bf16[2,1,2,512]{3,2,1,0:T(2,128)(2,1)} %param.7) | copy-start | bytes 12292
  59.5 53.4 %all-to-all-start = ((bf16[8,2,65536]{2,1,0:T(2,128)(2,1)}), bf16[8,2,65536]{2,1,0:T(2,128)(2,1)}, u32[]{:S(2)}, u32[]{:S(2)}) async-start(bf16[8,2,65536]{2,1,0:T(2,128)(2,1)} %reshape.86), calls=%async_computation | async-start | bytes 4194304 | tf_op jit(solution)/shard_map/all_to_all | solution.py:91
  67.5 81.9 %collective-permute-start.1 = (bf16[2,514,1,2,512]{4,3,2,1,0:T(2,128)(2,1)}, bf16[2,514,1,2,512]{4,3,2,1,0:T(2,128)(2,1)}, u32[]{:S(2)}, u32[]{:S(2)}) collective-permute-start(bf16[2,514,1,2,512]{4,3,2,1,0:T(2,128)(2,1)} %copy.112), channel_id=1, source_target_pairs={{8,0},{16,8},{24,16},{0,24},{9,1},{17,9},{25,17},{1,25},{10,2},{18... | collective-permute-start | bytes 6316040 | tf_op jit(solution)/shard_map/ppermute | solution.py:19
  70.0 92.0 %collective-permute-start = (bf16[2,514,1,2,512]{4,3,2,1,0:T(2,128)(2,1)}, bf16[2,514,1,2,512]{4,3,2,1,0:T(2,128)(2,1)}, u32[]{:S(2)}, u32[]{:S(2)}) collective-permute-start(bf16[2,514,1,2,512]{4,3,2,1,0:T(2,128)(2,1)} %copy.112), channel_id=1, source_target_pairs={{0,8},{8,16},{16,24},{24,0},{1,9},{9,17},{17,25},{25,1},{2,10},{10... | collective-permute-start | bytes 6316040 | tf_op jit(solution)/shard_map/ppermute | solution.py:16
  165.0 6.2 %copy-start = (bf16[2,514,2,1024]{3,1,2,0:T(8,128)(2,1)}, bf16[2,514,2,1024]{3,1,2,0:T(8,128)(2,1)S(1)}, u32[]{:S(2)}) copy-start(bf16[2,514,2,1024]{3,1,2,0:T(8,128)(2,1)S(1)} %maximum_bitcast_fusion) | copy-start | bytes 12632068
  165.0 2.0 copy-start.3
  174.9 2.2 copy-start.7
  182.4 6.5 %slice-start = ((s8[4259840]{0:T(1024)(128)(4,1)}), s8[4194304]{0:T(1024)(128)(4,1)S(1)}, s32[]{:S(2)}) async-start(s8[4259840]{0:T(1024)(128)(4,1)} %bitcast.103), calls=%async_computation.3 | async-start | bytes 8388608
  183.7 5.2 %slice-start.1 = ((s8[4259840]{0:T(1024)(128)(4,1)}), s8[65536]{0:T(1024)(128)(4,1)S(1)}, s32[]{:S(2)}) async-start(s8[4259840]{0:T(1024)(128)(4,1)} %bitcast.103), calls=%async_computation.4 | async-start | bytes 131072
  197.7 5.9 %copy-start.1 = (f32[2,2,512,512]{3,2,1,0:T(8,128)S(1)}, f32[2,2,512,512]{3,2,1,0:T(8,128)}, u32[]{:S(2)}) copy-start(f32[2,2,512,512]{3,2,1,0:T(8,128)} %fusion.25) | copy-start | bytes 12582916
  197.7 9.7 %copy-start.2 = (bf16[2,2,512,512]{2,3,1,0:T(8,128)(2,1)S(1)}, bf16[2,2,512,512]{2,3,1,0:T(8,128)(2,1)}, u32[]{:S(2)}) copy-start(bf16[2,2,512,512]{2,3,1,0:T(8,128)(2,1)} %fusion.7) | copy-start | bytes 6291460
  296.5 11.7 %copy-start.4 = (f32[2,1024]{1,0:T(2,128)S(1)}, f32[2,1024]{1,0:T(2,128)}, u32[]{:S(2)}) copy-start(f32[2,1024]{1,0:T(2,128)} %param.9) | copy-start | bytes 24580
  306.2 26.1 %collective-permute-start.3 = (bf16[2,64,4,1024]{3,1,2,0:T(8,128)(2,1)S(1)}, bf16[2,64,4,1024]{3,1,2,0:T(8,128)(2,1)S(1)}, u32[]{:S(2)}, u32[]{:S(2)}) collective-permute-start(bf16[2,64,4,1024]{3,1,2,0:T(8,128)(2,1)S(1)} %get-tuple-element.8), channel_id=1, source_target_pairs={{8,0},{16,8},{24,16},{0,24},{9,1},{17,9},{25,17},{1,25},{10,2},{18... | collective-permute-start | bytes 3145736 | tf_op jit(solution)/shard_map/ppermute | solution.py:19
  307.6 45.5 %collective-permute-start.2 = (bf16[2,64,4,1024]{3,1,2,0:T(8,128)(2,1)S(1)}, bf16[2,64,4,1024]{3,1,2,0:T(8,128)(2,1)S(1)}, u32[]{:S(2)}, u32[]{:S(2)}) collective-permute-start(bf16[2,64,4,1024]{3,1,2,0:T(8,128)(2,1)S(1)} %get-tuple-element.7), channel_id=1, source_target_pairs={{0,8},{8,16},{16,24},{24,0},{1,9},{9,17},{17,25},{25,1},{2,10},{10... | collective-permute-start | bytes 3145736 | tf_op jit(solution)/shard_map/ppermute | solution.py:16
where the time goes:
time: 374 us; the launch traced here: 368 us
  waiting for transfers between devices  126 us (34%)
  local copies, waits for them, and re-layouts  103 us (28%)
  blocking collectives  54 us (14%)
  matrix products  39.3 us (11%)
  other arithmetic  28.8 us (8%)
  starting transfers between devices  15.7 us (4%)
    all_to_all x1, blocking collectives, advance(): lax.all_to_all(analysis, 'mem', split_axis=1, concat_axis=3, tiled=True)  54 us
    all_to_all x1, waiting for transfers between devices, advance(): lax.all_to_all(grid_view, 'mem', split_axis=3, concat_axis=1, tiled=True)  40.7 us
    unnamed x28, local copies, waits for them, and re-layouts  39.9 us
    ppermute x2, waiting for transfers between devices, extended(): lax.ppermute(lax.slice_in_dim(block, block.shape[dim] - width, None, axis...  31.3 us
    all_to_all x1, waiting for transfers between devices, advance(): lax.all_to_all(hx_values, 'mem', split_axis=3, concat_axis=1, tiled=True)  29.9 us
    ppermute x2, waiting for transfers between devices, extended(): lax.ppermute(lax.slice_in_dim(block, 0, width, axis=dim), axis, backward)  24.1 us
    convert_element_type x2, local copies, waits for them, and re-layouts, patch_update(): member_vals = members.reshape(total, -1).astype(jnp.float32)  15.7 us
    dot_general x4, matrix products, patch_update(): jnp.dot(correction_half, inv_iterate.astype(jnp.bfloat16), preferred_elem...  12.4 us
  transfers between devices with their start and end apart: 6, of which 5 were waited for; matrix products, arithmetic and copies ran while one was open for 17% of the time, Pallas kernels for 0%

commit v1 on v0

v1 whole, which is shorter than its diff:
```python
import jax
import jax.numpy as jnp
import numpy as np
from jax import lax
from jax.experimental import pallas as pl
from jax.experimental.pallas import tpu as pltpu
from jax.sharding import PartitionSpec as P

ITERS = 4
STEPS = 4
F32 = jnp.float32
BF16 = jnp.bfloat16
VMEM_LIMIT = 48 * 1024 * 1024


def params(count):
    return pltpu.CompilerParams(
        dimension_semantics=("arbitrary",) * count, vmem_limit_bytes=VMEM_LIMIT
    )


def permutation(order):
    matrix = np.zeros((order.size, order.size), np.float32)
    matrix[np.arange(order.size), order.reshape(-1)] = 1.0
    return matrix.astype(jnp.bfloat16)


def permuted(matrix, rows):
    return jnp.dot(matrix, rows, preferred_element_type=F32).astype(BF16)


def pack_obs_kernel(order, rows, out):
    _, width, owners, block, own = out.shape
    flat = rows[...].reshape(order.shape[0], own)
    out[...] = permuted(order[...], flat).reshape(1, width, owners, block, own)


def pack_obs(hx_values, width):
    slabs, local, _, patches, own = hx_values.shape
    owners = patches // width
    block = 16
    index = np.arange(block * patches).reshape(block, owners, width)
    order = permutation(index.transpose(2, 1, 0))
    return pl.pallas_call(
        pack_obs_kernel,
        grid=(slabs, local // block),
        in_specs=[
            pl.BlockSpec(order.shape, lambda s, g: (0, 0)),
            pl.BlockSpec((1, block, 1, patches, own), lambda s, g: (s, g, 0, 0, 0)),
        ],
        out_specs=pl.BlockSpec((1, width, owners, block, own), lambda s, g: (s, 0, 0, g, 0)),
        out_shape=jax.ShapeDtypeStruct((slabs, width, owners, local, own), BF16),
        compiler_params=params(2),
    )(order, hx_values)


def lane_order(width, lanes):
    index = np.arange(width * lanes).reshape(width, width, lanes // width)
    return permutation(index.transpose(1, 0, 2)).T


def pack_state_kernel(order, swap, cells, out):
    _, width, owners, block, size = out.shape
    lanes = cells.shape[3] // owners
    tiles = size // lanes
    rows = permuted(order[...], cells[...].reshape(order.shape[0], cells.shape[3]))
    parts = []
    for owner in range(owners):
        for tile in range(tiles):
            pieces = [
                rows[
                    (half * tiles + tile) * block : (half * tiles + tile + 1) * block,
                    owner * lanes : (owner + 1) * lanes,
                ]
                for half in range(width)
            ]
            parts.append(jnp.concatenate(pieces, axis=1))
    mixed = permuted_lanes(jnp.concatenate(parts, axis=0), swap[...])
    for owner in range(owners):
        for tile in range(tiles):
            at = (owner * tiles + tile) * block
            for part in range(width):
                out[0, part, owner, :, tile * lanes : (tile + 1) * lanes] = mixed[
                    at : at + block, part * lanes : (part + 1) * lanes
                ]


def permuted_lanes(rows, matrix):
    return jnp.dot(rows, matrix, preferred_element_type=F32).astype(BF16)


def pack_state(member_state, width, owners):
    slabs, local, cells_a, cols = member_state.shape
    lanes = cols // owners
    size = cells_a * lanes // width
    block = 32
    index = np.arange(block * cells_a).reshape(block, cells_a)
    order = permutation(index.T)
    swap = lane_order(width, lanes)
    return pl.pallas_call(
        pack_state_kernel,
        grid=(slabs, local // block),
        in_specs=[
            pl.BlockSpec(order.shape, lambda s, g: (0, 0)),
            pl.BlockSpec(swap.shape, lambda s, g: (0, 0)),
            pl.BlockSpec((1, block, cells_a, cols), lambda s, g: (s, g, 0, 0)),
        ],
        out_specs=pl.BlockSpec((1, width, owners, block, size), lambda s, g: (s, 0, 0, g, 0)),
        out_shape=jax.ShapeDtypeStruct((slabs, width, owners, local, size), BF16),
        compiler_params=params(2),
    )(order, swap, member_state)


def unpack_state_kernel(order, swap, packed, out):
    _, width, owners, block, size = packed.shape
    cells_a = out.shape[2]
    tiles = cells_a // width
    lanes = size // tiles
    parts = []
    for owner in range(owners):
        for tile in range(tiles):
            pieces = [
                packed[0, part, owner, :, tile * lanes : (tile + 1) * lanes]
                for part in range(width)
            ]
            parts.append(jnp.concatenate(pieces, axis=1))
    mixed = permuted_lanes(jnp.concatenate(parts, axis=0), swap[...])
    columns = []
    for owner in range(owners):
        rows = []
        for cell in range(cells_a):
            half, tile = cell // tiles, cell % tiles
            at = (owner * tiles + tile) * block
            rows.append(mixed[at : at + block, half * lanes : (half + 1) * lanes])
        columns.append(jnp.concatenate(rows, axis=0))
    rows = permuted(order[...], jnp.concatenate(columns, axis=1))
    out[...] = rows.reshape(out.shape)


def unpack_state(packed, cells_a):
    slabs, width, owners, local, size = packed.shape
    lanes = size * width // cells_a
    cols = owners * lanes
    block = 32
    index = np.arange(block * cells_a).reshape(cells_a, block)
    order = permutation(index.T)
    swap = lane_order(width, lanes).T
    return pl.pallas_call(
        unpack_state_kernel,
        grid=(slabs, local // block),
        in_specs=[
            pl.BlockSpec(order.shape, lambda s, g: (0, 0)),
            pl.BlockSpec(swap.shape, lambda s, g: (0, 0)),
            pl.BlockSpec((1, width, owners, block, size), lambda s, g: (s, 0, 0, g, 0)),
        ],
        out_specs=pl.BlockSpec((1, block, cells_a, cols), lambda s, g: (s, g, 0, 0)),
        out_shape=jax.ShapeDtypeStruct((slabs, local, cells_a, cols), BF16),
        compiler_params=params(2),
    )(order, swap, packed)


def dot_bf16(left, right):
    return jnp.dot(left, right, preferred_element_type=F32)


def transform_kernel(before, middle, after, obs, scale, out, pert, weighted):
    total = middle.shape[1]
    half = before.shape[2]
    projected = jnp.zeros((total, 1), F32)
    start = 0
    for part in (before, middle, after):
        span = part.shape[2]
        for at in range(0, span, half):
            cols = slice(start, start + half)
            values = part[0, :, at : at + half].astype(F32)
            mean = jnp.sum(values, axis=0, keepdims=True) * (1.0 / total)
            centred = values - mean
            pert[:, cols] = centred.astype(BF16)
            scaled = (centred * scale[0, :, cols]).astype(BF16)
            weighted[:, cols] = scaled
            innovation = obs[0, :, cols] - mean
            projected += jnp.sum(scaled.astype(F32) * innovation, axis=1, keepdims=True)
            start += half
    rows = lax.broadcasted_iota(jnp.int32, (total, total), 0)
    columns = lax.broadcasted_iota(jnp.int32, (total, total), 1)
    diagonal = rows == columns
    gram = lax.dot_general(
        weighted[...], pert[...], (((1,), (1,)), ((), ())), preferred_element_type=F32
    )
    system = jnp.where(diagonal, total - 1.0, 0.0) + gram
    bound = jnp.max(jnp.sum(jnp.abs(system), axis=1, keepdims=True), axis=0, keepdims=True)
    root = (system / bound).astype(BF16)
    inverse = None
    for iteration in range(ITERS):
        product = root.astype(F32) if inverse is None else dot_bf16(inverse.astype(BF16), root)
        correction = (jnp.where(diagonal, 1.5, 0.0) - 0.5 * product).astype(BF16)
        if iteration + 1 < ITERS:
            root = dot_bf16(root, correction).astype(BF16)
        if inverse is None:
            inverse = correction.astype(F32)
        else:
            inverse = dot_bf16(correction, inverse.astype(BF16))
    flipped = inverse.T
    halfway = jnp.sum(flipped * projected, axis=0, keepdims=True)
    weight = jnp.sum(inverse * halfway, axis=1, keepdims=True)
    weight = jnp.broadcast_to(weight, (total, 128)).T[0:1, :] / bound
    out[0] = (jnp.sqrt((total - 1.0) / bound) * flipped + weight).astype(BF16)


def transforms(hx_rows, obs_rows, scale_rows, count, wraps):
    total, own = hx_rows.shape[1:]
    half = own // 2
    held = hx_rows.shape[0]
    shift = 0 if wraps else 1
    flops = count * (2 * total * total * 2 * own + 18 * total**3)
    return pl.pallas_call(
        transform_kernel,
        grid=(count,),
        in_specs=[
            pl.BlockSpec((1, total, half), lambda a: ((a + shift + held - 1) % held, 0, 1)),
            pl.BlockSpec((1, total, own), lambda a: (a + shift, 0, 0)),
            pl.BlockSpec((1, total, half), lambda a: ((a + shift + 1) % held, 0, 0)),
            pl.BlockSpec((1, 1, 2 * own), lambda a: (a, 0, 0)),
            pl.BlockSpec((1, 1, 2 * own), lambda a: (a, 0, 0)),
        ],
        out_specs=pl.BlockSpec((1, total, total), lambda a: (a, 0, 0)),
        out_shape=jax.ShapeDtypeStruct((count, total, total), BF16),
        scratch_shapes=[pltpu.VMEM((total, 2 * own), BF16), pltpu.VMEM((total, 2 * own), BF16)],
        compiler_params=params(1),
        cost_estimate=pl.CostEstimate(
            flops=flops, bytes_accessed=4 * count * total * total * 2, transcendentals=0
        ),
    )(hx_rows, hx_rows, hx_rows, obs_rows, scale_rows)


def centre(state, pert, means):
    for a in range(state.shape[0]):
        values = state[a].astype(F32)
        mean = jnp.sum(values, axis=0, keepdims=True) * (1.0 / state.shape[1])
        means[a] = mean
        pert[a] = (values - mean).astype(BF16)


def transport(tiles, here, ahead, behind, low):
    count, depth = len(tiles), len(tiles[0])
    size = tiles[0][0].shape[1]
    shift = size // 2
    for _ in range(STEPS):
        first = [pltpu.roll(column[0], shift, 1) for column in tiles]
        last = [pltpu.roll(column[depth - 1], shift, 1) for column in tiles]
        moved = []
        for a in range(count):
            column = []
            for k in range(depth):
                if k + 1 < depth:
                    after = tiles[a][k + 1]
                else:
                    after = jnp.where(low, first[a], first[(a + 1) % count])
                if k > 0:
                    prior = tiles[a][k - 1]
                else:
                    prior = jnp.where(low, last[(a + count - 1) % count], last[a])
                column.append(here * tiles[a][k] + ahead * after + behind * prior)
            moved.append(column)
        tiles = moved
    return tiles


def forecast_kernel(state, transform, speed, out, pert, means, fields):
    count, block, size = out.shape
    lanes = speed.shape[1]

    @pl.when(pl.program_id(0) == 0)
    def _():
        centre(state, pert, means)

    for a in range(count):
        fields[a] = (dot_bf16(transform[a], pert[a]) + means[a]).astype(BF16)
    chunk = 16
    c = jnp.broadcast_to(speed[...], (chunk, lanes))
    here, ahead, behind = 1.0 - c * c, 0.5 * (c * c - c), 0.5 * (c * c + c)
    low = lax.broadcasted_iota(jnp.int32, (chunk, lanes), 1) < lanes // 2

    def rows_at(step, carry):
        rows = pl.ds(pl.multiple_of(step * chunk, chunk), chunk)
        tiles = [
            [fields[a, rows, k * lanes : (k + 1) * lanes].astype(F32) for k in range(size // lanes)]
            for a in range(count)
        ]
        tiles = transport(tiles, here, ahead, behind, low)
        for a in range(count):
            for k in range(size // lanes):
                out[a, rows, k * lanes : (k + 1) * lanes] = tiles[a][k].astype(BF16)
        return carry

    lax.fori_loop(0, block // chunk, rows_at, 0)


def forecasts(state, transform, speed):
    count, total, size = state.shape
    block = min(total, 256)
    return pl.pallas_call(
        forecast_kernel,
        grid=(total // block,),
        in_specs=[
            pl.BlockSpec((count, total, size), lambda i: (0, 0, 0)),
            pl.BlockSpec((count, block, total), lambda i: (0, i, 0)),
            pl.BlockSpec(speed.shape, lambda i: (0, 0)),
        ],
        out_specs=pl.BlockSpec((count, block, size), lambda i: (0, i, 0)),
        out_shape=jax.ShapeDtypeStruct((count, total, size), BF16),
        scratch_shapes=[
            pltpu.VMEM((count, total, size), BF16),
            pltpu.VMEM((count, 1, size), F32),
            pltpu.VMEM((count, block, size), BF16),
        ],
        compiler_params=params(1),
    )(state, transform, speed)


def analysis_kernel(state, transform, out, pert, means):
    centre(state, pert, means)
    out[0] = (dot_bf16(transform[0], pert[0]) + means[0]).astype(BF16)


def analyses(state, transform):
    count, total, size = state.shape
    return pl.pallas_call(
        analysis_kernel,
        grid=(count,),
        in_specs=[
            pl.BlockSpec((1, total, size), lambda a: (a, 0, 0)),
            pl.BlockSpec((1, total, total), lambda a: (a, 0, 0)),
        ],
        out_specs=pl.BlockSpec((1, total, size), lambda a: (a, 0, 0)),
        out_shape=jax.ShapeDtypeStruct((count, total, size), BF16),
        scratch_shapes=[pltpu.VMEM((1, total, size), BF16), pltpu.VMEM((1, 1, size), F32)],
        compiler_params=params(1),
    )(state, transform)


def shared_transport(analysis, speed, width, jump):
    count, total, size = analysis.shape
    lanes = speed.shape[1]
    cells = lanes // width
    tiles = size // lanes
    fields = widened(analysis, jump).reshape(count + 2, total, tiles, width, cells)
    fields = fields.transpose(1, 0, 3, 2, 4).reshape(total, -1, cells).astype(F32)
    c = speed[0, :cells]
    for _ in range(STEPS):
        prior, here, after = fields[:, :-2], fields[:, 1:-1], fields[:, 2:]
        fields = (1.0 - c * c) * here + 0.5 * (c * c - c) * after + 0.5 * (c * c + c) * prior
    spare = tiles * width - STEPS
    fields = fields[:, spare : fields.shape[1] - spare].astype(BF16)
    fields = fields.reshape(total, count, width, tiles, cells)
    return fields.transpose(1, 0, 3, 2, 4).reshape(count, total, size)


def widened(blocks, jump):
    count = lax.axis_size("sub")
    forward = [(i, (i + jump) % count) for i in range(count)]
    backward = [(target, source) for source, target in forward]
    low = lax.ppermute(blocks[-1:], "sub", forward)
    high = lax.ppermute(blocks[:1], "sub", backward)
    return jnp.concatenate([low, blocks, high], axis=0)


def advance(member_state, hx_values, obs_value, obs_var, courant):
    slabs, local, cells_a, cols = member_state.shape
    patches, own = hx_values.shape[3:]
    owners = lax.axis_size("mem")
    lines = lax.axis_size("sub")
    width = patches // owners
    count = slabs * width
    groups = lines // count
    total = local * owners
    cells_b = cols // patches
    lane_cells = width * cells_b
    place = lax.axis_index("sub") % count
    slab, part = place // width, place % width

    index_groups = None
    if groups > 1:
        held = count * owners
        index_groups = [list(range(g * held, (g + 1) * held)) for g in range(groups)]

    def exchange(blocks):
        return lax.all_to_all(
            blocks,
            ("sub", "mem"),
            split_axis=0,
            concat_axis=0,
            tiled=True,
            axis_index_groups=index_groups,
        )

    hx_rows = exchange(pack_obs(hx_values, width).reshape(count * owners, local, own))
    hx_rows = hx_rows.reshape(count, total, own)

    stats = jnp.stack([obs_value[:, 0], obs_var[:, 0]], axis=2)
    stats = lax.all_gather(stats, "sub", axis=0)
    stats = lax.dynamic_slice(stats, (0, slab, part, 0, 0), (lines, 1, 1, 2, own))
    stats = stats.reshape(lines, 2, own).astype(F32)
    half = own // 2
    stats = jnp.concatenate(
        [jnp.roll(stats, 1, 0)[:, :, half:], stats, jnp.roll(stats, -1, 0)[:, :, :half]], axis=2
    )
    if groups > 1:
        first = lax.axis_index("sub") // count * count
        stats = lax.dynamic_slice_in_dim(stats, first, count, axis=0)
    taper = (jnp.arange(half, dtype=F32) + 1.0) / (half + 1.0)
    local_weight = jnp.concatenate([taper, jnp.ones((own,), F32), taper[::-1]])
    obs_rows = stats[:, 0:1]
    scale_rows = local_weight / stats[:, 1:2]

    state = exchange(pack_state(member_state, width, owners).reshape(count * owners, local, -1))
    state = state.reshape(count, total, -1)

    held_rows = hx_rows if groups == 1 else widened(hx_rows, count)
    transform = transforms(held_rows, obs_rows, scale_rows, count, groups == 1)

    column = (lax.axis_index("mem") * width + part) * cells_b
    speed = lax.dynamic_slice(courant, (slab, column), (1, cells_b))
    speed = jnp.concatenate([speed] * width, axis=1)
    if groups == 1 and width == 2:
        fields = forecasts(state, transform, speed)
    else:
        fields = shared_transport(analyses(state, transform), speed, width, count)
    back = exchange(fields.reshape(count * owners, local, -1))
    return unpack_state(back.reshape(slabs, width, owners, local, -1), cells_a)


def solution(mesh):
    in_specs = (
        P(None, "mem", "sub", None),
        P(None, "mem", "sub", None, None),
        P(None, "sub", "mem", None),
        P(None, "sub", "mem", None),
        P(),
    )
    out_specs = P(None, "mem", "sub", None)
    return jax.shard_map(advance, mesh=mesh, in_specs=in_specs, out_specs=out_specs, check_vma=False)
```

time: 374 us -> 187 us (0.50); the launches traced: 368 us -> 187 us
  local copies, waits for them, and re-layouts: 103 us -> 7.39 us
  waiting for transfers between devices: 126 us -> 56.7 us
  Pallas kernels: 0 us -> 42.1 us
  matrix products: 39.3 us -> 0 us
  other arithmetic: 28.8 us -> 0.18 us
  blocking collectives: 54 us -> 69.7 us
  starting transfers between devices: 15.7 us -> 10.3 us
    ppermute x4 -> x0, waiting for transfers between devices: 55.4 us -> none  [the longest x2 31.3 us: extended(): lax.ppermute(lax.slice_in_dim(block, block.shape[dim] - width, None, axis...]
    pallas_call x0 -> x5, Pallas kernels: none -> 42.1 us  [the longest x1 19.7 us: transforms(): pl.pallas_call(transform_kernel, grid=(count,), in_specs=[pl.BlockSpec((1...]
    dot_general x14 -> x0, matrix products: 39.3 us -> none  [the longest x4 12.4 us: patch_update(): jnp.dot(correction_half, inv_iterate.astype(jnp.bfloat16), preferred_elem...]
    unnamed x28 -> x22, local copies, waits for them, and re-layouts: 39.9 us -> 6.48 us
    reshape x4 -> x0, local copies, waits for them, and re-layouts: 27.7 us -> none  [the longest x2 11.6 us: advance(): member_state.reshape(slab_count, local_members, cells_a, patches_line, ce...]
    convert_element_type x3 -> x0, local copies, waits for them, and re-layouts: 18.2 us -> none  [the longest x2 15.7 us: patch_update(): member_vals = members.reshape(total, -1).astype(jnp.float32)]
    all_gather x0 -> x1, blocking collectives: none -> 17.7 us  [advance(): stats = lax.all_gather(stats, 'sub', axis=0)]
    all_to_all x2, waiting for transfers between devices: 70.6 us -> 56.7 us  [exchange(): lax.all_to_all(blocks, ('sub', 'mem'), split_axis=0, concat_axis=0, tiled...]
  transfers between devices with their start and end apart: 6 -> 2, of which waited for: 5 -> 2; matrix products, arithmetic and copies ran while one was open for 17% -> 1% of each run, Pallas kernels for 0% -> 12%
where the time goes in v1:
time: 187 us
  blocking collectives  69.7 us (37%)
  waiting for transfers between devices  56.7 us (30%)
  Pallas kernels  42.1 us (23%)
  starting transfers between devices  10.3 us (6%)
  local copies, waits for them, and re-layouts  7.39 us (4%)
    all_to_all x2, waiting for transfers between devices, exchange(): lax.all_to_all(blocks, ('sub', 'mem'), split_axis=0, concat_axis=0, tiled...  56.7 us
    all_to_all x1, blocking collectives, exchange(): lax.all_to_all(blocks, ('sub', 'mem'), split_axis=0, concat_axis=0, tiled...  52 us
    pallas_call x1, Pallas kernels, transforms(): pl.pallas_call(transform_kernel, grid=(count,), in_specs=[pl.BlockSpec((1...  19.7 us
    all_gather x1, blocking collectives, advance(): stats = lax.all_gather(stats, 'sub', axis=0)  17.7 us
    pallas_call x1, Pallas kernels, forecasts(): pl.pallas_call(forecast_kernel, grid=(total // block,), in_specs=[pl.Bloc...  14.7 us
    all_to_all x2, starting transfers between devices, exchange(): lax.all_to_all(blocks, ('sub', 'mem'), split_axis=0, concat_axis=0, tiled...  10.3 us
    unnamed x22, local copies, waits for them, and re-layouts  6.48 us
  transfers between devices with their start and end apart: 2, of which 2 were waited for; matrix products, arithmetic and copies ran while one was open for 1% of the time, Pallas kernels for 12%

profile of v1, /device:TPU:0, one launch (start us, length us, event | category | flops | bytes accessed | tf_op | source)
XLA Modules:
  0.0 186.5 jit_solution(3882284163313414064)
XLA Ops:
  0.0 0.0 copy-start.3
  0.0 1.6 copy-done.3
  1.6 0.0 copy-start.7
  1.6 0.9 copy-done.7
  2.5 1.9 %shard_map.101 = bf16[2,2,8,64,512]{4,3,2,1,0:T(8,128)(2,1)S(1)} custom-call(bf16[256,256]{1,0:T(8,128)(2,1)S(1)} %copy-done.7, bf16[2,64,1,16,512]{4,3,2,1,0:T(8,128)(2,1)S(1)} %copy-done.3), custom_call_target="tpu_custom_call" | custom-call | tf_op jit(solution)/shard_map/pallas_call | solution.py:44
  4.5 0.0 copy-start.1
  4.5 1.3 copy-done.1
  5.8 0.0 copy-start.4
  5.8 0.0 copy-start.5
  5.8 0.0 copy-start.8
  5.8 7.4 %all-to-all-start.1 = ((bf16[32,64,512]{2,1,0:T(8,128)(2,1)}), bf16[32,64,512]{2,1,0:T(8,128)(2,1)}, u32[]{:S(2)}, u32[]{:S(2)}) async-start(bf16[32,64,512]{2,1,0:T(8,128)(2,1)} %bitcast.22), calls=%async_computation.1 | async-start | bytes 4194304 | tf_op jit(solution)/shard_map/all_to_all | solution.py:388
  13.2 0.0 copy-done.4
  13.2 0.0 copy-done.5
  13.2 0.0 copy-done.8
  13.2 2.2 %shard_map.100 = bf16[2,2,8,64,512]{4,3,2,1,0:T(8,128)(2,1)S(1)} custom-call(bf16[256,256]{1,0:T(8,128)(2,1)S(1)} %copy-done.8, bf16[256,256]{1,0:T(8,128)(2,1)S(1)} %copy-done.5, bf16[2,64,8,1024]{3,2,1,0:T(8,128)(2,1)S(1)} %copy-done.4), custom_call_target="tpu_custom_call" | custom-call | tf_op jit(solution)/shard_map/pallas_call | solution.py:100
  15.5 0.0 copy-start
  15.5 1.3 copy-done
  16.8 46.5 %all-to-all-done.1 = bf16[32,64,512]{2,1,0:T(8,128)(2,1)} async-done(((bf16[32,64,512]{2,1,0:T(8,128)(2,1)}), bf16[32,64,512]{2,1,0:T(8,128)(2,1)}, u32[]{:S(2)}, u32[]{:S(2)}) %all-to-all-start.1) | async-done | bytes 2097184 | tf_op jit(solution)/shard_map/all_to_all | solution.py:388
  63.3 0.0 copy-start.9
  63.3 0.0 copy-start.10
  63.3 2.9 %all-to-all-start = ((bf16[32,64,512]{2,1,0:T(8,128)(2,1)}), bf16[32,64,512]{2,1,0:T(8,128)(2,1)S(1)}, u32[]{:S(2)}, u32[]{:S(2)}) async-start(bf16[32,64,512]{2,1,0:T(8,128)(2,1)} %bitcast.21), calls=%async_computation | async-start | bytes 4194304 | tf_op jit(solution)/shard_map/all_to_all | solution.py:388
  66.2 0.1 reverse.4
  66.3 0.0 copy-done.9
  66.3 0.0 copy-done.10
  66.4 17.7 %all-gather = bf16[8,2,2,512]{3,1,0,2:T(2,128)(2,1)S(1)} all-gather(bf16[2,2,2,512]{3,1,0,2:T(2,128)(2,1)S(1)} %pad_maximum_fusion.2), channel_id=2, replica_groups=mesh['sub'=4,'mem'=8] {'sub'}, dimensions={0}, use_global_device_ids=true | all-gather | bytes 40960 | tf_op jit(solution)/shard_map/all_gather | solution.py:401
  84.1 0.8 dynamic_slice.7
  84.8 0.1 pad_maximum_fusion.4.speed
  85.0 19.7 %shard_map.102.transform = bf16[4,512,512]{2,1,0:T(8,128)(2,1)S(1)} custom-call(bf16[4,512,512]{2,1,0:T(8,128)(2,1)} %bitcast.3.before.middle.after, bf16[4,512,512]{2,1,0:T(8,128)(2,1)} %bitcast.3.before.middle.after, bf16[4,512,512]{2,1,0:T(8,128)(2,1)} %bitcast.3.before.middle.after, f32[4,1,1024]{2,1,0:T(1,128)S(1)} %get-tuple-element.6.obs, ...), custom_call_target="tpu_custom_call" | custom-call | flops 11811160064 | bytes 8388608 | tf_op jit(solution)/shard_map/pallas_call | solution.py:216
  104.7 0.0 copy-start.2
  104.8 1.3 copy-done.2
  106.1 10.2 %all-to-all-done = bf16[32,64,512]{2,1,0:T(8,128)(2,1)S(1)} async-done(((bf16[32,64,512]{2,1,0:T(8,128)(2,1)}), bf16[32,64,512]{2,1,0:T(8,128)(2,1)S(1)}, u32[]{:S(2)}, u32[]{:S(2)}) %all-to-all-start) | async-done | bytes 2097184 | tf_op jit(solution)/shard_map/all_to_all | solution.py:388
  116.3 14.7 %shard_map.103 = bf16[4,512,512]{2,1,0:T(8,128)(2,1)S(1)} custom-call(bf16[4,512,512]{2,1,0:T(8,128)(2,1)S(1)} %bitcast.19, bf16[4,512,512]{2,1,0:T(8,128)(2,1)} %copy-done.2, f32[1,128]{1,0:T(1,128)S(1)} %pad_maximum_fusion.4.speed), custom_call_target="tpu_custom_call" | custom-call | tf_op jit(solution)/shard_map/pallas_call | solution.py:302
  130.9 0.0 copy-start.6
  131.0 52.0 %all_to_all.15 = bf16[32,64,512]{2,1,0:T(8,128)(2,1)S(1)} all-to-all(bf16[32,64,512]{2,1,0:T(8,128)(2,1)S(1)} %bitcast.20), channel_id=1, replica_groups=mesh['sub'=4,'mem'=8] {'sub','mem'}, dimensions={0} | all-to-all | bytes 4194304 | tf_op jit(solution)/shard_map/all_to_all | solution.py:388
  183.0 0.0 copy-done.6
  183.0 3.6 %shard_map.104 = bf16[2,64,8,1024]{3,2,1,0:T(8,128)(2,1)} custom-call(bf16[256,256]{1,0:T(8,128)(2,1)S(1)} %copy-done.6, bf16[256,256]{1,0:T(8,128)(2,1)S(1)} %copy-done.5, bf16[2,2,8,64,512]{4,3,2,1,0:T(8,128)(2,1)S(1)} %bitcast.23), custom_call_target="tpu_custom_call" | custom-call | tf_op jit(solution)/shard_map/pallas_call | solution.py:148
  (11 shorter events, 0.2 us)
Async XLA Ops:
  0.0 1.6 copy-start.3
  1.6 0.9 copy-start.7
  4.5 1.3 copy-start.1
  5.8 7.4 %copy-start.4 = (bf16[2,64,8,1024]{3,2,1,0:T(8,128)(2,1)S(1)}, bf16[2,64,8,1024]{3,2,1,0:T(8,128)(2,1)}, u32[]{:S(2)}) copy-start(bf16[2,64,8,1024]{3,2,1,0:T(8,128)(2,1)} %cells.1) | copy-start | bytes 6291460
  5.8 7.5 %copy-start.5 = (bf16[256,256]{1,0:T(8,128)(2,1)S(1)}, bf16[256,256]{1,0:T(8,128)(2,1)}, u32[]{:S(2)}) copy-start(bf16[256,256]{1,0:T(8,128)(2,1)} %constant.63.clone.swap) | copy-start | bytes 393220
  5.8 7.5 %copy-start.8 = (bf16[256,256]{1,0:T(8,128)(2,1)S(1)}, bf16[256,256]{1,0:T(8,128)(2,1)}, u32[]{:S(2)}) copy-start(bf16[256,256]{1,0:T(8,128)(2,1)} %constant.62.clone.order) | copy-start | bytes 393220
  5.8 57.5 %all-to-all-start.1 = ((bf16[32,64,512]{2,1,0:T(8,128)(2,1)}), bf16[32,64,512]{2,1,0:T(8,128)(2,1)}, u32[]{:S(2)}, u32[]{:S(2)}) async-start(bf16[32,64,512]{2,1,0:T(8,128)(2,1)} %bitcast.22), calls=%async_computation.1 | async-start | bytes 4194304 | tf_op jit(solution)/shard_map/all_to_all | solution.py:388
  15.5 1.3 copy-start
  63.3 3.0 %copy-start.9 = (bf16[2,1,2,512]{3,2,1,0:T(2,128)(2,1)S(1)}, bf16[2,1,2,512]{3,2,1,0:T(2,128)(2,1)}, u32[]{:S(2)}) copy-start(bf16[2,1,2,512]{3,2,1,0:T(2,128)(2,1)} %param.13) | copy-start | bytes 12292
  63.3 3.0 %copy-start.10 = (bf16[2,1,2,512]{3,2,1,0:T(2,128)(2,1)S(1)}, bf16[2,1,2,512]{3,2,1,0:T(2,128)(2,1)}, u32[]{:S(2)}) copy-start(bf16[2,1,2,512]{3,2,1,0:T(2,128)(2,1)} %param.12) | copy-start | bytes 12292
  63.3 53.0 %all-to-all-start = ((bf16[32,64,512]{2,1,0:T(8,128)(2,1)}), bf16[32,64,512]{2,1,0:T(8,128)(2,1)S(1)}, u32[]{:S(2)}, u32[]{:S(2)}) async-start(bf16[32,64,512]{2,1,0:T(8,128)(2,1)} %bitcast.21), calls=%async_computation | async-start | bytes 4194304 | tf_op jit(solution)/shard_map/all_to_all | solution.py:388
  104.7 1.3 copy-start.2
  130.9 52.0 %copy-start.6 = (bf16[256,256]{1,0:T(8,128)(2,1)S(1)}, bf16[256,256]{1,0:T(8,128)(2,1)}, u32[]{:S(2)}) copy-start(bf16[256,256]{1,0:T(8,128)(2,1)} %constant.64.clone.order) | copy-start | bytes 393220

commit v2 on v1

v2 whole, which is shorter than its diff:
```python
import jax
import jax.numpy as jnp
from jax import lax
from jax.experimental import pallas as pl
from jax.experimental.pallas import tpu as pltpu
from jax.sharding import PartitionSpec as P

ITERS = 4
STEPS = 4
F32 = jnp.float32
BF16 = jnp.bfloat16
VMEM_LIMIT = 48 * 1024 * 1024
ANY = pl.BlockSpec(memory_space=pl.ANY)


def params(count):
    return pltpu.CompilerParams(
        dimension_semantics=("arbitrary",) * count, vmem_limit_bytes=VMEM_LIMIT
    )


def split(value, size):
    return value >> (size.bit_length() - 1), value & (size - 1)


def iota(rows, cols, dim):
    return lax.broadcasted_iota(jnp.int32, (rows, cols), dim)


def dot_bf16(left, right):
    return jnp.dot(left, right, preferred_element_type=F32)


def moved(left, right):
    return dot_bf16(left, right).astype(BF16)


def ones_at(condition):
    return jnp.where(condition, 1.0, 0.0).astype(BF16)


def start_all(copies):
    for copy in copies:
        copy.start()
    return copies


def wait_all(copies):
    for copy in copies:
        copy.wait()


def place(count):
    return lax.axis_index("sub") & (count - 1), lax.axis_index("mem")


def partners(count, owners):
    column, member = place(count)
    return [
        (r, column ^ (r // owners), member ^ (r % owners)) for r in range(count * owners)
    ]


def send_out(packed, outs, sems):
    count, owners = packed.shape[:2]
    wait_all(
        start_all(
            [
                pltpu.make_async_copy(packed.at[column, member], outs[r], sems.at[r])
                for r, column, member in partners(count, owners)
            ]
        )
    )


def pack_obs_kernel(rows, *rest):
    *outs, order, packed, sems = rest
    _, block, _, patches, own = rows.shape
    owners = packed.shape[1]
    width = patches // owners
    slab, group = pl.program_id(0), pl.program_id(1)
    size = block * patches

    @pl.when((slab == 0) & (group == 0))
    def _():
        rest, member = split(iota(size, size, 0), block)
        part, owner = split(rest, owners)
        order[...] = ones_at(iota(size, size, 1) == member * patches + owner * width + part)

    flat = moved(order[...], rows[...].reshape(size, own))
    here = pl.ds(pl.multiple_of(group * block, block), block)
    packed[pl.ds(slab * width, width), :, here, :] = flat.reshape(width, owners, block, own)

    @pl.when((slab == pl.num_programs(0) - 1) & (group == pl.num_programs(1) - 1))
    def _():
        send_out(packed, outs, sems)


def pack_obs(hx_values, owners):
    slabs, local, _, patches, own = hx_values.shape
    width = patches // owners
    count = slabs * width
    block = 16
    return pl.pallas_call(
        pack_obs_kernel,
        grid=(slabs, local // block),
        in_specs=[pl.BlockSpec((1, block, 1, patches, own), lambda s, g: (s, g, 0, 0, 0))],
        out_specs=[ANY] * (count * owners),
        out_shape=[jax.ShapeDtypeStruct((local, own), BF16)] * (count * owners),
        scratch_shapes=[
            pltpu.VMEM((block * patches, block * patches), BF16),
            pltpu.VMEM((count, owners, local, own), BF16),
            pltpu.SemaphoreType.DMA((count * owners,)),
        ],
        compiler_params=params(2),
        name="pack_obs",
    )(hx_values)


def swapped(width, lanes):
    size = width * lanes
    outer, cell = split(iota(size, size, 1), lanes // width)
    first, second = split(outer, width)
    return ones_at(iota(size, size, 0) == (second * width + first) * (lanes // width) + cell)


def transposed(outer, inner):
    size = outer * inner
    first, second = split(iota(size, size, 0), inner)
    return ones_at(iota(size, size, 1) == second * outer + first)


def pack_state_kernel(cells, _, *rest):
    *outs, order, swap, packed, sems = rest
    owners, _, size = packed.shape[1:]
    block, cells_a, cols = cells.shape[1:]
    lanes = cols // owners
    tiles = size // lanes
    width = cells_a // tiles
    slab, group = pl.program_id(0), pl.program_id(1)

    @pl.when((slab == 0) & (group == 0))
    def _():
        order[...] = transposed(cells_a, block)
        swap[...] = swapped(width, lanes)

    rows = moved(order[...], cells[...].reshape(block * cells_a, cols))
    parts = []
    for owner in range(owners):
        for tile in range(tiles):
            pieces = [
                rows[
                    (half * tiles + tile) * block : (half * tiles + tile + 1) * block,
                    owner * lanes : (owner + 1) * lanes,
                ]
                for half in range(width)
            ]
            parts.append(jnp.concatenate(pieces, axis=1))
    mixed = moved(jnp.concatenate(parts, axis=0), swap[...])
    here = pl.ds(pl.multiple_of(group * block, block), block)
    for owner in range(owners):
        for tile in range(tiles):
            at = (owner * tiles + tile) * block
            for part in range(width):
                packed[slab * width + part, owner, here, tile * lanes : (tile + 1) * lanes] = mixed[
                    at : at + block, part * lanes : (part + 1) * lanes
                ]

    @pl.when((slab == pl.num_programs(0) - 1) & (group == pl.num_programs(1) - 1))
    def _():
        send_out(packed, outs, sems)


def pack_state(member_state, width, owners, after):
    slabs, local, cells_a, cols = member_state.shape
    lanes = cols // owners
    size = cells_a * lanes // width
    count = slabs * width
    block = 32
    return pl.pallas_call(
        pack_state_kernel,
        grid=(slabs, local // block),
        in_specs=[pl.BlockSpec((1, block, cells_a, cols), lambda s, g: (s, g, 0, 0)), ANY],
        out_specs=[ANY] * (count * owners),
        out_shape=[jax.ShapeDtypeStruct((local, size), BF16)] * (count * owners),
        scratch_shapes=[
            pltpu.VMEM((block * cells_a, block * cells_a), BF16),
            pltpu.VMEM((width * lanes, width * lanes), BF16),
            pltpu.VMEM((count, owners, local, size), BF16),
            pltpu.SemaphoreType.DMA((count * owners,)),
        ],
        compiler_params=params(2),
        name="pack_state",
    )(member_state, after)


def unpack_state_kernel(*refs, held):
    blocks = refs[:held]
    out, order, swap, packed, sems = refs[held:]
    count, owners, _, size = packed.shape
    block, cells_a, cols = out.shape[1:]
    lanes = cols // owners
    tiles = size // lanes
    width = cells_a // tiles
    slab, group = pl.program_id(0), pl.program_id(1)

    @pl.when((slab == 0) & (group == 0))
    def _():
        copies = start_all(
            [
                pltpu.make_async_copy(blocks[r], packed.at[column, member], sems.at[r])
                for r, column, member in partners(count, owners)
            ]
        )
        order[...] = transposed(block, cells_a)
        swap[...] = swapped(width, lanes)
        wait_all(copies)

    here = pl.ds(pl.multiple_of(group * block, block), block)
    parts = []
    for owner in range(owners):
        for tile in range(tiles):
            pieces = [
                packed[slab * width + part, owner, here, tile * lanes : (tile + 1) * lanes]
                for part in range(width)
            ]
            parts.append(jnp.concatenate(pieces, axis=1))
    mixed = moved(jnp.concatenate(parts, axis=0), swap[...])
    columns = []
    for owner in range(owners):
        rows = []
        for cell in range(cells_a):
            half, tile = cell // tiles, cell % tiles
            at = (owner * tiles + tile) * block
            rows.append(mixed[at : at + block, half * lanes : (half + 1) * lanes])
        columns.append(jnp.concatenate(rows, axis=0))
    rows = moved(order[...], jnp.concatenate(columns, axis=1))
    out[...] = rows.reshape(out.shape)


def unpack_state(blocks, slabs, width, cells_a):
    local, size = blocks[0].shape
    held = len(blocks)
    owners = held // (slabs * width)
    lanes = size * width // cells_a
    cols = owners * lanes
    block = 32

    def kernel(*refs):
        unpack_state_kernel(*refs, held=held)

    return pl.pallas_call(
        kernel,
        grid=(slabs, local // block),
        in_specs=[ANY] * held,
        out_specs=pl.BlockSpec((1, block, cells_a, cols), lambda s, g: (s, g, 0, 0)),
        out_shape=jax.ShapeDtypeStruct((slabs, local, cells_a, cols), BF16),
        scratch_shapes=[
            pltpu.VMEM((block * cells_a, block * cells_a), BF16),
            pltpu.VMEM((width * lanes, width * lanes), BF16),
            pltpu.VMEM((slabs * width, owners, local, size), BF16),
            pltpu.SemaphoreType.DMA((held,)),
        ],
        compiler_params=params(2),
        name="unpack_state",
    )(*blocks)


def gather_kernel(*refs, held, owners):
    blocks, (out, sems) = refs[:held], refs[held:]
    local = out.shape[1] // owners
    wait_all(
        start_all(
            [
                pltpu.make_async_copy(
                    blocks[r],
                    out.at[patch, pl.ds((r % owners) * local, local)],
                    sems.at[r],
                )
                for r, patch, _ in partners(held // owners, owners)
            ]
        )
    )


def gathered(blocks, count):
    local, size = blocks[0].shape
    held = len(blocks)
    owners = held // count

    def kernel(*refs):
        gather_kernel(*refs, held=held, owners=owners)

    return pl.pallas_call(
        kernel,
        in_specs=[ANY] * held,
        out_specs=ANY,
        out_shape=jax.ShapeDtypeStruct((count, owners * local, size), BF16),
        scratch_shapes=[pltpu.SemaphoreType.DMA((held,))],
        compiler_params=pltpu.CompilerParams(vmem_limit_bytes=VMEM_LIMIT),
        name="gather",
    )(*blocks)


def scatter_kernel(rows, *refs, owners):
    *outs, sems = refs
    local = rows.shape[1] // owners
    wait_all(
        start_all(
            [
                pltpu.make_async_copy(
                    rows.at[patch, pl.ds((r % owners) * local, local)], outs[r], sems.at[r]
                )
                for r, patch, _ in partners(rows.shape[0], owners)
            ]
        )
    )


def scattered(rows, owners):
    count, total, size = rows.shape
    held = count * owners

    def kernel(*refs):
        scatter_kernel(*refs, owners=owners)

    return pl.pallas_call(
        kernel,
        in_specs=[ANY],
        out_specs=[ANY] * held,
        out_shape=[jax.ShapeDtypeStruct((total // owners, size), BF16)] * held,
        scratch_shapes=[pltpu.SemaphoreType.DMA((held,))],
        compiler_params=pltpu.CompilerParams(vmem_limit_bytes=VMEM_LIMIT),
        name="scatter",
    )(rows)


def transform_kernel(before, middle, after, obs, scale, out, pert, weighted):
    total = middle.shape[1]
    half = before.shape[2]
    projected = jnp.zeros((total, 1), F32)
    start = 0
    for part in (before, middle, after):
        span = part.shape[2]
        for at in range(0, span, half):
            cols = slice(start, start + half)
            values = part[0, :, at : at + half].astype(F32)
            mean = jnp.sum(values, axis=0, keepdims=True) * (1.0 / total)
            centred = values - mean
            pert[:, cols] = centred.astype(BF16)
            scaled = (centred * scale[0, :, cols]).astype(BF16)
            weighted[:, cols] = scaled
            innovation = obs[0, :, cols] - mean
            projected += jnp.sum(scaled.astype(F32) * innovation, axis=1, keepdims=True)
            start += half
    diagonal = iota(total, total, 0) == iota(total, total, 1)
    gram = lax.dot_general(
        weighted[...], pert[...], (((1,), (1,)), ((), ())), preferred_element_type=F32
    )
    system = jnp.where(diagonal, total - 1.0, 0.0) + gram
    bound = jnp.max(jnp.sum(jnp.abs(system), axis=1, keepdims=True), axis=0, keepdims=True)
    root = (system / bound).astype(BF16)
    inverse = None
    for iteration in range(ITERS):
        product = root.astype(F32) if inverse is None else dot_bf16(inverse.astype(BF16), root)
        correction = (jnp.where(diagonal, 1.5, 0.0) - 0.5 * product).astype(BF16)
        if iteration + 1 < ITERS:
            root = moved(root, correction)
        if inverse is None:
            inverse = correction.astype(F32)
        else:
            inverse = dot_bf16(correction, inverse.astype(BF16))
    flipped = inverse.T
    halfway = jnp.sum(flipped * projected, axis=0, keepdims=True)
    weight = jnp.sum(inverse * halfway, axis=1, keepdims=True)
    weight = jnp.broadcast_to(weight, (total, 128)).T[0:1, :] / bound
    out[0] = (jnp.sqrt((total - 1.0) / bound) * flipped + weight).astype(BF16)


def transforms(hx_rows, obs_rows, scale_rows, count, wraps):
    held, total, own = hx_rows.shape
    half = own // 2
    shift = 0 if wraps else 1
    flops = count * (2 * total * total * 2 * own + 18 * total**3)
    return pl.pallas_call(
        transform_kernel,
        grid=(count,),
        in_specs=[
            pl.BlockSpec((1, total, half), lambda a: ((a + shift + held - 1) % held, 0, 1)),
            pl.BlockSpec((1, total, own), lambda a: (a + shift, 0, 0)),
            pl.BlockSpec((1, total, half), lambda a: ((a + shift + 1) % held, 0, 0)),
            pl.BlockSpec((1, 1, 2 * own), lambda a: (a, 0, 0)),
            pl.BlockSpec((1, 1, 2 * own), lambda a: (a, 0, 0)),
        ],
        out_specs=pl.BlockSpec((1, total, total), lambda a: (a, 0, 0)),
        out_shape=jax.ShapeDtypeStruct((count, total, total), BF16),
        scratch_shapes=[pltpu.VMEM((total, 2 * own), BF16), pltpu.VMEM((total, 2 * own), BF16)],
        compiler_params=params(1),
        cost_estimate=pl.CostEstimate(
            flops=flops, bytes_accessed=4 * count * total * total * 2, transcendentals=0
        ),
        name="transform",
    )(hx_rows, hx_rows, hx_rows, obs_rows, scale_rows)


def centred(values):
    values = values.astype(F32)
    mean = jnp.sum(values, axis=0, keepdims=True) * (1.0 / values.shape[0])
    return mean, (values - mean).astype(BF16)


def transport(tiles, here, ahead, behind, low):
    count, depth = len(tiles), len(tiles[0])
    shift = tiles[0][0].shape[1] // 2
    for _ in range(STEPS):
        first = [pltpu.roll(column[0], shift, 1) for column in tiles]
        last = [pltpu.roll(column[depth - 1], shift, 1) for column in tiles]
        later = []
        for a in range(count):
            column = []
            for k in range(depth):
                if k + 1 < depth:
                    after = tiles[a][k + 1]
                else:
                    after = jnp.where(low, first[a], first[(a + 1) % count])
                if k > 0:
                    prior = tiles[a][k - 1]
                else:
                    prior = jnp.where(low, last[(a + count - 1) % count], last[a])
                column.append(here * tiles[a][k] + ahead * after + behind * prior)
            later.append(column)
        tiles = later
    return tiles


def forecast_kernel(*refs, held, first, owners):
    blocks, (transform, speed) = refs[:held], refs[held : held + 2]
    outs = refs[held + 2 : -5]
    state, fields, results, in_sems, out_sems = refs[-5:]
    count, total, size = state.shape
    local = total // owners
    lanes = speed.shape[1]
    blocks_from = partners(count, owners)
    copies = start_all(
        [
            pltpu.make_async_copy(
                blocks[r],
                state.at[r // owners, pl.ds((r % owners) * local, local)],
                in_sems.at[r],
            )
            for r in range(held)
        ]
    )
    rows = results.shape[1]
    for near in range(count):
        wait_all(copies[near * owners : (near + 1) * owners])
        patch = blocks_from[near * owners][1]
        mean, pert = centred(state[near])
        fields[patch] = (dot_bf16(transform[patch], pert) + mean).astype(BF16).astype(F32)
    chunk = 16
    c = jnp.broadcast_to(speed[...], (8, lanes))
    here, ahead, behind = 1.0 - c * c, 0.5 * (c * c - c), 0.5 * (c * c + c)
    low = iota(8, lanes, 1) < lanes // 2

    def rows_at(step, carry):
        parts = []
        for half in range(chunk // 8):
            at = pl.ds(pl.multiple_of(step * chunk + half * 8, 8), 8)
            tiles = [
                [fields[a, at, k * lanes : (k + 1) * lanes] for k in range(size // lanes)]
                for a in range(count)
            ]
            parts.append(transport(tiles, here, ahead, behind, low))
        at = pl.ds(pl.multiple_of(step * chunk, chunk), chunk)
        for a in range(count):
            for k in range(size // lanes):
                value = jnp.concatenate([part[a][k] for part in parts], axis=0)
                results[a, at, k * lanes : (k + 1) * lanes] = value.astype(BF16)
        return carry

    sent = []
    for block in range(rows // local):
        lax.fori_loop(block * local // chunk, (block + 1) * local // chunk, rows_at, 0)
        for near in range(count):
            patch = blocks_from[near * owners][1]
            number = near * (rows // local) + block
            sent.append(
                pltpu.make_async_copy(
                    results.at[patch, pl.ds(block * local, local)],
                    outs[number],
                    out_sems.at[number],
                )
            )
            sent[-1].start()
    wait_all(sent)


def forecasts(blocks, transform, speed, owners, first, last):
    count, total, _ = transform.shape
    local, size = blocks[0].shape
    held = len(blocks)
    rows = (last - first) * local

    def kernel(*refs):
        forecast_kernel(*refs, held=held, first=first, owners=owners)

    return pl.pallas_call(
        kernel,
        grid=(1,),
        in_specs=[ANY] * held
        + [
            pl.BlockSpec((count, rows, total), lambda i: (0, first * local // rows, 0)),
            pl.BlockSpec(speed.shape, lambda i: (0, 0)),
        ],
        out_specs=[ANY] * (count * (last - first)),
        out_shape=[jax.ShapeDtypeStruct((local, size), BF16)] * (count * (last - first)),
        scratch_shapes=[
            pltpu.VMEM((count, total, size), BF16),
            pltpu.VMEM((count, rows, size), F32),
            pltpu.VMEM((count, rows, size), BF16),
            pltpu.SemaphoreType.DMA((held,)),
            pltpu.SemaphoreType.DMA((count * (last - first),)),
        ],
        compiler_params=params(1),
        cost_estimate=pl.CostEstimate(
            flops=2 * count * rows * total * size,
            bytes_accessed=4 * held * local * size,
            transcendentals=0,
        ),
        name="forecast",
    )(*blocks, transform, speed)


def analysis_kernel(state, transform, out):
    mean, pert = centred(state[0])
    out[0] = (dot_bf16(transform[0], pert) + mean).astype(BF16)


def analyses(state, transform):
    count, total, size = state.shape
    return pl.pallas_call(
        analysis_kernel,
        grid=(count,),
        in_specs=[
            pl.BlockSpec((1, total, size), lambda a: (a, 0, 0)),
            pl.BlockSpec((1, total, total), lambda a: (a, 0, 0)),
        ],
        out_specs=pl.BlockSpec((1, total, size), lambda a: (a, 0, 0)),
        out_shape=jax.ShapeDtypeStruct((count, total, size), BF16),
        compiler_params=params(1),
        name="analysis",
    )(state, transform)


def shared_transport(analysis, speed, width, jump):
    count, total, size = analysis.shape
    lanes = speed.shape[1]
    cells = lanes // width
    tiles = size // lanes
    fields = widened(analysis, jump).reshape(count + 2, total, tiles, width, cells)
    fields = fields.transpose(1, 0, 3, 2, 4).reshape(total, -1, cells).astype(F32)
    c = speed[0, :cells]
    for _ in range(STEPS):
        prior, here, after = fields[:, :-2], fields[:, 1:-1], fields[:, 2:]
        fields = (1.0 - c * c) * here + 0.5 * (c * c - c) * after + 0.5 * (c * c + c) * prior
    spare = tiles * width - STEPS
    fields = fields[:, spare : fields.shape[1] - spare].astype(BF16)
    fields = fields.reshape(total, count, width, tiles, cells)
    return fields.transpose(1, 0, 3, 2, 4).reshape(count, total, size)


def widened(blocks, jump):
    count = lax.axis_size("sub")
    forward = [(i, (i + jump) % count) for i in range(count)]
    backward = [(target, source) for source, target in forward]
    low = lax.ppermute(blocks[-1:], "sub", forward)
    high = lax.ppermute(blocks[:1], "sub", backward)
    return jnp.concatenate([low, blocks, high], axis=0)


def exchange(blocks, numbers, owners):
    lines = lax.axis_size("sub")
    order = sorted(range(len(blocks)), key=lambda i: -(numbers[i] % owners >= owners // 2))
    received = list(blocks)
    for i in order:
        column, member = numbers[i] // owners, numbers[i] % owners
        if numbers[i] == 0:
            continue
        pairs = [
            (s * owners + m, (s ^ column) * owners + (m ^ member))
            for s in range(lines)
            for m in range(owners)
        ]
        received[i] = lax.ppermute(blocks[i], ("sub", "mem"), pairs)
    return received


def advance(member_state, hx_values, obs_value, obs_var, courant):
    slabs, local, cells_a, cols = member_state.shape
    patches, own = hx_values.shape[3:]
    owners = lax.axis_size("mem")
    lines = lax.axis_size("sub")
    width = patches // owners
    count = slabs * width
    groups = lines // count
    cells_b = cols // patches
    column, member = place(count)
    slab, part = column // width, column % width
    numbers = list(range(count * owners))

    hx_blocks = exchange(pack_obs(hx_values, owners), numbers, owners)

    stats = jnp.stack([obs_value[:, 0], obs_var[:, 0]], axis=2)
    stats = lax.all_gather(stats, "sub", axis=0)
    stats = lax.dynamic_slice(stats, (0, slab, part, 0, 0), (lines, 1, 1, 2, own))
    stats = stats.reshape(lines, 2, own).astype(F32)
    half = own // 2
    stats = jnp.concatenate(
        [jnp.roll(stats, 1, 0)[:, :, half:], stats, jnp.roll(stats, -1, 0)[:, :, :half]], axis=2
    )
    if groups > 1:
        first = lax.axis_index("sub") // count * count
        stats = lax.dynamic_slice_in_dim(stats, first, count, axis=0)
    taper = (jnp.arange(half, dtype=F32) + 1.0) / (half + 1.0)
    local_weight = jnp.concatenate([taper, jnp.ones((own,), F32), taper[::-1]])
    obs_rows = stats[:, 0:1]
    scale_rows = local_weight / stats[:, 1:2]

    packed = pack_state(member_state, width, owners, hx_blocks[owners - 1])
    blocks = exchange(packed, numbers, owners)

    hx_rows = gathered(hx_blocks, count)
    if groups > 1:
        hx_rows = widened(hx_rows, count)
    transform = transforms(hx_rows, obs_rows, scale_rows, count, groups == 1)

    line = (member * width + part) * cells_b
    speed = lax.dynamic_slice(courant, (slab, line), (1, cells_b))
    speed = jnp.concatenate([speed] * width, axis=1)
    if groups == 1 and width == 2:
        middle = owners // 2
        back = [None] * (count * owners)
        for first, last in ((middle, owners), (0, middle)):
            chosen = [r * owners + i for r in range(count) for i in range(first, last)]
            fields = forecasts(blocks, transform, speed, owners, first, last)
            for r, block in zip(chosen, exchange(fields, chosen, owners)):
                back[r] = block
    else:
        fields = shared_transport(
            analyses(gathered(blocks, count), transform), speed, width, count
        )
        back = exchange(scattered(fields, owners), numbers, owners)
    return unpack_state(back, slabs, width, cells_a)


def solution(mesh):
    in_specs = (
        P(None, "mem", "sub", None),
        P(None, "mem", "sub", None, None),
        P(None, "sub", "mem", None),
        P(None, "sub", "mem", None),
        P(),
    )
    out_specs = P(None, "mem", "sub", None)
    return jax.shard_map(advance, mesh=mesh, in_specs=in_specs, out_specs=out_specs, check_vma=False)
```

time: 187 us -> 291 us (1.56)
  starting transfers between devices: 10.3 us -> 147 us
  blocking collectives: 69.7 us -> 8.95 us
  local copies, waits for them, and re-layouts: 7.39 us -> 40.5 us
  waiting for transfers between devices: 56.7 us -> 26.7 us
  Pallas kernels: 42.1 us -> 64.3 us
    ppermute x0 -> x93, starting transfers between devices: none -> 147 us  [exchange(): received[i] = lax.ppermute(blocks[i], ('sub', 'mem'), pairs)]
    all_to_all x2 -> x0, waiting for transfers between devices: 56.7 us -> none  [exchange(): lax.all_to_all(blocks, ('sub', 'mem'), split_axis=0, concat_axis=0, tiled...]
    all_to_all x1 -> x0, blocking collectives: 52 us -> none  [exchange(): lax.all_to_all(blocks, ('sub', 'mem'), split_axis=0, concat_axis=0, tiled...]
    unnamed x22 -> x138, local copies, waits for them, and re-layouts: 6.48 us -> 38.3 us
    ppermute x0 -> x93, waiting for transfers between devices: none -> 26.7 us  [exchange(): received[i] = lax.ppermute(blocks[i], ('sub', 'mem'), pairs)]
    pallas_call x2 -> x4, Pallas kernels: 18.2 us -> 35 us  [the longest x2 24.6 us: forecasts(): pl.pallas_call(kernel, grid=(1,), in_specs=[ANY] * held + [pl.BlockSpec((...]
    all_to_all x2 -> x0, starting transfers between devices: 10.3 us -> none  [exchange(): lax.all_to_all(blocks, ('sub', 'mem'), split_axis=0, concat_axis=0, tiled...]
    all_gather x1, blocking collectives: 17.7 us -> 8.95 us  [advance(): stats = lax.all_gather(stats, 'sub', axis=0)]
  transfers between devices with their start and end apart: 2 -> 93, of which waited for: 2 -> 16; matrix products, arithmetic and copies ran while one was open for 1% -> 1% of each run, Pallas kernels for 12% -> 14%
where the time goes in v2:
time: 291 us
  starting transfers between devices  147 us (51%)
  Pallas kernels  64.3 us (22%)
  local copies, waits for them, and re-layouts  40.5 us (14%)
  waiting for transfers between devices  26.7 us (9%)
  blocking collectives  8.95 us (3%)
    ppermute x93, starting transfers between devices, exchange(): received[i] = lax.ppermute(blocks[i], ('sub', 'mem'), pairs)  147 us
    unnamed x138, local copies, waits for them, and re-layouts  38.3 us
    ppermute x93, waiting for transfers between devices, exchange(): received[i] = lax.ppermute(blocks[i], ('sub', 'mem'), pairs)  26.7 us
    pallas_call x2, Pallas kernels, forecasts(): pl.pallas_call(kernel, grid=(1,), in_specs=[ANY] * held + [pl.BlockSpec((...  24.6 us
    pallas_call x1, Pallas kernels, transforms(): pl.pallas_call(transform_kernel, grid=(count,), in_specs=[pl.BlockSpec((1...  18.6 us
    all_gather x1, blocking collectives, advance(): stats = lax.all_gather(stats, 'sub', axis=0)  8.95 us
    pallas_call x1, Pallas kernels, unpack_state(): pl.pallas_call(kernel, grid=(slabs, local // block), in_specs=[ANY] * hel...  6.9 us
  transfers between devices with their start and end apart: 93, of which 16 were waited for; matrix products, arithmetic and copies ran while one was open for 1% of the time, Pallas kernels for 14%

profile of v2, /device:TPU:0, one launch (start us, length us, event | category | flops | bytes accessed | tf_op | source)
XLA Modules:
  0.0 290.6 jit_solution(3489026654929512501)
XLA Ops:
  0.0 1.6 copy-done
  1.6 5.2 %pack_obs.1 = (bf16[64,512]{1,0:T(8,128)(2,1)S(1)}, bf16[64,512]{1,0:T(8,128)(2,1)S(1)}, bf16[64,512]{1,0:T(8,128)(2,1)S(1)}, bf16[64,512]{1,0:T(8,128)(2,1)S(1)...) custom-call(bf16[2,64,1,16,512]{4,3,2,1,0:T(8,128)(2,1)S(1)} %copy-done), custom_call_target="tpu_custom_call" | custom-call | tf_op jit(solution)/shard_map/pack_obs/pallas_call | solution.py:104
  8.7 4.6 %collective-permute-start = (bf16[64,512]{1,0:T(8,128)(2,1)S(1)}, bf16[64,512]{1,0:T(8,128)(2,1)S(1)}, u32[]{:S(2)}, u32[]{:S(2)}) collective-permute-start(bf16[64,512]{1,0:T(8,128)(2,1)S(1)} %get-tuple-element.101), channel_id=1, source_target_pairs={{0,7},{1,6},{2,5},{3,4},{4,3},{5,2},{6,1},{7,0},{8,15},{9,14},{10,... | collective-permute-start | bytes 196616 | tf_op jit(solution)/shard_map/ppermute | solution.py:594
  14.0 1.4 collective-permute-start.34
  15.8 2.6 collective-permute-start.36
  18.4 1.8 collective-permute-start.37
  20.2 1.5 collective-permute-start.38
  21.6 3.0 %collective-permute-done.35.refs_4_ = bf16[64,512]{1,0:T(8,128)(2,1)S(1)} collective-permute-done((bf16[64,512]{1,0:T(8,128)(2,1)S(1)}, bf16[64,512]{1,0:T(8,128)(2,1)S(1)}, u32[]{:S(2)}, u32[]{:S(2)}) %collective-permute-start.35) | collective-permute-done | bytes 65568 | tf_op jit(solution)/shard_map/ppermute | solution.py:594
  24.7 1.4 collective-permute-done.36.refs_5_
  27.0 2.9 collective-permute-start.42
  31.1 1.8 collective-permute-start.44
  32.8 2.3 collective-permute-start.45
  35.2 1.7 collective-permute-start.46
  37.6 9.0 %all-gather = bf16[8,2,2,512]{3,1,0,2:T(2,128)(2,1)S(1)} all-gather(bf16[2,2,2,512]{3,1,0,2:T(2,128)(2,1)S(1)} %pad_maximum_fusion.2), channel_id=2, replica_groups=mesh['sub'=4,'mem'=8] {'sub'}, dimensions={0}, use_global_device_ids=true | all-gather | bytes 40960 | tf_op jit(solution)/shard_map/all_gather | solution.py:614
  48.7 4.8 %collective-permute-start.51 = (bf16[64,512]{1,0:T(8,128)(2,1)}, bf16[64,512]{1,0:T(8,128)(2,1)S(1)}, u32[]{:S(2)}, u32[]{:S(2)}) collective-permute-start(bf16[64,512]{1,0:T(8,128)(2,1)} %copy-done.51), channel_id=1, source_target_pairs={{0,21},{1,20},{2,23},{3,22},{4,17},{5,16},{6,19},{7,18},{8,29},{9,... | collective-permute-start | bytes 196616 | tf_op jit(solution)/shard_map/ppermute | solution.py:594
  54.9 1.5 collective-permute-start.53
  56.4 1.7 collective-permute-start.54
  58.1 3.2 %collective-permute-start.55 = (bf16[64,512]{1,0:T(8,128)(2,1)}, bf16[64,512]{1,0:T(8,128)(2,1)S(1)}, u32[]{:S(2)}, u32[]{:S(2)}) collective-permute-start(bf16[64,512]{1,0:T(8,128)(2,1)} %copy-done.42), channel_id=1, source_target_pairs={{0,25},{1,24},{2,27},{3,26},{4,29},{5,28},{6,31},{7,30},{8,17},{9,... | collective-permute-start | bytes 196616 | tf_op jit(solution)/shard_map/ppermute | solution.py:594
  61.3 1.5 collective-permute-done.51.refs_21_
  64.1 1.6 collective-permute-start.57
  66.4 5.5 %pack_state.1 = (bf16[64,512]{1,0:T(8,128)(2,1)S(1)}, bf16[64,512]{1,0:T(8,128)(2,1)}, bf16[64,512]{1,0:T(8,128)(2,1)S(1)}, bf16[64,512]{1,0:T(8,128)(2,1)S(1)},...) custom-call(bf16[2,64,8,1024]{3,2,1,0:T(8,128)(2,1)S(1)} %copy-done., ...), custom_call_target="tpu_custom_call" | custom-call | tf_op jit(solution)/shard_map/pack_state/pallas_call | solution.py:180
  93.1 5.2 %collective-permute-start.59 = (bf16[64,512]{1,0:T(8,128)(2,1)}, bf16[64,512]{1,0:T(8,128)(2,1)S(1)}, u32[]{:S(2)}, u32[]{:S(2)}) collective-permute-start(bf16[64,512]{1,0:T(8,128)(2,1)} %get-tuple-element.162), channel_id=1, source_target_pairs={{0,29},{1,28},{2,31},{3,30},{4,25},{5,24},{6,27},{7,26},{8,21},{9,... | collective-permute-start | bytes 196616 | tf_op jit(solution)/shard_map/ppermute | solution.py:594
  99.9 3.1 %collective-permute-start.61 = (bf16[64,512]{1,0:T(8,128)(2,1)}, bf16[64,512]{1,0:T(8,128)(2,1)S(1)}, u32[]{:S(2)}, u32[]{:S(2)}) collective-permute-start(bf16[64,512]{1,0:T(8,128)(2,1)} %get-tuple-element.164), channel_id=1, source_target_pairs={{0,31},{1,30},{2,29},{3,28},{4,27},{5,26},{6,25},{7,24},{8,23},{9,... | collective-permute-start | bytes 196616 | tf_op jit(solution)/shard_map/ppermute | solution.py:594
  103.6 2.3 collective-permute-start.1
  107.3 2.2 collective-permute-start.11
  110.8 3.9 %collective-permute-start.13 = (bf16[64,512]{1,0:T(8,128)(2,1)}, bf16[64,512]{1,0:T(8,128)(2,1)S(1)}, u32[]{:S(2)}, u32[]{:S(2)}) collective-permute-start(bf16[64,512]{1,0:T(8,128)(2,1)} %copy-done.63), channel_id=1, source_target_pairs={{0,13},{1,12},{2,15},{3,14},{4,9},{5,8},{6,11},{7,10},{8,5},{9,4},... | collective-permute-start | bytes 196616 | tf_op jit(solution)/shard_map/ppermute | solution.py:594
  114.7 4.1 %collective-permute-start.15 = (bf16[64,512]{1,0:T(8,128)(2,1)}, bf16[64,512]{1,0:T(8,128)(2,1)S(1)}, u32[]{:S(2)}, u32[]{:S(2)}) collective-permute-start(bf16[64,512]{1,0:T(8,128)(2,1)} %copy-done.61), channel_id=1, source_target_pairs={{0,15},{1,14},{2,13},{3,12},{4,11},{5,10},{6,9},{7,8},{8,7},{9,6},... | collective-permute-start | bytes 196616 | tf_op jit(solution)/shard_map/ppermute | solution.py:594
  121.0 1.4 collective-permute-done.14.refs_14_
  122.4 2.8 collective-permute-start.19
  127.5 2.2 collective-permute-start.21
  129.7 1.7 collective-permute-start.22
  131.4 3.0 %collective-permute-start.23 = (bf16[64,512]{1,0:T(8,128)(2,1)}, bf16[64,512]{1,0:T(8,128)(2,1)S(1)}, u32[]{:S(2)}, u32[]{:S(2)}) collective-permute-start(bf16[64,512]{1,0:T(8,128)(2,1)} %copy-done.52), channel_id=1, source_target_pairs={{0,23},{1,22},{2,21},{3,20},{4,19},{5,18},{6,17},{7,16},{8,31},{9,... | collective-permute-start | bytes 196616 | tf_op jit(solution)/shard_map/ppermute | solution.py:594
  134.4 1.5 collective-permute-start.24
  136.9 3.3 %collective-permute-done.21.refs_21_ = bf16[64,512]{1,0:T(8,128)(2,1)S(1)} collective-permute-done((bf16[64,512]{1,0:T(8,128)(2,1)}, bf16[64,512]{1,0:T(8,128)(2,1)S(1)}, u32[]{:S(2)}, u32[]{:S(2)}) %collective-permute-start.21) | collective-permute-done | bytes 65568 | tf_op jit(solution)/shard_map/ppermute | solution.py:594
  140.2 3.9 %collective-permute-start.27 = (bf16[64,512]{1,0:T(8,128)(2,1)}, bf16[64,512]{1,0:T(8,128)(2,1)S(1)}, u32[]{:S(2)}, u32[]{:S(2)}) collective-permute-start(bf16[64,512]{1,0:T(8,128)(2,1)} %copy-done.46), channel_id=1, source_target_pairs={{0,27},{1,26},{2,25},{3,24},{4,31},{5,30},{6,29},{7,28},{8,19},{9,... | collective-permute-start | bytes 196616 | tf_op jit(solution)/shard_map/ppermute | solution.py:594
  145.8 3.8 %collective-permute-start.29 = (bf16[64,512]{1,0:T(8,128)(2,1)}, bf16[64,512]{1,0:T(8,128)(2,1)S(1)}, u32[]{:S(2)}, u32[]{:S(2)}) collective-permute-start(bf16[64,512]{1,0:T(8,128)(2,1)} %copy-done.39), channel_id=1, source_target_pairs={{0,29},{1,28},{2,31},{3,30},{4,25},{5,24},{6,27},{7,26},{8,21},{9,... | collective-permute-start | bytes 196616 | tf_op jit(solution)/shard_map/ppermute | solution.py:594
  149.6 2.1 collective-permute-start.30
  151.7 3.6 %collective-permute-start.31 = (bf16[64,512]{1,0:T(8,128)(2,1)}, bf16[64,512]{1,0:T(8,128)(2,1)S(1)}, u32[]{:S(2)}, u32[]{:S(2)}) collective-permute-start(bf16[64,512]{1,0:T(8,128)(2,1)} %copy-done.36), channel_id=1, source_target_pairs={{0,31},{1,30},{2,29},{3,28},{4,27},{5,26},{6,25},{7,24},{8,23},{9,... | collective-permute-start | bytes 196616 | tf_op jit(solution)/shard_map/ppermute | solution.py:594
  164.7 3.4 %gather.1.before.middle.after = bf16[4,512,512]{2,1,0:T(8,128)(2,1)S(1)} custom-call(bf16[64,512]{1,0:T(8,128)(2,1)S(1)} %get-tuple-element.134.refs_0_, bf16[64,512]{1,0:T(8,128)(2,1)S(1)} %collective-permute-done.32.refs_1_, bf16[64,512]{1,0:T(8,128)(2,1)S(1)} %collective-permute-done.33.refs_2_, bf16[64,512]{1,0:T(8,128)(2,1)S(1)} %collective-permute-done.34.refs_3_, ...), custom_call_target="tpu_custom_call" | custom-call | tf_op jit(solution)/shard_map/gather/pallas_call | solution.py:294
  168.1 2.4 collective-permute-start.5
  171.7 2.7 collective-permute-start.7
  175.8 18.6 %transform.1.refs_32_ = bf16[4,512,512]{2,1,0:T(8,128)(2,1)S(1)} custom-call(bf16[4,512,512]{2,1,0:T(8,128)(2,1)S(1)} %gather.1.before.middle.after, bf16[4,512,512]{2,1,0:T(8,128)(2,1)S(1)} %gather.1.before.middle.after, bf16[4,512,512]{2,1,0:T(8,128)(2,1)S(1)} %gather.1.before.middle.after, f32[4,1,1024]{2,1,0:T(1,128)S(1)} %copy-done.24, ...), custom_call_target="tpu_custom_call" | custom-call | flops 11811160064 | bytes 8388608 | tf_op jit(solution)/shard_map/transform/pallas_call | solution.py:385
  194.4 12.5 %forecast.3 = (bf16[64,512]{1,0:T(8,128)(2,1)S(1)}, bf16[64,512]{1,0:T(8,128)(2,1)S(1)}, bf16[64,512]{1,0:T(8,128)(2,1)S(1)}, bf16[64,512]{1,0:T(8,128)(2,1)S(1)...) custom-call(bf16[64,512]{1,0:T(8,128)(2,1)S(1)} %get-tuple-element.1, ...), custom_call_target="tpu_custom_call" | custom-call | flops 536870912 | bytes 4194304 | tf_op jit(solution)/shard_map/forecast/pallas_call | solution.py:507
  207.0 3.0 %collective-permute-start.66 = (bf16[64,512]{1,0:T(8,128)(2,1)S(1)}, bf16[64,512]{1,0:T(8,128)(2,1)S(1)}, u32[]{:S(2)}, u32[]{:S(2)}) collective-permute-start(bf16[64,512]{1,0:T(8,128)(2,1)S(1)} %get-tuple-element.170), channel_id=1, source_target_pairs={{0,5},{1,4},{2,7},{3,6},{4,1},{5,0},{6,3},{7,2},{8,13},{9,12},{10,... | collective-permute-start | bytes 196616 | tf_op jit(solution)/shard_map/ppermute | solution.py:594
  210.5 2.7 collective-permute-start.68
  214.3 2.8 collective-permute-start.74
  217.1 3.8 %collective-permute-done.66.refs_5_ = bf16[64,512]{1,0:T(8,128)(2,1)S(1)} collective-permute-done((bf16[64,512]{1,0:T(8,128)(2,1)S(1)}, bf16[64,512]{1,0:T(8,128)(2,1)S(1)}, u32[]{:S(2)}, u32[]{:S(2)}) %collective-permute-start.66) | collective-permute-done | bytes 65568 | tf_op jit(solution)/shard_map/ppermute | solution.py:594
  220.9 4.3 %collective-permute-start.76 = (bf16[64,512]{1,0:T(8,128)(2,1)S(1)}, bf16[64,512]{1,0:T(8,128)(2,1)S(1)}, u32[]{:S(2)}, u32[]{:S(2)}) collective-permute-start(bf16[64,512]{1,0:T(8,128)(2,1)S(1)} %get-tuple-element.180), channel_id=1, source_target_pairs={{0,15},{1,14},{2,13},{3,12},{4,11},{5,10},{6,9},{7,8},{8,7},{9,6},... | collective-permute-start | bytes 196616 | tf_op jit(solution)/shard_map/ppermute | solution.py:594
  226.4 2.5 collective-permute-start.82
  228.9 2.4 collective-permute-done.74.refs_13_
  231.3 6.0 %collective-permute-start.84 = (bf16[64,512]{1,0:T(8,128)(2,1)S(1)}, bf16[64,512]{1,0:T(8,128)(2,1)S(1)}, u32[]{:S(2)}, u32[]{:S(2)}) collective-permute-start(bf16[64,512]{1,0:T(8,128)(2,1)S(1)} %get-tuple-element.188), channel_id=1, source_target_pairs={{0,23},{1,22},{2,21},{3,20},{4,19},{5,18},{6,17},{7,16},{8,31},{9,... | collective-permute-start | bytes 196616 | tf_op jit(solution)/shard_map/ppermute | solution.py:594
  237.9 2.2 collective-permute-start.90
  241.0 2.9 %collective-permute-start.91 = (bf16[64,512]{1,0:T(8,128)(2,1)S(1)}, bf16[64,512]{1,0:T(8,128)(2,1)S(1)}, u32[]{:S(2)}, u32[]{:S(2)}) collective-permute-start(bf16[64,512]{1,0:T(8,128)(2,1)S(1)} %get-tuple-element.195), channel_id=1, source_target_pairs={{0,30},{1,31},{2,28},{3,29},{4,26},{5,27},{6,24},{7,25},{8,22},{9,... | collective-permute-start | bytes 196616 | tf_op jit(solution)/shard_map/ppermute | solution.py:594
  244.0 3.1 %collective-permute-start.92 = (bf16[64,512]{1,0:T(8,128)(2,1)S(1)}, bf16[64,512]{1,0:T(8,128)(2,1)S(1)}, u32[]{:S(2)}, u32[]{:S(2)}) collective-permute-start(bf16[64,512]{1,0:T(8,128)(2,1)S(1)} %get-tuple-element.196), channel_id=1, source_target_pairs={{0,31},{1,30},{2,29},{3,28},{4,27},{5,26},{6,25},{7,24},{8,23},{9,... | collective-permute-start | bytes 196616 | tf_op jit(solution)/shard_map/ppermute | solution.py:594
  247.1 12.2 %forecast.2 = (bf16[64,512]{1,0:T(8,128)(2,1)S(1)}, bf16[64,512]{1,0:T(8,128)(2,1)S(1)}, bf16[64,512]{1,0:T(8,128)(2,1)S(1)}, bf16[64,512]{1,0:T(8,128)(2,1)S(1)...) custom-call(bf16[64,512]{1,0:T(8,128)(2,1)S(1)} %get-tuple-element.1, ...), custom_call_target="tpu_custom_call" | custom-call | flops 536870912 | bytes 4194304 | tf_op jit(solution)/shard_map/forecast/pallas_call | solution.py:507
  259.4 3.3 %collective-permute-start.63 = (bf16[64,512]{1,0:T(8,128)(2,1)S(1)}, bf16[64,512]{1,0:T(8,128)(2,1)S(1)}, u32[]{:S(2)}, u32[]{:S(2)}) collective-permute-start(bf16[64,512]{1,0:T(8,128)(2,1)S(1)} %get-tuple-element.167), channel_id=1, source_target_pairs={{0,2},{1,3},{2,0},{3,1},{4,6},{5,7},{6,4},{7,5},{8,10},{9,11},{10,... | collective-permute-start | bytes 196616 | tf_op jit(solution)/shard_map/ppermute | solution.py:594
  262.8 1.4 collective-permute-start.70
  264.2 1.7 collective-permute-start.71
  268.6 2.6 collective-permute-start.79
  271.6 2.9 %collective-permute-start.85 = (bf16[64,512]{1,0:T(8,128)(2,1)S(1)}, bf16[64,512]{1,0:T(8,128)(2,1)S(1)}, u32[]{:S(2)}, u32[]{:S(2)}) collective-permute-start(bf16[64,512]{1,0:T(8,128)(2,1)S(1)} %get-tuple-element.189), channel_id=1, source_target_pairs={{0,24},{1,25},{2,26},{3,27},{4,28},{5,29},{6,30},{7,31},{8,16},{9,... | collective-permute-start | bytes 196616 | tf_op jit(solution)/shard_map/ppermute | solution.py:594
  274.6 3.3 %collective-permute-start.87 = (bf16[64,512]{1,0:T(8,128)(2,1)S(1)}, bf16[64,512]{1,0:T(8,128)(2,1)S(1)}, u32[]{:S(2)}, u32[]{:S(2)}) collective-permute-start(bf16[64,512]{1,0:T(8,128)(2,1)S(1)} %get-tuple-element.191), channel_id=1, source_target_pairs={{0,26},{1,27},{2,24},{3,25},{4,30},{5,31},{6,28},{7,29},{8,18},{9,... | collective-permute-start | bytes 196616 | tf_op jit(solution)/shard_map/ppermute | solution.py:594
  279.4 1.4 collective-permute-done.87.refs_26_
  280.8 2.7 collective-permute-done.88.refs_27_
  283.5 6.9 %unpack_state.1 = bf16[2,64,8,1024]{3,2,1,0:T(8,128)(2,1)} custom-call(bf16[64,512]{1,0:T(8,128)(2,1)S(1)} %get-tuple-element.165.refs_0_, bf16[64,512]{1,0:T(8,128)(2,1)S(1)} %collective-permute-done.62.refs_1_, bf16[64,512]{1,0:T(8,128)(2,1)S(1)} %collective-permute-done.63.refs_2_, bf16[64,512]{1,0:T(8,128)(2,1)S(1)} %collective-permute-done.64.refs_3_, ...), custom_call_target="tpu_custom_call" | custom-call | tf_op jit(solution)/shard_map/unpack_state/pallas_call | solution.py:252
  (282 shorter events, 65.5 us)
Async XLA Ops:
  15.3 9.4 %collective-permute-start.35 = (bf16[64,512]{1,0:T(8,128)(2,1)S(1)}, bf16[64,512]{1,0:T(8,128)(2,1)S(1)}, u32[]{:S(2)}, u32[]{:S(2)}) collective-permute-start(bf16[64,512]{1,0:T(8,128)(2,1)S(1)} %get-tuple-element.138), channel_id=1, source_target_pairs={{0,4},{1,5},{2,6},{3,7},{4,0},{5,1},{6,2},{7,3},{8,12},{9,13},{10,... | collective-permute-start | bytes 196616 | tf_op jit(solution)/shard_map/ppermute | solution.py:594
  15.8 10.3 %collective-permute-start.36 = (bf16[64,512]{1,0:T(8,128)(2,1)S(1)}, bf16[64,512]{1,0:T(8,128)(2,1)S(1)}, u32[]{:S(2)}, u32[]{:S(2)}) collective-permute-start(bf16[64,512]{1,0:T(8,128)(2,1)S(1)} %get-tuple-element.139), channel_id=1, source_target_pairs={{0,5},{1,4},{2,7},{3,6},{4,1},{5,0},{6,3},{7,2},{8,13},{9,12},{10,... | collective-permute-start | bytes 196616 | tf_op jit(solution)/shard_map/ppermute | solution.py:594
  20.2 9.7 %collective-permute-start.38 = (bf16[64,512]{1,0:T(8,128)(2,1)S(1)}, bf16[64,512]{1,0:T(8,128)(2,1)S(1)}, u32[]{:S(2)}, u32[]{:S(2)}) collective-permute-start(bf16[64,512]{1,0:T(8,128)(2,1)S(1)} %get-tuple-element.141), channel_id=1, source_target_pairs={{0,8},{1,9},{2,10},{3,11},{4,12},{5,13},{6,14},{7,15},{8,0},{9,1},... | collective-permute-start | bytes 196616 | tf_op jit(solution)/shard_map/ppermute | solution.py:594
  21.6 9.4 %collective-permute-start.39 = (bf16[64,512]{1,0:T(8,128)(2,1)S(1)}, bf16[64,512]{1,0:T(8,128)(2,1)S(1)}, u32[]{:S(2)}, u32[]{:S(2)}) collective-permute-start(bf16[64,512]{1,0:T(8,128)(2,1)S(1)} %get-tuple-element.142), channel_id=1, source_target_pairs={{0,9},{1,8},{2,11},{3,10},{4,13},{5,12},{6,15},{7,14},{8,1},{9,0},... | collective-permute-start | bytes 196616 | tf_op jit(solution)/shard_map/ppermute | solution.py:594
  26.1 9.1 %collective-permute-start.41 = (bf16[64,512]{1,0:T(8,128)(2,1)S(1)}, bf16[64,512]{1,0:T(8,128)(2,1)S(1)}, u32[]{:S(2)}, u32[]{:S(2)}) collective-permute-start(bf16[64,512]{1,0:T(8,128)(2,1)S(1)} %get-tuple-element.144), channel_id=1, source_target_pairs={{0,11},{1,10},{2,9},{3,8},{4,15},{5,14},{6,13},{7,12},{8,3},{9,2},... | collective-permute-start | bytes 196616 | tf_op jit(solution)/shard_map/ppermute | solution.py:594
  27.0 10.2 %collective-permute-start.42 = (bf16[64,512]{1,0:T(8,128)(2,1)S(1)}, bf16[64,512]{1,0:T(8,128)(2,1)S(1)}, u32[]{:S(2)}, u32[]{:S(2)}) collective-permute-start(bf16[64,512]{1,0:T(8,128)(2,1)S(1)} %get-tuple-element.145), channel_id=1, source_target_pairs={{0,12},{1,13},{2,14},{3,15},{4,8},{5,9},{6,10},{7,11},{8,4},{9,5},... | collective-permute-start | bytes 196616 | tf_op jit(solution)/shard_map/ppermute | solution.py:594
  29.9 17.3 %collective-permute-start.43 = (bf16[64,512]{1,0:T(8,128)(2,1)S(1)}, bf16[64,512]{1,0:T(8,128)(2,1)S(1)}, u32[]{:S(2)}, u32[]{:S(2)}) collective-permute-start(bf16[64,512]{1,0:T(8,128)(2,1)S(1)} %get-tuple-element.146), channel_id=1, source_target_pairs={{0,13},{1,12},{2,15},{3,14},{4,9},{5,8},{6,11},{7,10},{8,5},{9,4},... | collective-permute-start | bytes 196616 | tf_op jit(solution)/shard_map/ppermute | solution.py:594
  31.1 16.2 %collective-permute-start.44 = (bf16[64,512]{1,0:T(8,128)(2,1)S(1)}, bf16[64,512]{1,0:T(8,128)(2,1)S(1)}, u32[]{:S(2)}, u32[]{:S(2)}) collective-permute-start(bf16[64,512]{1,0:T(8,128)(2,1)S(1)} %get-tuple-element.147), channel_id=1, source_target_pairs={{0,14},{1,15},{2,12},{3,13},{4,10},{5,11},{6,8},{7,9},{8,6},{9,7},... | collective-permute-start | bytes 196616 | tf_op jit(solution)/shard_map/ppermute | solution.py:594
  32.8 14.8 %collective-permute-start.45 = (bf16[64,512]{1,0:T(8,128)(2,1)S(1)}, bf16[64,512]{1,0:T(8,128)(2,1)S(1)}, u32[]{:S(2)}, u32[]{:S(2)}) collective-permute-start(bf16[64,512]{1,0:T(8,128)(2,1)S(1)} %get-tuple-element.148), channel_id=1, source_target_pairs={{0,15},{1,14},{2,13},{3,12},{4,11},{5,10},{6,9},{7,8},{8,7},{9,6},... | collective-permute-start | bytes 196616 | tf_op jit(solution)/shard_map/ppermute | solution.py:594
  35.2 13.5 %collective-permute-start.46 = (bf16[64,512]{1,0:T(8,128)(2,1)S(1)}, bf16[64,512]{1,0:T(8,128)(2,1)S(1)}, u32[]{:S(2)}, u32[]{:S(2)}) collective-permute-start(bf16[64,512]{1,0:T(8,128)(2,1)S(1)} %get-tuple-element.149), channel_id=1, source_target_pairs={{0,16},{1,17},{2,18},{3,19},{4,20},{5,21},{6,22},{7,23},{8,24},{9,... | collective-permute-start | bytes 196616 | tf_op jit(solution)/shard_map/ppermute | solution.py:594
  37.3 16.2 %collective-permute-start.47 = (bf16[64,512]{1,0:T(8,128)(2,1)}, bf16[64,512]{1,0:T(8,128)(2,1)S(1)}, u32[]{:S(2)}, u32[]{:S(2)}) collective-permute-start(bf16[64,512]{1,0:T(8,128)(2,1)} %get-tuple-element.150), channel_id=1, source_target_pairs={{0,17},{1,16},{2,19},{3,18},{4,21},{5,20},{6,23},{7,22},{8,25},{9,... | collective-permute-start | bytes 196616 | tf_op jit(solution)/shard_map/ppermute | solution.py:594
  47.2 9.1 %collective-permute-start.49 = (bf16[64,512]{1,0:T(8,128)(2,1)}, bf16[64,512]{1,0:T(8,128)(2,1)S(1)}, u32[]{:S(2)}, u32[]{:S(2)}) collective-permute-start(bf16[64,512]{1,0:T(8,128)(2,1)} %get-tuple-element.152), channel_id=1, source_target_pairs={{0,19},{1,18},{2,17},{3,16},{4,23},{5,22},{6,21},{7,20},{8,27},{9,... | collective-permute-start | bytes 196616 | tf_op jit(solution)/shard_map/ppermute | solution.py:594
  47.6 10.5 %collective-permute-start.50 = (bf16[64,512]{1,0:T(8,128)(2,1)}, bf16[64,512]{1,0:T(8,128)(2,1)S(1)}, u32[]{:S(2)}, u32[]{:S(2)}) collective-permute-start(bf16[64,512]{1,0:T(8,128)(2,1)} %get-tuple-element.153), channel_id=1, source_target_pairs={{0,20},{1,21},{2,22},{3,23},{4,16},{5,17},{6,18},{7,19},{8,28},{9,... | collective-permute-start | bytes 196616 | tf_op jit(solution)/shard_map/ppermute | solution.py:594
  48.7 14.2 %collective-permute-start.51 = (bf16[64,512]{1,0:T(8,128)(2,1)}, bf16[64,512]{1,0:T(8,128)(2,1)S(1)}, u32[]{:S(2)}, u32[]{:S(2)}) collective-permute-start(bf16[64,512]{1,0:T(8,128)(2,1)} %copy-done.51), channel_id=1, source_target_pairs={{0,21},{1,20},{2,23},{3,22},{4,17},{5,16},{6,19},{7,18},{8,29},{9,... | collective-permute-start | bytes 196616 | tf_op jit(solution)/shard_map/ppermute | solution.py:594
  53.4 10.0 %collective-permute-start.52 = (bf16[64,512]{1,0:T(8,128)(2,1)}, bf16[64,512]{1,0:T(8,128)(2,1)S(1)}, u32[]{:S(2)}, u32[]{:S(2)}) collective-permute-start(bf16[64,512]{1,0:T(8,128)(2,1)} %copy-done.50), channel_id=1, source_target_pairs={{0,22},{1,23},{2,20},{3,21},{4,18},{5,19},{6,16},{7,17},{8,30},{9,... | collective-permute-start | bytes 196616 | tf_op jit(solution)/shard_map/ppermute | solution.py:594
  54.9 35.8 %collective-permute-start.53 = (bf16[64,512]{1,0:T(8,128)(2,1)}, bf16[64,512]{1,0:T(8,128)(2,1)S(1)}, u32[]{:S(2)}, u32[]{:S(2)}) collective-permute-start(bf16[64,512]{1,0:T(8,128)(2,1)} %copy-done.44), channel_id=1, source_target_pairs={{0,23},{1,22},{2,21},{3,20},{4,19},{5,18},{6,17},{7,16},{8,31},{9,... | collective-permute-start | bytes 196616 | tf_op jit(solution)/shard_map/ppermute | solution.py:594
  56.4 36.0 %collective-permute-start.54 = (bf16[64,512]{1,0:T(8,128)(2,1)}, bf16[64,512]{1,0:T(8,128)(2,1)S(1)}, u32[]{:S(2)}, u32[]{:S(2)}) collective-permute-start(bf16[64,512]{1,0:T(8,128)(2,1)} %copy-done.43), channel_id=1, source_target_pairs={{0,24},{1,25},{2,26},{3,27},{4,28},{5,29},{6,30},{7,31},{8,16},{9,... | collective-permute-start | bytes 196616 | tf_op jit(solution)/shard_map/ppermute | solution.py:594
  58.1 40.2 %collective-permute-start.55 = (bf16[64,512]{1,0:T(8,128)(2,1)}, bf16[64,512]{1,0:T(8,128)(2,1)S(1)}, u32[]{:S(2)}, u32[]{:S(2)}) collective-permute-start(bf16[64,512]{1,0:T(8,128)(2,1)} %copy-done.42), channel_id=1, source_target_pairs={{0,25},{1,24},{2,27},{3,26},{4,29},{5,28},{6,31},{7,30},{8,17},{9,... | collective-permute-start | bytes 196616 | tf_op jit(solution)/shard_map/ppermute | solution.py:594
  63.5 35.8 %collective-permute-start.56 = (bf16[64,512]{1,0:T(8,128)(2,1)}, bf16[64,512]{1,0:T(8,128)(2,1)S(1)}, u32[]{:S(2)}, u32[]{:S(2)}) collective-permute-start(bf16[64,512]{1,0:T(8,128)(2,1)} %copy-done.41), channel_id=1, source_target_pairs={{0,26},{1,27},{2,24},{3,25},{4,30},{5,31},{6,28},{7,29},{8,18},{9,... | collective-permute-start | bytes 196616 | tf_op jit(solution)/shard_map/ppermute | solution.py:594
  64.1 38.9 %collective-permute-start.57 = (bf16[64,512]{1,0:T(8,128)(2,1)}, bf16[64,512]{1,0:T(8,128)(2,1)S(1)}, u32[]{:S(2)}, u32[]{:S(2)}) collective-permute-start(bf16[64,512]{1,0:T(8,128)(2,1)} %copy-done.40), channel_id=1, source_target_pairs={{0,27},{1,26},{2,25},{3,24},{4,31},{5,30},{6,29},{7,28},{8,19},{9,... | collective-permute-start | bytes 196616 | tf_op jit(solution)/shard_map/ppermute | solution.py:594
  91.3 14.7 %collective-permute-start.58 = (bf16[64,512]{1,0:T(8,128)(2,1)}, bf16[64,512]{1,0:T(8,128)(2,1)S(1)}, u32[]{:S(2)}, u32[]{:S(2)}) collective-permute-start(bf16[64,512]{1,0:T(8,128)(2,1)} %get-tuple-element.161), channel_id=1, source_target_pairs={{0,28},{1,29},{2,30},{3,31},{4,24},{5,25},{6,26},{7,27},{8,20},{9,... | collective-permute-start | bytes 196616 | tf_op jit(solution)/shard_map/ppermute | solution.py:594
  93.1 13.6 %collective-permute-start.59 = (bf16[64,512]{1,0:T(8,128)(2,1)}, bf16[64,512]{1,0:T(8,128)(2,1)S(1)}, u32[]{:S(2)}, u32[]{:S(2)}) collective-permute-start(bf16[64,512]{1,0:T(8,128)(2,1)} %get-tuple-element.162), channel_id=1, source_target_pairs={{0,29},{1,28},{2,31},{3,30},{4,25},{5,24},{6,27},{7,26},{8,21},{9,... | collective-permute-start | bytes 196616 | tf_op jit(solution)/shard_map/ppermute | solution.py:594
  98.9 10.6 %collective-permute-start.60 = (bf16[64,512]{1,0:T(8,128)(2,1)}, bf16[64,512]{1,0:T(8,128)(2,1)S(1)}, u32[]{:S(2)}, u32[]{:S(2)}) collective-permute-start(bf16[64,512]{1,0:T(8,128)(2,1)} %get-tuple-element.163), channel_id=1, source_target_pairs={{0,30},{1,31},{2,28},{3,29},{4,26},{5,27},{6,24},{7,25},{8,22},{9,... | collective-permute-start | bytes 196616 | tf_op jit(solution)/shard_map/ppermute | solution.py:594
  99.9 10.3 %collective-permute-start.61 = (bf16[64,512]{1,0:T(8,128)(2,1)}, bf16[64,512]{1,0:T(8,128)(2,1)S(1)}, u32[]{:S(2)}, u32[]{:S(2)}) collective-permute-start(bf16[64,512]{1,0:T(8,128)(2,1)} %get-tuple-element.164), channel_id=1, source_target_pairs={{0,31},{1,30},{2,29},{3,28},{4,27},{5,26},{6,25},{7,24},{8,23},{9,... | collective-permute-start | bytes 196616 | tf_op jit(solution)/shard_map/ppermute | solution.py:594
  103.6 11.1 %collective-permute-start.1 = (bf16[64,512]{1,0:T(8,128)(2,1)}, bf16[64,512]{1,0:T(8,128)(2,1)S(1)}, u32[]{:S(2)}, u32[]{:S(2)}) collective-permute-start(bf16[64,512]{1,0:T(8,128)(2,1)} %get-tuple-element.103), channel_id=1, source_target_pairs={{0,1},{1,0},{2,3},{3,2},{4,5},{5,4},{6,7},{7,6},{8,9},{9,8},{10,11... | collective-permute-start | bytes 196616 | tf_op jit(solution)/shard_map/ppermute | solution.py:594
  107.3 11.6 %collective-permute-start.11 = (bf16[64,512]{1,0:T(8,128)(2,1)}, bf16[64,512]{1,0:T(8,128)(2,1)S(1)}, u32[]{:S(2)}, u32[]{:S(2)}) collective-permute-start(bf16[64,512]{1,0:T(8,128)(2,1)} %copy-done.65), channel_id=1, source_target_pairs={{0,11},{1,10},{2,9},{3,8},{4,15},{5,14},{6,13},{7,12},{8,3},{9,2},... | collective-permute-start | bytes 196616 | tf_op jit(solution)/shard_map/ppermute | solution.py:594
  110.2 9.6 %collective-permute-start.12 = (bf16[64,512]{1,0:T(8,128)(2,1)}, bf16[64,512]{1,0:T(8,128)(2,1)S(1)}, u32[]{:S(2)}, u32[]{:S(2)}) collective-permute-start(bf16[64,512]{1,0:T(8,128)(2,1)} %copy-done.64), channel_id=1, source_target_pairs={{0,12},{1,13},{2,14},{3,15},{4,8},{5,9},{6,10},{7,11},{8,4},{9,5},... | collective-permute-start | bytes 196616 | tf_op jit(solution)/shard_map/ppermute | solution.py:594
  110.8 10.2 %collective-permute-start.13 = (bf16[64,512]{1,0:T(8,128)(2,1)}, bf16[64,512]{1,0:T(8,128)(2,1)S(1)}, u32[]{:S(2)}, u32[]{:S(2)}) collective-permute-start(bf16[64,512]{1,0:T(8,128)(2,1)} %copy-done.63), channel_id=1, source_target_pairs={{0,13},{1,12},{2,15},{3,14},{4,9},{5,8},{6,11},{7,10},{8,5},{9,4},... | collective-permute-start | bytes 196616 | tf_op jit(solution)/shard_map/ppermute | solution.py:594
  114.7 11.2 %collective-permute-start.15 = (bf16[64,512]{1,0:T(8,128)(2,1)}, bf16[64,512]{1,0:T(8,128)(2,1)S(1)}, u32[]{:S(2)}, u32[]{:S(2)}) collective-permute-start(bf16[64,512]{1,0:T(8,128)(2,1)} %copy-done.61), channel_id=1, source_target_pairs={{0,15},{1,14},{2,13},{3,12},{4,11},{5,10},{6,9},{7,8},{8,7},{9,6},... | collective-permute-start | bytes 196616 | tf_op jit(solution)/shard_map/ppermute | solution.py:594
  126.4 9.6 %collective-permute-start.20 = (bf16[64,512]{1,0:T(8,128)(2,1)}, bf16[64,512]{1,0:T(8,128)(2,1)S(1)}, u32[]{:S(2)}, u32[]{:S(2)}) collective-permute-start(bf16[64,512]{1,0:T(8,128)(2,1)} %copy-done.55), channel_id=1, source_target_pairs={{0,20},{1,21},{2,22},{3,23},{4,16},{5,17},{6,18},{7,19},{8,28},{9,... | collective-permute-start | bytes 196616 | tf_op jit(solution)/shard_map/ppermute | solution.py:594
  127.5 12.7 %collective-permute-start.21 = (bf16[64,512]{1,0:T(8,128)(2,1)}, bf16[64,512]{1,0:T(8,128)(2,1)S(1)}, u32[]{:S(2)}, u32[]{:S(2)}) collective-permute-start(bf16[64,512]{1,0:T(8,128)(2,1)} %copy-done.54), channel_id=1, source_target_pairs={{0,21},{1,20},{2,23},{3,22},{4,17},{5,16},{6,19},{7,18},{8,29},{9,... | collective-permute-start | bytes 196616 | tf_op jit(solution)/shard_map/ppermute | solution.py:594
  129.7 10.5 %collective-permute-start.22 = (bf16[64,512]{1,0:T(8,128)(2,1)}, bf16[64,512]{1,0:T(8,128)(2,1)S(1)}, u32[]{:S(2)}, u32[]{:S(2)}) collective-permute-start(bf16[64,512]{1,0:T(8,128)(2,1)} %copy-done.53), channel_id=1, source_target_pairs={{0,22},{1,23},{2,20},{3,21},{4,18},{5,19},{6,16},{7,17},{8,30},{9,... | collective-permute-start | bytes 196616 | tf_op jit(solution)/shard_map/ppermute | solution.py:594
  131.4 12.6 %collective-permute-start.23 = (bf16[64,512]{1,0:T(8,128)(2,1)}, bf16[64,512]{1,0:T(8,128)(2,1)S(1)}, u32[]{:S(2)}, u32[]{:S(2)}) collective-permute-start(bf16[64,512]{1,0:T(8,128)(2,1)} %copy-done.52), channel_id=1, source_target_pairs={{0,23},{1,22},{2,21},{3,20},{4,19},{5,18},{6,17},{7,16},{8,31},{9,... | collective-permute-start | bytes 196616 | tf_op jit(solution)/shard_map/ppermute | solution.py:594
  134.4 11.4 %collective-permute-start.24 = (bf16[64,512]{1,0:T(8,128)(2,1)}, bf16[64,512]{1,0:T(8,128)(2,1)S(1)}, u32[]{:S(2)}, u32[]{:S(2)}) collective-permute-start(bf16[64,512]{1,0:T(8,128)(2,1)} %copy-done.49), channel_id=1, source_target_pairs={{0,24},{1,25},{2,26},{3,27},{4,28},{5,29},{6,30},{7,31},{8,16},{9,... | collective-permute-start | bytes 196616 | tf_op jit(solution)/shard_map/ppermute | solution.py:594
  136.0 13.6 %collective-permute-start.25 = (bf16[64,512]{1,0:T(8,128)(2,1)}, bf16[64,512]{1,0:T(8,128)(2,1)S(1)}, u32[]{:S(2)}, u32[]{:S(2)}) collective-permute-start(bf16[64,512]{1,0:T(8,128)(2,1)} %copy-done.48), channel_id=1, source_target_pairs={{0,25},{1,24},{2,27},{3,26},{4,29},{5,28},{6,31},{7,30},{8,17},{9,... | collective-permute-start | bytes 196616 | tf_op jit(solution)/shard_map/ppermute | solution.py:594
  140.2 9.4 %collective-permute-start.26 = (bf16[64,512]{1,0:T(8,128)(2,1)}, bf16[64,512]{1,0:T(8,128)(2,1)S(1)}, u32[]{:S(2)}, u32[]{:S(2)}) collective-permute-start(bf16[64,512]{1,0:T(8,128)(2,1)} %copy-done.47), channel_id=1, source_target_pairs={{0,26},{1,27},{2,24},{3,25},{4,30},{5,31},{6,28},{7,29},{8,18},{9,... | collective-permute-start | bytes 196616 | tf_op jit(solution)/shard_map/ppermute | solution.py:594
  140.2 11.5 %collective-permute-start.27 = (bf16[64,512]{1,0:T(8,128)(2,1)}, bf16[64,512]{1,0:T(8,128)(2,1)S(1)}, u32[]{:S(2)}, u32[]{:S(2)}) collective-permute-start(bf16[64,512]{1,0:T(8,128)(2,1)} %copy-done.46), channel_id=1, source_target_pairs={{0,27},{1,26},{2,25},{3,24},{4,31},{5,30},{6,29},{7,28},{8,19},{9,... | collective-permute-start | bytes 196616 | tf_op jit(solution)/shard_map/ppermute | solution.py:594
  144.0 11.3 %collective-permute-start.28 = (bf16[64,512]{1,0:T(8,128)(2,1)}, bf16[64,512]{1,0:T(8,128)(2,1)S(1)}, u32[]{:S(2)}, u32[]{:S(2)}) collective-permute-start(bf16[64,512]{1,0:T(8,128)(2,1)} %copy-done.45), channel_id=1, source_target_pairs={{0,28},{1,29},{2,30},{3,31},{4,24},{5,25},{6,26},{7,27},{8,20},{9,... | collective-permute-start | bytes 196616 | tf_op jit(solution)/shard_map/ppermute | solution.py:594
  145.8 22.3 %collective-permute-start.29 = (bf16[64,512]{1,0:T(8,128)(2,1)}, bf16[64,512]{1,0:T(8,128)(2,1)S(1)}, u32[]{:S(2)}, u32[]{:S(2)}) collective-permute-start(bf16[64,512]{1,0:T(8,128)(2,1)} %copy-done.39), channel_id=1, source_target_pairs={{0,29},{1,28},{2,31},{3,30},{4,25},{5,24},{6,27},{7,26},{8,21},{9,... | collective-permute-start | bytes 196616 | tf_op jit(solution)/shard_map/ppermute | solution.py:594
  149.6 20.9 %collective-permute-start.3 = (bf16[64,512]{1,0:T(8,128)(2,1)}, bf16[64,512]{1,0:T(8,128)(2,1)S(1)}, u32[]{:S(2)}, u32[]{:S(2)}) collective-permute-start(bf16[64,512]{1,0:T(8,128)(2,1)} %copy-done.38), channel_id=1, source_target_pairs={{0,3},{1,2},{2,1},{3,0},{4,7},{5,6},{6,5},{7,4},{8,11},{9,10},{10,... | collective-permute-start | bytes 196616 | tf_op jit(solution)/shard_map/ppermute | solution.py:594
  149.6 22.1 %collective-permute-start.30 = (bf16[64,512]{1,0:T(8,128)(2,1)}, bf16[64,512]{1,0:T(8,128)(2,1)S(1)}, u32[]{:S(2)}, u32[]{:S(2)}) collective-permute-start(bf16[64,512]{1,0:T(8,128)(2,1)} %copy-done.37), channel_id=1, source_target_pairs={{0,30},{1,31},{2,28},{3,29},{4,26},{5,27},{6,24},{7,25},{8,22},{9,... | collective-permute-start | bytes 196616 | tf_op jit(solution)/shard_map/ppermute | solution.py:594
  151.7 22.7 %collective-permute-start.31 = (bf16[64,512]{1,0:T(8,128)(2,1)}, bf16[64,512]{1,0:T(8,128)(2,1)S(1)}, u32[]{:S(2)}, u32[]{:S(2)}) collective-permute-start(bf16[64,512]{1,0:T(8,128)(2,1)} %copy-done.36), channel_id=1, source_target_pairs={{0,31},{1,30},{2,29},{3,28},{4,27},{5,26},{6,25},{7,24},{8,23},{9,... | collective-permute-start | bytes 196616 | tf_op jit(solution)/shard_map/ppermute | solution.py:594
  155.3 20.4 %collective-permute-start.4 = (bf16[64,512]{1,0:T(8,128)(2,1)}, bf16[64,512]{1,0:T(8,128)(2,1)S(1)}, u32[]{:S(2)}, u32[]{:S(2)}) collective-permute-start(bf16[64,512]{1,0:T(8,128)(2,1)} %copy-done.35), channel_id=1, source_target_pairs={{0,4},{1,5},{2,6},{3,7},{4,0},{5,1},{6,2},{7,3},{8,12},{9,13},{10,... | collective-permute-start | bytes 196616 | tf_op jit(solution)/shard_map/ppermute | solution.py:594
  168.1 26.3 %collective-permute-start.5 = (bf16[64,512]{1,0:T(8,128)(2,1)S(1)}, bf16[64,512]{1,0:T(8,128)(2,1)S(1)}, u32[]{:S(2)}, u32[]{:S(2)}) collective-permute-start(bf16[64,512]{1,0:T(8,128)(2,1)S(1)} %copy-done.34), channel_id=1, source_target_pairs={{0,5},{1,4},{2,7},{3,6},{4,1},{5,0},{6,3},{7,2},{8,13},{9,12},{10,... | collective-permute-start | bytes 196616 | tf_op jit(solution)/shard_map/ppermute | solution.py:594
  170.5 23.9 %collective-permute-start.6 = (bf16[64,512]{1,0:T(8,128)(2,1)S(1)}, bf16[64,512]{1,0:T(8,128)(2,1)S(1)}, u32[]{:S(2)}, u32[]{:S(2)}) collective-permute-start(bf16[64,512]{1,0:T(8,128)(2,1)S(1)} %copy-done.32), channel_id=1, source_target_pairs={{0,6},{1,7},{2,4},{3,5},{4,2},{5,3},{6,0},{7,1},{8,14},{9,15},{10,... | collective-permute-start | bytes 196616 | tf_op jit(solution)/shard_map/ppermute | solution.py:594
  171.7 22.7 %collective-permute-start.7 = (bf16[64,512]{1,0:T(8,128)(2,1)S(1)}, bf16[64,512]{1,0:T(8,128)(2,1)S(1)}, u32[]{:S(2)}, u32[]{:S(2)}) collective-permute-start(bf16[64,512]{1,0:T(8,128)(2,1)S(1)} %copy-done.30), channel_id=1, source_target_pairs={{0,7},{1,6},{2,5},{3,4},{4,3},{5,2},{6,1},{7,0},{8,15},{9,14},{10,... | collective-permute-start | bytes 196616 | tf_op jit(solution)/shard_map/ppermute | solution.py:594
  174.4 20.0 %collective-permute-start.8 = (bf16[64,512]{1,0:T(8,128)(2,1)S(1)}, bf16[64,512]{1,0:T(8,128)(2,1)S(1)}, u32[]{:S(2)}, u32[]{:S(2)}) collective-permute-start(bf16[64,512]{1,0:T(8,128)(2,1)S(1)} %copy-done.28), channel_id=1, source_target_pairs={{0,8},{1,9},{2,10},{3,11},{4,12},{5,13},{6,14},{7,15},{8,0},{9,1},... | collective-permute-start | bytes 196616 | tf_op jit(solution)/shard_map/ppermute | solution.py:594
  175.7 18.8 %collective-permute-start.9 = (bf16[64,512]{1,0:T(8,128)(2,1)S(1)}, bf16[64,512]{1,0:T(8,128)(2,1)S(1)}, u32[]{:S(2)}, u32[]{:S(2)}) collective-permute-start(bf16[64,512]{1,0:T(8,128)(2,1)S(1)} %copy-done.26), channel_id=1, source_target_pairs={{0,9},{1,8},{2,11},{3,10},{4,13},{5,12},{6,15},{7,14},{8,1},{9,0},... | collective-permute-start | bytes 196616 | tf_op jit(solution)/shard_map/ppermute | solution.py:594
  207.0 13.9 %collective-permute-start.66 = (bf16[64,512]{1,0:T(8,128)(2,1)S(1)}, bf16[64,512]{1,0:T(8,128)(2,1)S(1)}, u32[]{:S(2)}, u32[]{:S(2)}) collective-permute-start(bf16[64,512]{1,0:T(8,128)(2,1)S(1)} %get-tuple-element.170), channel_id=1, source_target_pairs={{0,5},{1,4},{2,7},{3,6},{4,1},{5,0},{6,3},{7,2},{8,13},{9,12},{10,... | collective-permute-start | bytes 196616 | tf_op jit(solution)/shard_map/ppermute | solution.py:594
  210.0 10.9 %collective-permute-start.67 = (bf16[64,512]{1,0:T(8,128)(2,1)S(1)}, bf16[64,512]{1,0:T(8,128)(2,1)S(1)}, u32[]{:S(2)}, u32[]{:S(2)}) collective-permute-start(bf16[64,512]{1,0:T(8,128)(2,1)S(1)} %get-tuple-element.171), channel_id=1, source_target_pairs={{0,6},{1,7},{2,4},{3,5},{4,2},{5,3},{6,0},{7,1},{8,14},{9,15},{10,... | collective-permute-start | bytes 196616 | tf_op jit(solution)/shard_map/ppermute | solution.py:594
  210.5 14.6 %collective-permute-start.68 = (bf16[64,512]{1,0:T(8,128)(2,1)S(1)}, bf16[64,512]{1,0:T(8,128)(2,1)S(1)}, u32[]{:S(2)}, u32[]{:S(2)}) collective-permute-start(bf16[64,512]{1,0:T(8,128)(2,1)S(1)} %get-tuple-element.172), channel_id=1, source_target_pairs={{0,7},{1,6},{2,5},{3,4},{4,3},{5,2},{6,1},{7,0},{8,15},{9,14},{10,... | collective-permute-start | bytes 196616 | tf_op jit(solution)/shard_map/ppermute | solution.py:594
  213.2 13.2 %collective-permute-start.73 = (bf16[64,512]{1,0:T(8,128)(2,1)S(1)}, bf16[64,512]{1,0:T(8,128)(2,1)S(1)}, u32[]{:S(2)}, u32[]{:S(2)}) collective-permute-start(bf16[64,512]{1,0:T(8,128)(2,1)S(1)} %get-tuple-element.177), channel_id=1, source_target_pairs={{0,12},{1,13},{2,14},{3,15},{4,8},{5,9},{6,10},{7,11},{8,4},{9,5},... | collective-permute-start | bytes 196616 | tf_op jit(solution)/shard_map/ppermute | solution.py:594
  214.3 17.0 %collective-permute-start.74 = (bf16[64,512]{1,0:T(8,128)(2,1)S(1)}, bf16[64,512]{1,0:T(8,128)(2,1)S(1)}, u32[]{:S(2)}, u32[]{:S(2)}) collective-permute-start(bf16[64,512]{1,0:T(8,128)(2,1)S(1)} %get-tuple-element.178), channel_id=1, source_target_pairs={{0,13},{1,12},{2,15},{3,14},{4,9},{5,8},{6,11},{7,10},{8,5},{9,4},... | collective-permute-start | bytes 196616 | tf_op jit(solution)/shard_map/ppermute | solution.py:594
  220.9 10.4 %collective-permute-start.75 = (bf16[64,512]{1,0:T(8,128)(2,1)S(1)}, bf16[64,512]{1,0:T(8,128)(2,1)S(1)}, u32[]{:S(2)}, u32[]{:S(2)}) collective-permute-start(bf16[64,512]{1,0:T(8,128)(2,1)S(1)} %get-tuple-element.179), channel_id=1, source_target_pairs={{0,14},{1,15},{2,12},{3,13},{4,10},{5,11},{6,8},{7,9},{8,6},{9,7},... | collective-permute-start | bytes 196616 | tf_op jit(solution)/shard_map/ppermute | solution.py:594
  220.9 16.4 %collective-permute-start.76 = (bf16[64,512]{1,0:T(8,128)(2,1)S(1)}, bf16[64,512]{1,0:T(8,128)(2,1)S(1)}, u32[]{:S(2)}, u32[]{:S(2)}) collective-permute-start(bf16[64,512]{1,0:T(8,128)(2,1)S(1)} %get-tuple-element.180), channel_id=1, source_target_pairs={{0,15},{1,14},{2,13},{3,12},{4,11},{5,10},{6,9},{7,8},{8,7},{9,6},... | collective-permute-start | bytes 196616 | tf_op jit(solution)/shard_map/ppermute | solution.py:594
  225.2 12.8 %collective-permute-start.81 = (bf16[64,512]{1,0:T(8,128)(2,1)S(1)}, bf16[64,512]{1,0:T(8,128)(2,1)S(1)}, u32[]{:S(2)}, u32[]{:S(2)}) collective-permute-start(bf16[64,512]{1,0:T(8,128)(2,1)S(1)} %get-tuple-element.185), channel_id=1, source_target_pairs={{0,20},{1,21},{2,22},{3,23},{4,16},{5,17},{6,18},{7,19},{8,28},{9,... | collective-permute-start | bytes 196616 | tf_op jit(solution)/shard_map/ppermute | solution.py:594
  226.4 14.6 %collective-permute-start.82 = (bf16[64,512]{1,0:T(8,128)(2,1)S(1)}, bf16[64,512]{1,0:T(8,128)(2,1)S(1)}, u32[]{:S(2)}, u32[]{:S(2)}) collective-permute-start(bf16[64,512]{1,0:T(8,128)(2,1)S(1)} %get-tuple-element.186), channel_id=1, source_target_pairs={{0,21},{1,20},{2,23},{3,22},{4,17},{5,16},{6,19},{7,18},{8,29},{9,... | collective-permute-start | bytes 196616 | tf_op jit(solution)/shard_map/ppermute | solution.py:594
  231.3 12.7 %collective-permute-start.83 = (bf16[64,512]{1,0:T(8,128)(2,1)S(1)}, bf16[64,512]{1,0:T(8,128)(2,1)S(1)}, u32[]{:S(2)}, u32[]{:S(2)}) collective-permute-start(bf16[64,512]{1,0:T(8,128)(2,1)S(1)} %get-tuple-element.187), channel_id=1, source_target_pairs={{0,22},{1,23},{2,20},{3,21},{4,18},{5,19},{6,16},{7,17},{8,30},{9,... | collective-permute-start | bytes 196616 | tf_op jit(solution)/shard_map/ppermute | solution.py:594
  231.3 28.0 %collective-permute-start.84 = (bf16[64,512]{1,0:T(8,128)(2,1)S(1)}, bf16[64,512]{1,0:T(8,128)(2,1)S(1)}, u32[]{:S(2)}, u32[]{:S(2)}) collective-permute-start(bf16[64,512]{1,0:T(8,128)(2,1)S(1)} %get-tuple-element.188), channel_id=1, source_target_pairs={{0,23},{1,22},{2,21},{3,20},{4,19},{5,18},{6,17},{7,16},{8,31},{9,... | collective-permute-start | bytes 196616 | tf_op jit(solution)/shard_map/ppermute | solution.py:594
  237.3 22.1 %collective-permute-start.89 = (bf16[64,512]{1,0:T(8,128)(2,1)S(1)}, bf16[64,512]{1,0:T(8,128)(2,1)S(1)}, u32[]{:S(2)}, u32[]{:S(2)}) collective-permute-start(bf16[64,512]{1,0:T(8,128)(2,1)S(1)} %get-tuple-element.193), channel_id=1, source_target_pairs={{0,28},{1,29},{2,30},{3,31},{4,24},{5,25},{6,26},{7,27},{8,20},{9,... | collective-permute-start | bytes 196616 | tf_op jit(solution)/shard_map/ppermute | solution.py:594
  237.9 24.7 %collective-permute-start.90 = (bf16[64,512]{1,0:T(8,128)(2,1)S(1)}, bf16[64,512]{1,0:T(8,128)(2,1)S(1)}, u32[]{:S(2)}, u32[]{:S(2)}) collective-permute-start(bf16[64,512]{1,0:T(8,128)(2,1)S(1)} %get-tuple-element.194), channel_id=1, source_target_pairs={{0,29},{1,28},{2,31},{3,30},{4,25},{5,24},{6,27},{7,26},{8,21},{9,... | collective-permute-start | bytes 196616 | tf_op jit(solution)/shard_map/ppermute | solution.py:594
  241.0 21.6 %collective-permute-start.91 = (bf16[64,512]{1,0:T(8,128)(2,1)S(1)}, bf16[64,512]{1,0:T(8,128)(2,1)S(1)}, u32[]{:S(2)}, u32[]{:S(2)}) collective-permute-start(bf16[64,512]{1,0:T(8,128)(2,1)S(1)} %get-tuple-element.195), channel_id=1, source_target_pairs={{0,30},{1,31},{2,28},{3,29},{4,26},{5,27},{6,24},{7,25},{8,22},{9,... | collective-permute-start | bytes 196616 | tf_op jit(solution)/shard_map/ppermute | solution.py:594
  244.0 18.8 %collective-permute-start.92 = (bf16[64,512]{1,0:T(8,128)(2,1)S(1)}, bf16[64,512]{1,0:T(8,128)(2,1)S(1)}, u32[]{:S(2)}, u32[]{:S(2)}) collective-permute-start(bf16[64,512]{1,0:T(8,128)(2,1)S(1)} %get-tuple-element.196), channel_id=1, source_target_pairs={{0,31},{1,30},{2,29},{3,28},{4,27},{5,26},{6,25},{7,24},{8,23},{9,... | collective-permute-start | bytes 196616 | tf_op jit(solution)/shard_map/ppermute | solution.py:594
  268.6 9.2 %collective-permute-start.79 = (bf16[64,512]{1,0:T(8,128)(2,1)S(1)}, bf16[64,512]{1,0:T(8,128)(2,1)S(1)}, u32[]{:S(2)}, u32[]{:S(2)}) collective-permute-start(bf16[64,512]{1,0:T(8,128)(2,1)S(1)} %get-tuple-element.183), channel_id=1, source_target_pairs={{0,18},{1,19},{2,16},{3,17},{4,22},{5,23},{6,20},{7,21},{8,26},{9,... | collective-permute-start | bytes 196616 | tf_op jit(solution)/shard_map/ppermute | solution.py:594
  (98 other events, 501.6 us)

commit v3 on v1

--- a/solution.py
+++ b/solution.py
@@ -1,6 +1,5 @@
 import jax
 import jax.numpy as jnp
-import numpy as np
 from jax import lax
 from jax.experimental import pallas as pl
 from jax.experimental.pallas import tpu as pltpu
@@ -19,51 +18,80 @@
     )
 
 
-def permutation(order):
-    matrix = np.zeros((order.size, order.size), np.float32)
-    matrix[np.arange(order.size), order.reshape(-1)] = 1.0
-    return matrix.astype(jnp.bfloat16)
-
-
-def permuted(matrix, rows):
-    return jnp.dot(matrix, rows, preferred_element_type=F32).astype(BF16)
-
-
-def pack_obs_kernel(order, rows, out):
+def split(value, size):
+    return value >> (size.bit_length() - 1), value & (size - 1)
+
+
+def iota(rows, cols, dim):
+    return lax.broadcasted_iota(jnp.int32, (rows, cols), dim)
+
+
+def dot_bf16(left, right):
+    return jnp.dot(left, right, preferred_element_type=F32)
+
+
+def moved(left, right):
+    return dot_bf16(left, right).astype(BF16)
+
+
+def ones_at(condition):
+    return jnp.where(condition, 1.0, 0.0).astype(BF16)
+
+
+def pack_obs_kernel(rows, out, order):
     _, width, owners, block, own = out.shape
-    flat = rows[...].reshape(order.shape[0], own)
-    out[...] = permuted(order[...], flat).reshape(1, width, owners, block, own)
+    size = order.shape[0]
+    patches = width * owners
+
+    @pl.when((pl.program_id(0) == 0) & (pl.program_id(1) == 0))
+    def _():
+        rest, member = split(iota(size, size, 0), block)
+        part, owner = split(rest, owners)
+        order[...] = ones_at(iota(size, size, 1) == member * patches + owner * width + part)
+
+    out[...] = moved(order[...], rows[...].reshape(size, own)).reshape(out.shape)
 
 
 def pack_obs(hx_values, width):
     slabs, local, _, patches, own = hx_values.shape
     owners = patches // width
     block = 16
-    index = np.arange(block * patches).reshape(block, owners, width)
-    order = permutation(index.transpose(2, 1, 0))
     return pl.pallas_call(
         pack_obs_kernel,
         grid=(slabs, local // block),
-        in_specs=[
-            pl.BlockSpec(order.shape, lambda s, g: (0, 0)),
-            pl.BlockSpec((1, block, 1, patches, own), lambda s, g: (s, g, 0, 0, 0)),
-        ],
+        in_specs=[pl.BlockSpec((1, block, 1, patches, own), lambda s, g: (s, g, 0, 0, 0))],
         out_specs=pl.BlockSpec((1, width, owners, block, own), lambda s, g: (s, 0, 0, g, 0)),
         out_shape=jax.ShapeDtypeStruct((slabs, width, owners, local, own), BF16),
+        scratch_shapes=[pltpu.VMEM((block * patches, block * patches), BF16)],
         compiler_params=params(2),
-    )(order, hx_values)
-
-
-def lane_order(width, lanes):
-    index = np.arange(width * lanes).reshape(width, width, lanes // width)
-    return permutation(index.transpose(1, 0, 2)).T
-
-
-def pack_state_kernel(order, swap, cells, out):
+        name="pack_obs",
+    )(hx_values)
+
+
+def swapped(width, lanes):
+    size = width * lanes
+    outer, cell = split(iota(size, size, 1), lanes // width)
+    first, second = split(outer, width)
+    return ones_at(iota(size, size, 0) == (second * width + first) * (lanes // width) + cell)
+
+
+def transposed(outer, inner):
+    size = outer * inner
+    first, second = split(iota(size, size, 0), inner)
+    return ones_at(iota(size, size, 1) == second * outer + first)
+
+
+def pack_state_kernel(cells, out, order, swap):
     _, width, owners, block, size = out.shape
     lanes = cells.shape[3] // owners
     tiles = size // lanes
-    rows = permuted(order[...], cells[...].reshape(order.shape[0], cells.shape[3]))
+
+    @pl.when((pl.program_id(0) == 0) & (pl.program_id(1) == 0))
+    def _():
+        order[...] = transposed(cells.shape[2], block)
+        swap[...] = swapped(width, lanes)
+
+    rows = moved(order[...], cells[...].reshape(order.shape[0], cells.shape[3]))
     parts = []
     for owner in range(owners):
         for tile in range(tiles):
@@ -75,7 +103,7 @@
                 for half in range(width)
             ]
             parts.append(jnp.concatenate(pieces, axis=1))
-    mixed = permuted_lanes(jnp.concatenate(parts, axis=0), swap[...])
+    mixed = moved(jnp.concatenate(parts, axis=0), swap[...])
     for owner in range(owners):
         for tile in range(tiles):
             at = (owner * tiles + tile) * block
@@ -85,37 +113,39 @@
                 ]
 
 
-def permuted_lanes(rows, matrix):
-    return jnp.dot(rows, matrix, preferred_element_type=F32).astype(BF16)
-
-
 def pack_state(member_state, width, owners):
     slabs, local, cells_a, cols = member_state.shape
     lanes = cols // owners
     size = cells_a * lanes // width
     block = 32
-    index = np.arange(block * cells_a).reshape(block, cells_a)
-    order = permutation(index.T)
-    swap = lane_order(width, lanes)
     return pl.pallas_call(
         pack_state_kernel,
         grid=(slabs, local // block),
         in_specs=[
-            pl.BlockSpec(order.shape, lambda s, g: (0, 0)),
-            pl.BlockSpec(swap.shape, lambda s, g: (0, 0)),
             pl.BlockSpec((1, block, cells_a, cols), lambda s, g: (s, g, 0, 0)),
         ],
         out_specs=pl.BlockSpec((1, width, owners, block, size), lambda s, g: (s, 0, 0, g, 0)),
         out_shape=jax.ShapeDtypeStruct((slabs, width, owners, local, size), BF16),
+        scratch_shapes=[
+            pltpu.VMEM((block * cells_a, block * cells_a), BF16),
+            pltpu.VMEM((width * lanes, width * lanes), BF16),
+        ],
         compiler_params=params(2),
-    )(order, swap, member_state)
-
-
-def unpack_state_kernel(order, swap, packed, out):
+        name="pack_state",
+    )(member_state)
+
+
+def unpack_state_kernel(packed, out, order, swap):
     _, width, owners, block, size = packed.shape
     cells_a = out.shape[2]
     tiles = cells_a // width
     lanes = size // tiles
+
+    @pl.when((pl.program_id(0) == 0) & (pl.program_id(1) == 0))
+    def _():
+        order[...] = transposed(block, cells_a)
+        swap[...] = swapped(width, lanes)
+
     parts = []
     for owner in range(owners):
         for tile in range(tiles):
@@ -124,7 +154,7 @@
                 for part in range(width)
             ]
             parts.append(jnp.concatenate(pieces, axis=1))
-    mixed = permuted_lanes(jnp.concatenate(parts, axis=0), swap[...])
+    mixed = moved(jnp.concatenate(parts, axis=0), swap[...])
     columns = []
     for owner in range(owners):
         rows = []
@@ -133,7 +163,7 @@
             at = (owner * tiles + tile) * block
             rows.append(mixed[at : at + block, half * lanes : (half + 1) * lanes])
         columns.append(jnp.concatenate(rows, axis=0))
-    rows = permuted(order[...], jnp.concatenate(columns, axis=1))
+    rows = moved(order[...], jnp.concatenate(columns, axis=1))
     out[...] = rows.reshape(out.shape)
 
 
@@ -142,25 +172,21 @@
     lanes = size * width // cells_a
     cols = owners * lanes
     block = 32
-    index = np.arange(block * cells_a).reshape(cells_a, block)
-    order = permutation(index.T)
-    swap = lane_order(width, lanes).T
     return pl.pallas_call(
         unpack_state_kernel,
         grid=(slabs, local // block),
         in_specs=[
-            pl.BlockSpec(order.shape, lambda s, g: (0, 0)),
-            pl.BlockSpec(swap.shape, lambda s, g: (0, 0)),
             pl.BlockSpec((1, width, owners, block, size), lambda s, g: (s, 0, 0, g, 0)),
         ],
         out_specs=pl.BlockSpec((1, block, cells_a, cols), lambda s, g: (s, g, 0, 0)),
         out_shape=jax.ShapeDtypeStruct((slabs, local, cells_a, cols), BF16),
+        scratch_shapes=[
+            pltpu.VMEM((block * cells_a, block * cells_a), BF16),
+            pltpu.VMEM((width * lanes, width * lanes), BF16),
+        ],
         compiler_params=params(2),
-    )(order, swap, packed)
-
-
-def dot_bf16(left, right):
-    return jnp.dot(left, right, preferred_element_type=F32)
+        name="unpack_state",
+    )(packed)
 
 
 def transform_kernel(before, middle, after, obs, scale, out, pert, weighted):
@@ -181,9 +207,7 @@
             innovation = obs[0, :, cols] - mean
             projected += jnp.sum(scaled.astype(F32) * innovation, axis=1, keepdims=True)
             start += half
-    rows = lax.broadcasted_iota(jnp.int32, (total, total), 0)
-    columns = lax.broadcasted_iota(jnp.int32, (total, total), 1)
-    diagonal = rows == columns
+    diagonal = iota(total, total, 0) == iota(total, total, 1)
     gram = lax.dot_general(
         weighted[...], pert[...], (((1,), (1,)), ((), ())), preferred_element_type=F32
     )
@@ -195,7 +219,7 @@
         product = root.astype(F32) if inverse is None else dot_bf16(inverse.astype(BF16), root)
         correction = (jnp.where(diagonal, 1.5, 0.0) - 0.5 * product).astype(BF16)
         if iteration + 1 < ITERS:
-            root = dot_bf16(root, correction).astype(BF16)
+            root = moved(root, correction)
         if inverse is None:
             inverse = correction.astype(F32)
         else:
@@ -208,9 +232,8 @@
 
 
 def transforms(hx_rows, obs_rows, scale_rows, count, wraps):
-    total, own = hx_rows.shape[1:]
+    held, total, own = hx_rows.shape
     half = own // 2
-    held = hx_rows.shape[0]
     shift = 0 if wraps else 1
     flops = count * (2 * total * total * 2 * own + 18 * total**3)
     return pl.pallas_call(
@@ -230,40 +253,42 @@
         cost_estimate=pl.CostEstimate(
             flops=flops, bytes_accessed=4 * count * total * total * 2, transcendentals=0
         ),
+        name="transform",
     )(hx_rows, hx_rows, hx_rows, obs_rows, scale_rows)
 
 
-def centre(state, pert, means):
-    for a in range(state.shape[0]):
-        values = state[a].astype(F32)
-        mean = jnp.sum(values, axis=0, keepdims=True) * (1.0 / state.shape[1])
-        means[a] = mean
-        pert[a] = (values - mean).astype(BF16)
-
-
-def transport(tiles, here, ahead, behind, low):
+def centred(values):
+    values = values.astype(F32)
+    mean = jnp.sum(values, axis=0, keepdims=True) * (1.0 / values.shape[0])
+    return mean, (values - mean).astype(BF16)
+
+
+def stencil(c):
+    step = [0.5 * (c * c + c), 1.0 - c * c, 0.5 * (c * c - c)]
+    taps = step
+    for _ in range(STEPS - 1):
+        longer = [jnp.zeros_like(c)] * (len(taps) + 2)
+        for i, tap in enumerate(taps):
+            for j, weight in enumerate(step):
+                longer[i + j] = longer[i + j] + tap * weight
+        taps = longer
+    return taps
+
+
+def transport(tiles, taps, low):
     count, depth = len(tiles), len(tiles[0])
-    size = tiles[0][0].shape[1]
-    shift = size // 2
-    for _ in range(STEPS):
-        first = [pltpu.roll(column[0], shift, 1) for column in tiles]
-        last = [pltpu.roll(column[depth - 1], shift, 1) for column in tiles]
-        moved = []
-        for a in range(count):
-            column = []
-            for k in range(depth):
-                if k + 1 < depth:
-                    after = tiles[a][k + 1]
-                else:
-                    after = jnp.where(low, first[a], first[(a + 1) % count])
-                if k > 0:
-                    prior = tiles[a][k - 1]
-                else:
-                    prior = jnp.where(low, last[(a + count - 1) % count], last[a])
-                column.append(here * tiles[a][k] + ahead * after + behind * prior)
-            moved.append(column)
-        tiles = moved
-    return tiles
+    shift = tiles[0][0].shape[1] // 2
+    turned = [[pltpu.roll(tile, shift, 1) for tile in column] for column in tiles]
+    results = []
+    for a in range(count):
+        before = [jnp.where(low, u, v) for u, v in zip(turned[(a - 1) % count], turned[a])]
+        after = [jnp.where(low, u, v) for u, v in zip(turned[a], turned[(a + 1) % count])]
+        line = before + tiles[a] + after
+        start = depth - STEPS
+        results.append(
+            [sum(taps[t] * line[start + k + t] for t in range(len(taps))) for k in range(depth)]
+        )
+    return results
 
 
 def forecast_kernel(state, transform, speed, out, pert, means, fields):
@@ -272,25 +297,30 @@
 
     @pl.when(pl.program_id(0) == 0)
     def _():
-        centre(state, pert, means)
+        for a in range(count):
+            means[a], pert[a] = centred(state[a])
 
     for a in range(count):
-        fields[a] = (dot_bf16(transform[a], pert[a]) + means[a]).astype(BF16)
+        values = dot_bf16(transform[a], pert[a]) + means[a]
+        fields[a] = values.astype(BF16).astype(F32)
     chunk = 16
-    c = jnp.broadcast_to(speed[...], (chunk, lanes))
-    here, ahead, behind = 1.0 - c * c, 0.5 * (c * c - c), 0.5 * (c * c + c)
-    low = lax.broadcasted_iota(jnp.int32, (chunk, lanes), 1) < lanes // 2
+    taps = stencil(jnp.broadcast_to(speed[...], (8, lanes)))
+    low = iota(8, lanes, 1) < lanes // 2
 
     def rows_at(step, carry):
-        rows = pl.ds(pl.multiple_of(step * chunk, chunk), chunk)
-        tiles = [
-            [fields[a, rows, k * lanes : (k + 1) * lanes].astype(F32) for k in range(size // lanes)]
-            for a in range(count)
-        ]
-        tiles = transport(tiles, here, ahead, behind, low)
+        parts = []
+        for half in range(chunk // 8):
+            at = pl.ds(pl.multiple_of(step * chunk + half * 8, 8), 8)
+            tiles = [
+                [fields[a, at, k * lanes : (k + 1) * lanes] for k in range(size // lanes)]
+                for a in range(count)
+            ]
+            parts.append(transport(tiles, taps, low))
+        at = pl.ds(pl.multiple_of(step * chunk, chunk), chunk)
         for a in range(count):
             for k in range(size // lanes):
-                out[a, rows, k * lanes : (k + 1) * lanes] = tiles[a][k].astype(BF16)
+                value = jnp.concatenate([part[a][k] for part in parts], axis=0)
+                out[a, at, k * lanes : (k + 1) * lanes] = value.astype(BF16)
         return carry
 
     lax.fori_loop(0, block // chunk, rows_at, 0)
@@ -312,15 +342,16 @@
         scratch_shapes=[
             pltpu.VMEM((count, total, size), BF16),
             pltpu.VMEM((count, 1, size), F32),
-            pltpu.VMEM((count, block, size), BF16),
+            pltpu.VMEM((count, block, size), F32),
         ],
         compiler_params=params(1),
+        name="forecast",
     )(state, transform, speed)
 
 
-def analysis_kernel(state, transform, out, pert, means):
-    centre(state, pert, means)
-    out[0] = (dot_bf16(transform[0], pert[0]) + means[0]).astype(BF16)
+def analysis_kernel(state, transform, out):
+    mean, pert = centred(state[0])
+    out[0] = (dot_bf16(transform[0], pert) + mean).astype(BF16)
 
 
 def analyses(state, transform):
@@ -334,8 +365,8 @@
         ],
         out_specs=pl.BlockSpec((1, total, size), lambda a: (a, 0, 0)),
         out_shape=jax.ShapeDtypeStruct((count, total, size), BF16),
-        scratch_shapes=[pltpu.VMEM((1, total, size), BF16), pltpu.VMEM((1, 1, size), F32)],
         compiler_params=params(1),
+        name="analysis",
     )(state, transform)
 
 
@@ -422,7 +453,7 @@
     column = (lax.axis_index("mem") * width + part) * cells_b
     speed = lax.dynamic_slice(courant, (slab, column), (1, cells_b))
     speed = jnp.concatenate([speed] * width, axis=1)
-    if groups == 1 and width == 2:
+    if groups == 1 and width == 2 and cells_a // width >= STEPS:
         fields = forecasts(state, transform, speed)
     else:
         fields = shared_transport(analyses(state, transform), speed, width, count)

time: 187 us -> 180 us (0.963)
  Pallas kernels: 42.1 us -> 35.8 us
    pallas_call x1, Pallas kernels: 14.7 us -> 8.02 us  [forecasts(): pl.pallas_call(forecast_kernel, grid=(total // block,), in_specs=[pl.Bloc...]
    unnamed x22 -> x14, local copies, waits for them, and re-layouts: 6.48 us -> 5.55 us
where the time goes in v3:
time: 180 us; the launch traced here: 179 us
  blocking collectives  69.7 us (39%)
  waiting for transfers between devices  56.5 us (31%)
  Pallas kernels  35.8 us (20%)
  starting transfers between devices  10.3 us (6%)
  local copies, waits for them, and re-layouts  6.45 us (4%)
    all_to_all x2, waiting for transfers between devices, exchange(): lax.all_to_all(blocks, ('sub', 'mem'), split_axis=0, concat_axis=0, tiled...  56.5 us
    all_to_all x1, blocking collectives, exchange(): lax.all_to_all(blocks, ('sub', 'mem'), split_axis=0, concat_axis=0, tiled...  52 us
    pallas_call x1, Pallas kernels, transforms(): pl.pallas_call(transform_kernel, grid=(count,), in_specs=[pl.BlockSpec((1...  19.7 us
    all_gather x1, blocking collectives, advance(): stats = lax.all_gather(stats, 'sub', axis=0)  17.8 us
    all_to_all x2, starting transfers between devices, exchange(): lax.all_to_all(blocks, ('sub', 'mem'), split_axis=0, concat_axis=0, tiled...  10.3 us
    pallas_call x1, Pallas kernels, forecasts(): pl.pallas_call(forecast_kernel, grid=(total // block,), in_specs=[pl.Bloc...  8.02 us
    unnamed x14, local copies, waits for them, and re-layouts  5.55 us
    pallas_call x1, Pallas kernels, unpack_state(): pl.pallas_call(unpack_state_kernel, grid=(slabs, local // block), in_spec...  3.67 us
  transfers between devices with their start and end apart: 2, of which 2 were waited for; matrix products, arithmetic and copies ran while one was open for 1% of the time, Pallas kernels for 12%

profile of v3, /device:TPU:0, one launch (start us, length us, event | category | flops | bytes accessed | tf_op | source)
XLA Modules:
  0.0 179.2 jit_solution(11227441187648080615)
XLA Ops:
  0.0 0.0 copy-start.3
  0.0 1.6 copy-done.3
  1.6 2.1 %pack_obs.1 = bf16[2,2,8,64,512]{4,3,2,1,0:T(8,128)(2,1)S(1)} custom-call(bf16[2,64,1,16,512]{4,3,2,1,0:T(8,128)(2,1)S(1)} %copy-done.3), custom_call_target="tpu_custom_call" | custom-call | tf_op jit(solution)/shard_map/pack_obs/pallas_call | solution.py:59
  3.7 0.0 copy-start.1
  3.7 1.3 copy-done.1
  5.0 0.0 copy-start.4
  5.0 7.4 %all-to-all-start.1 = ((bf16[32,64,512]{2,1,0:T(8,128)(2,1)}), bf16[32,64,512]{2,1,0:T(8,128)(2,1)}, u32[]{:S(2)}, u32[]{:S(2)}) async-start(bf16[32,64,512]{2,1,0:T(8,128)(2,1)} %bitcast.22), calls=%async_computation.1 | async-start | bytes 4194304 | tf_op jit(solution)/shard_map/all_to_all | solution.py:419
  12.4 0.0 copy-done.4
  12.5 2.3 %pack_state.1 = bf16[2,2,8,64,512]{4,3,2,1,0:T(8,128)(2,1)S(1)} custom-call(bf16[2,64,8,1024]{3,2,1,0:T(8,128)(2,1)S(1)} %copy-done.4), custom_call_target="tpu_custom_call" | custom-call | tf_op jit(solution)/shard_map/pack_state/pallas_call | solution.py:121
  14.8 0.0 copy-start
  14.8 1.3 copy-done
  16.1 46.4 %all-to-all-done.1 = bf16[32,64,512]{2,1,0:T(8,128)(2,1)} async-done(((bf16[32,64,512]{2,1,0:T(8,128)(2,1)}), bf16[32,64,512]{2,1,0:T(8,128)(2,1)}, u32[]{:S(2)}, u32[]{:S(2)}) %all-to-all-start.1) | async-done | bytes 2097184 | tf_op jit(solution)/shard_map/all_to_all | solution.py:419
  62.5 0.0 copy-start.5
  62.5 0.0 copy-start.6
  62.5 2.9 %all-to-all-start = ((bf16[32,64,512]{2,1,0:T(8,128)(2,1)}), bf16[32,64,512]{2,1,0:T(8,128)(2,1)S(1)}, u32[]{:S(2)}, u32[]{:S(2)}) async-start(bf16[32,64,512]{2,1,0:T(8,128)(2,1)} %bitcast.21), calls=%async_computation | async-start | bytes 4194304 | tf_op jit(solution)/shard_map/all_to_all | solution.py:419
  65.4 0.0 copy-done.5
  65.5 0.0 copy-done.6
  65.5 17.8 %all-gather = bf16[8,2,2,512]{3,1,0,2:T(2,128)(2,1)S(1)} all-gather(bf16[2,2,2,512]{3,1,0,2:T(2,128)(2,1)S(1)} %pad_maximum_fusion.2), channel_id=2, replica_groups=mesh['sub'=4,'mem'=8] {'sub'}, dimensions={0}, use_global_device_ids=true | all-gather | bytes 40960 | tf_op jit(solution)/shard_map/all_gather | solution.py:432
  83.3 0.1 reverse.4
  83.4 0.8 dynamic_slice.7
  84.1 0.1 pad_maximum_fusion.4.speed
  84.4 19.7 %transform.1 = bf16[4,512,512]{2,1,0:T(8,128)(2,1)S(1)} custom-call(bf16[4,512,512]{2,1,0:T(8,128)(2,1)} %bitcast.3.before.middle.after, bf16[4,512,512]{2,1,0:T(8,128)(2,1)} %bitcast.3.before.middle.after, bf16[4,512,512]{2,1,0:T(8,128)(2,1)} %bitcast.3.before.middle.after, f32[4,1,1024]{2,1,0:T(1,128)S(1)} %get-tuple-element.6.obs, ...), custom_call_target="tpu_custom_call" | custom-call | flops 11811160064 | bytes 8388608 | tf_op jit(solution)/shard_map/transform/pallas_call | solution.py:239
  104.1 0.0 copy-start.2
  104.1 1.3 copy-done.2
  105.4 10.1 %all-to-all-done = bf16[32,64,512]{2,1,0:T(8,128)(2,1)S(1)} async-done(((bf16[32,64,512]{2,1,0:T(8,128)(2,1)}), bf16[32,64,512]{2,1,0:T(8,128)(2,1)S(1)}, u32[]{:S(2)}, u32[]{:S(2)}) %all-to-all-start) | async-done | bytes 2097184 | tf_op jit(solution)/shard_map/all_to_all | solution.py:419
  115.5 8.0 %forecast.1 = bf16[4,512,512]{2,1,0:T(8,128)(2,1)S(1)} custom-call(bf16[4,512,512]{2,1,0:T(8,128)(2,1)S(1)} %bitcast.19, bf16[4,512,512]{2,1,0:T(8,128)(2,1)} %copy-done.2, f32[1,128]{1,0:T(1,128)S(1)} %pad_maximum_fusion.4.speed), custom_call_target="tpu_custom_call" | custom-call | tf_op jit(solution)/shard_map/forecast/pallas_call | solution.py:332
  123.5 52.0 %all_to_all.15 = bf16[32,64,512]{2,1,0:T(8,128)(2,1)S(1)} all-to-all(bf16[32,64,512]{2,1,0:T(8,128)(2,1)S(1)} %bitcast.20), channel_id=1, replica_groups=mesh['sub'=4,'mem'=8] {'sub','mem'}, dimensions={0} | all-to-all | bytes 4194304 | tf_op jit(solution)/shard_map/all_to_all | solution.py:419
  175.5 3.7 %unpack_state.1 = bf16[2,64,8,1024]{3,2,1,0:T(8,128)(2,1)} custom-call(bf16[2,2,8,64,512]{4,3,2,1,0:T(8,128)(2,1)S(1)} %bitcast.23), custom_call_target="tpu_custom_call" | custom-call | tf_op jit(solution)/shard_map/unpack_state/pallas_call | solution.py:175
  (11 shorter events, 0.2 us)
Async XLA Ops:
  0.0 1.6 copy-start.3
  3.7 1.3 copy-start.1
  5.0 7.4 %copy-start.4 = (bf16[2,64,8,1024]{3,2,1,0:T(8,128)(2,1)S(1)}, bf16[2,64,8,1024]{3,2,1,0:T(8,128)(2,1)}, u32[]{:S(2)}) copy-start(bf16[2,64,8,1024]{3,2,1,0:T(8,128)(2,1)} %cells.1) | copy-start | bytes 6291460
  5.0 57.5 %all-to-all-start.1 = ((bf16[32,64,512]{2,1,0:T(8,128)(2,1)}), bf16[32,64,512]{2,1,0:T(8,128)(2,1)}, u32[]{:S(2)}, u32[]{:S(2)}) async-start(bf16[32,64,512]{2,1,0:T(8,128)(2,1)} %bitcast.22), calls=%async_computation.1 | async-start | bytes 4194304 | tf_op jit(solution)/shard_map/all_to_all | solution.py:419
  14.8 1.3 copy-start
  62.5 2.9 %copy-start.5 = (bf16[2,1,2,512]{3,2,1,0:T(2,128)(2,1)S(1)}, bf16[2,1,2,512]{3,2,1,0:T(2,128)(2,1)}, u32[]{:S(2)}) copy-start(bf16[2,1,2,512]{3,2,1,0:T(2,128)(2,1)} %param.8) | copy-start | bytes 12292
  62.5 2.9 %copy-start.6 = (bf16[2,1,2,512]{3,2,1,0:T(2,128)(2,1)S(1)}, bf16[2,1,2,512]{3,2,1,0:T(2,128)(2,1)}, u32[]{:S(2)}) copy-start(bf16[2,1,2,512]{3,2,1,0:T(2,128)(2,1)} %param.7) | copy-start | bytes 12292
  62.5 53.0 %all-to-all-start = ((bf16[32,64,512]{2,1,0:T(8,128)(2,1)}), bf16[32,64,512]{2,1,0:T(8,128)(2,1)S(1)}, u32[]{:S(2)}, u32[]{:S(2)}) async-start(bf16[32,64,512]{2,1,0:T(8,128)(2,1)} %bitcast.21), calls=%async_computation | async-start | bytes 4194304 | tf_op jit(solution)/shard_map/all_to_all | solution.py:419
  104.1 1.3 copy-start.2

commit v4 on v3

v4 whole, which is shorter than its diff:
```python
import jax
import jax.numpy as jnp
from jax import lax
from jax.experimental import pallas as pl
from jax.experimental.pallas import tpu as pltpu
from jax.sharding import PartitionSpec as P

ITERS = 4
STEPS = 4
PAIR = 2
SPARE = 16
F32 = jnp.float32
BF16 = jnp.bfloat16
VMEM_LIMIT = 60 * 1024 * 1024


def params(count):
    return pltpu.CompilerParams(
        dimension_semantics=("arbitrary",) * count, vmem_limit_bytes=VMEM_LIMIT
    )


def split(value, size):
    return value >> (size.bit_length() - 1), value & (size - 1)


def iota(rows, cols, dim):
    return lax.broadcasted_iota(jnp.int32, (rows, cols), dim)


def dot_bf16(left, right):
    return jnp.dot(left, right, preferred_element_type=F32)


def moved(left, right):
    return dot_bf16(left, right).astype(BF16)


def ones_at(condition):
    return jnp.where(condition, 1.0, 0.0).astype(BF16)


def own_layer():
    return lax.axis_index("mem") >> 1


def own_bit():
    return lax.axis_index("mem") & 1


def pack_obs_kernel(rows, *refs, layers, width, given):
    stats, outs, order = refs[:given], refs[given:-1], refs[-1]
    local, patches, own = rows.shape[1], rows.shape[3], rows.shape[4]
    size = order.shape[0]
    block = size // patches

    @pl.when(pl.program_id(0) == 0)
    def _():
        rest, member = split(iota(size, size, 0), block)
        rest, layer = split(rest, layers)
        part, bit = split(rest, PAIR)
        owner = (layer ^ own_layer()) * PAIR + bit
        order[...] = ones_at(iota(size, size, 1) == member * patches + owner * width + part)

    for at in range(0, local, block):
        flat = moved(order[...], rows[0, at : at + block].reshape(size, own))
        flat = flat.reshape(width * PAIR, layers, block, own)
        for layer in range(layers):
            if stats:
                start = layer * local + at
                outs[0][0, :, start : start + block, :] = flat[:, layer]
            else:
                outs[layer][0, :, at : at + block, :] = flat[:, layer]
    if stats:
        value, variance = (ref[0, 0].astype(F32) for ref in stats)
        line = iota(SPARE, own, 0)
        for part in range(width):
            spare = jnp.where(line == 0, value[part : part + 1], variance[part : part + 1])
            for bit in range(PAIR):
                outs[0][0, part * PAIR + bit, layers * local :, :] = spare.astype(BF16)


def pack_obs(hx_values, layers, piece, stats):
    slabs, members, _, patches, own = hx_values.shape
    width = patches // (layers * PAIR)
    local = members // 2
    block = 16

    def kernel(*refs):
        pack_obs_kernel(*refs, layers=layers, width=width, given=len(stats))

    held = width * PAIR
    shapes = [(held, local, own)] * layers
    if stats:
        shapes = [(held, layers * local + SPARE, own)]
    return pl.pallas_call(
        kernel,
        grid=(slabs,),
        in_specs=[pl.BlockSpec((1, local, 1, patches, own), lambda s: (s, piece, 0, 0, 0))]
        + [pl.BlockSpec((1, 1, width, own), lambda s: (s, 0, 0, 0))] * len(stats),
        out_specs=[pl.BlockSpec((1, *shape), lambda s: (s, 0, 0, 0)) for shape in shapes],
        out_shape=[jax.ShapeDtypeStruct((slabs, *shape), BF16) for shape in shapes],
        scratch_shapes=[pltpu.VMEM((block * patches, block * patches), BF16)],
        compiler_params=params(1),
        name="pack_obs",
    )(hx_values, *stats)


def swapped(width, lanes):
    size = width * lanes
    outer, cell = split(iota(size, size, 1), lanes // width)
    first, second = split(outer, width)
    return ones_at(iota(size, size, 0) == (second * width + first) * (lanes // width) + cell)


def transposed(outer, inner):
    size = outer * inner
    first, second = split(iota(size, size, 0), inner)
    return ones_at(iota(size, size, 1) == second * outer + first)


def pack_state_kernel(cells, out, order, swap):
    _, width, _, layers, block, size = out.shape
    cells_a, cols = cells.shape[2:]
    lanes = cols // (layers * PAIR)
    tiles = size // lanes

    @pl.when((pl.program_id(0) == 0) & (pl.program_id(1) == 0))
    def _():
        order[...] = transposed(cells_a, block)
        swap[...] = swapped(width, lanes)

    rows = moved(order[...], cells[...].reshape(block * cells_a, cols))
    parts = []
    for owner in range(layers * PAIR):
        for tile in range(tiles):
            pieces = [
                rows[
                    (half * tiles + tile) * block : (half * tiles + tile + 1) * block,
                    owner * lanes : (owner + 1) * lanes,
                ]
                for half in range(width)
            ]
            parts.append(jnp.concatenate(pieces, axis=1))
    mixed = moved(jnp.concatenate(parts, axis=0), swap[...])
    for owner in range(layers * PAIR):
        layer = own_layer() ^ (owner // PAIR)
        for tile in range(tiles):
            at = (owner * tiles + tile) * block
            for part in range(width):
                out[0, part, owner % PAIR, layer, :, tile * lanes : (tile + 1) * lanes] = mixed[
                    at : at + block, part * lanes : (part + 1) * lanes
                ]


def pack_state(member_state, layers, width):
    slabs, local, cells_a, cols = member_state.shape
    lanes = cols // (layers * PAIR)
    size = cells_a * lanes // width
    block = 32
    return pl.pallas_call(
        pack_state_kernel,
        grid=(slabs, local // block),
        in_specs=[pl.BlockSpec((1, block, cells_a, cols), lambda s, g: (s, g, 0, 0))],
        out_specs=pl.BlockSpec(
            (1, width, PAIR, layers, block, size), lambda s, g: (s, 0, 0, 0, g, 0)
        ),
        out_shape=jax.ShapeDtypeStruct((slabs, width, PAIR, layers, local, size), BF16),
        scratch_shapes=[
            pltpu.VMEM((block * cells_a, block * cells_a), BF16),
            pltpu.VMEM((width * lanes, width * lanes), BF16),
        ],
        compiler_params=params(2),
        name="pack_state",
    )(member_state)


def unpack_state_kernel(*refs, layers, width):
    blocks = refs[:layers]
    out, order, swap = refs[-3:]
    block, cells_a, cols = out.shape[1:]
    size = blocks[0].shape[2]
    lanes = cols // (layers * PAIR)
    tiles = size // lanes

    @pl.when(pl.program_id(0) == 0)
    def _():
        order[...] = transposed(block, cells_a)
        swap[...] = swapped(width, lanes)

    for layer in range(layers):
        parts = []
        for bit in range(PAIR):
            for tile in range(tiles):
                pieces = [
                    blocks[layer][part * PAIR + bit, :, tile * lanes : (tile + 1) * lanes]
                    for part in range(width)
                ]
                parts.append(jnp.concatenate(pieces, axis=1))
        mixed = moved(jnp.concatenate(parts, axis=0), swap[...])
        columns = []
        for bit in range(PAIR):
            rows = []
            for cell in range(cells_a):
                half, tile = cell // tiles, cell % tiles
                at = (bit * tiles + tile) * block
                rows.append(mixed[at : at + block, half * lanes : (half + 1) * lanes])
            columns.append(jnp.concatenate(rows, axis=0))
        rows = moved(order[...], jnp.concatenate(columns, axis=1))
        span = PAIR * lanes
        at = pl.multiple_of((own_layer() ^ layer) * span, span)
        out[0, :, :, pl.ds(at, span)] = rows.reshape(block, cells_a, span)


def unpack_state(blocks, specs, shape, piece, before):
    slabs, local, cells_a, cols = shape
    block = local // 2
    layers = len(blocks)
    size = blocks[0].shape[2]
    lanes = cols // (layers * PAIR)
    width = cells_a * lanes // size

    def kernel(*refs):
        unpack_state_kernel(*refs, layers=layers, width=width)

    kept = [] if before is None else [before]
    return pl.pallas_call(
        kernel,
        grid=(slabs,),
        in_specs=specs + [pl.BlockSpec(memory_space=pl.ANY)] * len(kept),
        out_specs=pl.BlockSpec((1, block, cells_a, cols), lambda s: (s, piece, 0, 0)),
        out_shape=jax.ShapeDtypeStruct(shape, BF16),
        scratch_shapes=[
            pltpu.VMEM((block * cells_a, block * cells_a), BF16),
            pltpu.VMEM((width * lanes, width * lanes), BF16),
        ],
        input_output_aliases={layers: 0} if kept else {},
        compiler_params=params(1),
        name="unpack_state",
    )(*blocks, *kept)


def transform_kernel(spread, *refs, layers, count, shift):
    seconds = refs[:layers]
    out, pert, weighted = refs[layers:]
    total = out.shape[1]
    own = spread.shape[2]
    half = own // 2
    local = total // (layers * PAIR * 2)
    held = spread.shape[0] // PAIR
    a = pl.program_id(0) + shift
    taper = (iota(1, half, 1).astype(F32) + 1.0) / (half + 1.0)
    fall = (half - iota(1, half, 1).astype(F32)) / (half + 1.0)
    level = jnp.ones((1, half), F32)
    sources = [
        (lax.rem(a + held - 1, held), half, taper),
        (a, 0, level),
        (a, half, level),
        (lax.rem(a + 1, held), 0, fall),
    ]
    projected = jnp.zeros((total, 1), F32)
    for number, (patch, start, weight) in enumerate(sources):
        cols = slice(start, start + half)
        pieces = []
        for layer in range(layers):
            for bit in range(PAIR):
                block = patch * PAIR + bit
                pieces.append(spread[block, layer * local : (layer + 1) * local, cols])
                pieces.append(seconds[layer][block, 0:local, cols])
        values = jnp.concatenate(pieces, axis=0).astype(F32)
        at = layers * local
        stats = seconds[0][patch * PAIR + own_bit(), at : at + SPARE, cols].astype(F32)
        mean = jnp.sum(values, axis=0, keepdims=True) * (1.0 / total)
        centre = values - mean
        place = slice(number * half, (number + 1) * half)
        pert[:, place] = centre.astype(BF16)
        scaled = (centre * (weight / stats[1:2])).astype(BF16)
        weighted[:, place] = scaled
        innovation = stats[0:1] - mean
        projected += jnp.sum(scaled.astype(F32) * innovation, axis=1, keepdims=True)
    diagonal = iota(total, total, 0) == iota(total, total, 1)
    gram = lax.dot_general(
        weighted[...], pert[...], (((1,), (1,)), ((), ())), preferred_element_type=F32
    )
    system = jnp.where(diagonal, total - 1.0, 0.0) + gram
    bound = jnp.max(jnp.sum(jnp.abs(system), axis=1, keepdims=True), axis=0, keepdims=True)
    root = (system / bound).astype(BF16)
    inverse = None
    for iteration in range(ITERS):
        product = root.astype(F32) if inverse is None else dot_bf16(inverse.astype(BF16), root)
        correction = (jnp.where(diagonal, 1.5, 0.0) - 0.5 * product).astype(BF16)
        if iteration + 1 < ITERS:
            root = moved(root, correction)
        if inverse is None:
            inverse = correction.astype(F32)
        else:
            inverse = dot_bf16(correction, inverse.astype(BF16))
    flipped = inverse.T
    halfway = jnp.sum(flipped * projected, axis=0, keepdims=True)
    weight = jnp.sum(inverse * halfway, axis=1, keepdims=True)
    weight = jnp.broadcast_to(weight, (total, 128)).T[0:1, :] / bound
    out[0] = (jnp.sqrt((total - 1.0) / bound) * flipped + weight).astype(BF16)


def transforms(spread, seconds, count):
    layers = len(seconds)
    held, rows, own = spread.shape
    total = rows * PAIR * 2
    shift = (held // PAIR - count) // 2
    flops = count * (2 * total * total * 2 * own + 18 * total**3)

    def kernel(*refs):
        transform_kernel(*refs, layers=layers, count=count, shift=shift)

    return pl.pallas_call(
        kernel,
        grid=(count,),
        in_specs=[
            pl.BlockSpec(array.shape, lambda a: (0, 0, 0)) for array in (spread, *seconds)
        ],
        out_specs=pl.BlockSpec((1, total, total), lambda a: (a, 0, 0)),
        out_shape=jax.ShapeDtypeStruct((count, total, total), BF16),
        scratch_shapes=[pltpu.VMEM((total, 2 * own), BF16), pltpu.VMEM((total, 2 * own), BF16)],
        compiler_params=params(1),
        cost_estimate=pl.CostEstimate(
            flops=flops, bytes_accessed=4 * count * total * total * 2, transcendentals=0
        ),
        name="transform",
    )(spread, *seconds)


def centred(values):
    values = values.astype(F32)
    mean = jnp.sum(values, axis=0, keepdims=True) * (1.0 / values.shape[0])
    return mean, (values - mean).astype(BF16)


def stencil(c):
    step = [0.5 * (c * c + c), 1.0 - c * c, 0.5 * (c * c - c)]
    taps = step
    for _ in range(STEPS - 1):
        longer = [jnp.zeros_like(c)] * (len(taps) + 2)
        for i, tap in enumerate(taps):
            for j, weight in enumerate(step):
                longer[i + j] = longer[i + j] + tap * weight
        taps = longer
    return taps


def transport(tiles, taps, low):
    count, depth = len(tiles), len(tiles[0])
    shift = tiles[0][0].shape[1] // 2
    turned = [[pltpu.roll(tile, shift, 1) for tile in column] for column in tiles]
    results = []
    for a in range(count):
        before = [jnp.where(low, u, v) for u, v in zip(turned[(a - 1) % count], turned[a])]
        after = [jnp.where(low, u, v) for u, v in zip(turned[a], turned[(a + 1) % count])]
        line = before + tiles[a] + after
        start = depth - STEPS
        results.append(
            [sum(taps[t] * line[start + k + t] for t in range(len(taps))) for k in range(depth)]
        )
    return results


def forecast_kernel(*refs, layers, spread):
    blocks, (transform, courant) = refs[:layers], refs[layers : layers + 2]
    outs, fields = refs[layers + 2 : -1], refs[-1]
    count, rows, size = fields.shape
    total = transform.shape[4]
    local = rows // (layers * PAIR)
    a = pl.program_id(0)
    values = jnp.concatenate(
        [block[...].reshape(total // layers, size) for block in blocks], axis=0
    )
    mean, pert = centred(values)
    update = dot_bf16(transform[...].reshape(rows, total), pert)
    fields[a] = (update + mean).astype(BF16).astype(F32)

    @pl.when(a == count - 1)
    def _():
        lanes = courant.shape[1] // (layers * PAIR)
        column = lax.axis_index("sub") & (count - 1)
        slab, part = column // 2, column % 2
        low = iota(8, lanes, 1) < lanes // 2
        at = pl.ds(pl.multiple_of(lax.axis_index("mem") * lanes, lanes), lanes)
        speeds = courant[:, at]
        speed = speeds[0:1]
        for other in range(1, speeds.shape[0]):
            speed = jnp.where(slab == other, speeds[other : other + 1], speed)
        speed = jnp.broadcast_to(speed, (8, lanes))
        speed = jnp.where(low == (part == 0), speed, pltpu.roll(speed, lanes // 2, 1))
        taps = stencil(speed)
        chunk = 16
        steps = local // chunk
        for layer in range(layers):

            def rows_at(step, carry):
                bit, inside = step // steps, step % steps
                start = (layer * PAIR + bit) * local + inside * chunk
                parts = []
                for half in range(chunk // 8):
                    at = pl.ds(pl.multiple_of(start + half * 8, 8), 8)
                    tiles = [
                        [fields[a, at, k * lanes : (k + 1) * lanes] for k in range(size // lanes)]
                        for a in range(count)
                    ]
                    parts.append(transport(tiles, taps, low))
                to = inside * chunk + (layer * local if spread else 0)
                at = pl.ds(pl.multiple_of(to, chunk), chunk)
                out = outs[0] if spread else outs[layer]
                for a in range(count):
                    for k in range(size // lanes):
                        value = jnp.concatenate([part[a][k] for part in parts], axis=0)
                        out[a * PAIR + bit, at, k * lanes : (k + 1) * lanes] = value.astype(BF16)
                return carry

            lax.fori_loop(0, PAIR * steps, rows_at, 0)


def forecasts(own_blocks, blocks, transform, courant, piece):
    held, layers, local, size = own_blocks.shape
    count = held // PAIR
    total = transform.shape[2]
    half = local // 2
    transform = transform.reshape(count, layers * PAIR, 2, half, total)
    shapes = [(held, half, size)] * layers
    if piece == 1:
        shapes = [(held, layers * half, size)]

    def kernel(*refs):
        forecast_kernel(*refs, layers=layers, spread=piece == 1)

    return pl.pallas_call(
        kernel,
        grid=(count,),
        in_specs=[
            pl.BlockSpec((PAIR, 1, local, size), lambda a: (a, 0, 0, 0)),
            *[pl.BlockSpec((PAIR, local, size), lambda a: (a, 0, 0)) for _ in blocks],
            pl.BlockSpec(
                (1, layers * PAIR, 1, half, total), lambda a: (a, 0, piece, 0, 0)
            ),
            pl.BlockSpec(courant.shape, lambda a: (0, 0)),
        ],
        out_specs=[pl.BlockSpec(shape, lambda a: (0, 0, 0)) for shape in shapes],
        out_shape=[jax.ShapeDtypeStruct(shape, BF16) for shape in shapes],
        scratch_shapes=[pltpu.VMEM((count, total // 2, size), F32)],
        compiler_params=params(1),
        cost_estimate=pl.CostEstimate(
            flops=count * total * total * size, bytes_accessed=4 * total * size * count, transcendentals=0
        ),
        name="forecast",
    )(own_blocks, *blocks, transform, courant)


def analysis_kernel(state, transform, out):
    mean, pert = centred(state[0])
    out[0] = (dot_bf16(transform[0], pert) + mean).astype(BF16)


def analyses(state, transform):
    count, total, size = state.shape
    return pl.pallas_call(
        analysis_kernel,
        grid=(count,),
        in_specs=[
            pl.BlockSpec((1, total, size), lambda a: (a, 0, 0)),
            pl.BlockSpec((1, total, total), lambda a: (a, 0, 0)),
        ],
        out_specs=pl.BlockSpec((1, total, size), lambda a: (a, 0, 0)),
        out_shape=jax.ShapeDtypeStruct((count, total, size), BF16),
        compiler_params=params(1),
        name="analysis",
    )(state, transform)


def shared_transport(analysis, speed, width, jump):
    count, total, size = analysis.shape
    lanes = speed.shape[1]
    cells = lanes // width
    tiles = size // lanes
    fields = widened(analysis, jump).reshape(count + 2, total, tiles, width, cells)
    fields = fields.transpose(1, 0, 3, 2, 4).reshape(total, -1, cells).astype(F32)
    c = speed[0, :cells]
    for _ in range(STEPS):
        prior, here, after = fields[:, :-2], fields[:, 1:-1], fields[:, 2:]
        fields = (1.0 - c * c) * here + 0.5 * (c * c - c) * after + 0.5 * (c * c + c) * prior
    spare = tiles * width - STEPS
    fields = fields[:, spare : fields.shape[1] - spare].astype(BF16)
    fields = fields.reshape(total, count, width, tiles, cells)
    return fields.transpose(1, 0, 3, 2, 4).reshape(count, total, size)


def widened(blocks, jump):
    count = lax.axis_size("sub")
    forward = [(i, (i + jump) % count) for i in range(count)]
    backward = [(target, source) for source, target in forward]
    span = blocks.shape[0] // jump
    low = lax.ppermute(blocks[-span:], "sub", forward)
    high = lax.ppermute(blocks[:span], "sub", backward)
    return jnp.concatenate([low, blocks, high], axis=0)


def advance(member_state, hx_values, obs_value, obs_var, courant):
    slabs, local, cells_a, cols = member_state.shape
    patches, own = hx_values.shape[3:]
    owners = lax.axis_size("mem")
    lines = lax.axis_size("sub")
    layers = owners // PAIR
    width = patches // owners
    count = slabs * width
    held = count * PAIR
    half = local // 2
    shared = lines > count
    cells_b = cols // patches
    far_first = range(layers - 1, 0, -1)

    layer_groups = [
        [s * owners + layer * PAIR + bit for s in range(g, g + count) for bit in range(PAIR)]
        for g in range(0, lines, count)
        for layer in range(layers)
    ]

    def within(blocks):
        return lax.all_to_all(
            blocks,
            ("sub", "mem"),
            split_axis=0,
            concat_axis=0,
            tiled=True,
            axis_index_groups=layer_groups,
        )

    def across(blocks):
        received = list(blocks)
        for layer in far_first:
            pairs = [
                (s * owners + m, s * owners + (m ^ (layer * PAIR)))
                for s in range(lines)
                for m in range(owners)
            ]
            received[layer] = lax.ppermute(blocks[layer], ("sub", "mem"), pairs)
        return received

    def layered(blocks, rows):
        return [blocks[:, layer * rows : (layer + 1) * rows] for layer in range(layers)]

    first = pack_obs(hx_values, layers, 0, ())
    first = across([block.reshape(held, half, own) for block in first])
    (second,) = pack_obs(hx_values, layers, 1, (obs_value, obs_var))
    second = within(second.reshape(held, -1, own))
    seconds = [second] + across(layered(second, half))[1:]
    state = pack_state(member_state, layers, width)
    size = state.shape[5]
    state = within(state.reshape(held, layers * local, size))
    states = across(layered(state, local))
    first = within(jnp.concatenate(first, axis=1))
    observed = [first, *seconds]
    if shared:
        observed = [widened(array, count) for array in observed]
    transform = transforms(observed[0], observed[1:], count)

    if not shared and width == 2 and cells_a // width >= STEPS:
        state = state.reshape(held, layers, local, size)
        back = forecasts(state, states[1:], transform, courant, 0)
        (last,) = forecasts(state, states[1:], transform, courant, 1)
    else:
        column = lax.axis_index("sub") % count
        line = (lax.axis_index("mem") * width + column % width) * cells_b
        speed = lax.dynamic_slice(courant, (column // width, line), (1, cells_b))
        speed = jnp.concatenate([speed] * width, axis=1)
        states = [block.reshape(count, PAIR * local, size) for block in states]
        analysis = analyses(jnp.concatenate(states, axis=1), transform)
        fields = shared_transport(analysis, speed, width, count)
        fields = fields.reshape(count, layers, PAIR, 2, half, size)
        fields = fields.transpose(3, 0, 2, 1, 4, 5).reshape(2, held, layers, half, size)
        back = [fields[0, :, layer] for layer in range(layers)]
        last = fields[1].reshape(held, layers * half, size)
    back = within(jnp.concatenate(across(back), axis=1))
    last = within(last)
    lasts = across(layered(last, half))

    def spec(layer):
        return pl.BlockSpec((width * PAIR, half, size), lambda s: (s, layer, 0))

    shape = member_state.shape
    done = unpack_state([back] * layers, [spec(i) for i in range(layers)], shape, 0, None)
    return unpack_state([last, *lasts[1:]], [spec(0)] * layers, shape, 1, done)


def solution(mesh):
    in_specs = (
        P(None, "mem", "sub", None),
        P(None, "mem", "sub", None, None),
        P(None, "sub", "mem", None),
        P(None, "sub", "mem", None),
        P(),
    )
    out_specs = P(None, "mem", "sub", None)
    return jax.shard_map(advance, mesh=mesh, in_specs=in_specs, out_specs=out_specs, check_vma=False)
```

time: 180 us -> 214 us (1.19)
  blocking collectives: 69.7 us -> 0 us
  starting transfers between devices: 10.3 us -> 58.5 us
  waiting for transfers between devices: 56.5 us -> 92.1 us
  Pallas kernels: 35.8 us -> 51.8 us
  other arithmetic: 0.18 us -> 3.98 us
    ppermute x0 -> x15, waiting for transfers between devices: none -> 72.4 us  [across(): received[layer] = lax.ppermute(blocks[layer], ('sub', 'mem'), pairs)]
    all_to_all x1 -> x0, blocking collectives: 52 us -> none  [exchange(): lax.all_to_all(blocks, ('sub', 'mem'), split_axis=0, concat_axis=0, tiled...]
    ppermute x0 -> x15, starting transfers between devices: none -> 37.4 us  [across(): received[layer] = lax.ppermute(blocks[layer], ('sub', 'mem'), pairs)]
    all_to_all x2 -> x5, waiting for transfers between devices: 56.5 us -> 19.7 us  [within(): lax.all_to_all(blocks, ('sub', 'mem'), split_axis=0, concat_axis=0, tiled...]
    all_gather x1 -> x0, blocking collectives: 17.8 us -> none  [advance(): stats = lax.all_gather(stats, 'sub', axis=0)]
    pallas_call x4 -> x7, Pallas kernels: 33.5 us -> 47 us  [the longest x1 21 us: transforms(): pl.pallas_call(kernel, grid=(count,), in_specs=[pl.BlockSpec(array.shape,...]
    all_to_all x2 -> x5, starting transfers between devices: 10.3 us -> 21.1 us  [within(): lax.all_to_all(blocks, ('sub', 'mem'), split_axis=0, concat_axis=0, tiled...]
    concatenate x3 -> x2, other arithmetic: 0.11 us -> 3.98 us  [the longest x1 1.99 us: advance(): first = within(jnp.concatenate(first, axis=1))]
  transfers between devices with their start and end apart: 2 -> 20, of which waited for: 2 -> 9; matrix products, arithmetic and copies ran while one was open for 1% -> 3% of each run, Pallas kernels for 12% -> 18%
where the time goes in v4:
time: 214 us; the launch traced here: 213 us
  waiting for transfers between devices  92.1 us (43%)
  starting transfers between devices  58.5 us (27%)
  Pallas kernels  51.8 us (24%)
  local copies, waits for them, and re-layouts  6.73 us (3%)
  other arithmetic  3.98 us (2%)
    ppermute x15, waiting for transfers between devices, across(): received[layer] = lax.ppermute(blocks[layer], ('sub', 'mem'), pairs)  72.4 us
    ppermute x15, starting transfers between devices, across(): received[layer] = lax.ppermute(blocks[layer], ('sub', 'mem'), pairs)  37.4 us
    all_to_all x5, starting transfers between devices, within(): lax.all_to_all(blocks, ('sub', 'mem'), split_axis=0, concat_axis=0, tiled...  21.1 us
    pallas_call x1, Pallas kernels, transforms(): pl.pallas_call(kernel, grid=(count,), in_specs=[pl.BlockSpec(array.shape,...  21 us
    all_to_all x5, waiting for transfers between devices, within(): lax.all_to_all(blocks, ('sub', 'mem'), split_axis=0, concat_axis=0, tiled...  19.7 us
    pallas_call x2, Pallas kernels, forecasts(): pl.pallas_call(kernel, grid=(count,), in_specs=[pl.BlockSpec((PAIR, 1, lo...  14.3 us
    pallas_call x2, Pallas kernels, unpack_state(): pl.pallas_call(kernel, grid=(slabs,), in_specs=specs + [pl.BlockSpec(memo...  6.46 us
    pallas_call x2, Pallas kernels, pack_obs(): pl.pallas_call(kernel, grid=(slabs,), in_specs=[pl.BlockSpec((1, local, 1...  5.2 us
  transfers between devices with their start and end apart: 20, of which 9 were waited for; matrix products, arithmetic and copies ran while one was open for 3% of the time, Pallas kernels for 18%

profile of v4, /device:TPU:0, one launch (start us, length us, event | category | flops | bytes accessed | tf_op | source)
XLA Modules:
  0.0 213.2 jit_solution(10078551474366475130)
XLA Ops:
  0.0 2.6 %pack_obs.3 = bf16[2,4,144,512]{3,2,1,0:T(8,128)(2,1)} custom-call(bf16[2,64,1,16,512]{4,3,2,1,0:T(8,128)(2,1)} %refs_0_.3, bf16[2,1,2,512]{3,2,1,0:T(2,128)(2,1)} %refs_1_.1, bf16[2,1,2,512]{3,2,1,0:T(2,128)(2,1)} %refs_2_.1), custom_call_target="tpu_custom_call" | custom-call | tf_op jit(solution)/shard_map/pack_obs/pallas_call | solution.py:96
  2.6 5.2 %all-to-all-start.2 = ((bf16[8,144,512]{2,1,0:T(8,128)(2,1)}), bf16[8,144,512]{2,1,0:T(8,128)(2,1)S(1)}, u32[]{:S(2)}, u32[]{:S(2)}) async-start(bf16[8,144,512]{2,1,0:T(8,128)(2,1)} %bitcast.13), calls=%async_computation.2 | async-start | bytes 2359296 | tf_op jit(solution)/shard_map/all_to_all | solution.py:525
  7.8 4.8 %pack_state.1 = bf16[2,2,2,4,64,512]{5,4,3,2,1,0:T(8,128)(2,1)} custom-call(bf16[2,64,8,1024]{3,2,1,0:T(8,128)(2,1)} %cells.1), custom_call_target="tpu_custom_call" | custom-call | tf_op jit(solution)/shard_map/pack_state/pallas_call | solution.py:161
  12.6 12.0 %all-to-all-done.2.refs_1_ = bf16[8,144,512]{2,1,0:T(8,128)(2,1)S(1)} async-done(((bf16[8,144,512]{2,1,0:T(8,128)(2,1)}), bf16[8,144,512]{2,1,0:T(8,128)(2,1)S(1)}, u32[]{:S(2)}, u32[]{:S(2)}) %all-to-all-start.2) | async-done | bytes 1179680 | tf_op jit(solution)/shard_map/all_to_all | solution.py:525
  24.6 3.6 %all-to-all-start = ((bf16[8,256,512]{2,1,0:T(8,128)(2,1)}), bf16[8,256,512]{2,1,0:T(8,128)(2,1)S(1)}, u32[]{:S(2)}, u32[]{:S(2)}) async-start(bf16[8,256,512]{2,1,0:T(8,128)(2,1)} %bitcast.10), calls=%async_computation | async-start | bytes 4194304 | tf_op jit(solution)/shard_map/all_to_all | solution.py:525
  28.2 2.6 %pack_obs.2 = (bf16[2,4,32,512]{3,2,1,0:T(8,128)(2,1)}, bf16[2,4,32,512]{3,2,1,0:T(8,128)(2,1)}, bf16[2,4,32,512]{3,2,1,0:T(8,128)(2,1)}, bf16[2,4,32,512]{3,2,1,0:T(8,128)(2,1)}) custom-call(bf16[2,64,1,16,512]{4,3,2,1,0:T(8,128)(2,1)} %refs_0_.3), custom_call_target="tpu_custom_call" | custom-call | tf_op jit(solution)/shard_map/pack_obs/pallas_call | solution.py:96
  30.8 1.6 collective-permute-start.3
  32.4 2.6 %collective-permute-start.4 = (bf16[8,32,512]{2,1,0:T(8,128)(2,1)}, bf16[8,32,512]{2,1,0:T(8,128)(2,1)S(1)}, u32[]{:S(2)}, u32[]{:S(2)}) collective-permute-start(bf16[8,32,512]{2,1,0:T(8,128)(2,1)} %bitcast.16), channel_id=1, source_target_pairs={{0,4},{1,5},{2,6},{3,7},{4,0},{5,1},{6,2},{7,3},{8,12},{9,13},{10,... | collective-permute-start | bytes 786440 | tf_op jit(solution)/shard_map/ppermute | solution.py:542
  35.0 0.2 collective-permute-start.5
  35.2 9.5 %collective-permute-done.3 = bf16[8,32,512]{2,1,0:T(8,128)(2,1)S(1)} collective-permute-done((bf16[8,32,512]{2,1,0:T(8,128)(2,1)}, bf16[8,32,512]{2,1,0:T(8,128)(2,1)S(1)}, u32[]{:S(2)}, u32[]{:S(2)}) %collective-permute-start.3) | collective-permute-done | bytes 262176 | tf_op jit(solution)/shard_map/ppermute | solution.py:542
  44.7 9.2 %collective-permute-done.4 = bf16[8,32,512]{2,1,0:T(8,128)(2,1)S(1)} collective-permute-done((bf16[8,32,512]{2,1,0:T(8,128)(2,1)}, bf16[8,32,512]{2,1,0:T(8,128)(2,1)S(1)}, u32[]{:S(2)}, u32[]{:S(2)}) %collective-permute-start.4) | collective-permute-done | bytes 262176 | tf_op jit(solution)/shard_map/ppermute | solution.py:542
  54.0 0.0 collective-permute-done.5
  54.0 2.0 pad_maximum_fusion
  56.0 0.0 all-to-all-done
  56.0 4.2 %all-to-all-start.1 = ((bf16[8,128,512]{2,1,0:T(8,128)(2,1)}), bf16[8,128,512]{2,1,0:T(8,128)(2,1)}, u32[]{:S(2)}, u32[]{:S(2)}) async-start(bf16[8,128,512]{2,1,0:T(8,128)(2,1)} %pad_maximum_fusion), calls=%async_computation.1 | async-start | bytes 2097152 | tf_op jit(solution)/shard_map/all_to_all | solution.py:525
  60.2 0.0 copy-done.3
  60.2 0.7 fusion.1
  61.0 2.5 %collective-permute-start.8 = (bf16[8,32,512]{2,1,0:T(8,128)(2,1)S(1)}, bf16[8,32,512]{2,1,0:T(8,128)(2,1)S(1)}, u32[]{:S(2)}, u32[]{:S(2)}) collective-permute-start(bf16[8,32,512]{2,1,0:T(8,128)(2,1)S(1)} %get-tuple-element.24), channel_id=1, source_target_pairs={{0,6},{1,7},{2,4},{3,5},{4,2},{5,3},{6,0},{7,1},{8,14},{9,15},{10,... | collective-permute-start | bytes 786440 | tf_op jit(solution)/shard_map/ppermute | solution.py:542
  63.5 4.3 %collective-permute-start.7 = (bf16[8,32,512]{2,1,0:T(8,128)(2,1)}, bf16[8,32,512]{2,1,0:T(8,128)(2,1)}, u32[]{:S(2)}, u32[]{:S(2)}) collective-permute-start(bf16[8,32,512]{2,1,0:T(8,128)(2,1)} %get-tuple-element.25), channel_id=1, source_target_pairs={{0,4},{1,5},{2,6},{3,7},{4,0},{5,1},{6,2},{7,3},{8,12},{9,13},{10,... | collective-permute-start | bytes 786440 | tf_op jit(solution)/shard_map/ppermute | solution.py:542
  67.8 0.1 collective-permute-start.6
  67.9 1.2 fusion
  69.0 0.0 copy-done
  69.0 2.4 %collective-permute-start.2 = (bf16[8,64,512]{2,1,0:T(8,128)(2,1)}, bf16[8,64,512]{2,1,0:T(8,128)(2,1)S(1)}, u32[]{:S(2)}, u32[]{:S(2)}) collective-permute-start(bf16[8,64,512]{2,1,0:T(8,128)(2,1)} %get-tuple-element.21), channel_id=1, source_target_pairs={{0,6},{1,7},{2,4},{3,5},{4,2},{5,3},{6,0},{7,1},{8,14},{9,15},{10,... | collective-permute-start | bytes 1572872 | tf_op jit(solution)/shard_map/ppermute | solution.py:542
  71.4 1.0 collective-permute-start.1
  72.4 0.0 collective-permute-done.8.refs_4_
  72.4 0.7 copy-done.10
  73.1 11.4 %collective-permute-start = (bf16[8,64,512]{2,1,0:T(8,128)(2,1)S(1)}, bf16[8,64,512]{2,1,0:T(8,128)(2,1)S(1)}, u32[]{:S(2)}, u32[]{:S(2)}) collective-permute-start(bf16[8,64,512]{2,1,0:T(8,128)(2,1)S(1)} %get-tuple-element.23), channel_id=1, source_target_pairs={{0,2},{1,3},{2,0},{3,1},{4,6},{5,7},{6,4},{7,5},{8,10},{9,11},{10,... | collective-permute-start | bytes 1572872 | tf_op jit(solution)/shard_map/ppermute | solution.py:542
  84.5 0.0 all-to-all-done.1.refs_0_
  84.5 26.4 %collective-permute-done.7.refs_3_ = bf16[8,32,512]{2,1,0:T(8,128)(2,1)} collective-permute-done((bf16[8,32,512]{2,1,0:T(8,128)(2,1)}, bf16[8,32,512]{2,1,0:T(8,128)(2,1)}, u32[]{:S(2)}, u32[]{:S(2)}) %collective-permute-start.7) | collective-permute-done | bytes 262176 | tf_op jit(solution)/shard_map/ppermute | solution.py:542
  110.9 0.0 collective-permute-done.6.refs_2_
  110.9 21.0 %transform.1 = bf16[4,512,512]{2,1,0:T(8,128)(2,1)} custom-call(bf16[8,128,512]{2,1,0:T(8,128)(2,1)} %all-to-all-done.1.refs_0_, bf16[8,144,512]{2,1,0:T(8,128)(2,1)} %copy-done.3, bf16[8,32,512]{2,1,0:T(8,128)(2,1)} %collective-permute-done.6.refs_2_, bf16[8,32,512]{2,1,0:T(8,128)(2,1)} %collective-permute-done.7.refs_3_, bf16[8,32,512]{2,1,0:T(8,128)(2,1)} %copy-done.10), custom_call_target="tpu_custom_call" | custom-call | flops 11811160064 | bytes 8388608 | tf_op jit(solution)/shard_map/transform/pallas_call | solution.py:315
  131.9 0.0 collective-permute-done.2.refs_3_
  131.9 1.3 collective-permute-done.1.refs_2_
  133.2 0.0 collective-permute-done.refs_1_
  133.2 0.0 copy-done.4
  133.2 0.8 copy-done.5
  134.0 0.2 copy-done.6
  134.2 7.1 %forecast.2 = bf16[8,128,512]{2,1,0:T(8,128)(2,1)} custom-call(bf16[8,4,64,512]{3,2,1,0:T(8,128)(2,1)} %bitcast.8, bf16[8,64,512]{2,1,0:T(8,128)(2,1)} %copy-done.6, bf16[8,64,512]{2,1,0:T(8,128)(2,1)} %copy-done.5, bf16[8,64,512]{2,1,0:T(8,128)(2,1)} %copy-done.4, bf16[4,8,2,32,512]{4,3,2,1,0:T(8,128)(2,1)} %bitcast.11, f32[2,1024]{1,0:T(2,128)} %refs_5_.3), custom_call_target="tpu_custom_call" | custom-call | flops 536870912 | bytes 4194304 | tf_op jit(solution)/shard_map/forecast/pallas_call | solution.py:434
  141.3 3.9 %all-to-all-start.3 = ((bf16[8,128,512]{2,1,0:T(8,128)(2,1)}), bf16[8,128,512]{2,1,0:T(8,128)(2,1)S(1)}, u32[]{:S(2)}, u32[]{:S(2)}) async-start(bf16[8,128,512]{2,1,0:T(8,128)(2,1)} %forecast.2), calls=%async_computation.3 | async-start | bytes 2097152 | tf_op jit(solution)/shard_map/all_to_all | solution.py:525
  145.2 7.2 %forecast.3 = (bf16[8,32,512]{2,1,0:T(8,128)(2,1)}, bf16[8,32,512]{2,1,0:T(8,128)(2,1)}, bf16[8,32,512]{2,1,0:T(8,128)(2,1)}, bf16[8,32,512]{2,1,0:T(8,128)(2,1)}) custom-call(bf16[8,4,64,512]{3,2,1,0:T(8,128)(2,1)} %bitcast.9, bf16[8,64,512]{2,1,0:T(8,128)(2,1)} %copy-done.6, bf16[8,64,512]{2,1,0:T(8,128)(2,1)} %copy-done.5, bf16[8,64,512]{2,1,0:T(8,128)(2,1)} %copy-done.4, ...), custom_call_target="tpu_custom_call" | custom-call | flops 536870912 | bytes 4194304 | tf_op jit(solution)/shard_map/forecast/pallas_call | solution.py:434
  152.4 0.0 collective-permute-start.12
  152.4 3.0 %collective-permute-start.13 = (bf16[8,32,512]{2,1,0:T(8,128)(2,1)}, bf16[8,32,512]{2,1,0:T(8,128)(2,1)S(1)}, u32[]{:S(2)}, u32[]{:S(2)}) collective-permute-start(bf16[8,32,512]{2,1,0:T(8,128)(2,1)} %get-tuple-element.19), channel_id=1, source_target_pairs={{0,4},{1,5},{2,6},{3,7},{4,0},{5,1},{6,2},{7,3},{8,12},{9,13},{10,... | collective-permute-start | bytes 786440 | tf_op jit(solution)/shard_map/ppermute | solution.py:542
  155.4 1.4 collective-permute-start.14
  156.8 9.8 %collective-permute-done.12 = bf16[8,32,512]{2,1,0:T(8,128)(2,1)S(1)} collective-permute-done((bf16[8,32,512]{2,1,0:T(8,128)(2,1)}, bf16[8,32,512]{2,1,0:T(8,128)(2,1)S(1)}, u32[]{:S(2)}, u32[]{:S(2)}) %collective-permute-start.12) | collective-permute-done | bytes 262176 | tf_op jit(solution)/shard_map/ppermute | solution.py:542
  166.6 7.4 %collective-permute-done.13 = bf16[8,32,512]{2,1,0:T(8,128)(2,1)S(1)} collective-permute-done((bf16[8,32,512]{2,1,0:T(8,128)(2,1)}, bf16[8,32,512]{2,1,0:T(8,128)(2,1)S(1)}, u32[]{:S(2)}, u32[]{:S(2)}) %collective-permute-start.13) | collective-permute-done | bytes 262176 | tf_op jit(solution)/shard_map/ppermute | solution.py:542
  174.0 0.0 collective-permute-done.14
  174.0 2.0 pad_maximum_fusion.1
  176.0 0.0 all-to-all-done.3.refs_0_
  176.0 4.3 %all-to-all-start.4 = ((bf16[8,128,512]{2,1,0:T(8,128)(2,1)}), bf16[8,128,512]{2,1,0:T(8,128)(2,1)S(1)}, u32[]{:S(2)}, u32[]{:S(2)}) async-start(bf16[8,128,512]{2,1,0:T(8,128)(2,1)} %pad_maximum_fusion.1), calls=%async_computation.4 | async-start | bytes 2097152 | tf_op jit(solution)/shard_map/all_to_all | solution.py:525
  180.2 0.8 fusion.2
  181.0 2.4 %collective-permute-start.11 = (bf16[8,32,512]{2,1,0:T(8,128)(2,1)}, bf16[8,32,512]{2,1,0:T(8,128)(2,1)S(1)}, u32[]{:S(2)}, u32[]{:S(2)}) collective-permute-start(bf16[8,32,512]{2,1,0:T(8,128)(2,1)} %get-tuple-element.27), channel_id=1, source_target_pairs={{0,6},{1,7},{2,4},{3,5},{4,2},{5,3},{6,0},{7,1},{8,14},{9,15},{10,... | collective-permute-start | bytes 786440 | tf_op jit(solution)/shard_map/ppermute | solution.py:542
  183.4 4.4 %collective-permute-start.10 = (bf16[8,32,512]{2,1,0:T(8,128)(2,1)S(1)}, bf16[8,32,512]{2,1,0:T(8,128)(2,1)S(1)}, u32[]{:S(2)}, u32[]{:S(2)}) collective-permute-start(bf16[8,32,512]{2,1,0:T(8,128)(2,1)S(1)} %get-tuple-element.28), channel_id=1, source_target_pairs={{0,4},{1,5},{2,6},{3,7},{4,0},{5,1},{6,2},{7,3},{8,12},{9,13},{10,... | collective-permute-start | bytes 786440 | tf_op jit(solution)/shard_map/ppermute | solution.py:542
  187.8 0.1 collective-permute-start.9
  187.9 7.7 %all-to-all-done.4.refs_0_.refs_1_.refs_2_.refs_3_ = bf16[8,128,512]{2,1,0:T(8,128)(2,1)S(1)} async-done(((bf16[8,128,512]{2,1,0:T(8,128)(2,1)}), bf16[8,128,512]{2,1,0:T(8,128)(2,1)S(1)}, u32[]{:S(2)}, u32[]{:S(2)}) %all-to-all-start.4) | async-done | bytes 1048608 | tf_op jit(solution)/shard_map/all_to_all | solution.py:525
  195.6 1.0 copy-done.1
  196.6 3.2 %unpack_state.2.refs_4_ = bf16[2,64,8,1024]{3,2,1,0:T(8,128)(2,1)} custom-call(bf16[8,128,512]{2,1,0:T(8,128)(2,1)} %copy-done.1, bf16[8,128,512]{2,1,0:T(8,128)(2,1)} %copy-done.1, bf16[8,128,512]{2,1,0:T(8,128)(2,1)} %copy-done.1, bf16[8,128,512]{2,1,0:T(8,128)(2,1)} %copy-done.1), custom_call_target="tpu_custom_call" | custom-call | tf_op jit(solution)/shard_map/unpack_state/pallas_call | solution.py:227
  199.8 0.0 copy-done.2
  199.8 0.0 collective-permute-done.11.refs_3_
  199.8 0.0 copy-start.7
  199.9 8.7 %collective-permute-done.10.refs_2_ = bf16[8,32,512]{2,1,0:T(8,128)(2,1)S(1)} collective-permute-done((bf16[8,32,512]{2,1,0:T(8,128)(2,1)S(1)}, bf16[8,32,512]{2,1,0:T(8,128)(2,1)S(1)}, u32[]{:S(2)}, u32[]{:S(2)}) %collective-permute-start.10) | collective-permute-done | bytes 262176 | tf_op jit(solution)/shard_map/ppermute | solution.py:542
  208.6 0.0 collective-permute-done.9.refs_1_
  208.6 0.7 copy-done.8
  209.3 0.7 copy-done.9
  210.0 3.2 %unpack_state.3 = bf16[2,64,8,1024]{3,2,1,0:T(8,128)(2,1)} custom-call(bf16[8,128,512]{2,1,0:T(8,128)(2,1)} %copy-done.2, bf16[8,32,512]{2,1,0:T(8,128)(2,1)} %copy-done.9, bf16[8,32,512]{2,1,0:T(8,128)(2,1)} %copy-done.8, bf16[8,32,512]{2,1,0:T(8,128)(2,1)} %copy-done.7, bf16[2,64,8,1024]{3,2,1,0:T(8,128)(2,1)} %unpack_state.2.refs_4_), custom_call_target="tpu_custom_call", output_to_operand_aliasing={{}: (4, {})} | custom-call | tf_op jit(solution)/shard_map/unpack_state/pallas_call | solution.py:227
  (11 shorter events, 0.0 us)
Async XLA Ops:
  2.6 22.0 %all-to-all-start.2 = ((bf16[8,144,512]{2,1,0:T(8,128)(2,1)}), bf16[8,144,512]{2,1,0:T(8,128)(2,1)S(1)}, u32[]{:S(2)}, u32[]{:S(2)}) async-start(bf16[8,144,512]{2,1,0:T(8,128)(2,1)} %bitcast.13), calls=%async_computation.2 | async-start | bytes 2359296 | tf_op jit(solution)/shard_map/all_to_all | solution.py:525
  24.6 35.6 %copy-start.3 = (bf16[8,144,512]{2,1,0:T(8,128)(2,1)}, bf16[8,144,512]{2,1,0:T(8,128)(2,1)S(1)}, u32[]{:S(2)}) copy-start(bf16[8,144,512]{2,1,0:T(8,128)(2,1)S(1)} %all-to-all-done.2.refs_1_) | copy-start | bytes 3538948
  24.6 31.4 %all-to-all-start = ((bf16[8,256,512]{2,1,0:T(8,128)(2,1)}), bf16[8,256,512]{2,1,0:T(8,128)(2,1)S(1)}, u32[]{:S(2)}, u32[]{:S(2)}) async-start(bf16[8,256,512]{2,1,0:T(8,128)(2,1)} %bitcast.10), calls=%async_computation | async-start | bytes 4194304 | tf_op jit(solution)/shard_map/all_to_all | solution.py:525
  30.8 13.9 %collective-permute-start.3 = (bf16[8,32,512]{2,1,0:T(8,128)(2,1)}, bf16[8,32,512]{2,1,0:T(8,128)(2,1)S(1)}, u32[]{:S(2)}, u32[]{:S(2)}) collective-permute-start(bf16[8,32,512]{2,1,0:T(8,128)(2,1)} %bitcast.17), channel_id=1, source_target_pairs={{0,2},{1,3},{2,0},{3,1},{4,6},{5,7},{6,4},{7,5},{8,10},{9,11},{10,... | collective-permute-start | bytes 786440 | tf_op jit(solution)/shard_map/ppermute | solution.py:542
  32.4 21.6 %collective-permute-start.4 = (bf16[8,32,512]{2,1,0:T(8,128)(2,1)}, bf16[8,32,512]{2,1,0:T(8,128)(2,1)S(1)}, u32[]{:S(2)}, u32[]{:S(2)}) collective-permute-start(bf16[8,32,512]{2,1,0:T(8,128)(2,1)} %bitcast.16), channel_id=1, source_target_pairs={{0,4},{1,5},{2,6},{3,7},{4,0},{5,1},{6,2},{7,3},{8,12},{9,13},{10,... | collective-permute-start | bytes 786440 | tf_op jit(solution)/shard_map/ppermute | solution.py:542
  35.0 19.0 %collective-permute-start.5 = (bf16[8,32,512]{2,1,0:T(8,128)(2,1)}, bf16[8,32,512]{2,1,0:T(8,128)(2,1)S(1)}, u32[]{:S(2)}, u32[]{:S(2)}) collective-permute-start(bf16[8,32,512]{2,1,0:T(8,128)(2,1)} %bitcast.15), channel_id=1, source_target_pairs={{0,6},{1,7},{2,4},{3,5},{4,2},{5,3},{6,0},{7,1},{8,14},{9,15},{10,... | collective-permute-start | bytes 786440 | tf_op jit(solution)/shard_map/ppermute | solution.py:542
  56.0 13.1 %copy-start = (bf16[8,256,512]{2,1,0:T(8,128)(2,1)}, bf16[8,256,512]{2,1,0:T(8,128)(2,1)S(1)}, u32[]{:S(2)}) copy-start(bf16[8,256,512]{2,1,0:T(8,128)(2,1)S(1)} %all-to-all-done) | copy-start | bytes 6291460
  56.0 28.5 %all-to-all-start.1 = ((bf16[8,128,512]{2,1,0:T(8,128)(2,1)}), bf16[8,128,512]{2,1,0:T(8,128)(2,1)}, u32[]{:S(2)}, u32[]{:S(2)}) async-start(bf16[8,128,512]{2,1,0:T(8,128)(2,1)} %pad_maximum_fusion), calls=%async_computation.1 | async-start | bytes 2097152 | tf_op jit(solution)/shard_map/all_to_all | solution.py:525
  61.0 11.4 %collective-permute-start.8 = (bf16[8,32,512]{2,1,0:T(8,128)(2,1)S(1)}, bf16[8,32,512]{2,1,0:T(8,128)(2,1)S(1)}, u32[]{:S(2)}, u32[]{:S(2)}) collective-permute-start(bf16[8,32,512]{2,1,0:T(8,128)(2,1)S(1)} %get-tuple-element.24), channel_id=1, source_target_pairs={{0,6},{1,7},{2,4},{3,5},{4,2},{5,3},{6,0},{7,1},{8,14},{9,15},{10,... | collective-permute-start | bytes 786440 | tf_op jit(solution)/shard_map/ppermute | solution.py:542
  63.5 47.4 %collective-permute-start.7 = (bf16[8,32,512]{2,1,0:T(8,128)(2,1)}, bf16[8,32,512]{2,1,0:T(8,128)(2,1)}, u32[]{:S(2)}, u32[]{:S(2)}) collective-permute-start(bf16[8,32,512]{2,1,0:T(8,128)(2,1)} %get-tuple-element.25), channel_id=1, source_target_pairs={{0,4},{1,5},{2,6},{3,7},{4,0},{5,1},{6,2},{7,3},{8,12},{9,13},{10,... | collective-permute-start | bytes 786440 | tf_op jit(solution)/shard_map/ppermute | solution.py:542
  67.8 43.1 %collective-permute-start.6 = (bf16[8,32,512]{2,1,0:T(8,128)(2,1)S(1)}, bf16[8,32,512]{2,1,0:T(8,128)(2,1)}, u32[]{:S(2)}, u32[]{:S(2)}) collective-permute-start(bf16[8,32,512]{2,1,0:T(8,128)(2,1)S(1)} %get-tuple-element.26), channel_id=1, source_target_pairs={{0,2},{1,3},{2,0},{3,1},{4,6},{5,7},{6,4},{7,5},{8,10},{9,11},{10,... | collective-permute-start | bytes 786440 | tf_op jit(solution)/shard_map/ppermute | solution.py:542
  69.0 62.8 %collective-permute-start.2 = (bf16[8,64,512]{2,1,0:T(8,128)(2,1)}, bf16[8,64,512]{2,1,0:T(8,128)(2,1)S(1)}, u32[]{:S(2)}, u32[]{:S(2)}) collective-permute-start(bf16[8,64,512]{2,1,0:T(8,128)(2,1)} %get-tuple-element.21), channel_id=1, source_target_pairs={{0,6},{1,7},{2,4},{3,5},{4,2},{5,3},{6,0},{7,1},{8,14},{9,15},{10,... | collective-permute-start | bytes 1572872 | tf_op jit(solution)/shard_map/ppermute | solution.py:542
  71.4 61.8 %collective-permute-start.1 = (bf16[8,64,512]{2,1,0:T(8,128)(2,1)}, bf16[8,64,512]{2,1,0:T(8,128)(2,1)S(1)}, u32[]{:S(2)}, u32[]{:S(2)}) collective-permute-start(bf16[8,64,512]{2,1,0:T(8,128)(2,1)} %get-tuple-element.22), channel_id=1, source_target_pairs={{0,4},{1,5},{2,6},{3,7},{4,0},{5,1},{6,2},{7,3},{8,12},{9,13},{10,... | collective-permute-start | bytes 1572872 | tf_op jit(solution)/shard_map/ppermute | solution.py:542
  72.4 0.7 copy-start.10
  73.1 60.1 %collective-permute-start = (bf16[8,64,512]{2,1,0:T(8,128)(2,1)S(1)}, bf16[8,64,512]{2,1,0:T(8,128)(2,1)S(1)}, u32[]{:S(2)}, u32[]{:S(2)}) collective-permute-start(bf16[8,64,512]{2,1,0:T(8,128)(2,1)S(1)} %get-tuple-element.23), channel_id=1, source_target_pairs={{0,2},{1,3},{2,0},{3,1},{4,6},{5,7},{6,4},{7,5},{8,10},{9,11},{10,... | collective-permute-start | bytes 1572872 | tf_op jit(solution)/shard_map/ppermute | solution.py:542
  131.9 1.3 copy-start.4
  133.2 0.8 copy-start.5
  133.2 1.0 copy-start.6
  141.3 34.7 %all-to-all-start.3 = ((bf16[8,128,512]{2,1,0:T(8,128)(2,1)}), bf16[8,128,512]{2,1,0:T(8,128)(2,1)S(1)}, u32[]{:S(2)}, u32[]{:S(2)}) async-start(bf16[8,128,512]{2,1,0:T(8,128)(2,1)} %forecast.2), calls=%async_computation.3 | async-start | bytes 2097152 | tf_op jit(solution)/shard_map/all_to_all | solution.py:525
  152.4 14.2 %collective-permute-start.12 = (bf16[8,32,512]{2,1,0:T(8,128)(2,1)}, bf16[8,32,512]{2,1,0:T(8,128)(2,1)S(1)}, u32[]{:S(2)}, u32[]{:S(2)}) collective-permute-start(bf16[8,32,512]{2,1,0:T(8,128)(2,1)} %get-tuple-element.18), channel_id=1, source_target_pairs={{0,2},{1,3},{2,0},{3,1},{4,6},{5,7},{6,4},{7,5},{8,10},{9,11},{10,... | collective-permute-start | bytes 786440 | tf_op jit(solution)/shard_map/ppermute | solution.py:542
  152.4 21.6 %collective-permute-start.13 = (bf16[8,32,512]{2,1,0:T(8,128)(2,1)}, bf16[8,32,512]{2,1,0:T(8,128)(2,1)S(1)}, u32[]{:S(2)}, u32[]{:S(2)}) collective-permute-start(bf16[8,32,512]{2,1,0:T(8,128)(2,1)} %get-tuple-element.19), channel_id=1, source_target_pairs={{0,4},{1,5},{2,6},{3,7},{4,0},{5,1},{6,2},{7,3},{8,12},{9,13},{10,... | collective-permute-start | bytes 786440 | tf_op jit(solution)/shard_map/ppermute | solution.py:542
  155.4 18.6 %collective-permute-start.14 = (bf16[8,32,512]{2,1,0:T(8,128)(2,1)}, bf16[8,32,512]{2,1,0:T(8,128)(2,1)S(1)}, u32[]{:S(2)}, u32[]{:S(2)}) collective-permute-start(bf16[8,32,512]{2,1,0:T(8,128)(2,1)} %get-tuple-element.20), channel_id=1, source_target_pairs={{0,6},{1,7},{2,4},{3,5},{4,2},{5,3},{6,0},{7,1},{8,14},{9,15},{10,... | collective-permute-start | bytes 786440 | tf_op jit(solution)/shard_map/ppermute | solution.py:542
  176.0 23.9 %copy-start.2 = (bf16[8,128,512]{2,1,0:T(8,128)(2,1)}, bf16[8,128,512]{2,1,0:T(8,128)(2,1)S(1)}, u32[]{:S(2)}) copy-start(bf16[8,128,512]{2,1,0:T(8,128)(2,1)S(1)} %all-to-all-done.3.refs_0_) | copy-start | bytes 3145732
  176.0 19.7 %all-to-all-start.4 = ((bf16[8,128,512]{2,1,0:T(8,128)(2,1)}), bf16[8,128,512]{2,1,0:T(8,128)(2,1)S(1)}, u32[]{:S(2)}, u32[]{:S(2)}) async-start(bf16[8,128,512]{2,1,0:T(8,128)(2,1)} %pad_maximum_fusion.1), calls=%async_computation.4 | async-start | bytes 2097152 | tf_op jit(solution)/shard_map/all_to_all | solution.py:525
  181.0 18.8 %collective-permute-start.11 = (bf16[8,32,512]{2,1,0:T(8,128)(2,1)}, bf16[8,32,512]{2,1,0:T(8,128)(2,1)S(1)}, u32[]{:S(2)}, u32[]{:S(2)}) collective-permute-start(bf16[8,32,512]{2,1,0:T(8,128)(2,1)} %get-tuple-element.27), channel_id=1, source_target_pairs={{0,6},{1,7},{2,4},{3,5},{4,2},{5,3},{6,0},{7,1},{8,14},{9,15},{10,... | collective-permute-start | bytes 786440 | tf_op jit(solution)/shard_map/ppermute | solution.py:542
  183.4 25.2 %collective-permute-start.10 = (bf16[8,32,512]{2,1,0:T(8,128)(2,1)S(1)}, bf16[8,32,512]{2,1,0:T(8,128)(2,1)S(1)}, u32[]{:S(2)}, u32[]{:S(2)}) collective-permute-start(bf16[8,32,512]{2,1,0:T(8,128)(2,1)S(1)} %get-tuple-element.28), channel_id=1, source_target_pairs={{0,4},{1,5},{2,6},{3,7},{4,0},{5,1},{6,2},{7,3},{8,12},{9,13},{10,... | collective-permute-start | bytes 786440 | tf_op jit(solution)/shard_map/ppermute | solution.py:542
  187.8 20.7 %collective-permute-start.9 = (bf16[8,32,512]{2,1,0:T(8,128)(2,1)S(1)}, bf16[8,32,512]{2,1,0:T(8,128)(2,1)S(1)}, u32[]{:S(2)}, u32[]{:S(2)}) collective-permute-start(bf16[8,32,512]{2,1,0:T(8,128)(2,1)S(1)} %get-tuple-element.29), channel_id=1, source_target_pairs={{0,2},{1,3},{2,0},{3,1},{4,6},{5,7},{6,4},{7,5},{8,10},{9,11},{10,... | collective-permute-start | bytes 786440 | tf_op jit(solution)/shard_map/ppermute | solution.py:542
  195.6 1.0 copy-start.1
  199.8 8.7 %copy-start.7 = (bf16[8,32,512]{2,1,0:T(8,128)(2,1)}, bf16[8,32,512]{2,1,0:T(8,128)(2,1)S(1)}, u32[]{:S(2)}) copy-start(bf16[8,32,512]{2,1,0:T(8,128)(2,1)S(1)} %collective-permute-done.11.refs_3_) | copy-start | bytes 786436
  208.6 0.7 copy-start.8
  209.3 0.7 copy-start.9

commit v5 on v4

--- a/solution.py
+++ b/solution.py
@@ -12,6 +12,7 @@
 F32 = jnp.float32
 BF16 = jnp.bfloat16
 VMEM_LIMIT = 60 * 1024 * 1024
+ANY = pl.BlockSpec(memory_space=pl.ANY)
 
 
 def params(count):
@@ -80,14 +81,15 @@
                 outs[0][0, part * PAIR + bit, layers * local :, :] = spare.astype(BF16)
 
 
-def pack_obs(hx_values, layers, piece, stats):
+def pack_obs(hx_values, layers, piece, stats, after):
     slabs, members, _, patches, own = hx_values.shape
     width = patches // (layers * PAIR)
     local = members // 2
     block = 16
 
     def kernel(*refs):
-        pack_obs_kernel(*refs, layers=layers, width=width, given=len(stats))
+        kept = refs[: 1 + len(stats)] + refs[1 + len(stats) + len(after) :]
+        pack_obs_kernel(*kept, layers=layers, width=width, given=len(stats))
 
     held = width * PAIR
     shapes = [(held, local, own)] * layers
@@ -97,13 +99,14 @@
         kernel,
         grid=(slabs,),
         in_specs=[pl.BlockSpec((1, local, 1, patches, own), lambda s: (s, piece, 0, 0, 0))]
-        + [pl.BlockSpec((1, 1, width, own), lambda s: (s, 0, 0, 0))] * len(stats),
+        + [pl.BlockSpec((1, 1, width, own), lambda s: (s, 0, 0, 0))] * len(stats)
+        + [ANY] * len(after),
         out_specs=[pl.BlockSpec((1, *shape), lambda s: (s, 0, 0, 0)) for shape in shapes],
         out_shape=[jax.ShapeDtypeStruct((slabs, *shape), BF16) for shape in shapes],
         scratch_shapes=[pltpu.VMEM((block * patches, block * patches), BF16)],
         compiler_params=params(1),
         name="pack_obs",
-    )(hx_values, *stats)
+    )(hx_values, *stats, *after)
 
 
 def swapped(width, lanes):
@@ -153,15 +156,20 @@
                 ]
 
 
-def pack_state(member_state, layers, width):
+def pack_state(member_state, layers, width, after):
     slabs, local, cells_a, cols = member_state.shape
     lanes = cols // (layers * PAIR)
     size = cells_a * lanes // width
     block = 32
+
+    def kernel(*refs):
+        pack_state_kernel(refs[0], *refs[1 + len(after) :])
+
     return pl.pallas_call(
-        pack_state_kernel,
+        kernel,
         grid=(slabs, local // block),
-        in_specs=[pl.BlockSpec((1, block, cells_a, cols), lambda s, g: (s, g, 0, 0))],
+        in_specs=[pl.BlockSpec((1, block, cells_a, cols), lambda s, g: (s, g, 0, 0))]
+        + [ANY] * len(after),
         out_specs=pl.BlockSpec(
             (1, width, PAIR, layers, block, size), lambda s, g: (s, 0, 0, 0, g, 0)
         ),
@@ -172,72 +180,94 @@
         ],
         compiler_params=params(2),
         name="pack_state",
-    )(member_state)
-
-
-def unpack_state_kernel(*refs, layers, width):
-    blocks = refs[:layers]
-    out, order, swap = refs[-3:]
-    block, cells_a, cols = out.shape[1:]
-    size = blocks[0].shape[2]
-    lanes = cols // (layers * PAIR)
-    tiles = size // lanes
-
-    @pl.when(pl.program_id(0) == 0)
+    )(member_state, *after)
+
+
+def unpack_state_kernel(packed, out, order, swap):
+    _, width, owners, block, size = packed.shape
+    cells_a = out.shape[2]
+    tiles = cells_a // width
+    lanes = size // tiles
+
+    @pl.when((pl.program_id(0) == 0) & (pl.program_id(1) == 0))
     def _():
         order[...] = transposed(block, cells_a)
         swap[...] = swapped(width, lanes)
 
-    for layer in range(layers):
-        parts = []
-        for bit in range(PAIR):
-            for tile in range(tiles):
-                pieces = [
-                    blocks[layer][part * PAIR + bit, :, tile * lanes : (tile + 1) * lanes]
-                    for part in range(width)
-                ]
-                parts.append(jnp.concatenate(pieces, axis=1))
-        mixed = moved(jnp.concatenate(parts, axis=0), swap[...])
-        columns = []
-        for bit in range(PAIR):
-            rows = []
-            for cell in range(cells_a):
-                half, tile = cell // tiles, cell % tiles
-                at = (bit * tiles + tile) * block
-                rows.append(mixed[at : at + block, half * lanes : (half + 1) * lanes])
-            columns.append(jnp.concatenate(rows, axis=0))
-        rows = moved(order[...], jnp.concatenate(columns, axis=1))
-        span = PAIR * lanes
-        at = pl.multiple_of((own_layer() ^ layer) * span, span)
-        out[0, :, :, pl.ds(at, span)] = rows.reshape(block, cells_a, span)
-
-
-def unpack_state(blocks, specs, shape, piece, before):
-    slabs, local, cells_a, cols = shape
-    block = local // 2
-    layers = len(blocks)
-    size = blocks[0].shape[2]
-    lanes = cols // (layers * PAIR)
-    width = cells_a * lanes // size
-
-    def kernel(*refs):
-        unpack_state_kernel(*refs, layers=layers, width=width)
-
-    kept = [] if before is None else [before]
+    parts = []
+    for owner in range(owners):
+        for tile in range(tiles):
+            pieces = [
+                packed[0, part, owner, :, tile * lanes : (tile + 1) * lanes]
+                for part in range(width)
+            ]
+            parts.append(jnp.concatenate(pieces, axis=1))
+    mixed = moved(jnp.concatenate(parts, axis=0), swap[...])
+    columns = []
+    for owner in range(owners):
+        rows = []
+        for cell in range(cells_a):
+            half, tile = cell // tiles, cell % tiles
+            at = (owner * tiles + tile) * block
+            rows.append(mixed[at : at + block, half * lanes : (half + 1) * lanes])
+        columns.append(jnp.concatenate(rows, axis=0))
+    rows = moved(order[...], jnp.concatenate(columns, axis=1))
+    out[...] = rows.reshape(out.shape)
+
+
+def unpack_state(packed, cells_a):
+    slabs, width, owners, local, size = packed.shape
+    lanes = size * width // cells_a
+    cols = owners * lanes
+    block = 32
     return pl.pallas_call(
-        kernel,
-        grid=(slabs,),
-        in_specs=specs + [pl.BlockSpec(memory_space=pl.ANY)] * len(kept),
-        out_specs=pl.BlockSpec((1, block, cells_a, cols), lambda s: (s, piece, 0, 0)),
-        out_shape=jax.ShapeDtypeStruct(shape, BF16),
+        unpack_state_kernel,
+        grid=(slabs, local // block),
+        in_specs=[
+            pl.BlockSpec((1, width, owners, block, size), lambda s, g: (s, 0, 0, g, 0)),
+        ],
+        out_specs=pl.BlockSpec((1, block, cells_a, cols), lambda s, g: (s, g, 0, 0)),
+        out_shape=jax.ShapeDtypeStruct((slabs, local, cells_a, cols), BF16),
         scratch_shapes=[
             pltpu.VMEM((block * cells_a, block * cells_a), BF16),
             pltpu.VMEM((width * lanes, width * lanes), BF16),
         ],
-        input_output_aliases={layers: 0} if kept else {},
-        compiler_params=params(1),
+        compiler_params=params(2),
         name="unpack_state",
-    )(*blocks, *kept)
+    )(packed)
+
+
+def join_kernel(*refs, layers):
+    out, sems = refs[-2:]
+    rows = out.shape[1] // layers
+    copies = [
+        pltpu.make_async_copy(
+            refs[layer], out.at[:, pl.ds(layer * rows, rows), :], sems.at[layer]
+        )
+        for layer in range(layers)
+    ]
+    for copy in copies:
+        copy.start()
+    for copy in copies:
+        copy.wait()
+
+
+def join(blocks, after):
+    layers = len(blocks)
+    held, rows, size = blocks[0].shape
+
+    def kernel(*refs):
+        join_kernel(*refs, layers=layers)
+
+    return pl.pallas_call(
+        kernel,
+        in_specs=[ANY] * (layers + len(after)),
+        out_specs=ANY,
+        out_shape=jax.ShapeDtypeStruct((held, layers * rows, size), BF16),
+        scratch_shapes=[pltpu.SemaphoreType.DMA((layers,))],
+        compiler_params=pltpu.CompilerParams(vmem_limit_bytes=VMEM_LIMIT),
+        name="join",
+    )(*blocks, *after)
 
 
 def transform_kernel(spread, *refs, layers, count, shift):
@@ -363,18 +393,17 @@
     return results
 
 
-def forecast_kernel(*refs, layers, spread):
+def forecast_kernel(*refs, layers):
     blocks, (transform, courant) = refs[:layers], refs[layers : layers + 2]
-    outs, fields = refs[layers + 2 : -1], refs[-1]
-    count, rows, size = fields.shape
-    total = transform.shape[4]
-    local = rows // (layers * PAIR)
+    out, fields = refs[-2:]
+    count, total, size = fields.shape
+    local = total // (layers * PAIR)
     a = pl.program_id(0)
     values = jnp.concatenate(
         [block[...].reshape(total // layers, size) for block in blocks], axis=0
     )
     mean, pert = centred(values)
-    update = dot_bf16(transform[...].reshape(rows, total), pert)
+    update = dot_bf16(transform[0], pert)
     fields[a] = (update + mean).astype(BF16).astype(F32)
 
     @pl.when(a == count - 1)
@@ -406,30 +435,24 @@
                         for a in range(count)
                     ]
                     parts.append(transport(tiles, taps, low))
-                to = inside * chunk + (layer * local if spread else 0)
-                at = pl.ds(pl.multiple_of(to, chunk), chunk)
-                out = outs[0] if spread else outs[layer]
+                at = pl.ds(pl.multiple_of(inside * chunk, chunk), chunk)
+                owner = (own_layer() ^ layer) * PAIR + bit
                 for a in range(count):
                     for k in range(size // lanes):
                         value = jnp.concatenate([part[a][k] for part in parts], axis=0)
-                        out[a * PAIR + bit, at, k * lanes : (k + 1) * lanes] = value.astype(BF16)
+                        out[a, owner, at, k * lanes : (k + 1) * lanes] = value.astype(BF16)
                 return carry
 
             lax.fori_loop(0, PAIR * steps, rows_at, 0)
 
 
-def forecasts(own_blocks, blocks, transform, courant, piece):
+def forecasts(own_blocks, blocks, transform, courant):
     held, layers, local, size = own_blocks.shape
-    count = held // PAIR
-    total = transform.shape[2]
-    half = local // 2
-    transform = transform.reshape(count, layers * PAIR, 2, half, total)
-    shapes = [(held, half, size)] * layers
-    if piece == 1:
-        shapes = [(held, layers * half, size)]
+    count, total, _ = transform.shape
+    owners = layers * PAIR
 
     def kernel(*refs):
-        forecast_kernel(*refs, layers=layers, spread=piece == 1)
+        forecast_kernel(*refs, layers=layers)
 
     return pl.pallas_call(
         kernel,
@@ -437,18 +460,13 @@
         in_specs=[
             pl.BlockSpec((PAIR, 1, local, size), lambda a: (a, 0, 0, 0)),
             *[pl.BlockSpec((PAIR, local, size), lambda a: (a, 0, 0)) for _ in blocks],
-            pl.BlockSpec(
-                (1, layers * PAIR, 1, half, total), lambda a: (a, 0, piece, 0, 0)
-            ),
+            pl.BlockSpec((1, total, total), lambda a: (a, 0, 0)),
             pl.BlockSpec(courant.shape, lambda a: (0, 0)),
         ],
-        out_specs=[pl.BlockSpec(shape, lambda a: (0, 0, 0)) for shape in shapes],
-        out_shape=[jax.ShapeDtypeStruct(shape, BF16) for shape in shapes],
-        scratch_shapes=[pltpu.VMEM((count, total // 2, size), F32)],
+        out_specs=pl.BlockSpec((count, owners, local, size), lambda a: (0, 0, 0, 0)),
+        out_shape=jax.ShapeDtypeStruct((count, owners, local, size), BF16),
+        scratch_shapes=[pltpu.VMEM((count, total, size), F32)],
         compiler_params=params(1),
-        cost_estimate=pl.CostEstimate(
-            flops=count * total * total * size, bytes_accessed=4 * total * size * count, transcendentals=0
-        ),
         name="forecast",
     )(own_blocks, *blocks, transform, courant)
 
@@ -545,16 +563,16 @@
     def layered(blocks, rows):
         return [blocks[:, layer * rows : (layer + 1) * rows] for layer in range(layers)]
 
-    first = pack_obs(hx_values, layers, 0, ())
-    first = across([block.reshape(held, half, own) for block in first])
-    (second,) = pack_obs(hx_values, layers, 1, (obs_value, obs_var))
+    packed = pack_obs(hx_values, layers, 0, (), ())
+    first = across([block.reshape(held, half, own) for block in packed])
+    (second,) = pack_obs(hx_values, layers, 1, (obs_value, obs_var), packed[:1])
     second = within(second.reshape(held, -1, own))
     seconds = [second] + across(layered(second, half))[1:]
-    state = pack_state(member_state, layers, width)
+    state = pack_state(member_state, layers, width, first[1:2] + first[-1:])
     size = state.shape[5]
     state = within(state.reshape(held, layers * local, size))
     states = across(layered(state, local))
-    first = within(jnp.concatenate(first, axis=1))
+    first = within(join(first, [state]))
     observed = [first, *seconds]
     if shared:
         observed = [widened(array, count) for array in observed]
@@ -562,8 +580,7 @@
 
     if not shared and width == 2 and cells_a // width >= STEPS:
         state = state.reshape(held, layers, local, size)
-        back = forecasts(state, states[1:], transform, courant, 0)
-        (last,) = forecasts(state, states[1:], transform, courant, 1)
+        fields = forecasts(state, states[1:], transform, courant)
     else:
         column = lax.axis_index("sub") % count
         line = (lax.axis_index("mem") * width + column % width) * cells_b
@@ -572,20 +589,23 @@
         states = [block.reshape(count, PAIR * local, size) for block in states]
         analysis = analyses(jnp.concatenate(states, axis=1), transform)
         fields = shared_transport(analysis, speed, width, count)
-        fields = fields.reshape(count, layers, PAIR, 2, half, size)
-        fields = fields.transpose(3, 0, 2, 1, 4, 5).reshape(2, held, layers, half, size)
-        back = [fields[0, :, layer] for layer in range(layers)]
-        last = fields[1].reshape(held, layers * half, size)
-    back = within(jnp.concatenate(across(back), axis=1))
-    last = within(last)
-    lasts = across(layered(last, half))
-
-    def spec(layer):
-        return pl.BlockSpec((width * PAIR, half, size), lambda s: (s, layer, 0))
-
-    shape = member_state.shape
-    done = unpack_state([back] * layers, [spec(i) for i in range(layers)], shape, 0, None)
-    return unpack_state([last, *lasts[1:]], [spec(0)] * layers, shape, 1, done)
+        fields = fields.reshape(count, layers, PAIR * local, size)
+        place = jnp.arange(layers) ^ own_layer()
+        fields = jnp.take(fields, place, axis=1)
+
+    groups = None
+    if shared:
+        span = count * owners
+        groups = [list(range(g, g + span)) for g in range(0, lines * owners, span)]
+    back = lax.all_to_all(
+        fields.reshape(count * owners, local, size),
+        ("sub", "mem"),
+        split_axis=0,
+        concat_axis=0,
+        tiled=True,
+        axis_index_groups=groups,
+    )
+    return unpack_state(back.reshape(slabs, width, owners, local, size), cells_a)
 
 
 def solution(mesh):

time: 214 us -> 253 us (1.18)
  blocking collectives: 0 us -> 54.9 us
  Pallas kernels: 51.8 us -> 79.4 us
  starting transfers between devices: 58.5 us -> 32.5 us
  waiting for transfers between devices: 92.1 us -> 81.5 us
  other arithmetic: 3.98 us -> 0 us
    all_to_all x0 -> x1, blocking collectives: none -> 54.9 us  [advance(): lax.all_to_all(fields.reshape(count * owners, local, size), ('sub', 'mem'...]
    pallas_call x3, Pallas kernels: 11.3 us -> 42.8 us  [the longest x1 32.9 us: join(): pl.pallas_call(kernel, in_specs=[ANY] * (layers + len(after)), out_specs=...]
    ppermute x15 -> x9, starting transfers between devices: 37.4 us -> 20.7 us  [across(): received[layer] = lax.ppermute(blocks[layer], ('sub', 'mem'), pairs)]
    ppermute x15 -> x9, waiting for transfers between devices: 72.4 us -> 57.5 us  [across(): received[layer] = lax.ppermute(blocks[layer], ('sub', 'mem'), pairs)]
    all_to_all x5 -> x3, starting transfers between devices: 21.1 us -> 11.8 us  [within(): lax.all_to_all(blocks, ('sub', 'mem'), split_axis=0, concat_axis=0, tiled...]
    all_to_all x5 -> x3, waiting for transfers between devices: 19.7 us -> 24 us  [within(): lax.all_to_all(blocks, ('sub', 'mem'), split_axis=0, concat_axis=0, tiled...]
    concatenate x2 -> x0, other arithmetic: 3.98 us -> none  [the longest x1 1.99 us: advance(): first = within(jnp.concatenate(first, axis=1))]
    pallas_call x2 -> x1, Pallas kernels: 14.3 us -> 10.4 us  [forecasts(): pl.pallas_call(kernel, grid=(count,), in_specs=[pl.BlockSpec((PAIR, 1, lo...]
  transfers between devices with their start and end apart: 20 -> 12, of which waited for: 9 -> 7; matrix products, arithmetic and copies ran while one was open for 3% -> 1% of each run, Pallas kernels for 18% -> 22%
where the time goes in v5:
time: 253 us
  waiting for transfers between devices  81.5 us (32%)
  Pallas kernels  79.4 us (31%)
  blocking collectives  54.9 us (22%)
  starting transfers between devices  32.5 us (13%)
  local copies, waits for them, and re-layouts  4.37 us (2%)
    ppermute x9, waiting for transfers between devices, across(): received[layer] = lax.ppermute(blocks[layer], ('sub', 'mem'), pairs)  57.5 us
    all_to_all x1, blocking collectives, advance(): lax.all_to_all(fields.reshape(count * owners, local, size), ('sub', 'mem'...  54.9 us
    pallas_call x1, Pallas kernels, join(): pl.pallas_call(kernel, in_specs=[ANY] * (layers + len(after)), out_specs=...  32.9 us
    all_to_all x3, waiting for transfers between devices, within(): lax.all_to_all(blocks, ('sub', 'mem'), split_axis=0, concat_axis=0, tiled...  24 us
    pallas_call x1, Pallas kernels, transforms(): pl.pallas_call(kernel, grid=(count,), in_specs=[pl.BlockSpec(array.shape,...  21 us
    ppermute x9, starting transfers between devices, across(): received[layer] = lax.ppermute(blocks[layer], ('sub', 'mem'), pairs)  20.7 us
    all_to_all x3, starting transfers between devices, within(): lax.all_to_all(blocks, ('sub', 'mem'), split_axis=0, concat_axis=0, tiled...  11.8 us
    pallas_call x1, Pallas kernels, forecasts(): pl.pallas_call(kernel, grid=(count,), in_specs=[pl.BlockSpec((PAIR, 1, lo...  10.4 us
  transfers between devices with their start and end apart: 12, of which 7 were waited for; matrix products, arithmetic and copies ran while one was open for 1% of the time, Pallas kernels for 22%

profile of v5, /device:TPU:0, one launch (start us, length us, event | category | flops | bytes accessed | tf_op | source)
XLA Modules:
  0.0 252.8 jit_solution(15751995612980544367)
XLA Ops:
  0.0 2.5 %pack_obs.2 = (bf16[2,4,32,512]{3,2,1,0:T(8,128)(2,1)}, bf16[2,4,32,512]{3,2,1,0:T(8,128)(2,1)}, bf16[2,4,32,512]{3,2,1,0:T(8,128)(2,1)}, bf16[2,4,32,512]{3,2,1,0:T(8,128)(2,1)}) custom-call(bf16[2,64,1,16,512]{4,3,2,1,0:T(8,128)(2,1)} %refs_0_.5), custom_call_target="tpu_custom_call" | custom-call | tf_op jit(solution)/shard_map/pack_obs/pallas_call | solution.py:98
  2.5 5.0 %collective-permute-start.1 = (bf16[8,32,512]{2,1,0:T(8,128)(2,1)}, bf16[8,32,512]{2,1,0:T(8,128)(2,1)S(1)}, u32[]{:S(2)}, u32[]{:S(2)}) collective-permute-start(bf16[8,32,512]{2,1,0:T(8,128)(2,1)} %bitcast.17), channel_id=1, source_target_pairs={{0,6},{1,7},{2,4},{3,5},{4,2},{5,3},{6,0},{7,1},{8,14},{9,15},{10,... | collective-permute-start | bytes 786440 | tf_op jit(solution)/shard_map/ppermute | solution.py:560
  7.6 0.0 collective-permute-start
  7.6 7.4 %collective-permute-done.1.refs_2_.refs_3_ = bf16[8,32,512]{2,1,0:T(8,128)(2,1)S(1)} collective-permute-done((bf16[8,32,512]{2,1,0:T(8,128)(2,1)}, bf16[8,32,512]{2,1,0:T(8,128)(2,1)S(1)}, u32[]{:S(2)}, u32[]{:S(2)}) %collective-permute-start.1) | collective-permute-done | bytes 262176 | tf_op jit(solution)/shard_map/ppermute | solution.py:560
  15.0 0.0 copy-start.3
  15.0 4.8 %collective-permute-done.refs_1_ = bf16[8,32,512]{2,1,0:T(8,128)(2,1)S(1)} collective-permute-done((bf16[8,32,512]{2,1,0:T(8,128)(2,1)}, bf16[8,32,512]{2,1,0:T(8,128)(2,1)S(1)}, u32[]{:S(2)}, u32[]{:S(2)}) %collective-permute-start) | collective-permute-done | bytes 262176 | tf_op jit(solution)/shard_map/ppermute | solution.py:560
  19.8 0.0 copy-done.3
  19.8 0.0 copy-start.4
  19.8 0.7 copy-done.4
  20.5 4.8 %pack_state.1 = bf16[2,2,2,4,64,512]{5,4,3,2,1,0:T(8,128)(2,1)} custom-call(bf16[2,64,8,1024]{3,2,1,0:T(8,128)(2,1)} %refs_0_.4, bf16[8,32,512]{2,1,0:T(8,128)(2,1)} %copy-done.4, bf16[8,32,512]{2,1,0:T(8,128)(2,1)} %copy-done.3), custom_call_target="tpu_custom_call" | custom-call | tf_op jit(solution)/shard_map/pack_state/pallas_call | solution.py:168
  25.3 3.7 %all-to-all-start = ((bf16[8,256,512]{2,1,0:T(8,128)(2,1)}), bf16[8,256,512]{2,1,0:T(8,128)(2,1)S(1)}, u32[]{:S(2)}, u32[]{:S(2)}) async-start(bf16[8,256,512]{2,1,0:T(8,128)(2,1)} %bitcast.11), calls=%async_computation | async-start | bytes 4194304 | tf_op jit(solution)/shard_map/all_to_all | solution.py:543
  29.1 0.0 copy-start.11
  29.1 2.7 %pack_obs.3 = bf16[2,4,144,512]{3,2,1,0:T(8,128)(2,1)} custom-call(bf16[2,64,1,16,512]{4,3,2,1,0:T(8,128)(2,1)} %refs_0_.5, bf16[2,1,2,512]{3,2,1,0:T(2,128)(2,1)} %refs_1_.1, bf16[2,1,2,512]{3,2,1,0:T(2,128)(2,1)} %refs_2_.1, bf16[2,4,32,512]{3,2,1,0:T(8,128)(2,1)} %get-tuple-element.11.refs_3_), custom_call_target="tpu_custom_call" | custom-call | tf_op jit(solution)/shard_map/pack_obs/pallas_call | solution.py:98
  31.7 24.0 %all-to-all-done.refs_4_ = bf16[8,256,512]{2,1,0:T(8,128)(2,1)S(1)} async-done(((bf16[8,256,512]{2,1,0:T(8,128)(2,1)}), bf16[8,256,512]{2,1,0:T(8,128)(2,1)S(1)}, u32[]{:S(2)}, u32[]{:S(2)}) %all-to-all-start) | async-done | bytes 2097184 | tf_op jit(solution)/shard_map/all_to_all | solution.py:543
  55.7 0.0 copy-start
  55.7 3.6 %all-to-all-start.2 = ((bf16[8,144,512]{2,1,0:T(8,128)(2,1)}), bf16[8,144,512]{2,1,0:T(8,128)(2,1)S(1)}, u32[]{:S(2)}, u32[]{:S(2)}) async-start(bf16[8,144,512]{2,1,0:T(8,128)(2,1)} %bitcast.13), calls=%async_computation.2 | async-start | bytes 2359296 | tf_op jit(solution)/shard_map/all_to_all | solution.py:543
  59.3 0.0 copy-done.11
  59.3 1.4 collective-permute-start.5
  60.7 13.7 %collective-permute-done.5.refs_2_ = bf16[8,32,512]{2,1,0:T(8,128)(2,1)S(1)} collective-permute-done((bf16[8,32,512]{2,1,0:T(8,128)(2,1)S(1)}, bf16[8,32,512]{2,1,0:T(8,128)(2,1)S(1)}, u32[]{:S(2)}, u32[]{:S(2)}) %collective-permute-start.5) | collective-permute-done | bytes 262176 | tf_op jit(solution)/shard_map/ppermute | solution.py:560
  74.4 0.0 copy-start.8
  74.4 0.0 copy-done
  74.4 0.7 copy-done.8
  75.1 32.9 %join.1 = bf16[8,128,512]{2,1,0:T(8,128)(2,1)} custom-call(bf16[8,32,512]{2,1,0:T(8,128)(2,1)} %bitcast.14, bf16[8,32,512]{2,1,0:T(8,128)(2,1)} %copy-done.4, bf16[8,32,512]{2,1,0:T(8,128)(2,1)} %copy-done.8, bf16[8,32,512]{2,1,0:T(8,128)(2,1)} %copy-done.3, bf16[8,256,512]{2,1,0:T(8,128)(2,1)} %copy-done), custom_call_target="tpu_custom_call" | custom-call | tf_op jit(solution)/shard_map/join/pallas_call | solution.py:262
  108.0 0.0 copy-start.1
  108.0 0.0 all-to-all-done.2.refs_1_
  108.1 0.0 copy-start.2
  108.1 4.5 %all-to-all-start.1 = ((bf16[8,128,512]{2,1,0:T(8,128)(2,1)}), bf16[8,128,512]{2,1,0:T(8,128)(2,1)}, u32[]{:S(2)}, u32[]{:S(2)}) async-start(bf16[8,128,512]{2,1,0:T(8,128)(2,1)} %join.1), calls=%async_computation.1 | async-start | bytes 2097152 | tf_op jit(solution)/shard_map/all_to_all | solution.py:543
  112.6 0.1 fusion.1
  112.6 1.8 collective-permute-start.8
  114.4 0.0 collective-permute-start.7
  114.4 2.7 %collective-permute-start.6 = (bf16[8,32,512]{2,1,0:T(8,128)(2,1)S(1)}, bf16[8,32,512]{2,1,0:T(8,128)(2,1)}, u32[]{:S(2)}, u32[]{:S(2)}) collective-permute-start(bf16[8,32,512]{2,1,0:T(8,128)(2,1)S(1)} %get-tuple-element.18), channel_id=1, source_target_pairs={{0,2},{1,3},{2,0},{3,1},{4,6},{5,7},{6,4},{7,5},{8,10},{9,11},{10,... | collective-permute-start | bytes 786440 | tf_op jit(solution)/shard_map/ppermute | solution.py:560
  117.1 0.0 copy-done.1
  117.1 1.2 fusion
  118.3 0.0 copy-done.2
  118.3 1.7 collective-permute-start.4
  120.0 0.0 collective-permute-start.3
  120.0 3.8 %collective-permute-done.8.refs_4_ = bf16[8,32,512]{2,1,0:T(8,128)(2,1)S(1)} collective-permute-done((bf16[8,32,512]{2,1,0:T(8,128)(2,1)S(1)}, bf16[8,32,512]{2,1,0:T(8,128)(2,1)S(1)}, u32[]{:S(2)}, u32[]{:S(2)}) %collective-permute-start.8) | collective-permute-done | bytes 262176 | tf_op jit(solution)/shard_map/ppermute | solution.py:560
  123.8 0.0 copy-start.9
  123.8 8.2 %collective-permute-start.2 = (bf16[8,64,512]{2,1,0:T(8,128)(2,1)}, bf16[8,64,512]{2,1,0:T(8,128)(2,1)S(1)}, u32[]{:S(2)}, u32[]{:S(2)}) collective-permute-start(bf16[8,64,512]{2,1,0:T(8,128)(2,1)} %get-tuple-element.15), channel_id=1, source_target_pairs={{0,2},{1,3},{2,0},{3,1},{4,6},{5,7},{6,4},{7,5},{8,10},{9,11},{10,... | collective-permute-start | bytes 1572872 | tf_op jit(solution)/shard_map/ppermute | solution.py:560
  131.9 27.6 %collective-permute-done.7.refs_3_ = bf16[8,32,512]{2,1,0:T(8,128)(2,1)S(1)} collective-permute-done((bf16[8,32,512]{2,1,0:T(8,128)(2,1)S(1)}, bf16[8,32,512]{2,1,0:T(8,128)(2,1)S(1)}, u32[]{:S(2)}, u32[]{:S(2)}) %collective-permute-start.7) | collective-permute-done | bytes 262176 | tf_op jit(solution)/shard_map/ppermute | solution.py:560
  159.5 0.0 copy-start.10
  159.5 0.7 copy-done.10
  160.2 0.0 collective-permute-done.6.refs_2_
  160.2 0.0 all-to-all-done.1.refs_0_
  160.2 0.0 copy-done.9
  160.2 21.0 %transform.1.refs_4_ = bf16[4,512,512]{2,1,0:T(8,128)(2,1)} custom-call(bf16[8,128,512]{2,1,0:T(8,128)(2,1)} %all-to-all-done.1.refs_0_, bf16[8,144,512]{2,1,0:T(8,128)(2,1)} %copy-done.2, bf16[8,32,512]{2,1,0:T(8,128)(2,1)} %collective-permute-done.6.refs_2_, bf16[8,32,512]{2,1,0:T(8,128)(2,1)} %copy-done.10, bf16[8,32,512]{2,1,0:T(8,128)(2,1)} %copy-done.9), custom_call_target="tpu_custom_call" | custom-call | flops 11811160064 | bytes 8388608 | tf_op jit(solution)/shard_map/transform/pallas_call | solution.py:345
  181.2 0.0 collective-permute-done.4.refs_3_
  181.2 0.0 copy-start.5
  181.2 0.2 collective-permute-done.3.refs_2_
  181.4 0.0 copy-start.6
  181.4 0.0 collective-permute-done.2.refs_1_
  181.4 0.0 copy-start.7
  181.4 0.6 copy-done.5
  182.0 0.2 copy-done.6
  182.2 0.2 copy-done.7
  182.4 10.4 %forecast.1 = bf16[4,8,64,512]{3,2,1,0:T(8,128)(2,1)} custom-call(bf16[8,4,64,512]{3,2,1,0:T(8,128)(2,1)} %bitcast.9, bf16[8,64,512]{2,1,0:T(8,128)(2,1)} %copy-done.7, bf16[8,64,512]{2,1,0:T(8,128)(2,1)} %copy-done.6, bf16[8,64,512]{2,1,0:T(8,128)(2,1)} %copy-done.5, bf16[4,512,512]{2,1,0:T(8,128)(2,1)} %transform.1.refs_4_, f32[2,1024]{1,0:T(2,128)} %refs_5_.1), custom_call_target="tpu_custom_call" | custom-call | tf_op jit(solution)/shard_map/forecast/pallas_call | solution.py:457
  192.8 54.9 %all_to_all.20 = bf16[32,64,512]{2,1,0:T(8,128)(2,1)} all-to-all(bf16[32,64,512]{2,1,0:T(8,128)(2,1)} %bitcast.10), channel_id=1, replica_groups=mesh['sub'=4,'mem'=8] {'sub','mem'}, dimensions={0} | all-to-all | bytes 4194304 | tf_op jit(solution)/shard_map/all_to_all | solution.py:600
  247.7 5.1 %unpack_state.1 = bf16[2,64,8,1024]{3,2,1,0:T(8,128)(2,1)} custom-call(bf16[2,2,8,64,512]{4,3,2,1,0:T(8,128)(2,1)} %bitcast.12), custom_call_target="tpu_custom_call" | custom-call | tf_op jit(solution)/shard_map/unpack_state/pallas_call | solution.py:223
Async XLA Ops:
  2.5 12.5 %collective-permute-start.1 = (bf16[8,32,512]{2,1,0:T(8,128)(2,1)}, bf16[8,32,512]{2,1,0:T(8,128)(2,1)S(1)}, u32[]{:S(2)}, u32[]{:S(2)}) collective-permute-start(bf16[8,32,512]{2,1,0:T(8,128)(2,1)} %bitcast.17), channel_id=1, source_target_pairs={{0,6},{1,7},{2,4},{3,5},{4,2},{5,3},{6,0},{7,1},{8,14},{9,15},{10,... | collective-permute-start | bytes 786440 | tf_op jit(solution)/shard_map/ppermute | solution.py:560
  7.6 12.2 %collective-permute-start = (bf16[8,32,512]{2,1,0:T(8,128)(2,1)}, bf16[8,32,512]{2,1,0:T(8,128)(2,1)S(1)}, u32[]{:S(2)}, u32[]{:S(2)}) collective-permute-start(bf16[8,32,512]{2,1,0:T(8,128)(2,1)} %bitcast.16), channel_id=1, source_target_pairs={{0,2},{1,3},{2,0},{3,1},{4,6},{5,7},{6,4},{7,5},{8,10},{9,11},{10,... | collective-permute-start | bytes 786440 | tf_op jit(solution)/shard_map/ppermute | solution.py:560
  15.0 4.8 %copy-start.3 = (bf16[8,32,512]{2,1,0:T(8,128)(2,1)}, bf16[8,32,512]{2,1,0:T(8,128)(2,1)S(1)}, u32[]{:S(2)}) copy-start(bf16[8,32,512]{2,1,0:T(8,128)(2,1)S(1)} %collective-permute-done.1.refs_2_.refs_3_) | copy-start | bytes 786436
  19.8 0.7 copy-start.4
  25.3 30.4 %all-to-all-start = ((bf16[8,256,512]{2,1,0:T(8,128)(2,1)}), bf16[8,256,512]{2,1,0:T(8,128)(2,1)S(1)}, u32[]{:S(2)}, u32[]{:S(2)}) async-start(bf16[8,256,512]{2,1,0:T(8,128)(2,1)} %bitcast.11), calls=%async_computation | async-start | bytes 4194304 | tf_op jit(solution)/shard_map/all_to_all | solution.py:543
  29.1 30.2 %copy-start.11 = (bf16[2,4,32,512]{3,2,1,0:T(8,128)(2,1)S(1)}, bf16[2,4,32,512]{3,2,1,0:T(8,128)(2,1)}, u32[]{:S(2)}) copy-start(bf16[2,4,32,512]{3,2,1,0:T(8,128)(2,1)} %get-tuple-element.12) | copy-start | bytes 786436
  55.7 18.7 %copy-start = (bf16[8,256,512]{2,1,0:T(8,128)(2,1)}, bf16[8,256,512]{2,1,0:T(8,128)(2,1)S(1)}, u32[]{:S(2)}) copy-start(bf16[8,256,512]{2,1,0:T(8,128)(2,1)S(1)} %all-to-all-done.refs_4_) | copy-start | bytes 6291460
  55.7 52.3 %all-to-all-start.2 = ((bf16[8,144,512]{2,1,0:T(8,128)(2,1)}), bf16[8,144,512]{2,1,0:T(8,128)(2,1)S(1)}, u32[]{:S(2)}, u32[]{:S(2)}) async-start(bf16[8,144,512]{2,1,0:T(8,128)(2,1)} %bitcast.13), calls=%async_computation.2 | async-start | bytes 2359296 | tf_op jit(solution)/shard_map/all_to_all | solution.py:543
  59.3 15.1 %collective-permute-start.5 = (bf16[8,32,512]{2,1,0:T(8,128)(2,1)S(1)}, bf16[8,32,512]{2,1,0:T(8,128)(2,1)S(1)}, u32[]{:S(2)}, u32[]{:S(2)}) collective-permute-start(bf16[8,32,512]{2,1,0:T(8,128)(2,1)S(1)} %bitcast.15), channel_id=1, source_target_pairs={{0,4},{1,5},{2,6},{3,7},{4,0},{5,1},{6,2},{7,3},{8,12},{9,13},{10,... | collective-permute-start | bytes 786440 | tf_op jit(solution)/shard_map/ppermute | solution.py:560
  74.4 0.7 copy-start.8
  108.0 9.1 %copy-start.1 = (bf16[8,256,512]{2,1,0:T(8,128)(2,1)S(1)}, bf16[8,256,512]{2,1,0:T(8,128)(2,1)}, u32[]{:S(2)}) copy-start(bf16[8,256,512]{2,1,0:T(8,128)(2,1)} %copy-done) | copy-start | bytes 6291460
  108.1 10.3 %copy-start.2 = (bf16[8,144,512]{2,1,0:T(8,128)(2,1)}, bf16[8,144,512]{2,1,0:T(8,128)(2,1)S(1)}, u32[]{:S(2)}) copy-start(bf16[8,144,512]{2,1,0:T(8,128)(2,1)S(1)} %all-to-all-done.2.refs_1_) | copy-start | bytes 3538948
  108.1 52.1 %all-to-all-start.1 = ((bf16[8,128,512]{2,1,0:T(8,128)(2,1)}), bf16[8,128,512]{2,1,0:T(8,128)(2,1)}, u32[]{:S(2)}, u32[]{:S(2)}) async-start(bf16[8,128,512]{2,1,0:T(8,128)(2,1)} %join.1), calls=%async_computation.1 | async-start | bytes 2097152 | tf_op jit(solution)/shard_map/all_to_all | solution.py:543
  112.6 11.1 %collective-permute-start.8 = (bf16[8,32,512]{2,1,0:T(8,128)(2,1)S(1)}, bf16[8,32,512]{2,1,0:T(8,128)(2,1)S(1)}, u32[]{:S(2)}, u32[]{:S(2)}) collective-permute-start(bf16[8,32,512]{2,1,0:T(8,128)(2,1)S(1)} %get-tuple-element.16), channel_id=1, source_target_pairs={{0,6},{1,7},{2,4},{3,5},{4,2},{5,3},{6,0},{7,1},{8,14},{9,15},{10,... | collective-permute-start | bytes 786440 | tf_op jit(solution)/shard_map/ppermute | solution.py:560
  114.4 45.1 %collective-permute-start.7 = (bf16[8,32,512]{2,1,0:T(8,128)(2,1)S(1)}, bf16[8,32,512]{2,1,0:T(8,128)(2,1)S(1)}, u32[]{:S(2)}, u32[]{:S(2)}) collective-permute-start(bf16[8,32,512]{2,1,0:T(8,128)(2,1)S(1)} %get-tuple-element.17), channel_id=1, source_target_pairs={{0,4},{1,5},{2,6},{3,7},{4,0},{5,1},{6,2},{7,3},{8,12},{9,13},{10,... | collective-permute-start | bytes 786440 | tf_op jit(solution)/shard_map/ppermute | solution.py:560
  114.4 45.8 %collective-permute-start.6 = (bf16[8,32,512]{2,1,0:T(8,128)(2,1)S(1)}, bf16[8,32,512]{2,1,0:T(8,128)(2,1)}, u32[]{:S(2)}, u32[]{:S(2)}) collective-permute-start(bf16[8,32,512]{2,1,0:T(8,128)(2,1)S(1)} %get-tuple-element.18), channel_id=1, source_target_pairs={{0,2},{1,3},{2,0},{3,1},{4,6},{5,7},{6,4},{7,5},{8,10},{9,11},{10,... | collective-permute-start | bytes 786440 | tf_op jit(solution)/shard_map/ppermute | solution.py:560
  118.3 62.9 %collective-permute-start.4 = (bf16[8,64,512]{2,1,0:T(8,128)(2,1)}, bf16[8,64,512]{2,1,0:T(8,128)(2,1)S(1)}, u32[]{:S(2)}, u32[]{:S(2)}) collective-permute-start(bf16[8,64,512]{2,1,0:T(8,128)(2,1)} %get-tuple-element.13), channel_id=1, source_target_pairs={{0,6},{1,7},{2,4},{3,5},{4,2},{5,3},{6,0},{7,1},{8,14},{9,15},{10,... | collective-permute-start | bytes 1572872 | tf_op jit(solution)/shard_map/ppermute | solution.py:560
  120.0 61.4 %collective-permute-start.3 = (bf16[8,64,512]{2,1,0:T(8,128)(2,1)}, bf16[8,64,512]{2,1,0:T(8,128)(2,1)S(1)}, u32[]{:S(2)}, u32[]{:S(2)}) collective-permute-start(bf16[8,64,512]{2,1,0:T(8,128)(2,1)} %get-tuple-element.14), channel_id=1, source_target_pairs={{0,4},{1,5},{2,6},{3,7},{4,0},{5,1},{6,2},{7,3},{8,12},{9,13},{10,... | collective-permute-start | bytes 1572872 | tf_op jit(solution)/shard_map/ppermute | solution.py:560
  123.8 36.4 %copy-start.9 = (bf16[8,32,512]{2,1,0:T(8,128)(2,1)}, bf16[8,32,512]{2,1,0:T(8,128)(2,1)S(1)}, u32[]{:S(2)}) copy-start(bf16[8,32,512]{2,1,0:T(8,128)(2,1)S(1)} %collective-permute-done.8.refs_4_) | copy-start | bytes 786436
  123.8 57.6 %collective-permute-start.2 = (bf16[8,64,512]{2,1,0:T(8,128)(2,1)}, bf16[8,64,512]{2,1,0:T(8,128)(2,1)S(1)}, u32[]{:S(2)}, u32[]{:S(2)}) collective-permute-start(bf16[8,64,512]{2,1,0:T(8,128)(2,1)} %get-tuple-element.15), channel_id=1, source_target_pairs={{0,2},{1,3},{2,0},{3,1},{4,6},{5,7},{6,4},{7,5},{8,10},{9,11},{10,... | collective-permute-start | bytes 1572872 | tf_op jit(solution)/shard_map/ppermute | solution.py:560
  159.5 0.7 copy-start.10
  181.2 0.8 copy-start.5
  181.4 0.8 copy-start.6
  181.4 1.0 copy-start.7

commit v6 on v4

--- a/solution.py
+++ b/solution.py
@@ -12,6 +12,7 @@
 F32 = jnp.float32
 BF16 = jnp.bfloat16
 VMEM_LIMIT = 60 * 1024 * 1024
+ANY = pl.BlockSpec(memory_space=pl.ANY)
 
 
 def params(count):
@@ -48,9 +49,11 @@
     return lax.axis_index("mem") & 1
 
 
-def pack_obs_kernel(rows, *refs, layers, width, given):
-    stats, outs, order = refs[:given], refs[given:-1], refs[-1]
-    local, patches, own = rows.shape[1], rows.shape[3], rows.shape[4]
+def pack_obs_kernel(rows, value, variance, *refs, layers):
+    *firsts, second, order = refs
+    _, local, _, patches, own = rows.shape
+    half = local // 2
+    width = value.shape[2]
     size = order.shape[0]
     block = size // patches
 
@@ -66,44 +69,40 @@
         flat = moved(order[...], rows[0, at : at + block].reshape(size, own))
         flat = flat.reshape(width * PAIR, layers, block, own)
         for layer in range(layers):
-            if stats:
-                start = layer * local + at
-                outs[0][0, :, start : start + block, :] = flat[:, layer]
+            if at < half:
+                firsts[layer][0, :, at : at + block, :] = flat[:, layer]
             else:
-                outs[layer][0, :, at : at + block, :] = flat[:, layer]
-    if stats:
-        value, variance = (ref[0, 0].astype(F32) for ref in stats)
-        line = iota(SPARE, own, 0)
-        for part in range(width):
-            spare = jnp.where(line == 0, value[part : part + 1], variance[part : part + 1])
-            for bit in range(PAIR):
-                outs[0][0, part * PAIR + bit, layers * local :, :] = spare.astype(BF16)
-
-
-def pack_obs(hx_values, layers, piece, stats):
-    slabs, members, _, patches, own = hx_values.shape
+                start = layer * half + at - half
+                second[0, :, start : start + block, :] = flat[:, layer]
+    values, variances = (ref[0, 0].astype(F32) for ref in (value, variance))
+    line = iota(SPARE, own, 0)
+    for part in range(width):
+        spare = jnp.where(line == 0, values[part : part + 1], variances[part : part + 1])
+        for bit in range(PAIR):
+            second[0, part * PAIR + bit, layers * half :, :] = spare.astype(BF16)
+
+
+def pack_obs(hx_values, obs_value, obs_var, layers):
+    slabs, local, _, patches, own = hx_values.shape
     width = patches // (layers * PAIR)
-    local = members // 2
     block = 16
 
     def kernel(*refs):
-        pack_obs_kernel(*refs, layers=layers, width=width, given=len(stats))
+        pack_obs_kernel(*refs, layers=layers)
 
     held = width * PAIR
-    shapes = [(held, local, own)] * layers
-    if stats:
-        shapes = [(held, layers * local + SPARE, own)]
+    shapes = [(held, local // 2, own)] * layers + [(held, layers * local // 2 + SPARE, own)]
     return pl.pallas_call(
         kernel,
         grid=(slabs,),
-        in_specs=[pl.BlockSpec((1, local, 1, patches, own), lambda s: (s, piece, 0, 0, 0))]
-        + [pl.BlockSpec((1, 1, width, own), lambda s: (s, 0, 0, 0))] * len(stats),
+        in_specs=[pl.BlockSpec((1, local, 1, patches, own), lambda s: (s, 0, 0, 0, 0))]
+        + [pl.BlockSpec((1, 1, width, own), lambda s: (s, 0, 0, 0))] * 2,
         out_specs=[pl.BlockSpec((1, *shape), lambda s: (s, 0, 0, 0)) for shape in shapes],
         out_shape=[jax.ShapeDtypeStruct((slabs, *shape), BF16) for shape in shapes],
         scratch_shapes=[pltpu.VMEM((block * patches, block * patches), BF16)],
         compiler_params=params(1),
         name="pack_obs",
-    )(hx_values, *stats)
+    )(hx_values, obs_value, obs_var)
 
 
 def swapped(width, lanes):
@@ -153,15 +152,20 @@
                 ]
 
 
-def pack_state(member_state, layers, width):
+def pack_state(member_state, layers, width, after):
     slabs, local, cells_a, cols = member_state.shape
     lanes = cols // (layers * PAIR)
     size = cells_a * lanes // width
     block = 32
-    return pl.pallas_call(
-        pack_state_kernel,
+
+    def kernel(*refs):
+        pack_state_kernel(refs[0], *refs[1 + len(after) :])
+
+    return pl.pallas_call(
+        kernel,
         grid=(slabs, local // block),
-        in_specs=[pl.BlockSpec((1, block, cells_a, cols), lambda s, g: (s, g, 0, 0))],
+        in_specs=[pl.BlockSpec((1, block, cells_a, cols), lambda s, g: (s, g, 0, 0))]
+        + [ANY] * len(after),
         out_specs=pl.BlockSpec(
             (1, width, PAIR, layers, block, size), lambda s, g: (s, 0, 0, 0, g, 0)
         ),
@@ -172,7 +176,7 @@
         ],
         compiler_params=params(2),
         name="pack_state",
-    )(member_state)
+    )(member_state, *after)
 
 
 def unpack_state_kernel(*refs, layers, width):
@@ -227,7 +231,7 @@
     return pl.pallas_call(
         kernel,
         grid=(slabs,),
-        in_specs=specs + [pl.BlockSpec(memory_space=pl.ANY)] * len(kept),
+        in_specs=specs + [ANY] * len(kept),
         out_specs=pl.BlockSpec((1, block, cells_a, cols), lambda s: (s, piece, 0, 0)),
         out_shape=jax.ShapeDtypeStruct(shape, BF16),
         scratch_shapes=[
@@ -238,6 +242,39 @@
         compiler_params=params(1),
         name="unpack_state",
     )(*blocks, *kept)
+
+
+def join(blocks, after):
+    layers = len(blocks)
+    held, rows, size = blocks[0].shape
+    span = held // 2
+
+    def kernel(*refs):
+        for layer in range(layers):
+            refs[-1][:, layer * rows : (layer + 1) * rows, :] = refs[layer][...]
+
+    return pl.pallas_call(
+        kernel,
+        grid=(2,),
+        in_specs=[pl.BlockSpec((span, rows, size), lambda i: (i, 0, 0))] * layers
+        + [ANY] * len(after),
+        out_specs=pl.BlockSpec((span, layers * rows, size), lambda i: (i, 0, 0)),
+        out_shape=jax.ShapeDtypeStruct((held, layers * rows, size), BF16),
+        compiler_params=params(1),
+        name="join",
+    )(*blocks, *after)
+
+
+def gate(array, after):
+    return pl.pallas_call(
+        lambda *refs: None,
+        in_specs=[ANY] * (1 + len(after)),
+        out_specs=ANY,
+        out_shape=jax.ShapeDtypeStruct(array.shape, array.dtype),
+        input_output_aliases={0: 0},
+        compiler_params=pltpu.CompilerParams(vmem_limit_bytes=VMEM_LIMIT),
+        name="gate",
+    )(array, *after)
 
 
 def transform_kernel(spread, *refs, layers, count, shift):
@@ -302,7 +339,7 @@
     out[0] = (jnp.sqrt((total - 1.0) / bound) * flipped + weight).astype(BF16)
 
 
-def transforms(spread, seconds, count):
+def transforms(spread, seconds, count, after):
     layers = len(seconds)
     held, rows, own = spread.shape
     total = rows * PAIR * 2
@@ -310,14 +347,16 @@
     flops = count * (2 * total * total * 2 * own + 18 * total**3)
 
     def kernel(*refs):
-        transform_kernel(*refs, layers=layers, count=count, shift=shift)
+        kept = refs[: 1 + layers] + refs[1 + layers + len(after) :]
+        transform_kernel(*kept, layers=layers, count=count, shift=shift)
 
     return pl.pallas_call(
         kernel,
         grid=(count,),
         in_specs=[
             pl.BlockSpec(array.shape, lambda a: (0, 0, 0)) for array in (spread, *seconds)
-        ],
+        ]
+        + [ANY] * len(after),
         out_specs=pl.BlockSpec((1, total, total), lambda a: (a, 0, 0)),
         out_shape=jax.ShapeDtypeStruct((count, total, total), BF16),
         scratch_shapes=[pltpu.VMEM((total, 2 * own), BF16), pltpu.VMEM((total, 2 * own), BF16)],
@@ -326,7 +365,7 @@
             flops=flops, bytes_accessed=4 * count * total * total * 2, transcendentals=0
         ),
         name="transform",
-    )(spread, *seconds)
+    )(spread, *seconds, *after)
 
 
 def centred(values):
@@ -418,7 +457,7 @@
             lax.fori_loop(0, PAIR * steps, rows_at, 0)
 
 
-def forecasts(own_blocks, blocks, transform, courant, piece):
+def forecasts(own_blocks, blocks, transform, courant, piece, after):
     held, layers, local, size = own_blocks.shape
     count = held // PAIR
     total = transform.shape[2]
@@ -429,7 +468,8 @@
         shapes = [(held, layers * half, size)]
 
     def kernel(*refs):
-        forecast_kernel(*refs, layers=layers, spread=piece == 1)
+        kept = refs[: layers + 2] + refs[layers + 2 + len(after) :]
+        forecast_kernel(*kept, layers=layers, spread=piece == 1)
 
     return pl.pallas_call(
         kernel,
@@ -441,6 +481,7 @@
                 (1, layers * PAIR, 1, half, total), lambda a: (a, 0, piece, 0, 0)
             ),
             pl.BlockSpec(courant.shape, lambda a: (0, 0)),
+            *[ANY] * len(after),
         ],
         out_specs=[pl.BlockSpec(shape, lambda a: (0, 0, 0)) for shape in shapes],
         out_shape=[jax.ShapeDtypeStruct(shape, BF16) for shape in shapes],
@@ -450,7 +491,7 @@
             flops=count * total * total * size, bytes_accessed=4 * total * size * count, transcendentals=0
         ),
         name="forecast",
-    )(own_blocks, *blocks, transform, courant)
+    )(own_blocks, *blocks, transform, courant, *after)
 
 
 def analysis_kernel(state, transform, out):
@@ -531,9 +572,12 @@
             axis_index_groups=layer_groups,
         )
 
-    def across(blocks):
+    def across(blocks, before=None):
         received = list(blocks)
+        blocks = list(blocks)
         for layer in far_first:
+            if before is not None and layer >= layers // 2:
+                blocks[layer] = gate(blocks[layer], [before[layer]])
             pairs = [
                 (s * owners + m, s * owners + (m ^ (layer * PAIR)))
                 for s in range(lines)
@@ -545,25 +589,25 @@
     def layered(blocks, rows):
         return [blocks[:, layer * rows : (layer + 1) * rows] for layer in range(layers)]
 
-    first = pack_obs(hx_values, layers, 0, ())
-    first = across([block.reshape(held, half, own) for block in first])
-    (second,) = pack_obs(hx_values, layers, 1, (obs_value, obs_var))
+    *firsts, second = pack_obs(hx_values, obs_value, obs_var, layers)
+    firsts = across([block.reshape(held, half, own) for block in firsts])
     second = within(second.reshape(held, -1, own))
-    seconds = [second] + across(layered(second, half))[1:]
-    state = pack_state(member_state, layers, width)
+    seconds = across(layered(second, half), firsts)
+    state = pack_state(member_state, layers, width, ())
     size = state.shape[5]
-    state = within(state.reshape(held, layers * local, size))
-    states = across(layered(state, local))
-    first = within(jnp.concatenate(first, axis=1))
-    observed = [first, *seconds]
+    state = gate(state.reshape(held, layers * local, size), [second, firsts[1]])
+    state = within(state)
+    states = across(layered(state, local), seconds)
+    first = within(join(firsts, [state]))
+    observed = [first, second, *seconds[1:]]
     if shared:
         observed = [widened(array, count) for array in observed]
-    transform = transforms(observed[0], observed[1:], count)
+    transform = transforms(observed[0], observed[1:], count, states[1:2])
 
     if not shared and width == 2 and cells_a // width >= STEPS:
         state = state.reshape(held, layers, local, size)
-        back = forecasts(state, states[1:], transform, courant, 0)
-        (last,) = forecasts(state, states[1:], transform, courant, 1)
+        back = forecasts(state, states[1:], transform, courant, 0, ())
+        (last,) = forecasts(state, states[1:], transform, courant, 1, back[:1])
     else:
         column = lax.axis_index("sub") % count
         line = (lax.axis_index("mem") * width + column % width) * cells_b
@@ -576,9 +620,10 @@
         fields = fields.transpose(3, 0, 2, 1, 4, 5).reshape(2, held, layers, half, size)
         back = [fields[0, :, layer] for layer in range(layers)]
         last = fields[1].reshape(held, layers * half, size)
-    back = within(jnp.concatenate(across(back), axis=1))
+    back = across(back)
     last = within(last)
-    lasts = across(layered(last, half))
+    lasts = across(layered(last, half), back)
+    back = within(join(back, [last]))
 
     def spec(layer):
         return pl.BlockSpec((width * PAIR, half, size), lambda s: (s, layer, 0))

time: 214 us -> 220 us (1.028); the launches traced: 213 us -> 216 us
  local copies, waits for them, and re-layouts: 6.73 us -> 12.8 us
  other arithmetic: 3.98 us -> 0 us
  Pallas kernels: 51.8 us -> 54 us
    unnamed x22 -> x56, local copies, waits for them, and re-layouts: 4.06 us -> 9.9 us
    pallas_call x3 -> x12, Pallas kernels: 11.3 us -> 15.6 us  [the longest x2 6.46 us: unpack_state(): pl.pallas_call(kernel, grid=(slabs,), in_specs=specs + [ANY] * len(kept),...]
    concatenate x2 -> x0, other arithmetic: 3.98 us -> none  [the longest x1 1.99 us: advance(): first = within(jnp.concatenate(first, axis=1))]
    pallas_call x2 -> x1, Pallas kernels: 5.2 us -> 3.15 us  [pack_obs(): pl.pallas_call(kernel, grid=(slabs,), in_specs=[pl.BlockSpec((1, local, 1...]
  transfers between devices with their start and end apart: 20 -> 20, of which waited for: 9 -> 13; matrix products, arithmetic and copies ran while one was open for 3% -> 1% of each run, Pallas kernels for 18% -> 13%
where the time goes in v6:
time: 220 us; the launch traced here: 216 us
  waiting for transfers between devices  92.5 us (42%)
  starting transfers between devices  56.6 us (26%)
  Pallas kernels  54 us (25%)
  local copies, waits for them, and re-layouts  12.8 us (6%)
    ppermute x15, waiting for transfers between devices, across(): received[layer] = lax.ppermute(blocks[layer], ('sub', 'mem'), pairs)  72 us
    ppermute x15, starting transfers between devices, across(): received[layer] = lax.ppermute(blocks[layer], ('sub', 'mem'), pairs)  35.8 us
    pallas_call x1, Pallas kernels, transforms(): pl.pallas_call(kernel, grid=(count,), in_specs=[pl.BlockSpec(array.shape,...  21 us
    all_to_all x5, starting transfers between devices, within(): lax.all_to_all(blocks, ('sub', 'mem'), split_axis=0, concat_axis=0, tiled...  20.8 us
    all_to_all x5, waiting for transfers between devices, within(): lax.all_to_all(blocks, ('sub', 'mem'), split_axis=0, concat_axis=0, tiled...  20.6 us
    pallas_call x2, Pallas kernels, forecasts(): pl.pallas_call(kernel, grid=(count,), in_specs=[pl.BlockSpec((PAIR, 1, lo...  14.3 us
    unnamed x56, local copies, waits for them, and re-layouts  9.9 us
    pallas_call x2, Pallas kernels, unpack_state(): pl.pallas_call(kernel, grid=(slabs,), in_specs=specs + [ANY] * len(kept),...  6.46 us
  transfers between devices with their start and end apart: 20, of which 13 were waited for; matrix products, arithmetic and copies ran while one was open for 1% of the time, Pallas kernels for 13%

profile of v6, /device:TPU:0, one launch (start us, length us, event | category | flops | bytes accessed | tf_op | source)
XLA Modules:
  0.0 216.0 jit_solution(5054319578056600353)
XLA Ops:
  0.0 3.1 %pack_obs.1 = (bf16[2,4,32,512]{3,2,1,0:T(8,128)(2,1)}, bf16[2,4,32,512]{3,2,1,0:T(8,128)(2,1)}, bf16[2,4,32,512]{3,2,1,0:T(8,128)(2,1)}, bf16[2,4,32,512]{3,2,1,0:T(8,128)(2,1)}, bf16[2,4,144,512]{3,2,1,0:T(8,128)(2,1)}) custom-call(bf16[2,64,1,16,512]{4,3,2,1,0:T(8,128)(2,1)} %refs_0_.3, bf16[2,1,2,512]{3,2,1,0:T(2,128)(2,1)} %refs_1_.1, ...), custom_call_target="tpu_custom_call" | custom-call | tf_op jit(solution)/shard_map/pack_obs/pallas_call | solution.py:95
  3.2 5.3 %all-to-all-start = ((bf16[8,144,512]{2,1,0:T(8,128)(2,1)}), bf16[8,144,512]{2,1,0:T(8,128)(2,1)S(1)}, u32[]{:S(2)}, u32[]{:S(2)}) async-start(bf16[8,144,512]{2,1,0:T(8,128)(2,1)} %bitcast.13), calls=%async_computation | async-start | bytes 2359296 | tf_op jit(solution)/shard_map/all_to_all | solution.py:566
  8.5 1.6 collective-permute-start
  10.1 4.8 %pack_state.1 = bf16[2,2,2,4,64,512]{5,4,3,2,1,0:T(8,128)(2,1)} custom-call(bf16[2,64,8,1024]{3,2,1,0:T(8,128)(2,1)} %refs_0_.2), custom_call_target="tpu_custom_call" | custom-call | tf_op jit(solution)/shard_map/pack_state/pallas_call | solution.py:164
  14.9 2.2 %collective-permute-done.refs_2_.refs_1_ = bf16[8,32,512]{2,1,0:T(8,128)(2,1)S(1)} collective-permute-done((bf16[8,32,512]{2,1,0:T(8,128)(2,1)S(1)}, bf16[8,32,512]{2,1,0:T(8,128)(2,1)S(1)}, u32[]{:S(2)}, u32[]{:S(2)}) %collective-permute-start) | collective-permute-done | bytes 262176 | tf_op jit(solution)/shard_map/ppermute | solution.py:586
  17.2 8.1 %all-to-all-done.refs_1_ = bf16[8,144,512]{2,1,0:T(8,128)(2,1)S(1)} async-done(((bf16[8,144,512]{2,1,0:T(8,128)(2,1)}), bf16[8,144,512]{2,1,0:T(8,128)(2,1)S(1)}, u32[]{:S(2)}, u32[]{:S(2)}) %all-to-all-start) | async-done | bytes 1179680 | tf_op jit(solution)/shard_map/all_to_all | solution.py:566
  25.3 1.0 copy-done.5
  26.3 3.7 %all-to-all-start.1 = ((bf16[8,256,512]{2,1,0:T(8,128)(2,1)}), bf16[8,256,512]{2,1,0:T(8,128)(2,1)S(1)}, u32[]{:S(2)}, u32[]{:S(2)}) async-start(bf16[8,256,512]{2,1,0:T(8,128)(2,1)} %gate.7), calls=%async_computation.1 | async-start | bytes 4194304 | tf_op jit(solution)/shard_map/all_to_all | solution.py:566
  30.1 2.7 %collective-permute-start.2 = (bf16[8,32,512]{2,1,0:T(8,128)(2,1)S(1)}, bf16[8,32,512]{2,1,0:T(8,128)(2,1)S(1)}, u32[]{:S(2)}, u32[]{:S(2)}) collective-permute-start(bf16[8,32,512]{2,1,0:T(8,128)(2,1)S(1)} %bitcast.16), channel_id=1, source_target_pairs={{0,4},{1,5},{2,6},{3,7},{4,0},{5,1},{6,2},{7,3},{8,12},{9,13},{10,... | collective-permute-start | bytes 786440 | tf_op jit(solution)/shard_map/ppermute | solution.py:586
  32.7 1.3 collective-permute-start.5
  34.1 17.3 %collective-permute-done.2.refs_1_.refs_2_ = bf16[8,32,512]{2,1,0:T(8,128)(2,1)S(1)} collective-permute-done((bf16[8,32,512]{2,1,0:T(8,128)(2,1)S(1)}, bf16[8,32,512]{2,1,0:T(8,128)(2,1)S(1)}, u32[]{:S(2)}, u32[]{:S(2)}) %collective-permute-start.2) | collective-permute-done | bytes 262176 | tf_op jit(solution)/shard_map/ppermute | solution.py:586
  51.4 0.0 collective-permute-done.5.refs_1_.refs_3_
  51.4 5.2 %all-to-all-done.1.refs_4_ = bf16[8,256,512]{2,1,0:T(8,128)(2,1)S(1)} async-done(((bf16[8,256,512]{2,1,0:T(8,128)(2,1)}), bf16[8,256,512]{2,1,0:T(8,128)(2,1)S(1)}, u32[]{:S(2)}, u32[]{:S(2)}) %all-to-all-start.1) | async-done | bytes 2097184 | tf_op jit(solution)/shard_map/all_to_all | solution.py:566
  56.6 1.3 copy-done
  57.9 2.1 join.2
  60.1 3.7 %all-to-all-start.2 = ((bf16[8,128,512]{2,1,0:T(8,128)(2,1)}), bf16[8,128,512]{2,1,0:T(8,128)(2,1)S(1)}, u32[]{:S(2)}, u32[]{:S(2)}) async-start(bf16[8,128,512]{2,1,0:T(8,128)(2,1)} %join.2), calls=%async_computation.2 | async-start | bytes 2097152 | tf_op jit(solution)/shard_map/all_to_all | solution.py:566
  63.8 1.2 fusion
  65.0 1.6 collective-permute-start.1
  66.6 0.8 fusion.1
  67.4 2.6 %collective-permute-start.3 = (bf16[8,32,512]{2,1,0:T(8,128)(2,1)}, bf16[8,32,512]{2,1,0:T(8,128)(2,1)S(1)}, u32[]{:S(2)}, u32[]{:S(2)}) collective-permute-start(bf16[8,32,512]{2,1,0:T(8,128)(2,1)} %gate.8), channel_id=1, source_target_pairs={{0,4},{1,5},{2,6},{3,7},{4,0},{5,1},{6,2},{7,3},{8,12},{9,13},{10,... | collective-permute-start | bytes 786440 | tf_op jit(solution)/shard_map/ppermute | solution.py:586
  70.0 0.2 collective-permute-start.6
  70.2 0.7 collective-permute-start.8
  70.9 13.7 %collective-permute-done.3.refs_1_.refs_3_ = bf16[8,32,512]{2,1,0:T(8,128)(2,1)S(1)} collective-permute-done((bf16[8,32,512]{2,1,0:T(8,128)(2,1)}, bf16[8,32,512]{2,1,0:T(8,128)(2,1)S(1)}, u32[]{:S(2)}, u32[]{:S(2)}) %collective-permute-start.3) | collective-permute-done | bytes 262176 | tf_op jit(solution)/shard_map/ppermute | solution.py:586
  84.6 0.7 copy-done.16
  85.3 3.3 %collective-permute-start.4 = (bf16[8,64,512]{2,1,0:T(8,128)(2,1)}, bf16[8,64,512]{2,1,0:T(8,128)(2,1)S(1)}, u32[]{:S(2)}, u32[]{:S(2)}) collective-permute-start(bf16[8,64,512]{2,1,0:T(8,128)(2,1)} %gate.9), channel_id=1, source_target_pairs={{0,4},{1,5},{2,6},{3,7},{4,0},{5,1},{6,2},{7,3},{8,12},{9,13},{10,... | collective-permute-start | bytes 1572872 | tf_op jit(solution)/shard_map/ppermute | solution.py:586
  88.6 4.6 %collective-permute-done.6.refs_1_.refs_4_ = bf16[8,32,512]{2,1,0:T(8,128)(2,1)S(1)} collective-permute-done((bf16[8,32,512]{2,1,0:T(8,128)(2,1)}, bf16[8,32,512]{2,1,0:T(8,128)(2,1)S(1)}, u32[]{:S(2)}, u32[]{:S(2)}) %collective-permute-start.6) | collective-permute-done | bytes 262176 | tf_op jit(solution)/shard_map/ppermute | solution.py:586
  93.2 0.7 copy-done.17
  93.9 1.2 collective-permute-start.7
  95.1 5.8 %collective-permute-done.8.refs_2_ = bf16[8,32,512]{2,1,0:T(8,128)(2,1)} collective-permute-done((bf16[8,32,512]{2,1,0:T(8,128)(2,1)S(1)}, bf16[8,32,512]{2,1,0:T(8,128)(2,1)}, u32[]{:S(2)}, u32[]{:S(2)}) %collective-permute-start.8) | collective-permute-done | bytes 262176 | tf_op jit(solution)/shard_map/ppermute | solution.py:586
  101.0 0.0 collective-permute-done.1.refs_5_.refs_1_
  101.0 0.0 all-to-all-done.2.refs_0_
  101.0 0.8 copy-done.7
  101.8 1.0 copy-done.15
  102.7 21.0 %transform.1 = bf16[4,512,512]{2,1,0:T(8,128)(2,1)} custom-call(bf16[8,128,512]{2,1,0:T(8,128)(2,1)} %copy-done.15, bf16[8,144,512]{2,1,0:T(8,128)(2,1)} %copy-done.5, bf16[8,32,512]{2,1,0:T(8,128)(2,1)} %collective-permute-done.8.refs_2_, bf16[8,32,512]{2,1,0:T(8,128)(2,1)} %copy-done.16, bf16[8,32,512]{2,1,0:T(8,128)(2,1)} %copy-done.17, ...), custom_call_target="tpu_custom_call" | custom-call | flops 11811160064 | bytes 8388608 | tf_op jit(solution)/shard_map/transform/pallas_call | solution.py:353
  123.7 4.5 %collective-permute-done.4.refs_2_ = bf16[8,64,512]{2,1,0:T(8,128)(2,1)S(1)} collective-permute-done((bf16[8,64,512]{2,1,0:T(8,128)(2,1)}, bf16[8,64,512]{2,1,0:T(8,128)(2,1)S(1)}, u32[]{:S(2)}, u32[]{:S(2)}) %collective-permute-start.4) | collective-permute-done | bytes 524320 | tf_op jit(solution)/shard_map/ppermute | solution.py:586
  128.2 0.0 collective-permute-done.7.refs_3_
  128.2 0.8 copy-done.8
  129.0 0.2 copy-done.9
  129.2 7.2 %forecast.2 = (bf16[8,32,512]{2,1,0:T(8,128)(2,1)}, bf16[8,32,512]{2,1,0:T(8,128)(2,1)}, bf16[8,32,512]{2,1,0:T(8,128)(2,1)}, bf16[8,32,512]{2,1,0:T(8,128)(2,1)}) custom-call(bf16[8,4,64,512]{3,2,1,0:T(8,128)(2,1)} %bitcast.8, bf16[8,64,512]{2,1,0:T(8,128)(2,1)} %copy-done.7, bf16[8,64,512]{2,1,0:T(8,128)(2,1)} %copy-done.8, bf16[8,64,512]{2,1,0:T(8,128)(2,1)} %copy-done.9, ...), custom_call_target="tpu_custom_call" | custom-call | flops 536870912 | bytes 4194304 | tf_op jit(solution)/shard_map/forecast/pallas_call | solution.py:474
  136.3 7.2 %forecast.3 = bf16[8,128,512]{2,1,0:T(8,128)(2,1)} custom-call(bf16[8,4,64,512]{3,2,1,0:T(8,128)(2,1)} %bitcast.9, bf16[8,64,512]{2,1,0:T(8,128)(2,1)} %copy-done.7, bf16[8,64,512]{2,1,0:T(8,128)(2,1)} %copy-done.8, bf16[8,64,512]{2,1,0:T(8,128)(2,1)} %copy-done.9, bf16[4,8,2,32,512]{4,3,2,1,0:T(8,128)(2,1)} %bitcast.12, f32[2,1024]{1,0:T(2,128)} %refs_5_.3, ...), custom_call_target="tpu_custom_call" | custom-call | flops 536870912 | bytes 4194304 | tf_op jit(solution)/shard_map/forecast/pallas_call | solution.py:474
  143.5 4.1 %all-to-all-start.3 = ((bf16[8,128,512]{2,1,0:T(8,128)(2,1)}), bf16[8,128,512]{2,1,0:T(8,128)(2,1)S(1)}, u32[]{:S(2)}, u32[]{:S(2)}) async-start(bf16[8,128,512]{2,1,0:T(8,128)(2,1)} %forecast.3), calls=%async_computation.3 | async-start | bytes 2097152 | tf_op jit(solution)/shard_map/all_to_all | solution.py:566
  147.6 12.2 %collective-permute-start.10 = (bf16[8,32,512]{2,1,0:T(8,128)(2,1)S(1)}, bf16[8,32,512]{2,1,0:T(8,128)(2,1)S(1)}, u32[]{:S(2)}, u32[]{:S(2)}) collective-permute-start(bf16[8,32,512]{2,1,0:T(8,128)(2,1)S(1)} %copy-done.26), channel_id=1, source_target_pairs={{0,4},{1,5},{2,6},{3,7},{4,0},{5,1},{6,2},{7,3},{8,12},{9,13},{10,... | collective-permute-start | bytes 786440 | tf_op jit(solution)/shard_map/ppermute | solution.py:586
  159.8 1.0 collective-permute-start.12
  160.8 0.0 collective-permute-start.14
  160.8 17.4 %collective-permute-done.10.refs_1_.refs_2_ = bf16[8,32,512]{2,1,0:T(8,128)(2,1)S(1)} collective-permute-done((bf16[8,32,512]{2,1,0:T(8,128)(2,1)S(1)}, bf16[8,32,512]{2,1,0:T(8,128)(2,1)S(1)}, u32[]{:S(2)}, u32[]{:S(2)}) %collective-permute-start.10) | collective-permute-done | bytes 262176 | tf_op jit(solution)/shard_map/ppermute | solution.py:586
  178.3 0.0 collective-permute-done.12.refs_1_.refs_3_
  178.3 1.1 collective-permute-done.14.refs_1_
  179.3 0.0 all-to-all-done.3.refs_4_.refs_0_
  179.4 0.7 copy-done.21
  180.0 1.0 copy-done.3
  181.0 2.1 join.3
  183.2 4.0 %all-to-all-start.4 = ((bf16[8,128,512]{2,1,0:T(8,128)(2,1)}), bf16[8,128,512]{2,1,0:T(8,128)(2,1)S(1)}, u32[]{:S(2)}, u32[]{:S(2)}) async-start(bf16[8,128,512]{2,1,0:T(8,128)(2,1)} %join.3), calls=%async_computation.4 | async-start | bytes 2097152 | tf_op jit(solution)/shard_map/all_to_all | solution.py:566
  187.1 0.9 fusion.2
  188.0 4.5 %collective-permute-start.11 = (bf16[8,32,512]{2,1,0:T(8,128)(2,1)}, bf16[8,32,512]{2,1,0:T(8,128)(2,1)S(1)}, u32[]{:S(2)}, u32[]{:S(2)}) collective-permute-start(bf16[8,32,512]{2,1,0:T(8,128)(2,1)} %gate.12), channel_id=1, source_target_pairs={{0,4},{1,5},{2,6},{3,7},{4,0},{5,1},{6,2},{7,3},{8,12},{9,13},{10,... | collective-permute-start | bytes 786440 | tf_op jit(solution)/shard_map/ppermute | solution.py:586
  192.5 2.8 %collective-permute-start.13 = (bf16[8,32,512]{2,1,0:T(8,128)(2,1)}, bf16[8,32,512]{2,1,0:T(8,128)(2,1)S(1)}, u32[]{:S(2)}, u32[]{:S(2)}) collective-permute-start(bf16[8,32,512]{2,1,0:T(8,128)(2,1)} %gate.13), channel_id=1, source_target_pairs={{0,6},{1,7},{2,4},{3,5},{4,2},{5,3},{6,0},{7,1},{8,14},{9,15},{10,... | collective-permute-start | bytes 786440 | tf_op jit(solution)/shard_map/ppermute | solution.py:586
  195.3 0.0 collective-permute-start.9
  195.3 7.2 %all-to-all-done.4.refs_0_.refs_1_.refs_2_.refs_3_ = bf16[8,128,512]{2,1,0:T(8,128)(2,1)S(1)} async-done(((bf16[8,128,512]{2,1,0:T(8,128)(2,1)}), bf16[8,128,512]{2,1,0:T(8,128)(2,1)S(1)}, u32[]{:S(2)}, u32[]{:S(2)}) %all-to-all-start.4) | async-done | bytes 1048608 | tf_op jit(solution)/shard_map/all_to_all | solution.py:566
  202.5 1.0 copy-done.2
  203.5 3.2 %unpack_state.2.refs_4_ = bf16[2,64,8,1024]{3,2,1,0:T(8,128)(2,1)} custom-call(bf16[8,128,512]{2,1,0:T(8,128)(2,1)} %copy-done.2, bf16[8,128,512]{2,1,0:T(8,128)(2,1)} %copy-done.2, bf16[8,128,512]{2,1,0:T(8,128)(2,1)} %copy-done.2, bf16[8,128,512]{2,1,0:T(8,128)(2,1)} %copy-done.2), custom_call_target="tpu_custom_call" | custom-call | tf_op jit(solution)/shard_map/unpack_state/pallas_call | solution.py:231
  206.8 4.4 %collective-permute-done.11.refs_2_ = bf16[8,32,512]{2,1,0:T(8,128)(2,1)S(1)} collective-permute-done((bf16[8,32,512]{2,1,0:T(8,128)(2,1)}, bf16[8,32,512]{2,1,0:T(8,128)(2,1)S(1)}, u32[]{:S(2)}, u32[]{:S(2)}) %collective-permute-start.11) | collective-permute-done | bytes 262176 | tf_op jit(solution)/shard_map/ppermute | solution.py:586
  211.1 0.0 collective-permute-done.13.refs_3_
  211.1 0.9 collective-permute-done.9.refs_1_
  212.1 0.7 copy-done.20
  212.7 3.2 %unpack_state.3 = bf16[2,64,8,1024]{3,2,1,0:T(8,128)(2,1)} custom-call(bf16[8,128,512]{2,1,0:T(8,128)(2,1)} %copy-done.3, bf16[8,32,512]{2,1,0:T(8,128)(2,1)} %copy-done.20, bf16[8,32,512]{2,1,0:T(8,128)(2,1)} %copy-done.18, bf16[8,32,512]{2,1,0:T(8,128)(2,1)} %copy-done.19, bf16[2,64,8,1024]{3,2,1,0:T(8,128)(2,1)} %unpack_state.2.refs_4_), custom_call_target="tpu_custom_call", output_to_operand_aliasing={{}: (4, {})} | custom-call | tf_op jit(solution)/shard_map/unpack_state/pallas_call | solution.py:231
  (51 shorter events, 0.1 us)
Async XLA Ops:
  3.1 5.3 %copy-start.27 = (bf16[2,4,32,512]{3,2,1,0:T(8,128)(2,1)S(1)}, bf16[2,4,32,512]{3,2,1,0:T(8,128)(2,1)}, u32[]{:S(2)}) copy-start(bf16[2,4,32,512]{3,2,1,0:T(8,128)(2,1)} %get-tuple-element.15) | copy-start | bytes 786436
  3.2 22.1 %all-to-all-start = ((bf16[8,144,512]{2,1,0:T(8,128)(2,1)}), bf16[8,144,512]{2,1,0:T(8,128)(2,1)S(1)}, u32[]{:S(2)}, u32[]{:S(2)}) async-start(bf16[8,144,512]{2,1,0:T(8,128)(2,1)} %bitcast.13), calls=%async_computation | async-start | bytes 2359296 | tf_op jit(solution)/shard_map/all_to_all | solution.py:566
  8.5 8.7 %collective-permute-start = (bf16[8,32,512]{2,1,0:T(8,128)(2,1)S(1)}, bf16[8,32,512]{2,1,0:T(8,128)(2,1)S(1)}, u32[]{:S(2)}, u32[]{:S(2)}) collective-permute-start(bf16[8,32,512]{2,1,0:T(8,128)(2,1)S(1)} %bitcast.17), channel_id=1, source_target_pairs={{0,2},{1,3},{2,0},{3,1},{4,6},{5,7},{6,4},{7,5},{8,10},{9,11},{10,... | collective-permute-start | bytes 786440 | tf_op jit(solution)/shard_map/ppermute | solution.py:586
  17.2 8.1 %copy-start.12 = (bf16[8,32,512]{2,1,0:T(8,128)(2,1)}, bf16[8,32,512]{2,1,0:T(8,128)(2,1)S(1)}, u32[]{:S(2)}) copy-start(bf16[8,32,512]{2,1,0:T(8,128)(2,1)S(1)} %collective-permute-done.refs_2_.refs_1_) | copy-start | bytes 786436
  25.3 1.0 copy-start.5
  26.3 3.8 %copy-start.23 = (bf16[2,4,32,512]{3,2,1,0:T(8,128)(2,1)S(1)}, bf16[2,4,32,512]{3,2,1,0:T(8,128)(2,1)}, u32[]{:S(2)}) copy-start(bf16[2,4,32,512]{3,2,1,0:T(8,128)(2,1)} %get-tuple-element.16) | copy-start | bytes 786436
  26.3 6.4 %copy-start.22 = (bf16[2,4,32,512]{3,2,1,0:T(8,128)(2,1)S(1)}, bf16[2,4,32,512]{3,2,1,0:T(8,128)(2,1)}, u32[]{:S(2)}) copy-start(bf16[2,4,32,512]{3,2,1,0:T(8,128)(2,1)} %get-tuple-element.17) | copy-start | bytes 786436
  26.3 30.3 %all-to-all-start.1 = ((bf16[8,256,512]{2,1,0:T(8,128)(2,1)}), bf16[8,256,512]{2,1,0:T(8,128)(2,1)S(1)}, u32[]{:S(2)}, u32[]{:S(2)}) async-start(bf16[8,256,512]{2,1,0:T(8,128)(2,1)} %gate.7), calls=%async_computation.1 | async-start | bytes 4194304 | tf_op jit(solution)/shard_map/all_to_all | solution.py:566
  30.1 21.3 %collective-permute-start.2 = (bf16[8,32,512]{2,1,0:T(8,128)(2,1)S(1)}, bf16[8,32,512]{2,1,0:T(8,128)(2,1)S(1)}, u32[]{:S(2)}, u32[]{:S(2)}) collective-permute-start(bf16[8,32,512]{2,1,0:T(8,128)(2,1)S(1)} %bitcast.16), channel_id=1, source_target_pairs={{0,4},{1,5},{2,6},{3,7},{4,0},{5,1},{6,2},{7,3},{8,12},{9,13},{10,... | collective-permute-start | bytes 786440 | tf_op jit(solution)/shard_map/ppermute | solution.py:586
  32.7 18.7 %collective-permute-start.5 = (bf16[8,32,512]{2,1,0:T(8,128)(2,1)S(1)}, bf16[8,32,512]{2,1,0:T(8,128)(2,1)S(1)}, u32[]{:S(2)}, u32[]{:S(2)}) collective-permute-start(bf16[8,32,512]{2,1,0:T(8,128)(2,1)S(1)} %bitcast.15), channel_id=1, source_target_pairs={{0,6},{1,7},{2,4},{3,5},{4,2},{5,3},{6,0},{7,1},{8,14},{9,15},{10,... | collective-permute-start | bytes 786440 | tf_op jit(solution)/shard_map/ppermute | solution.py:586
  51.4 5.2 %copy-start.13 = (bf16[8,32,512]{2,1,0:T(8,128)(2,1)}, bf16[8,32,512]{2,1,0:T(8,128)(2,1)S(1)}, u32[]{:S(2)}) copy-start(bf16[8,32,512]{2,1,0:T(8,128)(2,1)S(1)} %collective-permute-done.2.refs_1_.refs_2_) | copy-start | bytes 786436
  51.4 5.2 %copy-start.10 = (bf16[8,32,512]{2,1,0:T(8,128)(2,1)}, bf16[8,32,512]{2,1,0:T(8,128)(2,1)S(1)}, u32[]{:S(2)}) copy-start(bf16[8,32,512]{2,1,0:T(8,128)(2,1)S(1)} %collective-permute-done.5.refs_1_.refs_3_) | copy-start | bytes 786436
  56.6 1.3 copy-start
  60.1 3.7 %copy-start.1 = (bf16[8,256,512]{2,1,0:T(8,128)(2,1)S(1)}, bf16[8,256,512]{2,1,0:T(8,128)(2,1)}, u32[]{:S(2)}) copy-start(bf16[8,256,512]{2,1,0:T(8,128)(2,1)} %copy-done) | copy-start | bytes 6291460
  60.1 40.9 %all-to-all-start.2 = ((bf16[8,128,512]{2,1,0:T(8,128)(2,1)}), bf16[8,128,512]{2,1,0:T(8,128)(2,1)S(1)}, u32[]{:S(2)}, u32[]{:S(2)}) async-start(bf16[8,128,512]{2,1,0:T(8,128)(2,1)} %join.2), calls=%async_computation.2 | async-start | bytes 2097152 | tf_op jit(solution)/shard_map/all_to_all | solution.py:566
  63.8 2.8 %copy-start.6 = (bf16[8,144,512]{2,1,0:T(8,128)(2,1)S(1)}, bf16[8,144,512]{2,1,0:T(8,128)(2,1)}, u32[]{:S(2)}) copy-start(bf16[8,144,512]{2,1,0:T(8,128)(2,1)} %copy-done.5) | copy-start | bytes 3538948
  65.0 36.0 %collective-permute-start.1 = (bf16[8,64,512]{2,1,0:T(8,128)(2,1)S(1)}, bf16[8,64,512]{2,1,0:T(8,128)(2,1)S(1)}, u32[]{:S(2)}, u32[]{:S(2)}) collective-permute-start(bf16[8,64,512]{2,1,0:T(8,128)(2,1)S(1)} %get-tuple-element.25), channel_id=1, source_target_pairs={{0,2},{1,3},{2,0},{3,1},{4,6},{5,7},{6,4},{7,5},{8,10},{9,11},{10,... | collective-permute-start | bytes 1572872 | tf_op jit(solution)/shard_map/ppermute | solution.py:586
  67.4 17.2 %collective-permute-start.3 = (bf16[8,32,512]{2,1,0:T(8,128)(2,1)}, bf16[8,32,512]{2,1,0:T(8,128)(2,1)S(1)}, u32[]{:S(2)}, u32[]{:S(2)}) collective-permute-start(bf16[8,32,512]{2,1,0:T(8,128)(2,1)} %gate.8), channel_id=1, source_target_pairs={{0,4},{1,5},{2,6},{3,7},{4,0},{5,1},{6,2},{7,3},{8,12},{9,13},{10,... | collective-permute-start | bytes 786440 | tf_op jit(solution)/shard_map/ppermute | solution.py:586
  70.0 23.2 %collective-permute-start.6 = (bf16[8,32,512]{2,1,0:T(8,128)(2,1)}, bf16[8,32,512]{2,1,0:T(8,128)(2,1)S(1)}, u32[]{:S(2)}, u32[]{:S(2)}) collective-permute-start(bf16[8,32,512]{2,1,0:T(8,128)(2,1)} %gate.10), channel_id=1, source_target_pairs={{0,6},{1,7},{2,4},{3,5},{4,2},{5,3},{6,0},{7,1},{8,14},{9,15},{10,... | collective-permute-start | bytes 786440 | tf_op jit(solution)/shard_map/ppermute | solution.py:586
  70.2 30.7 %collective-permute-start.8 = (bf16[8,32,512]{2,1,0:T(8,128)(2,1)S(1)}, bf16[8,32,512]{2,1,0:T(8,128)(2,1)}, u32[]{:S(2)}, u32[]{:S(2)}) collective-permute-start(bf16[8,32,512]{2,1,0:T(8,128)(2,1)S(1)} %get-tuple-element.26), channel_id=1, source_target_pairs={{0,2},{1,3},{2,0},{3,1},{4,6},{5,7},{6,4},{7,5},{8,10},{9,11},{10,... | collective-permute-start | bytes 786440 | tf_op jit(solution)/shard_map/ppermute | solution.py:586
  84.6 0.7 copy-start.16
  85.3 42.9 %collective-permute-start.4 = (bf16[8,64,512]{2,1,0:T(8,128)(2,1)}, bf16[8,64,512]{2,1,0:T(8,128)(2,1)S(1)}, u32[]{:S(2)}, u32[]{:S(2)}) collective-permute-start(bf16[8,64,512]{2,1,0:T(8,128)(2,1)} %gate.9), channel_id=1, source_target_pairs={{0,4},{1,5},{2,6},{3,7},{4,0},{5,1},{6,2},{7,3},{8,12},{9,13},{10,... | collective-permute-start | bytes 1572872 | tf_op jit(solution)/shard_map/ppermute | solution.py:586
  93.2 0.7 copy-start.17
  93.9 34.3 %collective-permute-start.7 = (bf16[8,64,512]{2,1,0:T(8,128)(2,1)}, bf16[8,64,512]{2,1,0:T(8,128)(2,1)S(1)}, u32[]{:S(2)}, u32[]{:S(2)}) collective-permute-start(bf16[8,64,512]{2,1,0:T(8,128)(2,1)} %gate.11), channel_id=1, source_target_pairs={{0,6},{1,7},{2,4},{3,5},{4,2},{5,3},{6,0},{7,1},{8,14},{9,15},{10,... | collective-permute-start | bytes 1572872 | tf_op jit(solution)/shard_map/ppermute | solution.py:586
  101.0 0.8 copy-start.7
  101.8 1.0 copy-start.15
  128.2 0.8 copy-start.8
  128.2 1.0 copy-start.9
  143.5 4.1 %copy-start.26 = (bf16[8,32,512]{2,1,0:T(8,128)(2,1)S(1)}, bf16[8,32,512]{2,1,0:T(8,128)(2,1)}, u32[]{:S(2)}) copy-start(bf16[8,32,512]{2,1,0:T(8,128)(2,1)} %get-tuple-element.20) | copy-start | bytes 786436
  143.5 16.3 %copy-start.25 = (bf16[8,32,512]{2,1,0:T(8,128)(2,1)S(1)}, bf16[8,32,512]{2,1,0:T(8,128)(2,1)}, u32[]{:S(2)}) copy-start(bf16[8,32,512]{2,1,0:T(8,128)(2,1)} %get-tuple-element.21) | copy-start | bytes 786436
  143.5 17.3 %copy-start.24 = (bf16[8,32,512]{2,1,0:T(8,128)(2,1)S(1)}, bf16[8,32,512]{2,1,0:T(8,128)(2,1)}, u32[]{:S(2)}) copy-start(bf16[8,32,512]{2,1,0:T(8,128)(2,1)} %get-tuple-element.22) | copy-start | bytes 786436
  143.5 35.8 %all-to-all-start.3 = ((bf16[8,128,512]{2,1,0:T(8,128)(2,1)}), bf16[8,128,512]{2,1,0:T(8,128)(2,1)S(1)}, u32[]{:S(2)}, u32[]{:S(2)}) async-start(bf16[8,128,512]{2,1,0:T(8,128)(2,1)} %forecast.3), calls=%async_computation.3 | async-start | bytes 2097152 | tf_op jit(solution)/shard_map/all_to_all | solution.py:566
  147.6 30.7 %collective-permute-start.10 = (bf16[8,32,512]{2,1,0:T(8,128)(2,1)S(1)}, bf16[8,32,512]{2,1,0:T(8,128)(2,1)S(1)}, u32[]{:S(2)}, u32[]{:S(2)}) collective-permute-start(bf16[8,32,512]{2,1,0:T(8,128)(2,1)S(1)} %copy-done.26), channel_id=1, source_target_pairs={{0,4},{1,5},{2,6},{3,7},{4,0},{5,1},{6,2},{7,3},{8,12},{9,13},{10,... | collective-permute-start | bytes 786440 | tf_op jit(solution)/shard_map/ppermute | solution.py:586
  159.8 18.4 %collective-permute-start.12 = (bf16[8,32,512]{2,1,0:T(8,128)(2,1)S(1)}, bf16[8,32,512]{2,1,0:T(8,128)(2,1)S(1)}, u32[]{:S(2)}, u32[]{:S(2)}) collective-permute-start(bf16[8,32,512]{2,1,0:T(8,128)(2,1)S(1)} %copy-done.25), channel_id=1, source_target_pairs={{0,6},{1,7},{2,4},{3,5},{4,2},{5,3},{6,0},{7,1},{8,14},{9,15},{10,... | collective-permute-start | bytes 786440 | tf_op jit(solution)/shard_map/ppermute | solution.py:586
  160.8 18.5 %collective-permute-start.14 = (bf16[8,32,512]{2,1,0:T(8,128)(2,1)S(1)}, bf16[8,32,512]{2,1,0:T(8,128)(2,1)S(1)}, u32[]{:S(2)}, u32[]{:S(2)}) collective-permute-start(bf16[8,32,512]{2,1,0:T(8,128)(2,1)S(1)} %copy-done.24), channel_id=1, source_target_pairs={{0,2},{1,3},{2,0},{3,1},{4,6},{5,7},{6,4},{7,5},{8,10},{9,11},{10,... | collective-permute-start | bytes 786440 | tf_op jit(solution)/shard_map/ppermute | solution.py:586
  178.3 1.1 copy-start.14
  178.3 1.1 copy-start.11
  179.3 0.7 copy-start.21
  180.0 1.0 copy-start.3
  183.2 4.0 %copy-start.4 = (bf16[8,128,512]{2,1,0:T(8,128)(2,1)S(1)}, bf16[8,128,512]{2,1,0:T(8,128)(2,1)}, u32[]{:S(2)}) copy-start(bf16[8,128,512]{2,1,0:T(8,128)(2,1)} %copy-done.3) | copy-start | bytes 3145732
  183.2 19.4 %all-to-all-start.4 = ((bf16[8,128,512]{2,1,0:T(8,128)(2,1)}), bf16[8,128,512]{2,1,0:T(8,128)(2,1)S(1)}, u32[]{:S(2)}, u32[]{:S(2)}) async-start(bf16[8,128,512]{2,1,0:T(8,128)(2,1)} %join.3), calls=%async_computation.4 | async-start | bytes 2097152 | tf_op jit(solution)/shard_map/all_to_all | solution.py:566
  188.0 23.1 %collective-permute-start.11 = (bf16[8,32,512]{2,1,0:T(8,128)(2,1)}, bf16[8,32,512]{2,1,0:T(8,128)(2,1)S(1)}, u32[]{:S(2)}, u32[]{:S(2)}) collective-permute-start(bf16[8,32,512]{2,1,0:T(8,128)(2,1)} %gate.12), channel_id=1, source_target_pairs={{0,4},{1,5},{2,6},{3,7},{4,0},{5,1},{6,2},{7,3},{8,12},{9,13},{10,... | collective-permute-start | bytes 786440 | tf_op jit(solution)/shard_map/ppermute | solution.py:586
  192.5 18.7 %collective-permute-start.13 = (bf16[8,32,512]{2,1,0:T(8,128)(2,1)}, bf16[8,32,512]{2,1,0:T(8,128)(2,1)S(1)}, u32[]{:S(2)}, u32[]{:S(2)}) collective-permute-start(bf16[8,32,512]{2,1,0:T(8,128)(2,1)} %gate.13), channel_id=1, source_target_pairs={{0,6},{1,7},{2,4},{3,5},{4,2},{5,3},{6,0},{7,1},{8,14},{9,15},{10,... | collective-permute-start | bytes 786440 | tf_op jit(solution)/shard_map/ppermute | solution.py:586
  195.3 16.7 %collective-permute-start.9 = (bf16[8,32,512]{2,1,0:T(8,128)(2,1)S(1)}, bf16[8,32,512]{2,1,0:T(8,128)(2,1)S(1)}, u32[]{:S(2)}, u32[]{:S(2)}) collective-permute-start(bf16[8,32,512]{2,1,0:T(8,128)(2,1)S(1)} %get-tuple-element.31), channel_id=1, source_target_pairs={{0,2},{1,3},{2,0},{3,1},{4,6},{5,7},{6,4},{7,5},{8,10},{9,11},{10,... | collective-permute-start | bytes 786440 | tf_op jit(solution)/shard_map/ppermute | solution.py:586
  202.5 1.0 copy-start.2
  211.1 0.9 copy-start.18
  211.1 0.9 copy-start.19
  212.0 0.7 copy-start.20

commit v7 on v3

--- a/solution.py
+++ b/solution.py
@@ -9,12 +9,13 @@
 STEPS = 4
 F32 = jnp.float32
 BF16 = jnp.bfloat16
-VMEM_LIMIT = 48 * 1024 * 1024
-
-
-def params(count):
+MIB = 1024 * 1024
+WHOLE = pl.BlockSpec(memory_space=pltpu.VMEM)
+
+
+def params(count, limit=40):
     return pltpu.CompilerParams(
-        dimension_semantics=("arbitrary",) * count, vmem_limit_bytes=VMEM_LIMIT
+        dimension_semantics=("arbitrary",) * count, vmem_limit_bytes=limit * MIB
     )
 
 
@@ -63,7 +64,7 @@
         out_specs=pl.BlockSpec((1, width, owners, block, own), lambda s, g: (s, 0, 0, g, 0)),
         out_shape=jax.ShapeDtypeStruct((slabs, width, owners, local, own), BF16),
         scratch_shapes=[pltpu.VMEM((block * patches, block * patches), BF16)],
-        compiler_params=params(2),
+        compiler_params=params(2, 60),
         name="pack_obs",
     )(hx_values)
 
@@ -130,14 +131,16 @@
             pltpu.VMEM((block * cells_a, block * cells_a), BF16),
             pltpu.VMEM((width * lanes, width * lanes), BF16),
         ],
-        compiler_params=params(2),
+        compiler_params=params(2, 60),
         name="pack_state",
     )(member_state)
 
 
 def unpack_state_kernel(packed, out, order, swap):
-    _, width, owners, block, size = packed.shape
-    cells_a = out.shape[2]
+    _, width, owners, _, size = packed.shape
+    block, cells_a = out.shape[1:3]
+    slab, group = pl.program_id(0), pl.program_id(1)
+    here = pl.ds(pl.multiple_of(group * block, block), block)
     tiles = cells_a // width
     lanes = size // tiles
 
@@ -150,7 +153,7 @@
     for owner in range(owners):
         for tile in range(tiles):
             pieces = [
-                packed[0, part, owner, :, tile * lanes : (tile + 1) * lanes]
+                packed[slab, part, owner, here, tile * lanes : (tile + 1) * lanes]
                 for part in range(width)
             ]
             parts.append(jnp.concatenate(pieces, axis=1))
@@ -175,9 +178,7 @@
     return pl.pallas_call(
         unpack_state_kernel,
         grid=(slabs, local // block),
-        in_specs=[
-            pl.BlockSpec((1, width, owners, block, size), lambda s, g: (s, 0, 0, g, 0)),
-        ],
+        in_specs=[WHOLE],
         out_specs=pl.BlockSpec((1, block, cells_a, cols), lambda s, g: (s, g, 0, 0)),
         out_shape=jax.ShapeDtypeStruct((slabs, local, cells_a, cols), BF16),
         scratch_shapes=[
@@ -189,7 +190,7 @@
     )(packed)
 
 
-def transform_kernel(before, middle, after, obs, scale, out, pert, weighted):
+def transform_kernel(before, middle, after, obs, scale, out, rest, pert, weighted):
     total = middle.shape[1]
     half = before.shape[2]
     projected = jnp.zeros((total, 1), F32)
@@ -228,7 +229,10 @@
     halfway = jnp.sum(flipped * projected, axis=0, keepdims=True)
     weight = jnp.sum(inverse * halfway, axis=1, keepdims=True)
     weight = jnp.broadcast_to(weight, (total, 128)).T[0:1, :] / bound
-    out[0] = (jnp.sqrt((total - 1.0) / bound) * flipped + weight).astype(BF16)
+    result = (jnp.sqrt((total - 1.0) / bound) * flipped + weight).astype(BF16)
+    out[0] = result
+    sums = jnp.sum(result.astype(F32), axis=1, keepdims=True)
+    rest[0] = jnp.broadcast_to(1.0 - sums, (total, 128))
 
 
 def transforms(hx_rows, obs_rows, scale_rows, count, wraps):
@@ -246,8 +250,14 @@
             pl.BlockSpec((1, 1, 2 * own), lambda a: (a, 0, 0)),
             pl.BlockSpec((1, 1, 2 * own), lambda a: (a, 0, 0)),
         ],
-        out_specs=pl.BlockSpec((1, total, total), lambda a: (a, 0, 0)),
-        out_shape=jax.ShapeDtypeStruct((count, total, total), BF16),
+        out_specs=[
+            pl.BlockSpec((1, total, total), lambda a: (a, 0, 0)),
+            pl.BlockSpec((1, total, 128), lambda a: (a, 0, 0)),
+        ],
+        out_shape=[
+            jax.ShapeDtypeStruct((count, total, total), BF16),
+            jax.ShapeDtypeStruct((count, total, 128), F32),
+        ],
         scratch_shapes=[pltpu.VMEM((total, 2 * own), BF16), pltpu.VMEM((total, 2 * own), BF16)],
         compiler_params=params(1),
         cost_estimate=pl.CostEstimate(
@@ -291,18 +301,16 @@
     return results
 
 
-def forecast_kernel(state, transform, speed, out, pert, means, fields):
-    count, block, size = out.shape
+def forecast_kernel(state, transform, rest, speed, out, fields):
+    count, total, size = out.shape
     lanes = speed.shape[1]
-
-    @pl.when(pl.program_id(0) == 0)
-    def _():
-        for a in range(count):
-            means[a], pert[a] = centred(state[a])
-
     for a in range(count):
-        values = dot_bf16(transform[a], pert[a]) + means[a]
-        fields[a] = values.astype(BF16).astype(F32)
+        mean = jnp.sum(state[a].astype(F32), axis=0, keepdims=True) * (1.0 / total)
+        values = dot_bf16(transform[a], state[a])
+        for k in range(size // lanes):
+            part = slice(k * lanes, (k + 1) * lanes)
+            analysis = values[:, part] + rest[a] * mean[:, part]
+            fields[a, :, part] = analysis.astype(BF16).astype(F32)
     chunk = 16
     taps = stencil(jnp.broadcast_to(speed[...], (8, lanes)))
     low = iota(8, lanes, 1) < lanes // 2
@@ -323,30 +331,20 @@
                 out[a, at, k * lanes : (k + 1) * lanes] = value.astype(BF16)
         return carry
 
-    lax.fori_loop(0, block // chunk, rows_at, 0)
-
-
-def forecasts(state, transform, speed):
+    lax.fori_loop(0, total // chunk, rows_at, 0)
+
+
+def forecasts(state, transform, rest, speed):
     count, total, size = state.shape
-    block = min(total, 256)
     return pl.pallas_call(
         forecast_kernel,
-        grid=(total // block,),
-        in_specs=[
-            pl.BlockSpec((count, total, size), lambda i: (0, 0, 0)),
-            pl.BlockSpec((count, block, total), lambda i: (0, i, 0)),
-            pl.BlockSpec(speed.shape, lambda i: (0, 0)),
-        ],
-        out_specs=pl.BlockSpec((count, block, size), lambda i: (0, i, 0)),
+        in_specs=[WHOLE] * 4,
+        out_specs=WHOLE,
         out_shape=jax.ShapeDtypeStruct((count, total, size), BF16),
-        scratch_shapes=[
-            pltpu.VMEM((count, total, size), BF16),
-            pltpu.VMEM((count, 1, size), F32),
-            pltpu.VMEM((count, block, size), F32),
-        ],
-        compiler_params=params(1),
+        scratch_shapes=[pltpu.VMEM((count, total, size), F32)],
+        compiler_params=pltpu.CompilerParams(vmem_limit_bytes=40 * MIB),
         name="forecast",
-    )(state, transform, speed)
+    )(state, transform, rest, speed)
 
 
 def analysis_kernel(state, transform, out):
@@ -448,13 +446,13 @@
     state = state.reshape(count, total, -1)
 
     held_rows = hx_rows if groups == 1 else widened(hx_rows, count)
-    transform = transforms(held_rows, obs_rows, scale_rows, count, groups == 1)
+    transform, rest = transforms(held_rows, obs_rows, scale_rows, count, groups == 1)
 
     column = (lax.axis_index("mem") * width + part) * cells_b
     speed = lax.dynamic_slice(courant, (slab, column), (1, cells_b))
     speed = jnp.concatenate([speed] * width, axis=1)
-    if groups == 1 and width == 2 and cells_a // width >= STEPS:
-        fields = forecasts(state, transform, speed)
+    if groups == 1 and 2 * cells_b == 128 and width == 2 and cells_a // width >= STEPS:
+        fields = forecasts(state, transform, rest, speed)
     else:
         fields = shared_transport(analyses(state, transform), speed, width, count)
     back = exchange(fields.reshape(count * owners, local, -1))

time: 180 us -> 182 us (1.011)
  Pallas kernels: 35.8 us -> 40 us
  waiting for transfers between devices: 56.5 us -> 54.1 us
    pallas_call x1, Pallas kernels: 2.08 us -> 6.5 us  [pack_obs(): pl.pallas_call(pack_obs_kernel, grid=(slabs, local // block), in_specs=[p...]
    pallas_call x1, Pallas kernels: 2.33 us -> 4.84 us  [pack_state(): pl.pallas_call(pack_state_kernel, grid=(slabs, local // block), in_specs=...]
    all_to_all x2, waiting for transfers between devices: 56.5 us -> 54.1 us  [exchange(): lax.all_to_all(blocks, ('sub', 'mem'), split_axis=0, concat_axis=0, tiled...]
    pallas_call x1, Pallas kernels: 8.02 us -> 5.79 us  [forecasts(): pl.pallas_call(forecast_kernel, in_specs=[WHOLE] * 4, out_specs=WHOLE, ou...]
    unnamed x14 -> x12, local copies, waits for them, and re-layouts: 5.55 us -> 5.84 us
  transfers between devices with their start and end apart: 2 -> 2, of which waited for: 2 -> 2; matrix products, arithmetic and copies ran while one was open for 1% -> 1% of each run, Pallas kernels for 12% -> 13%
where the time goes in v7:
time: 182 us; the launch traced here: 181 us
  blocking collectives  69.8 us (38%)
  waiting for transfers between devices  54.1 us (30%)
  Pallas kernels  40 us (22%)
  starting transfers between devices  10.1 us (6%)
  local copies, waits for them, and re-layouts  6.75 us (4%)
    all_to_all x2, waiting for transfers between devices, exchange(): lax.all_to_all(blocks, ('sub', 'mem'), split_axis=0, concat_axis=0, tiled...  54.1 us
    all_to_all x1, blocking collectives, exchange(): lax.all_to_all(blocks, ('sub', 'mem'), split_axis=0, concat_axis=0, tiled...  52 us
    pallas_call x1, Pallas kernels, transforms(): pl.pallas_call(transform_kernel, grid=(count,), in_specs=[pl.BlockSpec((1...  19.4 us
    all_gather x1, blocking collectives, advance(): stats = lax.all_gather(stats, 'sub', axis=0)  17.8 us
    all_to_all x2, starting transfers between devices, exchange(): lax.all_to_all(blocks, ('sub', 'mem'), split_axis=0, concat_axis=0, tiled...  10.1 us
    pallas_call x1, Pallas kernels, pack_obs(): pl.pallas_call(pack_obs_kernel, grid=(slabs, local // block), in_specs=[p...  6.5 us
    unnamed x12, local copies, waits for them, and re-layouts  5.84 us
    pallas_call x1, Pallas kernels, forecasts(): pl.pallas_call(forecast_kernel, in_specs=[WHOLE] * 4, out_specs=WHOLE, ou...  5.79 us
  transfers between devices with their start and end apart: 2, of which 2 were waited for; matrix products, arithmetic and copies ran while one was open for 1% of the time, Pallas kernels for 13%

profile of v7, /device:TPU:0, one launch (start us, length us, event | category | flops | bytes accessed | tf_op | source)
XLA Modules:
  0.0 181.1 jit_solution(3729467589492206893)
XLA Ops:
  0.0 6.5 %pack_obs.1 = bf16[2,2,8,64,512]{4,3,2,1,0:T(8,128)(2,1)} custom-call(bf16[2,64,1,16,512]{4,3,2,1,0:T(8,128)(2,1)} %rows.1), custom_call_target="tpu_custom_call" | custom-call | tf_op jit(solution)/shard_map/pack_obs/pallas_call | solution.py:60
  6.5 7.3 %all-to-all-start.1 = ((bf16[32,64,512]{2,1,0:T(8,128)(2,1)}), bf16[32,64,512]{2,1,0:T(8,128)(2,1)S(1)}, u32[]{:S(2)}, u32[]{:S(2)}) async-start(bf16[32,64,512]{2,1,0:T(8,128)(2,1)} %bitcast.26), calls=%async_computation.1 | async-start | bytes 4194304 | tf_op jit(solution)/shard_map/all_to_all | solution.py:417
  13.8 4.8 %pack_state.1 = bf16[2,2,8,64,512]{4,3,2,1,0:T(8,128)(2,1)} custom-call(bf16[2,64,8,1024]{3,2,1,0:T(8,128)(2,1)} %cells.1), custom_call_target="tpu_custom_call" | custom-call | tf_op jit(solution)/shard_map/pack_state/pallas_call | solution.py:122
  18.6 45.3 %all-to-all-done.1 = bf16[32,64,512]{2,1,0:T(8,128)(2,1)S(1)} async-done(((bf16[32,64,512]{2,1,0:T(8,128)(2,1)}), bf16[32,64,512]{2,1,0:T(8,128)(2,1)S(1)}, u32[]{:S(2)}, u32[]{:S(2)}) %all-to-all-start.1) | async-done | bytes 2097184 | tf_op jit(solution)/shard_map/all_to_all | solution.py:417
  63.9 0.0 copy-start
  63.9 1.3 copy-done
  65.2 0.0 copy-start.4
  65.2 0.0 copy-start.5
  65.2 2.9 %all-to-all-start = ((bf16[32,64,512]{2,1,0:T(8,128)(2,1)}), bf16[32,64,512]{2,1,0:T(8,128)(2,1)S(1)}, u32[]{:S(2)}, u32[]{:S(2)}) async-start(bf16[32,64,512]{2,1,0:T(8,128)(2,1)} %bitcast.25), calls=%async_computation | async-start | bytes 4194304 | tf_op jit(solution)/shard_map/all_to_all | solution.py:417
  68.2 0.0 copy-done.4
  68.2 0.0 copy-done.5
  68.2 17.8 %all-gather = bf16[8,2,2,512]{3,1,0,2:T(2,128)(2,1)S(1)} all-gather(bf16[2,2,2,512]{3,1,0,2:T(2,128)(2,1)S(1)} %pad_maximum_fusion.2), channel_id=2, replica_groups=mesh['sub'=4,'mem'=8] {'sub'}, dimensions={0}, use_global_device_ids=true | all-gather | bytes 40960 | tf_op jit(solution)/shard_map/all_gather | solution.py:430
  86.0 0.1 reverse.4
  86.1 0.8 dynamic_slice.7
  86.9 0.1 pad_maximum_fusion.4.speed
  87.1 0.0 copy-start.1
  87.1 1.6 copy-done.1
  88.7 19.4 %transform.1 = (bf16[4,512,512]{2,1,0:T(8,128)(2,1)S(1)}, f32[4,512,128]{2,1,0:T(8,128)S(1)}) custom-call(bf16[4,512,512]{2,1,0:T(8,128)(2,1)S(1)} %bitcast.22, bf16[4,512,512]{2,1,0:T(8,128)(2,1)S(1)} %bitcast.23, bf16[4,512,512]{2,1,0:T(8,128)(2,1)S(1)} %bitcast.24, f32[4,1,1024]{2,1,0:T(1,128)S(1)} %get-tuple-element.10.obs, ...), custom_call_target="tpu_custom_call" | custom-call | flops 11811160064 | bytes 8388608 | tf_op jit(solution)/shard_map/transform/pallas_call | solution.py:243
  108.0 0.0 copy-start.2
  108.0 1.3 copy-done.2
  109.4 8.8 %all-to-all-done = bf16[32,64,512]{2,1,0:T(8,128)(2,1)S(1)} async-done(((bf16[32,64,512]{2,1,0:T(8,128)(2,1)}), bf16[32,64,512]{2,1,0:T(8,128)(2,1)S(1)}, u32[]{:S(2)}, u32[]{:S(2)}) %all-to-all-start) | async-done | bytes 2097184 | tf_op jit(solution)/shard_map/all_to_all | solution.py:417
  118.2 0.0 copy-start.3
  118.2 1.6 copy-done.3
  119.8 5.8 %forecast.1 = bf16[4,512,512]{2,1,0:T(8,128)(2,1)S(1)} custom-call(bf16[4,512,512]{2,1,0:T(8,128)(2,1)S(1)} %bitcast.20, bf16[4,512,512]{2,1,0:T(8,128)(2,1)S(1)} %copy-done.3, f32[4,512,128]{2,1,0:T(8,128)S(1)} %get-tuple-element.8.rest, f32[1,128]{1,0:T(1,128)S(1)} %pad_maximum_fusion.4.speed), custom_call_target="tpu_custom_call" | custom-call | tf_op jit(solution)/shard_map/forecast/pallas_call | solution.py:339
  125.6 52.0 %all_to_all.15 = bf16[32,64,512]{2,1,0:T(8,128)(2,1)S(1)} all-to-all(bf16[32,64,512]{2,1,0:T(8,128)(2,1)S(1)} %bitcast.21), channel_id=1, replica_groups=mesh['sub'=4,'mem'=8] {'sub','mem'}, dimensions={0} | all-to-all | bytes 4194304 | tf_op jit(solution)/shard_map/all_to_all | solution.py:417
  177.6 3.5 %unpack_state.1 = bf16[2,64,8,1024]{3,2,1,0:T(8,128)(2,1)} custom-call(bf16[2,2,8,64,512]{4,3,2,1,0:T(8,128)(2,1)S(1)} %bitcast.19), custom_call_target="tpu_custom_call" | custom-call | tf_op jit(solution)/shard_map/unpack_state/pallas_call | solution.py:178
  (11 shorter events, 0.2 us)
Async XLA Ops:
  6.5 57.4 %all-to-all-start.1 = ((bf16[32,64,512]{2,1,0:T(8,128)(2,1)}), bf16[32,64,512]{2,1,0:T(8,128)(2,1)S(1)}, u32[]{:S(2)}, u32[]{:S(2)}) async-start(bf16[32,64,512]{2,1,0:T(8,128)(2,1)} %bitcast.26), calls=%async_computation.1 | async-start | bytes 4194304 | tf_op jit(solution)/shard_map/all_to_all | solution.py:417
  63.9 1.3 copy-start
  65.2 2.9 %copy-start.4 = (bf16[2,1,2,512]{3,2,1,0:T(2,128)(2,1)S(1)}, bf16[2,1,2,512]{3,2,1,0:T(2,128)(2,1)}, u32[]{:S(2)}) copy-start(bf16[2,1,2,512]{3,2,1,0:T(2,128)(2,1)} %param.8) | copy-start | bytes 12292
  65.2 2.9 %copy-start.5 = (bf16[2,1,2,512]{3,2,1,0:T(2,128)(2,1)S(1)}, bf16[2,1,2,512]{3,2,1,0:T(2,128)(2,1)}, u32[]{:S(2)}) copy-start(bf16[2,1,2,512]{3,2,1,0:T(2,128)(2,1)} %param.7) | copy-start | bytes 12292
  65.2 53.0 %all-to-all-start = ((bf16[32,64,512]{2,1,0:T(8,128)(2,1)}), bf16[32,64,512]{2,1,0:T(8,128)(2,1)S(1)}, u32[]{:S(2)}, u32[]{:S(2)}) async-start(bf16[32,64,512]{2,1,0:T(8,128)(2,1)} %bitcast.25), calls=%async_computation | async-start | bytes 4194304 | tf_op jit(solution)/shard_map/all_to_all | solution.py:417
  87.1 1.6 copy-start.1
  108.0 1.3 copy-start.2
  118.2 1.6 copy-start.3

commit v8 on v7

--- a/solution.py
+++ b/solution.py
@@ -40,17 +40,23 @@
 
 
 def pack_obs_kernel(rows, out, order):
-    _, width, owners, block, own = out.shape
-    size = order.shape[0]
-    patches = width * owners
-
-    @pl.when((pl.program_id(0) == 0) & (pl.program_id(1) == 0))
+    _, local, _, patches, own = rows.shape
+    owners = out.shape[2]
+    width = patches // owners
+    block = order.shape[1] // patches
+    part = pl.program_id(1)
+    lead = block * owners
+
+    @pl.when((pl.program_id(0) == 0) & (part == 0))
     def _():
-        rest, member = split(iota(size, size, 0), block)
-        part, owner = split(rest, owners)
-        order[...] = ones_at(iota(size, size, 1) == member * patches + owner * width + part)
-
-    out[...] = moved(order[...], rows[...].reshape(size, own)).reshape(out.shape)
+        rest, member = split(iota(*order.shape, 0), block)
+        side, owner = split(rest, owners)
+        order[...] = ones_at(iota(*order.shape, 1) == member * patches + owner * width + side)
+
+    turn = order[pl.ds(pl.multiple_of(part * lead, lead), lead), :]
+    for at in range(0, local, block):
+        flat = moved(turn, rows[0, at : at + block].reshape(block * patches, own))
+        out[0, 0, :, at : at + block, :] = flat.reshape(owners, block, own)
 
 
 def pack_obs(hx_values, width):
@@ -59,9 +65,9 @@
     block = 16
     return pl.pallas_call(
         pack_obs_kernel,
-        grid=(slabs, local // block),
-        in_specs=[pl.BlockSpec((1, block, 1, patches, own), lambda s, g: (s, g, 0, 0, 0))],
-        out_specs=pl.BlockSpec((1, width, owners, block, own), lambda s, g: (s, 0, 0, g, 0)),
+        grid=(slabs, width),
+        in_specs=[pl.BlockSpec((1, local, 1, patches, own), lambda s, p: (s, 0, 0, 0, 0))],
+        out_specs=pl.BlockSpec((1, 1, owners, local, own), lambda s, p: (s, p, 0, 0, 0)),
         out_shape=jax.ShapeDtypeStruct((slabs, width, owners, local, own), BF16),
         scratch_shapes=[pltpu.VMEM((block * patches, block * patches), BF16)],
         compiler_params=params(2, 60),
@@ -259,7 +265,7 @@
             jax.ShapeDtypeStruct((count, total, 128), F32),
         ],
         scratch_shapes=[pltpu.VMEM((total, 2 * own), BF16), pltpu.VMEM((total, 2 * own), BF16)],
-        compiler_params=params(1),
+        compiler_params=params(1, 60),
         cost_estimate=pl.CostEstimate(
             flops=flops, bytes_accessed=4 * count * total * total * 2, transcendentals=0
         ),
@@ -301,11 +307,17 @@
     return results
 
 
-def forecast_kernel(state, transform, rest, speed, out, fields):
+def forecast_kernel(state, transforms, rest, speed, out, transform, fields, sems):
     count, total, size = out.shape
     lanes = speed.shape[1]
+    copies = [
+        pltpu.make_async_copy(transforms.at[a], transform.at[a], sems.at[a]) for a in range(count)
+    ]
+    for copy in copies:
+        copy.start()
     for a in range(count):
         mean = jnp.sum(state[a].astype(F32), axis=0, keepdims=True) * (1.0 / total)
+        copies[a].wait()
         values = dot_bf16(transform[a], state[a])
         for k in range(size // lanes):
             part = slice(k * lanes, (k + 1) * lanes)
@@ -338,10 +350,14 @@
     count, total, size = state.shape
     return pl.pallas_call(
         forecast_kernel,
-        in_specs=[WHOLE] * 4,
+        in_specs=[WHOLE, pl.BlockSpec(memory_space=pl.ANY), WHOLE, WHOLE],
         out_specs=WHOLE,
         out_shape=jax.ShapeDtypeStruct((count, total, size), BF16),
-        scratch_shapes=[pltpu.VMEM((count, total, size), F32)],
+        scratch_shapes=[
+            pltpu.VMEM((count, total, total), BF16),
+            pltpu.VMEM((count, total, size), F32),
+            pltpu.SemaphoreType.DMA((count,)),
+        ],
         compiler_params=pltpu.CompilerParams(vmem_limit_bytes=40 * MIB),
         name="forecast",
     )(state, transform, rest, speed)

time: 182 us -> 182 us (level)
    pallas_call x1, Pallas kernels: 19.4 us -> 21.2 us  [transforms(): pl.pallas_call(transform_kernel, grid=(count,), in_specs=[pl.BlockSpec((1...]
    unnamed x12 -> x10, local copies, waits for them, and re-layouts: 5.84 us -> 4.16 us
  transfers between devices with their start and end apart: 2 -> 2, of which waited for: 2 -> 2; matrix products, arithmetic and copies ran while one was open for 1% -> 1% of each run, Pallas kernels for 13% -> 14%
where the time goes in v8:
time: 182 us; the launch traced here: 181 us
  blocking collectives  69.7 us (38%)
  waiting for transfers between devices  54.6 us (30%)
  Pallas kernels  40.8 us (22%)
  starting transfers between devices  10 us (5%)
  local copies, waits for them, and re-layouts  5.06 us (3%)
    all_to_all x2, waiting for transfers between devices, exchange(): lax.all_to_all(blocks, ('sub', 'mem'), split_axis=0, concat_axis=0, tiled...  54.6 us
    all_to_all x1, blocking collectives, exchange(): lax.all_to_all(blocks, ('sub', 'mem'), split_axis=0, concat_axis=0, tiled...  52 us
    pallas_call x1, Pallas kernels, transforms(): pl.pallas_call(transform_kernel, grid=(count,), in_specs=[pl.BlockSpec((1...  21.2 us
    all_gather x1, blocking collectives, advance(): stats = lax.all_gather(stats, 'sub', axis=0)  17.8 us
    all_to_all x2, starting transfers between devices, exchange(): lax.all_to_all(blocks, ('sub', 'mem'), split_axis=0, concat_axis=0, tiled...  10 us
    pallas_call x1, Pallas kernels, forecasts(): pl.pallas_call(forecast_kernel, in_specs=[WHOLE, pl.BlockSpec(memory_spac...  6.51 us
    pallas_call x1, Pallas kernels, pack_state(): pl.pallas_call(pack_state_kernel, grid=(slabs, local // block), in_specs=...  4.84 us
    pallas_call x1, Pallas kernels, pack_obs(): pl.pallas_call(pack_obs_kernel, grid=(slabs, width), in_specs=[pl.BlockSp...  4.66 us
  transfers between devices with their start and end apart: 2, of which 2 were waited for; matrix products, arithmetic and copies ran while one was open for 1% of the time, Pallas kernels for 14%

profile of v8, /device:TPU:0, one launch (start us, length us, event | category | flops | bytes accessed | tf_op | source)
XLA Modules:
  0.0 181.1 jit_solution(6420368317506514596)
XLA Ops:
  0.0 4.7 %pack_obs.1 = bf16[2,2,8,64,512]{4,3,2,1,0:T(8,128)(2,1)} custom-call(bf16[2,64,1,16,512]{4,3,2,1,0:T(8,128)(2,1)} %rows.1), custom_call_target="tpu_custom_call" | custom-call | tf_op jit(solution)/shard_map/pack_obs/pallas_call | solution.py:66
  4.7 7.3 %all-to-all-start.1 = ((bf16[32,64,512]{2,1,0:T(8,128)(2,1)}), bf16[32,64,512]{2,1,0:T(8,128)(2,1)S(1)}, u32[]{:S(2)}, u32[]{:S(2)}) async-start(bf16[32,64,512]{2,1,0:T(8,128)(2,1)} %bitcast.23), calls=%async_computation.1 | async-start | bytes 4194304 | tf_op jit(solution)/shard_map/all_to_all | solution.py:433
  12.0 4.8 %pack_state.1 = bf16[2,2,8,64,512]{4,3,2,1,0:T(8,128)(2,1)} custom-call(bf16[2,64,8,1024]{3,2,1,0:T(8,128)(2,1)} %cells.1), custom_call_target="tpu_custom_call" | custom-call | tf_op jit(solution)/shard_map/pack_state/pallas_call | solution.py:128
  16.8 45.3 %all-to-all-done.1 = bf16[32,64,512]{2,1,0:T(8,128)(2,1)S(1)} async-done(((bf16[32,64,512]{2,1,0:T(8,128)(2,1)}), bf16[32,64,512]{2,1,0:T(8,128)(2,1)S(1)}, u32[]{:S(2)}, u32[]{:S(2)}) %all-to-all-start.1) | async-done | bytes 2097184 | tf_op jit(solution)/shard_map/all_to_all | solution.py:433
  62.1 0.0 copy-start.2
  62.1 0.0 copy-start.3
  62.1 0.0 copy-start.4
  62.1 1.3 copy-done.2
  63.4 2.7 %all-to-all-start = ((bf16[32,64,512]{2,1,0:T(8,128)(2,1)}), bf16[32,64,512]{2,1,0:T(8,128)(2,1)S(1)}, u32[]{:S(2)}, u32[]{:S(2)}) async-start(bf16[32,64,512]{2,1,0:T(8,128)(2,1)} %bitcast.22), calls=%async_computation | async-start | bytes 4194304 | tf_op jit(solution)/shard_map/all_to_all | solution.py:433
  66.2 0.0 copy-done.3
  66.2 0.0 copy-done.4
  66.2 17.8 %all-gather = bf16[8,2,2,512]{3,1,0,2:T(2,128)(2,1)S(1)} all-gather(bf16[2,2,2,512]{3,1,0,2:T(2,128)(2,1)S(1)} %pad_maximum_fusion.2), channel_id=2, replica_groups=mesh['sub'=4,'mem'=8] {'sub'}, dimensions={0}, use_global_device_ids=true | all-gather | bytes 40960 | tf_op jit(solution)/shard_map/all_gather | solution.py:446
  84.1 0.1 reverse.4
  84.1 0.8 dynamic_slice.7
  84.9 0.1 pad_maximum_fusion.4.speed
  85.1 0.6 slice_divide_fusion
  85.7 21.2 %transform.1 = (bf16[4,512,512]{2,1,0:T(8,128)(2,1)}, f32[4,512,128]{2,1,0:T(8,128)}) custom-call(bf16[4,512,512]{2,1,0:T(8,128)(2,1)} %bitcast.24, bf16[4,512,512]{2,1,0:T(8,128)(2,1)} %bitcast.25, bf16[4,512,512]{2,1,0:T(8,128)(2,1)} %bitcast.26, f32[4,1,1024]{2,1,0:T(1,128)} %get-tuple-element.10.obs, f32[4,1,1024]{2,1,0:T(1,128)} %get-tuple-element.9.scale), custom_call_target="tpu_custom_call" | custom-call | flops 11811160064 | bytes 8388608 | tf_op jit(solution)/shard_map/transform/pallas_call | solution.py:249
  106.9 9.3 %all-to-all-done = bf16[32,64,512]{2,1,0:T(8,128)(2,1)S(1)} async-done(((bf16[32,64,512]{2,1,0:T(8,128)(2,1)}), bf16[32,64,512]{2,1,0:T(8,128)(2,1)S(1)}, u32[]{:S(2)}, u32[]{:S(2)}) %all-to-all-start) | async-done | bytes 2097184 | tf_op jit(solution)/shard_map/all_to_all | solution.py:433
  116.3 0.0 copy-start
  116.3 1.6 copy-done
  117.9 0.0 copy-start.1
  117.9 1.2 copy-done.1
  119.1 6.5 %forecast.1 = bf16[4,512,512]{2,1,0:T(8,128)(2,1)S(1)} custom-call(bf16[4,512,512]{2,1,0:T(8,128)(2,1)S(1)} %bitcast.20, bf16[4,512,512]{2,1,0:T(8,128)(2,1)S(1)} %copy-done, f32[4,512,128]{2,1,0:T(8,128)S(1)} %copy-done.1, f32[1,128]{1,0:T(1,128)S(1)} %pad_maximum_fusion.4.speed), custom_call_target="tpu_custom_call" | custom-call | tf_op jit(solution)/shard_map/forecast/pallas_call | solution.py:351
  125.6 52.0 %all_to_all.15 = bf16[32,64,512]{2,1,0:T(8,128)(2,1)S(1)} all-to-all(bf16[32,64,512]{2,1,0:T(8,128)(2,1)S(1)} %bitcast.21), channel_id=1, replica_groups=mesh['sub'=4,'mem'=8] {'sub','mem'}, dimensions={0} | all-to-all | bytes 4194304 | tf_op jit(solution)/shard_map/all_to_all | solution.py:433
  177.6 3.5 %unpack_state.1 = bf16[2,64,8,1024]{3,2,1,0:T(8,128)(2,1)} custom-call(bf16[2,2,8,64,512]{4,3,2,1,0:T(8,128)(2,1)S(1)} %bitcast.19), custom_call_target="tpu_custom_call" | custom-call | tf_op jit(solution)/shard_map/unpack_state/pallas_call | solution.py:184
  (10 shorter events, 0.1 us)
Async XLA Ops:
  4.7 57.4 %all-to-all-start.1 = ((bf16[32,64,512]{2,1,0:T(8,128)(2,1)}), bf16[32,64,512]{2,1,0:T(8,128)(2,1)S(1)}, u32[]{:S(2)}, u32[]{:S(2)}) async-start(bf16[32,64,512]{2,1,0:T(8,128)(2,1)} %bitcast.23), calls=%async_computation.1 | async-start | bytes 4194304 | tf_op jit(solution)/shard_map/all_to_all | solution.py:433
  62.1 1.3 copy-start.2
  62.1 4.1 %copy-start.3 = (bf16[2,1,2,512]{3,2,1,0:T(2,128)(2,1)S(1)}, bf16[2,1,2,512]{3,2,1,0:T(2,128)(2,1)}, u32[]{:S(2)}) copy-start(bf16[2,1,2,512]{3,2,1,0:T(2,128)(2,1)} %param.8) | copy-start | bytes 12292
  62.1 4.1 %copy-start.4 = (bf16[2,1,2,512]{3,2,1,0:T(2,128)(2,1)S(1)}, bf16[2,1,2,512]{3,2,1,0:T(2,128)(2,1)}, u32[]{:S(2)}) copy-start(bf16[2,1,2,512]{3,2,1,0:T(2,128)(2,1)} %param.7) | copy-start | bytes 12292
  63.4 52.8 %all-to-all-start = ((bf16[32,64,512]{2,1,0:T(8,128)(2,1)}), bf16[32,64,512]{2,1,0:T(8,128)(2,1)S(1)}, u32[]{:S(2)}, u32[]{:S(2)}) async-start(bf16[32,64,512]{2,1,0:T(8,128)(2,1)} %bitcast.22), calls=%async_computation | async-start | bytes 4194304 | tf_op jit(solution)/shard_map/all_to_all | solution.py:433
  116.3 1.6 copy-start
  117.9 1.2 copy-start.1

commit v9 on v7

--- a/solution.py
+++ b/solution.py
@@ -11,9 +11,10 @@
 BF16 = jnp.bfloat16
 MIB = 1024 * 1024
 WHOLE = pl.BlockSpec(memory_space=pltpu.VMEM)
-
-
-def params(count, limit=40):
+ANY = pl.BlockSpec(memory_space=pl.ANY)
+
+
+def params(count, limit=48):
     return pltpu.CompilerParams(
         dimension_semantics=("arbitrary",) * count, vmem_limit_bytes=limit * MIB
     )
@@ -39,18 +40,36 @@
     return jnp.where(condition, 1.0, 0.0).astype(BF16)
 
 
-def pack_obs_kernel(rows, out, order):
-    _, width, owners, block, own = out.shape
-    size = order.shape[0]
+def pack_obs_kernel(rows, out, order, held, packed, in_sems, out_sems):
+    slabs, width, owners, local, own = packed.shape
     patches = width * owners
-
-    @pl.when((pl.program_id(0) == 0) & (pl.program_id(1) == 0))
-    def _():
-        rest, member = split(iota(size, size, 0), block)
-        part, owner = split(rest, owners)
-        order[...] = ones_at(iota(size, size, 1) == member * patches + owner * width + part)
-
-    out[...] = moved(order[...], rows[...].reshape(size, own)).reshape(out.shape)
+    block = order.shape[0] // patches
+    count = local // block
+    copies = [
+        pltpu.make_async_copy(
+            rows.at[slab, pl.ds(at * block, block)],
+            held.at[slab, pl.ds(at * block, block)],
+            in_sems.at[slab * count + at],
+        )
+        for slab in range(slabs)
+        for at in range(count)
+    ]
+    for copy in copies:
+        copy.start()
+    rest, member = split(iota(*order.shape, 0), block)
+    side, owner = split(rest, owners)
+    order[...] = ones_at(iota(*order.shape, 1) == member * patches + owner * width + side)
+    sent = []
+    for slab in range(slabs):
+        for at in range(count):
+            copies[slab * count + at].wait()
+            here = slice(at * block, (at + 1) * block)
+            flat = moved(order[...], held[slab, here].reshape(block * patches, own))
+            packed[slab, :, :, here, :] = flat.reshape(width, owners, block, own)
+        sent.append(pltpu.make_async_copy(packed.at[slab], out.at[slab], out_sems.at[slab]))
+        sent[-1].start()
+    for copy in sent:
+        copy.wait()
 
 
 def pack_obs(hx_values, width):
@@ -59,14 +78,19 @@
     block = 16
     return pl.pallas_call(
         pack_obs_kernel,
-        grid=(slabs, local // block),
-        in_specs=[pl.BlockSpec((1, block, 1, patches, own), lambda s, g: (s, g, 0, 0, 0))],
-        out_specs=pl.BlockSpec((1, width, owners, block, own), lambda s, g: (s, 0, 0, g, 0)),
+        in_specs=[ANY],
+        out_specs=ANY,
         out_shape=jax.ShapeDtypeStruct((slabs, width, owners, local, own), BF16),
-        scratch_shapes=[pltpu.VMEM((block * patches, block * patches), BF16)],
-        compiler_params=params(2, 60),
+        scratch_shapes=[
+            pltpu.VMEM((block * patches, block * patches), BF16),
+            pltpu.VMEM((slabs, local, patches, own), BF16),
+            pltpu.VMEM((slabs, width, owners, local, own), BF16),
+            pltpu.SemaphoreType.DMA((slabs * local // block,)),
+            pltpu.SemaphoreType.DMA((slabs,)),
+        ],
+        compiler_params=pltpu.CompilerParams(vmem_limit_bytes=60 * MIB),
         name="pack_obs",
-    )(hx_values)
+    )(hx_values.reshape(slabs, local, patches, own))
 
 
 def swapped(width, lanes):
@@ -136,56 +160,65 @@
     )(member_state)
 
 
-def unpack_state_kernel(packed, out, order, swap):
-    _, width, owners, _, size = packed.shape
-    block, cells_a = out.shape[1:3]
-    slab, group = pl.program_id(0), pl.program_id(1)
-    here = pl.ds(pl.multiple_of(group * block, block), block)
+def unpack_state_kernel(packed, out, held, sems):
+    slabs, width, owners, local, size = packed.shape
+    cells_a = out.shape[2]
     tiles = cells_a // width
     lanes = size // tiles
-
-    @pl.when((pl.program_id(0) == 0) & (pl.program_id(1) == 0))
-    def _():
-        order[...] = transposed(block, cells_a)
-        swap[...] = swapped(width, lanes)
-
-    parts = []
-    for owner in range(owners):
-        for tile in range(tiles):
-            pieces = [
-                packed[slab, part, owner, here, tile * lanes : (tile + 1) * lanes]
-                for part in range(width)
-            ]
-            parts.append(jnp.concatenate(pieces, axis=1))
-    mixed = moved(jnp.concatenate(parts, axis=0), swap[...])
-    columns = []
-    for owner in range(owners):
-        rows = []
-        for cell in range(cells_a):
-            half, tile = cell // tiles, cell % tiles
-            at = (owner * tiles + tile) * block
-            rows.append(mixed[at : at + block, half * lanes : (half + 1) * lanes])
-        columns.append(jnp.concatenate(rows, axis=0))
-    rows = moved(order[...], jnp.concatenate(columns, axis=1))
-    out[...] = rows.reshape(out.shape)
+    count = sems.shape[0] // slabs
+    block = local // count
+    order = transposed(block, cells_a)
+    swap = swapped(width, lanes)
+    sent = []
+    for slab in range(slabs):
+        for at in range(count):
+            here = slice(at * block, (at + 1) * block)
+            parts = []
+            for owner in range(owners):
+                for tile in range(tiles):
+                    pieces = [
+                        packed[slab, part, owner, here, tile * lanes : (tile + 1) * lanes]
+                        for part in range(width)
+                    ]
+                    parts.append(jnp.concatenate(pieces, axis=1))
+            mixed = moved(jnp.concatenate(parts, axis=0), swap)
+            columns = []
+            for owner in range(owners):
+                rows = []
+                for cell in range(cells_a):
+                    half, tile = cell // tiles, cell % tiles
+                    start = (owner * tiles + tile) * block
+                    rows.append(mixed[start : start + block, half * lanes : (half + 1) * lanes])
+                columns.append(jnp.concatenate(rows, axis=0))
+            rows = moved(order, jnp.concatenate(columns, axis=1))
+            held[slab, here] = rows.reshape(block, cells_a, owners * lanes)
+            sent.append(
+                pltpu.make_async_copy(
+                    held.at[slab, pl.ds(at * block, block)],
+                    out.at[slab, pl.ds(at * block, block)],
+                    sems.at[slab * count + at],
+                )
+            )
+            sent[-1].start()
+    for copy in sent:
+        copy.wait()
 
 
 def unpack_state(packed, cells_a):
     slabs, width, owners, local, size = packed.shape
     lanes = size * width // cells_a
-    cols = owners * lanes
+    shape = (slabs, local, cells_a, owners * lanes)
     block = 32
     return pl.pallas_call(
         unpack_state_kernel,
-        grid=(slabs, local // block),
         in_specs=[WHOLE],
-        out_specs=pl.BlockSpec((1, block, cells_a, cols), lambda s, g: (s, g, 0, 0)),
-        out_shape=jax.ShapeDtypeStruct((slabs, local, cells_a, cols), BF16),
+        out_specs=ANY,
+        out_shape=jax.ShapeDtypeStruct(shape, BF16),
         scratch_shapes=[
-            pltpu.VMEM((block * cells_a, block * cells_a), BF16),
-            pltpu.VMEM((width * lanes, width * lanes), BF16),
-        ],
-        compiler_params=params(2),
+            pltpu.VMEM(shape, BF16),
+            pltpu.SemaphoreType.DMA((slabs * local // block,)),
+        ],
+        compiler_params=pltpu.CompilerParams(vmem_limit_bytes=48 * MIB),
         name="unpack_state",
     )(packed)
 
@@ -301,11 +334,23 @@
     return results
 
 
-def forecast_kernel(state, transform, rest, speed, out, fields):
+def forecast_kernel(state, transforms, rests, speed, out, transform, rest, fields, sems):
     count, total, size = out.shape
     lanes = speed.shape[1]
+    copies = [
+        [
+            pltpu.make_async_copy(source.at[a], target.at[a], sems.at[i, a])
+            for i, (source, target) in enumerate(((transforms, transform), (rests, rest)))
+        ]
+        for a in range(count)
+    ]
+    for pair in copies:
+        for copy in pair:
+            copy.start()
     for a in range(count):
         mean = jnp.sum(state[a].astype(F32), axis=0, keepdims=True) * (1.0 / total)
+        for copy in copies[a]:
+            copy.wait()
         values = dot_bf16(transform[a], state[a])
         for k in range(size // lanes):
             part = slice(k * lanes, (k + 1) * lanes)
@@ -338,11 +383,16 @@
     count, total, size = state.shape
     return pl.pallas_call(
         forecast_kernel,
-        in_specs=[WHOLE] * 4,
+        in_specs=[WHOLE, ANY, ANY, WHOLE],
         out_specs=WHOLE,
         out_shape=jax.ShapeDtypeStruct((count, total, size), BF16),
-        scratch_shapes=[pltpu.VMEM((count, total, size), F32)],
-        compiler_params=pltpu.CompilerParams(vmem_limit_bytes=40 * MIB),
+        scratch_shapes=[
+            pltpu.VMEM((count, total, total), BF16),
+            pltpu.VMEM(rest.shape, F32),
+            pltpu.VMEM((count, total, size), F32),
+            pltpu.SemaphoreType.DMA((2, count)),
+        ],
+        compiler_params=pltpu.CompilerParams(vmem_limit_bytes=48 * MIB),
         name="forecast",
     )(state, transform, rest, speed)
 

time: 182 us -> 178 us (0.978)
  Pallas kernels: 40 us -> 37.8 us
    pallas_call x3, Pallas kernels: 15.8 us -> 13.6 us  [the longest x1 7.38 us: forecasts(): pl.pallas_call(forecast_kernel, in_specs=[WHOLE, ANY, ANY, WHOLE], out_sp...]
    unnamed x12 -> x10, local copies, waits for them, and re-layouts: 5.84 us -> 4.26 us
  transfers between devices with their start and end apart: 2 -> 2, of which waited for: 2 -> 2; matrix products, arithmetic and copies ran while one was open for 1% -> 1% of each run, Pallas kernels for 13% -> 14%
where the time goes in v9:
time: 178 us; the launch traced here: 177 us
  blocking collectives  69.8 us (39%)
  waiting for transfers between devices  54.1 us (30%)
  Pallas kernels  37.8 us (21%)
  starting transfers between devices  10.2 us (6%)
  local copies, waits for them, and re-layouts  5.16 us (3%)
    all_to_all x2, waiting for transfers between devices, exchange(): lax.all_to_all(blocks, ('sub', 'mem'), split_axis=0, concat_axis=0, tiled...  54.1 us
    all_to_all x1, blocking collectives, exchange(): lax.all_to_all(blocks, ('sub', 'mem'), split_axis=0, concat_axis=0, tiled...  52 us
    pallas_call x1, Pallas kernels, transforms(): pl.pallas_call(transform_kernel, grid=(count,), in_specs=[pl.BlockSpec((1...  19.4 us
    all_gather x1, blocking collectives, advance(): stats = lax.all_gather(stats, 'sub', axis=0)  17.8 us
    all_to_all x2, starting transfers between devices, exchange(): lax.all_to_all(blocks, ('sub', 'mem'), split_axis=0, concat_axis=0, tiled...  10.2 us
    pallas_call x1, Pallas kernels, forecasts(): pl.pallas_call(forecast_kernel, in_specs=[WHOLE, ANY, ANY, WHOLE], out_sp...  7.38 us
    pallas_call x1, Pallas kernels, pack_state(): pl.pallas_call(pack_state_kernel, grid=(slabs, local // block), in_specs=...  4.84 us
    unnamed x10, local copies, waits for them, and re-layouts  4.26 us
  transfers between devices with their start and end apart: 2, of which 2 were waited for; matrix products, arithmetic and copies ran while one was open for 1% of the time, Pallas kernels for 14%

profile of v9, /device:TPU:0, one launch (start us, length us, event | category | flops | bytes accessed | tf_op | source)
XLA Modules:
  0.0 177.3 jit_solution(9444440341304236614)
XLA Ops:
  0.0 3.9 %pack_obs.1 = bf16[2,2,8,64,512]{4,3,2,1,0:T(8,128)(2,1)} custom-call(bf16[2,64,16,512]{3,2,1,0:T(8,128)(2,1)} %bitcast.28), custom_call_target="tpu_custom_call" | custom-call | tf_op jit(solution)/shard_map/pack_obs/pallas_call | solution.py:79
  3.9 7.3 %all-to-all-start.1 = ((bf16[32,64,512]{2,1,0:T(8,128)(2,1)}), bf16[32,64,512]{2,1,0:T(8,128)(2,1)S(1)}, u32[]{:S(2)}, u32[]{:S(2)}) async-start(bf16[32,64,512]{2,1,0:T(8,128)(2,1)} %bitcast.27), calls=%async_computation.1 | async-start | bytes 4194304 | tf_op jit(solution)/shard_map/all_to_all | solution.py:467
  11.2 4.8 %pack_state.1 = bf16[2,2,8,64,512]{4,3,2,1,0:T(8,128)(2,1)} custom-call(bf16[2,64,8,1024]{3,2,1,0:T(8,128)(2,1)} %cells.1), custom_call_target="tpu_custom_call" | custom-call | tf_op jit(solution)/shard_map/pack_state/pallas_call | solution.py:146
  16.1 45.3 %all-to-all-done.1 = bf16[32,64,512]{2,1,0:T(8,128)(2,1)S(1)} async-done(((bf16[32,64,512]{2,1,0:T(8,128)(2,1)}), bf16[32,64,512]{2,1,0:T(8,128)(2,1)S(1)}, u32[]{:S(2)}, u32[]{:S(2)}) %all-to-all-start.1) | async-done | bytes 2097184 | tf_op jit(solution)/shard_map/all_to_all | solution.py:467
  61.3 0.0 copy-start
  61.3 1.3 copy-done
  62.7 0.0 copy-start.3
  62.7 0.0 copy-start.4
  62.7 2.9 %all-to-all-start = ((bf16[32,64,512]{2,1,0:T(8,128)(2,1)}), bf16[32,64,512]{2,1,0:T(8,128)(2,1)S(1)}, u32[]{:S(2)}, u32[]{:S(2)}) async-start(bf16[32,64,512]{2,1,0:T(8,128)(2,1)} %bitcast.26), calls=%async_computation | async-start | bytes 4194304 | tf_op jit(solution)/shard_map/all_to_all | solution.py:467
  65.6 0.0 copy-done.3
  65.6 0.0 copy-done.4
  65.6 17.8 %all-gather = bf16[8,2,2,512]{3,1,0,2:T(2,128)(2,1)S(1)} all-gather(bf16[2,2,2,512]{3,1,0,2:T(2,128)(2,1)S(1)} %pad_maximum_fusion.2), channel_id=2, replica_groups=mesh['sub'=4,'mem'=8] {'sub'}, dimensions={0}, use_global_device_ids=true | all-gather | bytes 40960 | tf_op jit(solution)/shard_map/all_gather | solution.py:480
  83.4 0.1 reverse.4
  83.5 0.8 dynamic_slice.7
  84.3 0.1 pad_maximum_fusion.4.speed
  84.5 0.0 copy-start.1
  84.5 1.6 copy-done.1
  86.1 19.4 %transform.1 = (bf16[4,512,512]{2,1,0:T(8,128)(2,1)S(1)}, f32[4,512,128]{2,1,0:T(8,128)S(1)}) custom-call(bf16[4,512,512]{2,1,0:T(8,128)(2,1)S(1)} %bitcast.23, bf16[4,512,512]{2,1,0:T(8,128)(2,1)S(1)} %bitcast.24, bf16[4,512,512]{2,1,0:T(8,128)(2,1)S(1)} %bitcast.25, f32[4,1,1024]{2,1,0:T(1,128)S(1)} %get-tuple-element.10.obs, ...), custom_call_target="tpu_custom_call" | custom-call | flops 11811160064 | bytes 8388608 | tf_op jit(solution)/shard_map/transform/pallas_call | solution.py:276
  105.5 0.0 copy-start.2
  105.5 1.3 copy-done.2
  106.8 8.8 %all-to-all-done = bf16[32,64,512]{2,1,0:T(8,128)(2,1)S(1)} async-done(((bf16[32,64,512]{2,1,0:T(8,128)(2,1)}), bf16[32,64,512]{2,1,0:T(8,128)(2,1)S(1)}, u32[]{:S(2)}, u32[]{:S(2)}) %all-to-all-start) | async-done | bytes 2097184 | tf_op jit(solution)/shard_map/all_to_all | solution.py:467
  115.6 7.4 %forecast.1 = bf16[4,512,512]{2,1,0:T(8,128)(2,1)S(1)} custom-call(bf16[4,512,512]{2,1,0:T(8,128)(2,1)S(1)} %bitcast.21, bf16[4,512,512]{2,1,0:T(8,128)(2,1)} %copy-done.2, f32[4,512,128]{2,1,0:T(8,128)S(1)} %get-tuple-element.8.rests, f32[1,128]{1,0:T(1,128)S(1)} %pad_maximum_fusion.4.speed), custom_call_target="tpu_custom_call" | custom-call | tf_op jit(solution)/shard_map/forecast/pallas_call | solution.py:384
  123.0 52.0 %all_to_all.15 = bf16[32,64,512]{2,1,0:T(8,128)(2,1)S(1)} all-to-all(bf16[32,64,512]{2,1,0:T(8,128)(2,1)S(1)} %bitcast.22), channel_id=1, replica_groups=mesh['sub'=4,'mem'=8] {'sub','mem'}, dimensions={0} | all-to-all | bytes 4194304 | tf_op jit(solution)/shard_map/all_to_all | solution.py:467
  175.0 2.3 %unpack_state.1 = bf16[2,64,8,1024]{3,2,1,0:T(8,128)(2,1)} custom-call(bf16[2,2,8,64,512]{4,3,2,1,0:T(8,128)(2,1)S(1)} %bitcast.20), custom_call_target="tpu_custom_call" | custom-call | tf_op jit(solution)/shard_map/unpack_state/pallas_call | solution.py:212
  (11 shorter events, 0.2 us)
Async XLA Ops:
  3.9 57.4 %all-to-all-start.1 = ((bf16[32,64,512]{2,1,0:T(8,128)(2,1)}), bf16[32,64,512]{2,1,0:T(8,128)(2,1)S(1)}, u32[]{:S(2)}, u32[]{:S(2)}) async-start(bf16[32,64,512]{2,1,0:T(8,128)(2,1)} %bitcast.27), calls=%async_computation.1 | async-start | bytes 4194304 | tf_op jit(solution)/shard_map/all_to_all | solution.py:467
  61.3 1.3 copy-start
  62.7 2.9 %copy-start.3 = (bf16[2,1,2,512]{3,2,1,0:T(2,128)(2,1)S(1)}, bf16[2,1,2,512]{3,2,1,0:T(2,128)(2,1)}, u32[]{:S(2)}) copy-start(bf16[2,1,2,512]{3,2,1,0:T(2,128)(2,1)} %param.8) | copy-start | bytes 12292
  62.7 2.9 %copy-start.4 = (bf16[2,1,2,512]{3,2,1,0:T(2,128)(2,1)S(1)}, bf16[2,1,2,512]{3,2,1,0:T(2,128)(2,1)}, u32[]{:S(2)}) copy-start(bf16[2,1,2,512]{3,2,1,0:T(2,128)(2,1)} %param.7) | copy-start | bytes 12292
  62.7 53.0 %all-to-all-start = ((bf16[32,64,512]{2,1,0:T(8,128)(2,1)}), bf16[32,64,512]{2,1,0:T(8,128)(2,1)S(1)}, u32[]{:S(2)}, u32[]{:S(2)}) async-start(bf16[32,64,512]{2,1,0:T(8,128)(2,1)} %bitcast.26), calls=%async_computation | async-start | bytes 4194304 | tf_op jit(solution)/shard_map/all_to_all | solution.py:467
  84.5 1.6 copy-start.1
  105.5 1.3 copy-start.2

commit v10 on v9

--- a/solution.py
+++ b/solution.py
@@ -155,7 +155,7 @@
             pltpu.VMEM((block * cells_a, block * cells_a), BF16),
             pltpu.VMEM((width * lanes, width * lanes), BF16),
         ],
-        compiler_params=params(2, 60),
+        compiler_params=params(2, 63),
         name="pack_state",
     )(member_state)
 
@@ -292,7 +292,7 @@
             jax.ShapeDtypeStruct((count, total, 128), F32),
         ],
         scratch_shapes=[pltpu.VMEM((total, 2 * own), BF16), pltpu.VMEM((total, 2 * own), BF16)],
-        compiler_params=params(1),
+        compiler_params=params(1, 32),
         cost_estimate=pl.CostEstimate(
             flops=flops, bytes_accessed=4 * count * total * total * 2, transcendentals=0
         ),
@@ -334,23 +334,11 @@
     return results
 
 
-def forecast_kernel(state, transforms, rests, speed, out, transform, rest, fields, sems):
+def forecast_kernel(state, transform, rest, speed, out, fields):
     count, total, size = out.shape
     lanes = speed.shape[1]
-    copies = [
-        [
-            pltpu.make_async_copy(source.at[a], target.at[a], sems.at[i, a])
-            for i, (source, target) in enumerate(((transforms, transform), (rests, rest)))
-        ]
-        for a in range(count)
-    ]
-    for pair in copies:
-        for copy in pair:
-            copy.start()
     for a in range(count):
         mean = jnp.sum(state[a].astype(F32), axis=0, keepdims=True) * (1.0 / total)
-        for copy in copies[a]:
-            copy.wait()
         values = dot_bf16(transform[a], state[a])
         for k in range(size // lanes):
             part = slice(k * lanes, (k + 1) * lanes)
@@ -383,16 +371,11 @@
     count, total, size = state.shape
     return pl.pallas_call(
         forecast_kernel,
-        in_specs=[WHOLE, ANY, ANY, WHOLE],
+        in_specs=[WHOLE] * 4,
         out_specs=WHOLE,
         out_shape=jax.ShapeDtypeStruct((count, total, size), BF16),
-        scratch_shapes=[
-            pltpu.VMEM((count, total, total), BF16),
-            pltpu.VMEM(rest.shape, F32),
-            pltpu.VMEM((count, total, size), F32),
-            pltpu.SemaphoreType.DMA((2, count)),
-        ],
-        compiler_params=pltpu.CompilerParams(vmem_limit_bytes=48 * MIB),
+        scratch_shapes=[pltpu.VMEM((count, total, size), F32)],
+        compiler_params=pltpu.CompilerParams(vmem_limit_bytes=20 * MIB),
         name="forecast",
     )(state, transform, rest, speed)
 

time: 178 us -> 177 us (level)
    unnamed x10 -> x8, local copies, waits for them, and re-layouts: 4.26 us -> 2.92 us
where the time goes in v10:
time: 177 us; the launch traced here: 176 us
  blocking collectives  69.8 us (39%)
  waiting for transfers between devices  54.6 us (31%)
  Pallas kernels  37.3 us (21%)
  starting transfers between devices  10.3 us (6%)
  local copies, waits for them, and re-layouts  3.82 us (2%)
    all_to_all x2, waiting for transfers between devices, exchange(): lax.all_to_all(blocks, ('sub', 'mem'), split_axis=0, concat_axis=0, tiled...  54.6 us
    all_to_all x1, blocking collectives, exchange(): lax.all_to_all(blocks, ('sub', 'mem'), split_axis=0, concat_axis=0, tiled...  52 us
    pallas_call x1, Pallas kernels, transforms(): pl.pallas_call(transform_kernel, grid=(count,), in_specs=[pl.BlockSpec((1...  20.5 us
    all_gather x1, blocking collectives, advance(): stats = lax.all_gather(stats, 'sub', axis=0)  17.8 us
    all_to_all x2, starting transfers between devices, exchange(): lax.all_to_all(blocks, ('sub', 'mem'), split_axis=0, concat_axis=0, tiled...  10.3 us
    pallas_call x1, Pallas kernels, forecasts(): pl.pallas_call(forecast_kernel, in_specs=[WHOLE] * 4, out_specs=WHOLE, ou...  5.79 us
    pallas_call x1, Pallas kernels, pack_state(): pl.pallas_call(pack_state_kernel, grid=(slabs, local // block), in_specs=...  4.84 us
    pallas_call x1, Pallas kernels, pack_obs(): pl.pallas_call(pack_obs_kernel, in_specs=[ANY], out_specs=ANY, out_shape=...  3.91 us
  transfers between devices with their start and end apart: 2, of which 2 were waited for; matrix products, arithmetic and copies ran while one was open for 1% of the time, Pallas kernels for 14%

profile of v10, /device:TPU:0, one launch (start us, length us, event | category | flops | bytes accessed | tf_op | source)
XLA Modules:
  0.0 176.1 jit_solution(8392999519405291198)
XLA Ops:
  0.0 3.9 %pack_obs.1 = bf16[2,2,8,64,512]{4,3,2,1,0:T(8,128)(2,1)} custom-call(bf16[2,64,16,512]{3,2,1,0:T(8,128)(2,1)} %bitcast.25), custom_call_target="tpu_custom_call" | custom-call | tf_op jit(solution)/shard_map/pack_obs/pallas_call | solution.py:79
  3.9 7.4 %all-to-all-start.1 = ((bf16[32,64,512]{2,1,0:T(8,128)(2,1)}), bf16[32,64,512]{2,1,0:T(8,128)(2,1)}, u32[]{:S(2)}, u32[]{:S(2)}) async-start(bf16[32,64,512]{2,1,0:T(8,128)(2,1)} %bitcast.24), calls=%async_computation.1 | async-start | bytes 4194304 | tf_op jit(solution)/shard_map/all_to_all | solution.py:450
  11.3 4.8 %pack_state.1 = bf16[2,2,8,64,512]{4,3,2,1,0:T(8,128)(2,1)} custom-call(bf16[2,64,8,1024]{3,2,1,0:T(8,128)(2,1)} %cells.1), custom_call_target="tpu_custom_call" | custom-call | tf_op jit(solution)/shard_map/pack_state/pallas_call | solution.py:146
  16.2 45.2 %all-to-all-done.1 = bf16[32,64,512]{2,1,0:T(8,128)(2,1)} async-done(((bf16[32,64,512]{2,1,0:T(8,128)(2,1)}), bf16[32,64,512]{2,1,0:T(8,128)(2,1)}, u32[]{:S(2)}, u32[]{:S(2)}) %all-to-all-start.1) | async-done | bytes 2097184 | tf_op jit(solution)/shard_map/all_to_all | solution.py:450
  61.4 0.0 copy-start.2
  61.4 0.0 copy-start.3
  61.4 2.9 %all-to-all-start = ((bf16[32,64,512]{2,1,0:T(8,128)(2,1)}), bf16[32,64,512]{2,1,0:T(8,128)(2,1)S(1)}, u32[]{:S(2)}, u32[]{:S(2)}) async-start(bf16[32,64,512]{2,1,0:T(8,128)(2,1)} %bitcast.23), calls=%async_computation | async-start | bytes 4194304 | tf_op jit(solution)/shard_map/all_to_all | solution.py:450
  64.4 0.0 copy-done.2
  64.4 0.0 copy-done.3
  64.4 17.8 %all-gather = bf16[8,2,2,512]{3,1,0,2:T(2,128)(2,1)S(1)} all-gather(bf16[2,2,2,512]{3,1,0,2:T(2,128)(2,1)S(1)} %pad_maximum_fusion.2), channel_id=2, replica_groups=mesh['sub'=4,'mem'=8] {'sub'}, dimensions={0}, use_global_device_ids=true | all-gather | bytes 40960 | tf_op jit(solution)/shard_map/all_gather | solution.py:463
  82.2 0.1 reverse.4
  82.3 0.8 dynamic_slice.7
  83.0 0.1 pad_maximum_fusion.4.speed
  83.3 20.5 %transform.1 = (bf16[4,512,512]{2,1,0:T(8,128)(2,1)S(1)}, f32[4,512,128]{2,1,0:T(8,128)S(1)}) custom-call(bf16[4,512,512]{2,1,0:T(8,128)(2,1)} %bitcast.4.before.middle.after, bf16[4,512,512]{2,1,0:T(8,128)(2,1)} %bitcast.4.before.middle.after, bf16[4,512,512]{2,1,0:T(8,128)(2,1)} %bitcast.4.before.middle.after, f32[4,1,1024]{2,1,0:T(1,128)S(1)} %get-tuple-element.10.obs, ...), custom_call_target="tpu_custom_call" | custom-call | flops 11811160064 | bytes 8388608 | tf_op jit(solution)/shard_map/transform/pallas_call | solution.py:276
  103.7 0.0 copy-start
  103.8 1.3 copy-done
  105.1 9.3 %all-to-all-done = bf16[32,64,512]{2,1,0:T(8,128)(2,1)S(1)} async-done(((bf16[32,64,512]{2,1,0:T(8,128)(2,1)}), bf16[32,64,512]{2,1,0:T(8,128)(2,1)S(1)}, u32[]{:S(2)}, u32[]{:S(2)}) %all-to-all-start) | async-done | bytes 2097184 | tf_op jit(solution)/shard_map/all_to_all | solution.py:450
  114.4 0.0 copy-start.1
  114.4 1.6 copy-done.1
  116.0 5.8 %forecast.1 = bf16[4,512,512]{2,1,0:T(8,128)(2,1)S(1)} custom-call(bf16[4,512,512]{2,1,0:T(8,128)(2,1)S(1)} %bitcast.21, bf16[4,512,512]{2,1,0:T(8,128)(2,1)S(1)} %copy-done.1, f32[4,512,128]{2,1,0:T(8,128)S(1)} %get-tuple-element.8.rest, f32[1,128]{1,0:T(1,128)S(1)} %pad_maximum_fusion.4.speed), custom_call_target="tpu_custom_call" | custom-call | tf_op jit(solution)/shard_map/forecast/pallas_call | solution.py:372
  121.8 52.0 %all_to_all.15 = bf16[32,64,512]{2,1,0:T(8,128)(2,1)S(1)} all-to-all(bf16[32,64,512]{2,1,0:T(8,128)(2,1)S(1)} %bitcast.22), channel_id=1, replica_groups=mesh['sub'=4,'mem'=8] {'sub','mem'}, dimensions={0} | all-to-all | bytes 4194304 | tf_op jit(solution)/shard_map/all_to_all | solution.py:450
  173.8 2.3 %unpack_state.1 = bf16[2,64,8,1024]{3,2,1,0:T(8,128)(2,1)} custom-call(bf16[2,2,8,64,512]{4,3,2,1,0:T(8,128)(2,1)S(1)} %bitcast.20), custom_call_target="tpu_custom_call" | custom-call | tf_op jit(solution)/shard_map/unpack_state/pallas_call | solution.py:212
  (11 shorter events, 0.2 us)
Async XLA Ops:
  3.9 57.5 %all-to-all-start.1 = ((bf16[32,64,512]{2,1,0:T(8,128)(2,1)}), bf16[32,64,512]{2,1,0:T(8,128)(2,1)}, u32[]{:S(2)}, u32[]{:S(2)}) async-start(bf16[32,64,512]{2,1,0:T(8,128)(2,1)} %bitcast.24), calls=%async_computation.1 | async-start | bytes 4194304 | tf_op jit(solution)/shard_map/all_to_all | solution.py:450
  61.4 2.9 %copy-start.2 = (bf16[2,1,2,512]{3,2,1,0:T(2,128)(2,1)S(1)}, bf16[2,1,2,512]{3,2,1,0:T(2,128)(2,1)}, u32[]{:S(2)}) copy-start(bf16[2,1,2,512]{3,2,1,0:T(2,128)(2,1)} %param.8) | copy-start | bytes 12292
  61.4 2.9 %copy-start.3 = (bf16[2,1,2,512]{3,2,1,0:T(2,128)(2,1)S(1)}, bf16[2,1,2,512]{3,2,1,0:T(2,128)(2,1)}, u32[]{:S(2)}) copy-start(bf16[2,1,2,512]{3,2,1,0:T(2,128)(2,1)} %param.7) | copy-start | bytes 12292
  61.4 53.0 %all-to-all-start = ((bf16[32,64,512]{2,1,0:T(8,128)(2,1)}), bf16[32,64,512]{2,1,0:T(8,128)(2,1)S(1)}, u32[]{:S(2)}, u32[]{:S(2)}) async-start(bf16[32,64,512]{2,1,0:T(8,128)(2,1)} %bitcast.23), calls=%async_computation | async-start | bytes 4194304 | tf_op jit(solution)/shard_map/all_to_all | solution.py:450
  103.7 1.3 copy-start
  114.4 1.6 copy-start.1

commit v11 on v10

--- a/solution.py
+++ b/solution.py
@@ -7,6 +7,7 @@
 
 ITERS = 4
 STEPS = 4
+PIECES = 2
 F32 = jnp.float32
 BF16 = jnp.bfloat16
 MIB = 1024 * 1024
@@ -66,8 +67,15 @@
             here = slice(at * block, (at + 1) * block)
             flat = moved(order[...], held[slab, here].reshape(block * patches, own))
             packed[slab, :, :, here, :] = flat.reshape(width, owners, block, own)
-        sent.append(pltpu.make_async_copy(packed.at[slab], out.at[slab], out_sems.at[slab]))
-        sent[-1].start()
+            rows_here = pl.ds(at * block, block)
+            sent.append(
+                pltpu.make_async_copy(
+                    packed.at[slab, :, :, rows_here],
+                    out.at[slab, :, :, rows_here],
+                    out_sems.at[slab * count + at],
+                )
+            )
+            sent[-1].start()
     for copy in sent:
         copy.wait()
 
@@ -86,7 +94,7 @@
             pltpu.VMEM((slabs, local, patches, own), BF16),
             pltpu.VMEM((slabs, width, owners, local, own), BF16),
             pltpu.SemaphoreType.DMA((slabs * local // block,)),
-            pltpu.SemaphoreType.DMA((slabs,)),
+            pltpu.SemaphoreType.DMA((slabs * local // block,)),
         ],
         compiler_params=pltpu.CompilerParams(vmem_limit_bytes=60 * MIB),
         name="pack_obs",
@@ -223,7 +231,8 @@
     )(packed)
 
 
-def transform_kernel(before, middle, after, obs, scale, out, rest, pert, weighted):
+def transform_kernel(before, middle, after, obs, scale, *refs):
+    *outs, rest, pert, weighted = refs
     total = middle.shape[1]
     half = before.shape[2]
     projected = jnp.zeros((total, 1), F32)
@@ -263,7 +272,14 @@
     weight = jnp.sum(inverse * halfway, axis=1, keepdims=True)
     weight = jnp.broadcast_to(weight, (total, 128)).T[0:1, :] / bound
     result = (jnp.sqrt((total - 1.0) / bound) * flipped + weight).astype(BF16)
-    out[0] = result
+    a = pl.program_id(0)
+    span = pl.num_programs(0) // len(outs)
+    for number, out in enumerate(outs):
+
+        @pl.when((a >= number * span) & (a < (number + 1) * span))
+        def _(out=out):
+            out[0] = result
+
     sums = jnp.sum(result.astype(F32), axis=1, keepdims=True)
     rest[0] = jnp.broadcast_to(1.0 - sums, (total, 128))
 
@@ -273,6 +289,11 @@
     half = own // 2
     shift = 0 if wraps else 1
     flops = count * (2 * total * total * 2 * own + 18 * total**3)
+    span = count // PIECES
+
+    def held_at(number):
+        return lambda a: (jnp.clip(a - number * span, 0, span - 1), 0, 0)
+
     return pl.pallas_call(
         transform_kernel,
         grid=(count,),
@@ -284,11 +305,11 @@
             pl.BlockSpec((1, 1, 2 * own), lambda a: (a, 0, 0)),
         ],
         out_specs=[
-            pl.BlockSpec((1, total, total), lambda a: (a, 0, 0)),
+            *[pl.BlockSpec((1, total, total), held_at(number)) for number in range(PIECES)],
             pl.BlockSpec((1, total, 128), lambda a: (a, 0, 0)),
         ],
         out_shape=[
-            jax.ShapeDtypeStruct((count, total, total), BF16),
+            *[jax.ShapeDtypeStruct((span, total, total), BF16)] * PIECES,
             jax.ShapeDtypeStruct((count, total, 128), F32),
         ],
         scratch_shapes=[pltpu.VMEM((total, 2 * own), BF16), pltpu.VMEM((total, 2 * own), BF16)],
@@ -334,16 +355,18 @@
     return results
 
 
-def forecast_kernel(state, transform, rest, speed, out, fields):
+def forecast_kernel(state, *refs):
+    *transforms, rest, speed, out, fields = refs
     count, total, size = out.shape
+    span = count // len(transforms)
     lanes = speed.shape[1]
     for a in range(count):
         mean = jnp.sum(state[a].astype(F32), axis=0, keepdims=True) * (1.0 / total)
-        values = dot_bf16(transform[a], state[a])
+        values = dot_bf16(transforms[a // span][a % span], state[a])
         for k in range(size // lanes):
             part = slice(k * lanes, (k + 1) * lanes)
             analysis = values[:, part] + rest[a] * mean[:, part]
-            fields[a, :, part] = analysis.astype(BF16).astype(F32)
+            fields[a, :, part] = analysis
     chunk = 16
     taps = stencil(jnp.broadcast_to(speed[...], (8, lanes)))
     low = iota(8, lanes, 1) < lanes // 2
@@ -371,13 +394,13 @@
     count, total, size = state.shape
     return pl.pallas_call(
         forecast_kernel,
-        in_specs=[WHOLE] * 4,
+        in_specs=[WHOLE] * (3 + len(transform)),
         out_specs=WHOLE,
         out_shape=jax.ShapeDtypeStruct((count, total, size), BF16),
         scratch_shapes=[pltpu.VMEM((count, total, size), F32)],
         compiler_params=pltpu.CompilerParams(vmem_limit_bytes=20 * MIB),
         name="forecast",
-    )(state, transform, rest, speed)
+    )(state, *transform, rest, speed)
 
 
 def analysis_kernel(state, transform, out):
@@ -479,7 +502,7 @@
     state = state.reshape(count, total, -1)
 
     held_rows = hx_rows if groups == 1 else widened(hx_rows, count)
-    transform, rest = transforms(held_rows, obs_rows, scale_rows, count, groups == 1)
+    *transform, rest = transforms(held_rows, obs_rows, scale_rows, count, groups == 1)
 
     column = (lax.axis_index("mem") * width + part) * cells_b
     speed = lax.dynamic_slice(courant, (slab, column), (1, cells_b))
@@ -487,7 +510,7 @@
     if groups == 1 and 2 * cells_b == 128 and width == 2 and cells_a // width >= STEPS:
         fields = forecasts(state, transform, rest, speed)
     else:
-        fields = shared_transport(analyses(state, transform), speed, width, count)
+        fields = shared_transport(analyses(state, jnp.concatenate(transform)), speed, width, count)
     back = exchange(fields.reshape(count * owners, local, -1))
     return unpack_state(back.reshape(slabs, width, owners, local, -1), cells_a)
 

time: 177 us -> 177 us (level)
    unnamed x8 -> x12, local copies, waits for them, and re-layouts: 2.92 us -> 4.42 us
where the time goes in v11:
time: 177 us
  blocking collectives  69.7 us (39%)
  waiting for transfers between devices  53.9 us (30%)
  Pallas kernels  37 us (21%)
  starting transfers between devices  10.3 us (6%)
  local copies, waits for them, and re-layouts  5.32 us (3%)
    all_to_all x2, waiting for transfers between devices, exchange(): lax.all_to_all(blocks, ('sub', 'mem'), split_axis=0, concat_axis=0, tiled...  53.9 us
    all_to_all x1, blocking collectives, exchange(): lax.all_to_all(blocks, ('sub', 'mem'), split_axis=0, concat_axis=0, tiled...  52 us
    pallas_call x1, Pallas kernels, transforms(): pl.pallas_call(transform_kernel, grid=(count,), in_specs=[pl.BlockSpec((1...  20.5 us
    all_gather x1, blocking collectives, advance(): stats = lax.all_gather(stats, 'sub', axis=0)  17.8 us
    all_to_all x2, starting transfers between devices, exchange(): lax.all_to_all(blocks, ('sub', 'mem'), split_axis=0, concat_axis=0, tiled...  10.3 us
    pallas_call x1, Pallas kernels, forecasts(): pl.pallas_call(forecast_kernel, in_specs=[WHOLE] * (3 + len(transform)),...  5.72 us
    pallas_call x1, Pallas kernels, pack_state(): pl.pallas_call(pack_state_kernel, grid=(slabs, local // block), in_specs=...  4.84 us
    unnamed x12, local copies, waits for them, and re-layouts  4.42 us
  transfers between devices with their start and end apart: 2, of which 2 were waited for; matrix products, arithmetic and copies ran while one was open for 1% of the time, Pallas kernels for 14%

profile of v11, /device:TPU:0, one launch (start us, length us, event | category | flops | bytes accessed | tf_op | source)
XLA Modules:
  0.0 176.7 jit_solution(9711856106173537145)
XLA Ops:
  0.0 3.7 %pack_obs.1 = bf16[2,2,8,64,512]{4,3,2,1,0:T(8,128)(2,1)} custom-call(bf16[2,64,16,512]{3,2,1,0:T(8,128)(2,1)} %bitcast.25), custom_call_target="tpu_custom_call" | custom-call | tf_op jit(solution)/shard_map/pack_obs/pallas_call | solution.py:87
  3.7 7.4 %all-to-all-start.1 = ((bf16[32,64,512]{2,1,0:T(8,128)(2,1)}), bf16[32,64,512]{2,1,0:T(8,128)(2,1)}, u32[]{:S(2)}, u32[]{:S(2)}) async-start(bf16[32,64,512]{2,1,0:T(8,128)(2,1)} %bitcast.24), calls=%async_computation.1 | async-start | bytes 4194304 | tf_op jit(solution)/shard_map/all_to_all | solution.py:473
  11.1 4.8 %pack_state.1 = bf16[2,2,8,64,512]{4,3,2,1,0:T(8,128)(2,1)} custom-call(bf16[2,64,8,1024]{3,2,1,0:T(8,128)(2,1)} %cells.1), custom_call_target="tpu_custom_call" | custom-call | tf_op jit(solution)/shard_map/pack_state/pallas_call | solution.py:154
  16.0 45.2 %all-to-all-done.1 = bf16[32,64,512]{2,1,0:T(8,128)(2,1)} async-done(((bf16[32,64,512]{2,1,0:T(8,128)(2,1)}), bf16[32,64,512]{2,1,0:T(8,128)(2,1)}, u32[]{:S(2)}, u32[]{:S(2)}) %all-to-all-start.1) | async-done | bytes 2097184 | tf_op jit(solution)/shard_map/all_to_all | solution.py:473
  61.2 0.0 copy-start.4
  61.2 0.0 copy-start.5
  61.2 2.9 %all-to-all-start = ((bf16[32,64,512]{2,1,0:T(8,128)(2,1)}), bf16[32,64,512]{2,1,0:T(8,128)(2,1)S(1)}, u32[]{:S(2)}, u32[]{:S(2)}) async-start(bf16[32,64,512]{2,1,0:T(8,128)(2,1)} %bitcast.23), calls=%async_computation | async-start | bytes 4194304 | tf_op jit(solution)/shard_map/all_to_all | solution.py:473
  64.1 0.0 copy-done.4
  64.1 0.0 copy-done.5
  64.2 17.8 %all-gather = bf16[8,2,2,512]{3,1,0,2:T(2,128)(2,1)S(1)} all-gather(bf16[2,2,2,512]{3,1,0,2:T(2,128)(2,1)S(1)} %pad_maximum_fusion.2), channel_id=2, replica_groups=mesh['sub'=4,'mem'=8] {'sub'}, dimensions={0}, use_global_device_ids=true | all-gather | bytes 40960 | tf_op jit(solution)/shard_map/all_gather | solution.py:486
  82.0 0.1 reverse.4
  82.1 0.8 dynamic_slice.7
  82.8 0.1 pad_maximum_fusion.4.refs_3_
  83.0 20.5 %transform.1 = (bf16[2,512,512]{2,1,0:T(8,128)(2,1)S(1)}, bf16[2,512,512]{2,1,0:T(8,128)(2,1)S(1)}, f32[4,512,128]{2,1,0:T(8,128)S(1)}) custom-call(bf16[4,512,512]{2,1,0:T(8,128)(2,1)} %bitcast.4.before.middle.after, bf16[4,512,512]{2,1,0:T(8,128)(2,1)} %bitcast.4.before.middle.after, bf16[4,512,512]{2,1,0:T(8,128)(2,1)} %bitcast.4.before.middle.after, ...), custom_call_target="tpu_custom_call" | custom-call | flops 11811160064 | bytes 8388608 | tf_op jit(solution)/shard_map/transform/pallas_call | solution.py:297
  103.5 0.0 copy-start
  103.6 1.0 copy-done
  104.5 0.0 copy-start.2
  104.5 1.0 copy-done.2
  105.5 8.7 %all-to-all-done = bf16[32,64,512]{2,1,0:T(8,128)(2,1)S(1)} async-done(((bf16[32,64,512]{2,1,0:T(8,128)(2,1)}), bf16[32,64,512]{2,1,0:T(8,128)(2,1)S(1)}, u32[]{:S(2)}, u32[]{:S(2)}) %all-to-all-start) | async-done | bytes 2097184 | tf_op jit(solution)/shard_map/all_to_all | solution.py:473
  114.2 0.0 copy-start.1
  114.2 1.2 copy-done.1
  115.4 0.0 copy-start.3
  115.4 1.2 copy-done.3
  116.6 5.7 %forecast.1 = bf16[4,512,512]{2,1,0:T(8,128)(2,1)S(1)} custom-call(bf16[4,512,512]{2,1,0:T(8,128)(2,1)S(1)} %bitcast.21, bf16[2,512,512]{2,1,0:T(8,128)(2,1)S(1)} %get-tuple-element.8.refs_0_, bf16[2,512,512]{2,1,0:T(8,128)(2,1)S(1)} %copy-done.1, f32[4,512,128]{2,1,0:T(8,128)S(1)} %copy-done.3, f32[1,128]{1,0:T(1,128)S(1)} %pad_maximum_fusion.4.refs_3_), custom_call_target="tpu_custom_call" | custom-call | tf_op jit(solution)/shard_map/forecast/pallas_call | solution.py:395
  122.4 52.0 %all_to_all.15 = bf16[32,64,512]{2,1,0:T(8,128)(2,1)S(1)} all-to-all(bf16[32,64,512]{2,1,0:T(8,128)(2,1)S(1)} %bitcast.22), channel_id=1, replica_groups=mesh['sub'=4,'mem'=8] {'sub','mem'}, dimensions={0} | all-to-all | bytes 4194304 | tf_op jit(solution)/shard_map/all_to_all | solution.py:473
  174.4 2.3 %unpack_state.1 = bf16[2,64,8,1024]{3,2,1,0:T(8,128)(2,1)} custom-call(bf16[2,2,8,64,512]{4,3,2,1,0:T(8,128)(2,1)S(1)} %bitcast.20), custom_call_target="tpu_custom_call" | custom-call | tf_op jit(solution)/shard_map/unpack_state/pallas_call | solution.py:220
  (11 shorter events, 0.2 us)
Async XLA Ops:
  3.7 57.5 %all-to-all-start.1 = ((bf16[32,64,512]{2,1,0:T(8,128)(2,1)}), bf16[32,64,512]{2,1,0:T(8,128)(2,1)}, u32[]{:S(2)}, u32[]{:S(2)}) async-start(bf16[32,64,512]{2,1,0:T(8,128)(2,1)} %bitcast.24), calls=%async_computation.1 | async-start | bytes 4194304 | tf_op jit(solution)/shard_map/all_to_all | solution.py:473
  61.2 2.9 %copy-start.4 = (bf16[2,1,2,512]{3,2,1,0:T(2,128)(2,1)S(1)}, bf16[2,1,2,512]{3,2,1,0:T(2,128)(2,1)}, u32[]{:S(2)}) copy-start(bf16[2,1,2,512]{3,2,1,0:T(2,128)(2,1)} %param.8) | copy-start | bytes 12292
  61.2 2.9 %copy-start.5 = (bf16[2,1,2,512]{3,2,1,0:T(2,128)(2,1)S(1)}, bf16[2,1,2,512]{3,2,1,0:T(2,128)(2,1)}, u32[]{:S(2)}) copy-start(bf16[2,1,2,512]{3,2,1,0:T(2,128)(2,1)} %param.7) | copy-start | bytes 12292
  61.2 53.0 %all-to-all-start = ((bf16[32,64,512]{2,1,0:T(8,128)(2,1)}), bf16[32,64,512]{2,1,0:T(8,128)(2,1)S(1)}, u32[]{:S(2)}, u32[]{:S(2)}) async-start(bf16[32,64,512]{2,1,0:T(8,128)(2,1)} %bitcast.23), calls=%async_computation | async-start | bytes 4194304 | tf_op jit(solution)/shard_map/all_to_all | solution.py:473
  103.5 1.0 copy-start
  104.5 1.0 copy-start.2
  114.2 1.2 copy-start.1
  115.4 1.2 copy-start.3

commit v12 on v10

--- a/solution.py
+++ b/solution.py
@@ -66,8 +66,15 @@
             here = slice(at * block, (at + 1) * block)
             flat = moved(order[...], held[slab, here].reshape(block * patches, own))
             packed[slab, :, :, here, :] = flat.reshape(width, owners, block, own)
-        sent.append(pltpu.make_async_copy(packed.at[slab], out.at[slab], out_sems.at[slab]))
-        sent[-1].start()
+            rows_here = pl.ds(at * block, block)
+            sent.append(
+                pltpu.make_async_copy(
+                    packed.at[slab, :, :, rows_here],
+                    out.at[slab, :, :, rows_here],
+                    out_sems.at[slab * count + at],
+                )
+            )
+            sent[-1].start()
     for copy in sent:
         copy.wait()
 
@@ -86,7 +93,7 @@
             pltpu.VMEM((slabs, local, patches, own), BF16),
             pltpu.VMEM((slabs, width, owners, local, own), BF16),
             pltpu.SemaphoreType.DMA((slabs * local // block,)),
-            pltpu.SemaphoreType.DMA((slabs,)),
+            pltpu.SemaphoreType.DMA((slabs * local // block,)),
         ],
         compiler_params=pltpu.CompilerParams(vmem_limit_bytes=60 * MIB),
         name="pack_obs",
@@ -223,7 +230,7 @@
     )(packed)
 
 
-def transform_kernel(before, middle, after, obs, scale, out, rest, pert, weighted):
+def transform_kernel(before, middle, after, obs, scale, out, pert, weighted):
     total = middle.shape[1]
     half = before.shape[2]
     projected = jnp.zeros((total, 1), F32)
@@ -262,10 +269,7 @@
     halfway = jnp.sum(flipped * projected, axis=0, keepdims=True)
     weight = jnp.sum(inverse * halfway, axis=1, keepdims=True)
     weight = jnp.broadcast_to(weight, (total, 128)).T[0:1, :] / bound
-    result = (jnp.sqrt((total - 1.0) / bound) * flipped + weight).astype(BF16)
-    out[0] = result
-    sums = jnp.sum(result.astype(F32), axis=1, keepdims=True)
-    rest[0] = jnp.broadcast_to(1.0 - sums, (total, 128))
+    out[0] = (jnp.sqrt((total - 1.0) / bound) * flipped + weight).astype(BF16)
 
 
 def transforms(hx_rows, obs_rows, scale_rows, count, wraps):
@@ -283,14 +287,8 @@
             pl.BlockSpec((1, 1, 2 * own), lambda a: (a, 0, 0)),
             pl.BlockSpec((1, 1, 2 * own), lambda a: (a, 0, 0)),
         ],
-        out_specs=[
-            pl.BlockSpec((1, total, total), lambda a: (a, 0, 0)),
-            pl.BlockSpec((1, total, 128), lambda a: (a, 0, 0)),
-        ],
-        out_shape=[
-            jax.ShapeDtypeStruct((count, total, total), BF16),
-            jax.ShapeDtypeStruct((count, total, 128), F32),
-        ],
+        out_specs=pl.BlockSpec((1, total, total), lambda a: (a, 0, 0)),
+        out_shape=jax.ShapeDtypeStruct((count, total, total), BF16),
         scratch_shapes=[pltpu.VMEM((total, 2 * own), BF16), pltpu.VMEM((total, 2 * own), BF16)],
         compiler_params=params(1, 32),
         cost_estimate=pl.CostEstimate(
@@ -334,16 +332,16 @@
     return results
 
 
-def forecast_kernel(state, transform, rest, speed, out, fields):
+def forecast_kernel(state, transform, speed, out, fields):
     count, total, size = out.shape
     lanes = speed.shape[1]
     for a in range(count):
         mean = jnp.sum(state[a].astype(F32), axis=0, keepdims=True) * (1.0 / total)
         values = dot_bf16(transform[a], state[a])
+        rest = 1.0 - dot_bf16(transform[a], jnp.ones((total, lanes), BF16))
         for k in range(size // lanes):
             part = slice(k * lanes, (k + 1) * lanes)
-            analysis = values[:, part] + rest[a] * mean[:, part]
-            fields[a, :, part] = analysis.astype(BF16).astype(F32)
+            fields[a, :, part] = values[:, part] + rest * mean[:, part]
     chunk = 16
     taps = stencil(jnp.broadcast_to(speed[...], (8, lanes)))
     low = iota(8, lanes, 1) < lanes // 2
@@ -367,17 +365,17 @@
     lax.fori_loop(0, total // chunk, rows_at, 0)
 
 
-def forecasts(state, transform, rest, speed):
+def forecasts(state, transform, speed):
     count, total, size = state.shape
     return pl.pallas_call(
         forecast_kernel,
-        in_specs=[WHOLE] * 4,
+        in_specs=[WHOLE] * 3,
         out_specs=WHOLE,
         out_shape=jax.ShapeDtypeStruct((count, total, size), BF16),
         scratch_shapes=[pltpu.VMEM((count, total, size), F32)],
         compiler_params=pltpu.CompilerParams(vmem_limit_bytes=20 * MIB),
         name="forecast",
-    )(state, transform, rest, speed)
+    )(state, transform, speed)
 
 
 def analysis_kernel(state, transform, out):
@@ -479,13 +477,13 @@
     state = state.reshape(count, total, -1)
 
     held_rows = hx_rows if groups == 1 else widened(hx_rows, count)
-    transform, rest = transforms(held_rows, obs_rows, scale_rows, count, groups == 1)
+    transform = transforms(held_rows, obs_rows, scale_rows, count, groups == 1)
 
     column = (lax.axis_index("mem") * width + part) * cells_b
     speed = lax.dynamic_slice(courant, (slab, column), (1, cells_b))
     speed = jnp.concatenate([speed] * width, axis=1)
-    if groups == 1 and 2 * cells_b == 128 and width == 2 and cells_a // width >= STEPS:
-        fields = forecasts(state, transform, rest, speed)
+    if groups == 1 and width == 2 and cells_a // width >= STEPS:
+        fields = forecasts(state, transform, speed)
     else:
         fields = shared_transport(analyses(state, transform), speed, width, count)
     back = exchange(fields.reshape(count * owners, local, -1))

time: 177 us -> 177 us (level)
  no operation moved by 1% of the time
where the time goes in v12:
time: 177 us; the launch traced here: 176 us
  blocking collectives  69.7 us (39%)
  waiting for transfers between devices  55.4 us (31%)
  Pallas kernels  36.8 us (21%)
  starting transfers between devices  10.3 us (6%)
  local copies, waits for them, and re-layouts  3.82 us (2%)
    all_to_all x2, waiting for transfers between devices, exchange(): lax.all_to_all(blocks, ('sub', 'mem'), split_axis=0, concat_axis=0, tiled...  55.4 us
    all_to_all x1, blocking collectives, exchange(): lax.all_to_all(blocks, ('sub', 'mem'), split_axis=0, concat_axis=0, tiled...  52 us
    pallas_call x1, Pallas kernels, transforms(): pl.pallas_call(transform_kernel, grid=(count,), in_specs=[pl.BlockSpec((1...  19.7 us
    all_gather x1, blocking collectives, advance(): stats = lax.all_gather(stats, 'sub', axis=0)  17.8 us
    all_to_all x2, starting transfers between devices, exchange(): lax.all_to_all(blocks, ('sub', 'mem'), split_axis=0, concat_axis=0, tiled...  10.3 us
    pallas_call x1, Pallas kernels, forecasts(): pl.pallas_call(forecast_kernel, in_specs=[WHOLE] * 3, out_specs=WHOLE, ou...  6.3 us
    pallas_call x1, Pallas kernels, pack_state(): pl.pallas_call(pack_state_kernel, grid=(slabs, local // block), in_specs=...  4.84 us
    pallas_call x1, Pallas kernels, pack_obs(): pl.pallas_call(pack_obs_kernel, in_specs=[ANY], out_specs=ANY, out_shape=...  3.66 us
  transfers between devices with their start and end apart: 2, of which 2 were waited for; matrix products, arithmetic and copies ran while one was open for 1% of the time, Pallas kernels for 14%

profile of v12, /device:TPU:0, one launch (start us, length us, event | category | flops | bytes accessed | tf_op | source)
XLA Modules:
  0.0 176.4 jit_solution(9098444648926062656)
XLA Ops:
  0.0 3.7 %pack_obs.1 = bf16[2,2,8,64,512]{4,3,2,1,0:T(8,128)(2,1)} custom-call(bf16[2,64,16,512]{3,2,1,0:T(8,128)(2,1)} %bitcast.25), custom_call_target="tpu_custom_call" | custom-call | tf_op jit(solution)/shard_map/pack_obs/pallas_call | solution.py:86
  3.7 7.4 %all-to-all-start.1 = ((bf16[32,64,512]{2,1,0:T(8,128)(2,1)}), bf16[32,64,512]{2,1,0:T(8,128)(2,1)}, u32[]{:S(2)}, u32[]{:S(2)}) async-start(bf16[32,64,512]{2,1,0:T(8,128)(2,1)} %bitcast.24), calls=%async_computation.1 | async-start | bytes 4194304 | tf_op jit(solution)/shard_map/all_to_all | solution.py:448
  11.1 4.8 %pack_state.1 = bf16[2,2,8,64,512]{4,3,2,1,0:T(8,128)(2,1)} custom-call(bf16[2,64,8,1024]{3,2,1,0:T(8,128)(2,1)} %cells.1), custom_call_target="tpu_custom_call" | custom-call | tf_op jit(solution)/shard_map/pack_state/pallas_call | solution.py:153
  16.0 45.2 %all-to-all-done.1 = bf16[32,64,512]{2,1,0:T(8,128)(2,1)} async-done(((bf16[32,64,512]{2,1,0:T(8,128)(2,1)}), bf16[32,64,512]{2,1,0:T(8,128)(2,1)}, u32[]{:S(2)}, u32[]{:S(2)}) %all-to-all-start.1) | async-done | bytes 2097184 | tf_op jit(solution)/shard_map/all_to_all | solution.py:448
  61.2 0.0 copy-start.2
  61.2 0.0 copy-start.3
  61.2 2.9 %all-to-all-start = ((bf16[32,64,512]{2,1,0:T(8,128)(2,1)}), bf16[32,64,512]{2,1,0:T(8,128)(2,1)S(1)}, u32[]{:S(2)}, u32[]{:S(2)}) async-start(bf16[32,64,512]{2,1,0:T(8,128)(2,1)} %bitcast.23), calls=%async_computation | async-start | bytes 4194304 | tf_op jit(solution)/shard_map/all_to_all | solution.py:448
  64.1 0.0 copy-done.2
  64.1 0.0 copy-done.3
  64.2 17.8 %all-gather = bf16[8,2,2,512]{3,1,0,2:T(2,128)(2,1)S(1)} all-gather(bf16[2,2,2,512]{3,1,0,2:T(2,128)(2,1)S(1)} %pad_maximum_fusion.2), channel_id=2, replica_groups=mesh['sub'=4,'mem'=8] {'sub'}, dimensions={0}, use_global_device_ids=true | all-gather | bytes 40960 | tf_op jit(solution)/shard_map/all_gather | solution.py:461
  82.0 0.1 reverse.4
  82.1 0.8 dynamic_slice.7
  82.8 0.1 pad_maximum_fusion.4.speed
  83.0 19.7 %transform.1 = bf16[4,512,512]{2,1,0:T(8,128)(2,1)S(1)} custom-call(bf16[4,512,512]{2,1,0:T(8,128)(2,1)} %bitcast.4.before.middle.after, bf16[4,512,512]{2,1,0:T(8,128)(2,1)} %bitcast.4.before.middle.after, bf16[4,512,512]{2,1,0:T(8,128)(2,1)} %bitcast.4.before.middle.after, f32[4,1,1024]{2,1,0:T(1,128)S(1)} %get-tuple-element.6.obs, ...), custom_call_target="tpu_custom_call" | custom-call | flops 11811160064 | bytes 8388608 | tf_op jit(solution)/shard_map/transform/pallas_call | solution.py:280
  102.7 0.0 copy-start
  102.7 1.3 copy-done
  104.1 10.1 %all-to-all-done = bf16[32,64,512]{2,1,0:T(8,128)(2,1)S(1)} async-done(((bf16[32,64,512]{2,1,0:T(8,128)(2,1)}), bf16[32,64,512]{2,1,0:T(8,128)(2,1)S(1)}, u32[]{:S(2)}, u32[]{:S(2)}) %all-to-all-start) | async-done | bytes 2097184 | tf_op jit(solution)/shard_map/all_to_all | solution.py:448
  114.2 0.0 copy-start.1
  114.2 1.6 copy-done.1
  115.8 6.3 %forecast.1 = bf16[4,512,512]{2,1,0:T(8,128)(2,1)S(1)} custom-call(bf16[4,512,512]{2,1,0:T(8,128)(2,1)S(1)} %bitcast.20, bf16[4,512,512]{2,1,0:T(8,128)(2,1)S(1)} %copy-done.1, f32[1,128]{1,0:T(1,128)S(1)} %pad_maximum_fusion.4.speed), custom_call_target="tpu_custom_call" | custom-call | tf_op jit(solution)/shard_map/forecast/pallas_call | solution.py:370
  122.1 52.0 %all_to_all.15 = bf16[32,64,512]{2,1,0:T(8,128)(2,1)S(1)} all-to-all(bf16[32,64,512]{2,1,0:T(8,128)(2,1)S(1)} %bitcast.21), channel_id=1, replica_groups=mesh['sub'=4,'mem'=8] {'sub','mem'}, dimensions={0} | all-to-all | bytes 4194304 | tf_op jit(solution)/shard_map/all_to_all | solution.py:448
  174.1 2.3 %unpack_state.1 = bf16[2,64,8,1024]{3,2,1,0:T(8,128)(2,1)} custom-call(bf16[2,2,8,64,512]{4,3,2,1,0:T(8,128)(2,1)S(1)} %bitcast.22), custom_call_target="tpu_custom_call" | custom-call | tf_op jit(solution)/shard_map/unpack_state/pallas_call | solution.py:219
  (11 shorter events, 0.2 us)
Async XLA Ops:
  3.7 57.5 %all-to-all-start.1 = ((bf16[32,64,512]{2,1,0:T(8,128)(2,1)}), bf16[32,64,512]{2,1,0:T(8,128)(2,1)}, u32[]{:S(2)}, u32[]{:S(2)}) async-start(bf16[32,64,512]{2,1,0:T(8,128)(2,1)} %bitcast.24), calls=%async_computation.1 | async-start | bytes 4194304 | tf_op jit(solution)/shard_map/all_to_all | solution.py:448
  61.2 2.9 %copy-start.2 = (bf16[2,1,2,512]{3,2,1,0:T(2,128)(2,1)S(1)}, bf16[2,1,2,512]{3,2,1,0:T(2,128)(2,1)}, u32[]{:S(2)}) copy-start(bf16[2,1,2,512]{3,2,1,0:T(2,128)(2,1)} %param.8) | copy-start | bytes 12292
  61.2 2.9 %copy-start.3 = (bf16[2,1,2,512]{3,2,1,0:T(2,128)(2,1)S(1)}, bf16[2,1,2,512]{3,2,1,0:T(2,128)(2,1)}, u32[]{:S(2)}) copy-start(bf16[2,1,2,512]{3,2,1,0:T(2,128)(2,1)} %param.7) | copy-start | bytes 12292
  61.2 53.0 %all-to-all-start = ((bf16[32,64,512]{2,1,0:T(8,128)(2,1)}), bf16[32,64,512]{2,1,0:T(8,128)(2,1)S(1)}, u32[]{:S(2)}, u32[]{:S(2)}) async-start(bf16[32,64,512]{2,1,0:T(8,128)(2,1)} %bitcast.23), calls=%async_computation | async-start | bytes 4194304 | tf_op jit(solution)/shard_map/all_to_all | solution.py:448
  102.7 1.3 copy-start
  114.2 1.6 copy-start.1

commit v13 on v12

--- a/solution.py
+++ b/solution.py
@@ -332,11 +332,19 @@
     return results
 
 
-def forecast_kernel(state, transform, speed, out, fields):
+def forecast_kernel(state, transforms, speed, out, transform, fields, sems):
     count, total, size = out.shape
     lanes = speed.shape[1]
-    for a in range(count):
-        mean = jnp.sum(state[a].astype(F32), axis=0, keepdims=True) * (1.0 / total)
+    copies = [
+        pltpu.make_async_copy(transforms.at[a], transform.at[a], sems.at[a]) for a in range(count)
+    ]
+    for copy in copies:
+        copy.start()
+    means = [
+        jnp.sum(state[a].astype(F32), axis=0, keepdims=True) * (1.0 / total) for a in range(count)
+    ]
+    for a, mean in enumerate(means):
+        copies[a].wait()
         values = dot_bf16(transform[a], state[a])
         rest = 1.0 - dot_bf16(transform[a], jnp.ones((total, lanes), BF16))
         for k in range(size // lanes):
@@ -369,11 +377,15 @@
     count, total, size = state.shape
     return pl.pallas_call(
         forecast_kernel,
-        in_specs=[WHOLE] * 3,
+        in_specs=[WHOLE, ANY, WHOLE],
         out_specs=WHOLE,
         out_shape=jax.ShapeDtypeStruct((count, total, size), BF16),
-        scratch_shapes=[pltpu.VMEM((count, total, size), F32)],
-        compiler_params=pltpu.CompilerParams(vmem_limit_bytes=20 * MIB),
+        scratch_shapes=[
+            pltpu.VMEM((count, total, total), BF16),
+            pltpu.VMEM((count, total, size), F32),
+            pltpu.SemaphoreType.DMA((count,)),
+        ],
+        compiler_params=pltpu.CompilerParams(vmem_limit_bytes=56 * MIB),
         name="forecast",
     )(state, transform, speed)
 

time: 177 us -> 182 us (1.028)
  Pallas kernels: 36.8 us -> 41.8 us
    pallas_call x1, Pallas kernels: 6.3 us -> 11.3 us  [forecasts(): pl.pallas_call(forecast_kernel, in_specs=[WHOLE, ANY, WHOLE], out_specs=W...]
  transfers between devices with their start and end apart: 2 -> 2, of which waited for: 2 -> 2; matrix products, arithmetic and copies ran while one was open for 1% -> 1% of each run, Pallas kernels for 14% -> 13%
where the time goes in v13:
time: 182 us
  blocking collectives  70.6 us (39%)
  waiting for transfers between devices  54.8 us (30%)
  Pallas kernels  41.8 us (23%)
  starting transfers between devices  10.3 us (6%)
  local copies, waits for them, and re-layouts  3.55 us (2%)
    all_to_all x2, waiting for transfers between devices, exchange(): lax.all_to_all(blocks, ('sub', 'mem'), split_axis=0, concat_axis=0, tiled...  54.8 us
    all_to_all x1, blocking collectives, exchange(): lax.all_to_all(blocks, ('sub', 'mem'), split_axis=0, concat_axis=0, tiled...  52.8 us
    pallas_call x1, Pallas kernels, transforms(): pl.pallas_call(transform_kernel, grid=(count,), in_specs=[pl.BlockSpec((1...  19.7 us
    all_gather x1, blocking collectives, advance(): stats = lax.all_gather(stats, 'sub', axis=0)  17.8 us
    pallas_call x1, Pallas kernels, forecasts(): pl.pallas_call(forecast_kernel, in_specs=[WHOLE, ANY, WHOLE], out_specs=W...  11.3 us
    all_to_all x2, starting transfers between devices, exchange(): lax.all_to_all(blocks, ('sub', 'mem'), split_axis=0, concat_axis=0, tiled...  10.3 us
    pallas_call x1, Pallas kernels, pack_state(): pl.pallas_call(pack_state_kernel, grid=(slabs, local // block), in_specs=...  4.84 us
    pallas_call x1, Pallas kernels, pack_obs(): pl.pallas_call(pack_obs_kernel, in_specs=[ANY], out_specs=ANY, out_shape=...  3.66 us
  transfers between devices with their start and end apart: 2, of which 2 were waited for; matrix products, arithmetic and copies ran while one was open for 1% of the time, Pallas kernels for 13%

profile of v13, /device:TPU:0, one launch (start us, length us, event | category | flops | bytes accessed | tf_op | source)
XLA Modules:
  0.0 181.9 jit_solution(14550802929910060615)
XLA Ops:
  0.0 3.7 %pack_obs.1 = bf16[2,2,8,64,512]{4,3,2,1,0:T(8,128)(2,1)} custom-call(bf16[2,64,16,512]{3,2,1,0:T(8,128)(2,1)} %bitcast.25), custom_call_target="tpu_custom_call" | custom-call | tf_op jit(solution)/shard_map/pack_obs/pallas_call | solution.py:86
  3.7 7.4 %all-to-all-start.1 = ((bf16[32,64,512]{2,1,0:T(8,128)(2,1)}), bf16[32,64,512]{2,1,0:T(8,128)(2,1)}, u32[]{:S(2)}, u32[]{:S(2)}) async-start(bf16[32,64,512]{2,1,0:T(8,128)(2,1)} %bitcast.24), calls=%async_computation.1 | async-start | bytes 4194304 | tf_op jit(solution)/shard_map/all_to_all | solution.py:460
  11.1 4.8 %pack_state.1 = bf16[2,2,8,64,512]{4,3,2,1,0:T(8,128)(2,1)} custom-call(bf16[2,64,8,1024]{3,2,1,0:T(8,128)(2,1)} %cells.1), custom_call_target="tpu_custom_call" | custom-call | tf_op jit(solution)/shard_map/pack_state/pallas_call | solution.py:153
  16.0 45.2 %all-to-all-done.1 = bf16[32,64,512]{2,1,0:T(8,128)(2,1)} async-done(((bf16[32,64,512]{2,1,0:T(8,128)(2,1)}), bf16[32,64,512]{2,1,0:T(8,128)(2,1)}, u32[]{:S(2)}, u32[]{:S(2)}) %all-to-all-start.1) | async-done | bytes 2097184 | tf_op jit(solution)/shard_map/all_to_all | solution.py:460
  61.2 0.0 copy-start.2
  61.2 0.0 copy-start.3
  61.2 2.9 %all-to-all-start = ((bf16[32,64,512]{2,1,0:T(8,128)(2,1)}), bf16[32,64,512]{2,1,0:T(8,128)(2,1)S(1)}, u32[]{:S(2)}, u32[]{:S(2)}) async-start(bf16[32,64,512]{2,1,0:T(8,128)(2,1)} %bitcast.23), calls=%async_computation | async-start | bytes 4194304 | tf_op jit(solution)/shard_map/all_to_all | solution.py:460
  64.1 0.0 copy-done.2
  64.1 0.0 copy-done.3
  64.2 17.8 %all-gather = bf16[8,2,2,512]{3,1,0,2:T(2,128)(2,1)S(1)} all-gather(bf16[2,2,2,512]{3,1,0,2:T(2,128)(2,1)S(1)} %pad_maximum_fusion.2), channel_id=2, replica_groups=mesh['sub'=4,'mem'=8] {'sub'}, dimensions={0}, use_global_device_ids=true | all-gather | bytes 40960 | tf_op jit(solution)/shard_map/all_gather | solution.py:473
  82.0 0.1 reverse.4
  82.1 0.8 dynamic_slice.7
  82.8 0.7 pad_maximum_fusion.4.speed
  83.6 19.7 %transform.1.transforms = bf16[4,512,512]{2,1,0:T(8,128)(2,1)S(1)} custom-call(bf16[4,512,512]{2,1,0:T(8,128)(2,1)} %bitcast.4.before.middle.after, bf16[4,512,512]{2,1,0:T(8,128)(2,1)} %bitcast.4.before.middle.after, bf16[4,512,512]{2,1,0:T(8,128)(2,1)} %bitcast.4.before.middle.after, f32[4,1,1024]{2,1,0:T(1,128)S(1)} %get-tuple-element.6.obs, ...), custom_call_target="tpu_custom_call" | custom-call | flops 11811160064 | bytes 8388608 | tf_op jit(solution)/shard_map/transform/pallas_call | solution.py:280
  103.3 0.0 copy-start
  103.3 1.3 copy-done
  104.7 9.5 %all-to-all-done = bf16[32,64,512]{2,1,0:T(8,128)(2,1)S(1)} async-done(((bf16[32,64,512]{2,1,0:T(8,128)(2,1)}), bf16[32,64,512]{2,1,0:T(8,128)(2,1)S(1)}, u32[]{:S(2)}, u32[]{:S(2)}) %all-to-all-start) | async-done | bytes 2097184 | tf_op jit(solution)/shard_map/all_to_all | solution.py:460
  114.2 0.0 copy-start.1
  114.2 1.3 copy-done.1
  115.5 11.3 %forecast.1 = bf16[4,512,512]{2,1,0:T(8,128)(2,1)} custom-call(bf16[4,512,512]{2,1,0:T(8,128)(2,1)} %bitcast.21, bf16[4,512,512]{2,1,0:T(8,128)(2,1)} %copy-done, f32[1,128]{1,0:T(1,128)} %pad_maximum_fusion.4.speed), custom_call_target="tpu_custom_call" | custom-call | tf_op jit(solution)/shard_map/forecast/pallas_call | solution.py:378
  126.8 52.8 %all_to_all.15 = bf16[32,64,512]{2,1,0:T(8,128)(2,1)S(1)} all-to-all(bf16[32,64,512]{2,1,0:T(8,128)(2,1)} %bitcast.22), channel_id=1, replica_groups=mesh['sub'=4,'mem'=8] {'sub','mem'}, dimensions={0} | all-to-all | bytes 4194304 | tf_op jit(solution)/shard_map/all_to_all | solution.py:460
  179.6 2.3 %unpack_state.1 = bf16[2,64,8,1024]{3,2,1,0:T(8,128)(2,1)} custom-call(bf16[2,2,8,64,512]{4,3,2,1,0:T(8,128)(2,1)S(1)} %bitcast.20), custom_call_target="tpu_custom_call" | custom-call | tf_op jit(solution)/shard_map/unpack_state/pallas_call | solution.py:219
  (11 shorter events, 0.2 us)
Async XLA Ops:
  3.7 57.5 %all-to-all-start.1 = ((bf16[32,64,512]{2,1,0:T(8,128)(2,1)}), bf16[32,64,512]{2,1,0:T(8,128)(2,1)}, u32[]{:S(2)}, u32[]{:S(2)}) async-start(bf16[32,64,512]{2,1,0:T(8,128)(2,1)} %bitcast.24), calls=%async_computation.1 | async-start | bytes 4194304 | tf_op jit(solution)/shard_map/all_to_all | solution.py:460
  61.2 2.9 %copy-start.2 = (bf16[2,1,2,512]{3,2,1,0:T(2,128)(2,1)S(1)}, bf16[2,1,2,512]{3,2,1,0:T(2,128)(2,1)}, u32[]{:S(2)}) copy-start(bf16[2,1,2,512]{3,2,1,0:T(2,128)(2,1)} %param.8) | copy-start | bytes 12292
  61.2 2.9 %copy-start.3 = (bf16[2,1,2,512]{3,2,1,0:T(2,128)(2,1)S(1)}, bf16[2,1,2,512]{3,2,1,0:T(2,128)(2,1)}, u32[]{:S(2)}) copy-start(bf16[2,1,2,512]{3,2,1,0:T(2,128)(2,1)} %param.7) | copy-start | bytes 12292
  61.2 53.0 %all-to-all-start = ((bf16[32,64,512]{2,1,0:T(8,128)(2,1)}), bf16[32,64,512]{2,1,0:T(8,128)(2,1)S(1)}, u32[]{:S(2)}, u32[]{:S(2)}) async-start(bf16[32,64,512]{2,1,0:T(8,128)(2,1)} %bitcast.23), calls=%async_computation | async-start | bytes 4194304 | tf_op jit(solution)/shard_map/all_to_all | solution.py:460
  103.3 1.3 copy-start
  114.2 1.3 copy-start.1

commit v14 on v13

--- a/solution.py
+++ b/solution.py
@@ -385,7 +385,7 @@
             pltpu.VMEM((count, total, size), F32),
             pltpu.SemaphoreType.DMA((count,)),
         ],
-        compiler_params=pltpu.CompilerParams(vmem_limit_bytes=56 * MIB),
+        compiler_params=pltpu.CompilerParams(vmem_limit_bytes=48 * MIB),
         name="forecast",
     )(state, transform, speed)
 

time: 182 us -> 177 us (0.973)
  Pallas kernels: 41.8 us -> 38.9 us
    pallas_call x1, Pallas kernels: 11.3 us -> 8.38 us  [forecasts(): pl.pallas_call(forecast_kernel, in_specs=[WHOLE, ANY, WHOLE], out_specs=W...]
  transfers between devices with their start and end apart: 2 -> 2, of which waited for: 2 -> 2; matrix products, arithmetic and copies ran while one was open for 1% -> 1% of each run, Pallas kernels for 13% -> 14%
where the time goes in v14:
time: 177 us
  blocking collectives  69.8 us (39%)
  waiting for transfers between devices  55.3 us (31%)
  Pallas kernels  38.9 us (22%)
  starting transfers between devices  10.3 us (6%)
  local copies, waits for them, and re-layouts  2.23 us (1%)
    all_to_all x2, waiting for transfers between devices, exchange(): lax.all_to_all(blocks, ('sub', 'mem'), split_axis=0, concat_axis=0, tiled...  55.3 us
    all_to_all x1, blocking collectives, exchange(): lax.all_to_all(blocks, ('sub', 'mem'), split_axis=0, concat_axis=0, tiled...  52 us
    pallas_call x1, Pallas kernels, transforms(): pl.pallas_call(transform_kernel, grid=(count,), in_specs=[pl.BlockSpec((1...  19.7 us
    all_gather x1, blocking collectives, advance(): stats = lax.all_gather(stats, 'sub', axis=0)  17.8 us
    all_to_all x2, starting transfers between devices, exchange(): lax.all_to_all(blocks, ('sub', 'mem'), split_axis=0, concat_axis=0, tiled...  10.3 us
    pallas_call x1, Pallas kernels, forecasts(): pl.pallas_call(forecast_kernel, in_specs=[WHOLE, ANY, WHOLE], out_specs=W...  8.38 us
    pallas_call x1, Pallas kernels, pack_state(): pl.pallas_call(pack_state_kernel, grid=(slabs, local // block), in_specs=...  4.84 us
    pallas_call x1, Pallas kernels, pack_obs(): pl.pallas_call(pack_obs_kernel, in_specs=[ANY], out_specs=ANY, out_shape=...  3.65 us
  transfers between devices with their start and end apart: 2, of which 2 were waited for; matrix products, arithmetic and copies ran while one was open for 1% of the time, Pallas kernels for 14%

profile of v14, /device:TPU:0, one launch (start us, length us, event | category | flops | bytes accessed | tf_op | source)
XLA Modules:
  0.0 176.9 jit_solution(10592379963035333002)
XLA Ops:
  0.0 3.7 %pack_obs.1 = bf16[2,2,8,64,512]{4,3,2,1,0:T(8,128)(2,1)} custom-call(bf16[2,64,16,512]{3,2,1,0:T(8,128)(2,1)} %bitcast.25), custom_call_target="tpu_custom_call" | custom-call | tf_op jit(solution)/shard_map/pack_obs/pallas_call | solution.py:86
  3.7 7.4 %all-to-all-start.1 = ((bf16[32,64,512]{2,1,0:T(8,128)(2,1)}), bf16[32,64,512]{2,1,0:T(8,128)(2,1)}, u32[]{:S(2)}, u32[]{:S(2)}) async-start(bf16[32,64,512]{2,1,0:T(8,128)(2,1)} %bitcast.24), calls=%async_computation.1 | async-start | bytes 4194304 | tf_op jit(solution)/shard_map/all_to_all | solution.py:460
  11.1 4.8 %pack_state.1 = bf16[2,2,8,64,512]{4,3,2,1,0:T(8,128)(2,1)} custom-call(bf16[2,64,8,1024]{3,2,1,0:T(8,128)(2,1)} %cells.1), custom_call_target="tpu_custom_call" | custom-call | tf_op jit(solution)/shard_map/pack_state/pallas_call | solution.py:153
  16.0 45.2 %all-to-all-done.1 = bf16[32,64,512]{2,1,0:T(8,128)(2,1)} async-done(((bf16[32,64,512]{2,1,0:T(8,128)(2,1)}), bf16[32,64,512]{2,1,0:T(8,128)(2,1)}, u32[]{:S(2)}, u32[]{:S(2)}) %all-to-all-start.1) | async-done | bytes 2097184 | tf_op jit(solution)/shard_map/all_to_all | solution.py:460
  61.2 0.0 copy-start.1
  61.2 0.0 copy-start.2
  61.2 2.9 %all-to-all-start = ((bf16[32,64,512]{2,1,0:T(8,128)(2,1)}), bf16[32,64,512]{2,1,0:T(8,128)(2,1)S(1)}, u32[]{:S(2)}, u32[]{:S(2)}) async-start(bf16[32,64,512]{2,1,0:T(8,128)(2,1)} %bitcast.23), calls=%async_computation | async-start | bytes 4194304 | tf_op jit(solution)/shard_map/all_to_all | solution.py:460
  64.1 0.0 copy-done.1
  64.1 0.0 copy-done.2
  64.2 17.8 %all-gather = bf16[8,2,2,512]{3,1,0,2:T(2,128)(2,1)S(1)} all-gather(bf16[2,2,2,512]{3,1,0,2:T(2,128)(2,1)S(1)} %pad_maximum_fusion.2), channel_id=2, replica_groups=mesh['sub'=4,'mem'=8] {'sub'}, dimensions={0}, use_global_device_ids=true | all-gather | bytes 40960 | tf_op jit(solution)/shard_map/all_gather | solution.py:473
  82.0 0.1 reverse.4
  82.1 0.8 dynamic_slice.7
  82.8 0.1 pad_maximum_fusion.4.speed
  83.0 19.7 %transform.1.transforms = bf16[4,512,512]{2,1,0:T(8,128)(2,1)S(1)} custom-call(bf16[4,512,512]{2,1,0:T(8,128)(2,1)} %bitcast.4.before.middle.after, bf16[4,512,512]{2,1,0:T(8,128)(2,1)} %bitcast.4.before.middle.after, bf16[4,512,512]{2,1,0:T(8,128)(2,1)} %bitcast.4.before.middle.after, f32[4,1,1024]{2,1,0:T(1,128)S(1)} %get-tuple-element.6.obs, ...), custom_call_target="tpu_custom_call" | custom-call | flops 11811160064 | bytes 8388608 | tf_op jit(solution)/shard_map/transform/pallas_call | solution.py:280
  102.7 0.0 copy-start
  102.8 1.3 copy-done
  104.1 10.1 %all-to-all-done = bf16[32,64,512]{2,1,0:T(8,128)(2,1)S(1)} async-done(((bf16[32,64,512]{2,1,0:T(8,128)(2,1)}), bf16[32,64,512]{2,1,0:T(8,128)(2,1)S(1)}, u32[]{:S(2)}, u32[]{:S(2)}) %all-to-all-start) | async-done | bytes 2097184 | tf_op jit(solution)/shard_map/all_to_all | solution.py:460
  114.2 8.4 %forecast.1 = bf16[4,512,512]{2,1,0:T(8,128)(2,1)S(1)} custom-call(bf16[4,512,512]{2,1,0:T(8,128)(2,1)S(1)} %bitcast.20, bf16[4,512,512]{2,1,0:T(8,128)(2,1)} %copy-done, f32[1,128]{1,0:T(1,128)S(1)} %pad_maximum_fusion.4.speed), custom_call_target="tpu_custom_call" | custom-call | tf_op jit(solution)/shard_map/forecast/pallas_call | solution.py:378
  122.6 52.0 %all_to_all.15 = bf16[32,64,512]{2,1,0:T(8,128)(2,1)S(1)} all-to-all(bf16[32,64,512]{2,1,0:T(8,128)(2,1)S(1)} %bitcast.21), channel_id=1, replica_groups=mesh['sub'=4,'mem'=8] {'sub','mem'}, dimensions={0} | all-to-all | bytes 4194304 | tf_op jit(solution)/shard_map/all_to_all | solution.py:460
  174.6 2.3 %unpack_state.1 = bf16[2,64,8,1024]{3,2,1,0:T(8,128)(2,1)} custom-call(bf16[2,2,8,64,512]{4,3,2,1,0:T(8,128)(2,1)S(1)} %bitcast.22), custom_call_target="tpu_custom_call" | custom-call | tf_op jit(solution)/shard_map/unpack_state/pallas_call | solution.py:219
  (11 shorter events, 0.2 us)
Async XLA Ops:
  3.7 57.5 %all-to-all-start.1 = ((bf16[32,64,512]{2,1,0:T(8,128)(2,1)}), bf16[32,64,512]{2,1,0:T(8,128)(2,1)}, u32[]{:S(2)}, u32[]{:S(2)}) async-start(bf16[32,64,512]{2,1,0:T(8,128)(2,1)} %bitcast.24), calls=%async_computation.1 | async-start | bytes 4194304 | tf_op jit(solution)/shard_map/all_to_all | solution.py:460
  61.2 2.9 %copy-start.1 = (bf16[2,1,2,512]{3,2,1,0:T(2,128)(2,1)S(1)}, bf16[2,1,2,512]{3,2,1,0:T(2,128)(2,1)}, u32[]{:S(2)}) copy-start(bf16[2,1,2,512]{3,2,1,0:T(2,128)(2,1)} %param.8) | copy-start | bytes 12292
  61.2 2.9 %copy-start.2 = (bf16[2,1,2,512]{3,2,1,0:T(2,128)(2,1)S(1)}, bf16[2,1,2,512]{3,2,1,0:T(2,128)(2,1)}, u32[]{:S(2)}) copy-start(bf16[2,1,2,512]{3,2,1,0:T(2,128)(2,1)} %param.7) | copy-start | bytes 12292
  61.2 53.0 %all-to-all-start = ((bf16[32,64,512]{2,1,0:T(8,128)(2,1)}), bf16[32,64,512]{2,1,0:T(8,128)(2,1)S(1)}, u32[]{:S(2)}, u32[]{:S(2)}) async-start(bf16[32,64,512]{2,1,0:T(8,128)(2,1)} %bitcast.23), calls=%async_computation | async-start | bytes 4194304 | tf_op jit(solution)/shard_map/all_to_all | solution.py:460
  102.7 1.3 copy-start

commit v15 on v10

--- a/solution.py
+++ b/solution.py
@@ -66,8 +66,15 @@
             here = slice(at * block, (at + 1) * block)
             flat = moved(order[...], held[slab, here].reshape(block * patches, own))
             packed[slab, :, :, here, :] = flat.reshape(width, owners, block, own)
-        sent.append(pltpu.make_async_copy(packed.at[slab], out.at[slab], out_sems.at[slab]))
-        sent[-1].start()
+            rows_here = pl.ds(at * block, block)
+            sent.append(
+                pltpu.make_async_copy(
+                    packed.at[slab, :, :, rows_here],
+                    out.at[slab, :, :, rows_here],
+                    out_sems.at[slab * count + at],
+                )
+            )
+            sent[-1].start()
     for copy in sent:
         copy.wait()
 
@@ -86,7 +93,7 @@
             pltpu.VMEM((slabs, local, patches, own), BF16),
             pltpu.VMEM((slabs, width, owners, local, own), BF16),
             pltpu.SemaphoreType.DMA((slabs * local // block,)),
-            pltpu.SemaphoreType.DMA((slabs,)),
+            pltpu.SemaphoreType.DMA((slabs * local // block,)),
         ],
         compiler_params=pltpu.CompilerParams(vmem_limit_bytes=60 * MIB),
         name="pack_obs",
@@ -342,8 +349,7 @@
         values = dot_bf16(transform[a], state[a])
         for k in range(size // lanes):
             part = slice(k * lanes, (k + 1) * lanes)
-            analysis = values[:, part] + rest[a] * mean[:, part]
-            fields[a, :, part] = analysis.astype(BF16).astype(F32)
+            fields[a, :, part] = values[:, part] + rest[a] * mean[:, part]
     chunk = 16
     taps = stencil(jnp.broadcast_to(speed[...], (8, lanes)))
     low = iota(8, lanes, 1) < lanes // 2
@@ -364,7 +370,7 @@
                 out[a, at, k * lanes : (k + 1) * lanes] = value.astype(BF16)
         return carry
 
-    lax.fori_loop(0, total // chunk, rows_at, 0)
+    lax.fori_loop(0, total // chunk, rows_at, 0, unroll=2)
 
 
 def forecasts(state, transform, rest, speed):

time: 177 us -> 175 us (0.989)
  no operation moved by 1% of the time
where the time goes in v15:
time: 175 us
  blocking collectives  69.7 us (40%)
  waiting for transfers between devices  54.6 us (31%)
  Pallas kernels  35.8 us (20%)
  starting transfers between devices  10.3 us (6%)
  local copies, waits for them, and re-layouts  3.82 us (2%)
    all_to_all x2, waiting for transfers between devices, exchange(): lax.all_to_all(blocks, ('sub', 'mem'), split_axis=0, concat_axis=0, tiled...  54.6 us
    all_to_all x1, blocking collectives, exchange(): lax.all_to_all(blocks, ('sub', 'mem'), split_axis=0, concat_axis=0, tiled...  52 us
    pallas_call x1, Pallas kernels, transforms(): pl.pallas_call(transform_kernel, grid=(count,), in_specs=[pl.BlockSpec((1...  20.5 us
    all_gather x1, blocking collectives, advance(): stats = lax.all_gather(stats, 'sub', axis=0)  17.8 us
    all_to_all x2, starting transfers between devices, exchange(): lax.all_to_all(blocks, ('sub', 'mem'), split_axis=0, concat_axis=0, tiled...  10.3 us
    pallas_call x1, Pallas kernels, pack_state(): pl.pallas_call(pack_state_kernel, grid=(slabs, local // block), in_specs=...  4.84 us
    pallas_call x1, Pallas kernels, forecasts(): pl.pallas_call(forecast_kernel, in_specs=[WHOLE] * 4, out_specs=WHOLE, ou...  4.48 us
    pallas_call x1, Pallas kernels, pack_obs(): pl.pallas_call(pack_obs_kernel, in_specs=[ANY], out_specs=ANY, out_shape=...  3.69 us
  transfers between devices with their start and end apart: 2, of which 2 were waited for; matrix products, arithmetic and copies ran while one was open for 1% of the time, Pallas kernels for 14%

profile of v15, /device:TPU:0, one launch (start us, length us, event | category | flops | bytes accessed | tf_op | source)
XLA Modules:
  0.0 174.6 jit_solution(16359870875410295661)
XLA Ops:
  0.0 3.7 %pack_obs.1 = bf16[2,2,8,64,512]{4,3,2,1,0:T(8,128)(2,1)} custom-call(bf16[2,64,16,512]{3,2,1,0:T(8,128)(2,1)} %bitcast.25), custom_call_target="tpu_custom_call" | custom-call | tf_op jit(solution)/shard_map/pack_obs/pallas_call | solution.py:86
  3.7 7.4 %all-to-all-start.1 = ((bf16[32,64,512]{2,1,0:T(8,128)(2,1)}), bf16[32,64,512]{2,1,0:T(8,128)(2,1)}, u32[]{:S(2)}, u32[]{:S(2)}) async-start(bf16[32,64,512]{2,1,0:T(8,128)(2,1)} %bitcast.24), calls=%async_computation.1 | async-start | bytes 4194304 | tf_op jit(solution)/shard_map/all_to_all | solution.py:456
  11.2 4.8 %pack_state.1 = bf16[2,2,8,64,512]{4,3,2,1,0:T(8,128)(2,1)} custom-call(bf16[2,64,8,1024]{3,2,1,0:T(8,128)(2,1)} %cells.1), custom_call_target="tpu_custom_call" | custom-call | tf_op jit(solution)/shard_map/pack_state/pallas_call | solution.py:153
  16.0 45.2 %all-to-all-done.1 = bf16[32,64,512]{2,1,0:T(8,128)(2,1)} async-done(((bf16[32,64,512]{2,1,0:T(8,128)(2,1)}), bf16[32,64,512]{2,1,0:T(8,128)(2,1)}, u32[]{:S(2)}, u32[]{:S(2)}) %all-to-all-start.1) | async-done | bytes 2097184 | tf_op jit(solution)/shard_map/all_to_all | solution.py:456
  61.2 0.0 copy-start.2
  61.2 0.0 copy-start.3
  61.2 2.9 %all-to-all-start = ((bf16[32,64,512]{2,1,0:T(8,128)(2,1)}), bf16[32,64,512]{2,1,0:T(8,128)(2,1)S(1)}, u32[]{:S(2)}, u32[]{:S(2)}) async-start(bf16[32,64,512]{2,1,0:T(8,128)(2,1)} %bitcast.23), calls=%async_computation | async-start | bytes 4194304 | tf_op jit(solution)/shard_map/all_to_all | solution.py:456
  64.2 0.0 copy-done.2
  64.2 0.0 copy-done.3
  64.2 17.8 %all-gather = bf16[8,2,2,512]{3,1,0,2:T(2,128)(2,1)S(1)} all-gather(bf16[2,2,2,512]{3,1,0,2:T(2,128)(2,1)S(1)} %pad_maximum_fusion.2), channel_id=2, replica_groups=mesh['sub'=4,'mem'=8] {'sub'}, dimensions={0}, use_global_device_ids=true | all-gather | bytes 40960 | tf_op jit(solution)/shard_map/all_gather | solution.py:469
  82.0 0.1 reverse.4
  82.1 0.8 dynamic_slice.7
  82.9 0.1 pad_maximum_fusion.4.speed
  83.1 20.5 %transform.1 = (bf16[4,512,512]{2,1,0:T(8,128)(2,1)S(1)}, f32[4,512,128]{2,1,0:T(8,128)S(1)}) custom-call(bf16[4,512,512]{2,1,0:T(8,128)(2,1)} %bitcast.4.before.middle.after, bf16[4,512,512]{2,1,0:T(8,128)(2,1)} %bitcast.4.before.middle.after, bf16[4,512,512]{2,1,0:T(8,128)(2,1)} %bitcast.4.before.middle.after, f32[4,1,1024]{2,1,0:T(1,128)S(1)} %get-tuple-element.10.obs, ...), custom_call_target="tpu_custom_call" | custom-call | flops 11811160064 | bytes 8388608 | tf_op jit(solution)/shard_map/transform/pallas_call | solution.py:283
  103.5 0.0 copy-start
  103.6 1.3 copy-done
  104.9 9.3 %all-to-all-done = bf16[32,64,512]{2,1,0:T(8,128)(2,1)S(1)} async-done(((bf16[32,64,512]{2,1,0:T(8,128)(2,1)}), bf16[32,64,512]{2,1,0:T(8,128)(2,1)S(1)}, u32[]{:S(2)}, u32[]{:S(2)}) %all-to-all-start) | async-done | bytes 2097184 | tf_op jit(solution)/shard_map/all_to_all | solution.py:456
  114.2 0.0 copy-start.1
  114.2 1.6 copy-done.1
  115.8 4.5 %forecast.1 = bf16[4,512,512]{2,1,0:T(8,128)(2,1)S(1)} custom-call(bf16[4,512,512]{2,1,0:T(8,128)(2,1)S(1)} %bitcast.21, bf16[4,512,512]{2,1,0:T(8,128)(2,1)S(1)} %copy-done.1, f32[4,512,128]{2,1,0:T(8,128)S(1)} %get-tuple-element.8.rest, f32[1,128]{1,0:T(1,128)S(1)} %pad_maximum_fusion.4.speed), custom_call_target="tpu_custom_call" | custom-call | tf_op jit(solution)/shard_map/forecast/pallas_call | solution.py:378
  120.3 52.0 %all_to_all.15 = bf16[32,64,512]{2,1,0:T(8,128)(2,1)S(1)} all-to-all(bf16[32,64,512]{2,1,0:T(8,128)(2,1)S(1)} %bitcast.22), channel_id=1, replica_groups=mesh['sub'=4,'mem'=8] {'sub','mem'}, dimensions={0} | all-to-all | bytes 4194304 | tf_op jit(solution)/shard_map/all_to_all | solution.py:456
  172.3 2.3 %unpack_state.1 = bf16[2,64,8,1024]{3,2,1,0:T(8,128)(2,1)} custom-call(bf16[2,2,8,64,512]{4,3,2,1,0:T(8,128)(2,1)S(1)} %bitcast.20), custom_call_target="tpu_custom_call" | custom-call | tf_op jit(solution)/shard_map/unpack_state/pallas_call | solution.py:219
  (11 shorter events, 0.2 us)
Async XLA Ops:
  3.7 57.5 %all-to-all-start.1 = ((bf16[32,64,512]{2,1,0:T(8,128)(2,1)}), bf16[32,64,512]{2,1,0:T(8,128)(2,1)}, u32[]{:S(2)}, u32[]{:S(2)}) async-start(bf16[32,64,512]{2,1,0:T(8,128)(2,1)} %bitcast.24), calls=%async_computation.1 | async-start | bytes 4194304 | tf_op jit(solution)/shard_map/all_to_all | solution.py:456
  61.2 2.9 %copy-start.2 = (bf16[2,1,2,512]{3,2,1,0:T(2,128)(2,1)S(1)}, bf16[2,1,2,512]{3,2,1,0:T(2,128)(2,1)}, u32[]{:S(2)}) copy-start(bf16[2,1,2,512]{3,2,1,0:T(2,128)(2,1)} %param.8) | copy-start | bytes 12292
  61.2 2.9 %copy-start.3 = (bf16[2,1,2,512]{3,2,1,0:T(2,128)(2,1)S(1)}, bf16[2,1,2,512]{3,2,1,0:T(2,128)(2,1)}, u32[]{:S(2)}) copy-start(bf16[2,1,2,512]{3,2,1,0:T(2,128)(2,1)} %param.7) | copy-start | bytes 12292
  61.2 53.0 %all-to-all-start = ((bf16[32,64,512]{2,1,0:T(8,128)(2,1)}), bf16[32,64,512]{2,1,0:T(8,128)(2,1)S(1)}, u32[]{:S(2)}, u32[]{:S(2)}) async-start(bf16[32,64,512]{2,1,0:T(8,128)(2,1)} %bitcast.23), calls=%async_computation | async-start | bytes 4194304 | tf_op jit(solution)/shard_map/all_to_all | solution.py:456
  103.5 1.3 copy-start
  114.2 1.6 copy-start.1

commit v16 on v15

--- a/solution.py
+++ b/solution.py
@@ -370,7 +370,7 @@
                 out[a, at, k * lanes : (k + 1) * lanes] = value.astype(BF16)
         return carry
 
-    lax.fori_loop(0, total // chunk, rows_at, 0, unroll=2)
+    lax.fori_loop(0, total // chunk, rows_at, 0, unroll=4)
 
 
 def forecasts(state, transform, rest, speed):

time: 175 us -> 175 us (level)
  transfers between devices with their start and end apart: 2 -> 2, of which waited for: 2 -> 2; matrix products, arithmetic and copies ran while one was open for 1% -> 1% of each run, Pallas kernels for 14% -> 15%
where the time goes in v16:
time: 175 us; the launch traced here: 174 us
  blocking collectives  69.8 us (40%)
  waiting for transfers between devices  54.6 us (31%)
  Pallas kernels  35.6 us (20%)
  starting transfers between devices  10.3 us (6%)
  local copies, waits for them, and re-layouts  3.82 us (2%)
    all_to_all x2, waiting for transfers between devices, exchange(): lax.all_to_all(blocks, ('sub', 'mem'), split_axis=0, concat_axis=0, tiled...  54.6 us
    all_to_all x1, blocking collectives, exchange(): lax.all_to_all(blocks, ('sub', 'mem'), split_axis=0, concat_axis=0, tiled...  52 us
    pallas_call x1, Pallas kernels, transforms(): pl.pallas_call(transform_kernel, grid=(count,), in_specs=[pl.BlockSpec((1...  20.5 us
    all_gather x1, blocking collectives, advance(): stats = lax.all_gather(stats, 'sub', axis=0)  17.8 us
    all_to_all x2, starting transfers between devices, exchange(): lax.all_to_all(blocks, ('sub', 'mem'), split_axis=0, concat_axis=0, tiled...  10.3 us
    pallas_call x1, Pallas kernels, pack_state(): pl.pallas_call(pack_state_kernel, grid=(slabs, local // block), in_specs=...  4.84 us
    pallas_call x1, Pallas kernels, forecasts(): pl.pallas_call(forecast_kernel, in_specs=[WHOLE] * 4, out_specs=WHOLE, ou...  4.28 us
    pallas_call x1, Pallas kernels, pack_obs(): pl.pallas_call(pack_obs_kernel, in_specs=[ANY], out_specs=ANY, out_shape=...  3.69 us
  transfers between devices with their start and end apart: 2, of which 2 were waited for; matrix products, arithmetic and copies ran while one was open for 1% of the time, Pallas kernels for 15%

profile of v16, /device:TPU:0, one launch (start us, length us, event | category | flops | bytes accessed | tf_op | source)
XLA Modules:
  0.0 174.4 jit_solution(8353805943776139300)
XLA Ops:
  0.0 3.7 %pack_obs.1 = bf16[2,2,8,64,512]{4,3,2,1,0:T(8,128)(2,1)} custom-call(bf16[2,64,16,512]{3,2,1,0:T(8,128)(2,1)} %bitcast.25), custom_call_target="tpu_custom_call" | custom-call | tf_op jit(solution)/shard_map/pack_obs/pallas_call | solution.py:86
  3.7 7.4 %all-to-all-start.1 = ((bf16[32,64,512]{2,1,0:T(8,128)(2,1)}), bf16[32,64,512]{2,1,0:T(8,128)(2,1)}, u32[]{:S(2)}, u32[]{:S(2)}) async-start(bf16[32,64,512]{2,1,0:T(8,128)(2,1)} %bitcast.24), calls=%async_computation.1 | async-start | bytes 4194304 | tf_op jit(solution)/shard_map/all_to_all | solution.py:456
  11.2 4.8 %pack_state.1 = bf16[2,2,8,64,512]{4,3,2,1,0:T(8,128)(2,1)} custom-call(bf16[2,64,8,1024]{3,2,1,0:T(8,128)(2,1)} %cells.1), custom_call_target="tpu_custom_call" | custom-call | tf_op jit(solution)/shard_map/pack_state/pallas_call | solution.py:153
  16.0 45.2 %all-to-all-done.1 = bf16[32,64,512]{2,1,0:T(8,128)(2,1)} async-done(((bf16[32,64,512]{2,1,0:T(8,128)(2,1)}), bf16[32,64,512]{2,1,0:T(8,128)(2,1)}, u32[]{:S(2)}, u32[]{:S(2)}) %all-to-all-start.1) | async-done | bytes 2097184 | tf_op jit(solution)/shard_map/all_to_all | solution.py:456
  61.2 0.0 copy-start.2
  61.2 0.0 copy-start.3
  61.2 2.9 %all-to-all-start = ((bf16[32,64,512]{2,1,0:T(8,128)(2,1)}), bf16[32,64,512]{2,1,0:T(8,128)(2,1)S(1)}, u32[]{:S(2)}, u32[]{:S(2)}) async-start(bf16[32,64,512]{2,1,0:T(8,128)(2,1)} %bitcast.23), calls=%async_computation | async-start | bytes 4194304 | tf_op jit(solution)/shard_map/all_to_all | solution.py:456
  64.2 0.0 copy-done.2
  64.2 0.0 copy-done.3
  64.2 17.8 %all-gather = bf16[8,2,2,512]{3,1,0,2:T(2,128)(2,1)S(1)} all-gather(bf16[2,2,2,512]{3,1,0,2:T(2,128)(2,1)S(1)} %pad_maximum_fusion.2), channel_id=2, replica_groups=mesh['sub'=4,'mem'=8] {'sub'}, dimensions={0}, use_global_device_ids=true | all-gather | bytes 40960 | tf_op jit(solution)/shard_map/all_gather | solution.py:469
  82.0 0.1 reverse.4
  82.1 0.8 dynamic_slice.7
  82.9 0.1 pad_maximum_fusion.4.speed
  83.1 20.5 %transform.1 = (bf16[4,512,512]{2,1,0:T(8,128)(2,1)S(1)}, f32[4,512,128]{2,1,0:T(8,128)S(1)}) custom-call(bf16[4,512,512]{2,1,0:T(8,128)(2,1)} %bitcast.4.before.middle.after, bf16[4,512,512]{2,1,0:T(8,128)(2,1)} %bitcast.4.before.middle.after, bf16[4,512,512]{2,1,0:T(8,128)(2,1)} %bitcast.4.before.middle.after, f32[4,1,1024]{2,1,0:T(1,128)S(1)} %get-tuple-element.10.obs, ...), custom_call_target="tpu_custom_call" | custom-call | flops 11811160064 | bytes 8388608 | tf_op jit(solution)/shard_map/transform/pallas_call | solution.py:283
  103.5 0.0 copy-start
  103.6 1.3 copy-done
  104.9 9.3 %all-to-all-done = bf16[32,64,512]{2,1,0:T(8,128)(2,1)S(1)} async-done(((bf16[32,64,512]{2,1,0:T(8,128)(2,1)}), bf16[32,64,512]{2,1,0:T(8,128)(2,1)S(1)}, u32[]{:S(2)}, u32[]{:S(2)}) %all-to-all-start) | async-done | bytes 2097184 | tf_op jit(solution)/shard_map/all_to_all | solution.py:456
  114.2 0.0 copy-start.1
  114.2 1.6 copy-done.1
  115.8 4.3 %forecast.1 = bf16[4,512,512]{2,1,0:T(8,128)(2,1)S(1)} custom-call(bf16[4,512,512]{2,1,0:T(8,128)(2,1)S(1)} %bitcast.21, bf16[4,512,512]{2,1,0:T(8,128)(2,1)S(1)} %copy-done.1, f32[4,512,128]{2,1,0:T(8,128)S(1)} %get-tuple-element.8.rest, f32[1,128]{1,0:T(1,128)S(1)} %pad_maximum_fusion.4.speed), custom_call_target="tpu_custom_call" | custom-call | tf_op jit(solution)/shard_map/forecast/pallas_call | solution.py:378
  120.1 52.0 %all_to_all.15 = bf16[32,64,512]{2,1,0:T(8,128)(2,1)S(1)} all-to-all(bf16[32,64,512]{2,1,0:T(8,128)(2,1)S(1)} %bitcast.22), channel_id=1, replica_groups=mesh['sub'=4,'mem'=8] {'sub','mem'}, dimensions={0} | all-to-all | bytes 4194304 | tf_op jit(solution)/shard_map/all_to_all | solution.py:456
  172.1 2.3 %unpack_state.1 = bf16[2,64,8,1024]{3,2,1,0:T(8,128)(2,1)} custom-call(bf16[2,2,8,64,512]{4,3,2,1,0:T(8,128)(2,1)S(1)} %bitcast.20), custom_call_target="tpu_custom_call" | custom-call | tf_op jit(solution)/shard_map/unpack_state/pallas_call | solution.py:219
  (11 shorter events, 0.2 us)
Async XLA Ops:
  3.7 57.5 %all-to-all-start.1 = ((bf16[32,64,512]{2,1,0:T(8,128)(2,1)}), bf16[32,64,512]{2,1,0:T(8,128)(2,1)}, u32[]{:S(2)}, u32[]{:S(2)}) async-start(bf16[32,64,512]{2,1,0:T(8,128)(2,1)} %bitcast.24), calls=%async_computation.1 | async-start | bytes 4194304 | tf_op jit(solution)/shard_map/all_to_all | solution.py:456
  61.2 2.9 %copy-start.2 = (bf16[2,1,2,512]{3,2,1,0:T(2,128)(2,1)S(1)}, bf16[2,1,2,512]{3,2,1,0:T(2,128)(2,1)}, u32[]{:S(2)}) copy-start(bf16[2,1,2,512]{3,2,1,0:T(2,128)(2,1)} %param.8) | copy-start | bytes 12292
  61.2 2.9 %copy-start.3 = (bf16[2,1,2,512]{3,2,1,0:T(2,128)(2,1)S(1)}, bf16[2,1,2,512]{3,2,1,0:T(2,128)(2,1)}, u32[]{:S(2)}) copy-start(bf16[2,1,2,512]{3,2,1,0:T(2,128)(2,1)} %param.7) | copy-start | bytes 12292
  61.2 53.0 %all-to-all-start = ((bf16[32,64,512]{2,1,0:T(8,128)(2,1)}), bf16[32,64,512]{2,1,0:T(8,128)(2,1)S(1)}, u32[]{:S(2)}, u32[]{:S(2)}) async-start(bf16[32,64,512]{2,1,0:T(8,128)(2,1)} %bitcast.23), calls=%async_computation | async-start | bytes 4194304 | tf_op jit(solution)/shard_map/all_to_all | solution.py:456
  103.5 1.3 copy-start
  114.2 1.6 copy-start.1

commit v17 on v15

--- a/solution.py
+++ b/solution.py
@@ -215,7 +215,7 @@
     slabs, width, owners, local, size = packed.shape
     lanes = size * width // cells_a
     shape = (slabs, local, cells_a, owners * lanes)
-    block = 32
+    block = 16
     return pl.pallas_call(
         unpack_state_kernel,
         in_specs=[WHOLE],

time: 175 us -> 175 us (level)
  no operation moved by 1% of the time
where the time goes in v17:
time: 175 us
  blocking collectives  69.7 us (40%)
  waiting for transfers between devices  54.6 us (31%)
  Pallas kernels  35.8 us (20%)
  starting transfers between devices  10.3 us (6%)
  local copies, waits for them, and re-layouts  3.82 us (2%)
    all_to_all x2, waiting for transfers between devices, exchange(): lax.all_to_all(blocks, ('sub', 'mem'), split_axis=0, concat_axis=0, tiled...  54.6 us
    all_to_all x1, blocking collectives, exchange(): lax.all_to_all(blocks, ('sub', 'mem'), split_axis=0, concat_axis=0, tiled...  52 us
    pallas_call x1, Pallas kernels, transforms(): pl.pallas_call(transform_kernel, grid=(count,), in_specs=[pl.BlockSpec((1...  20.5 us
    all_gather x1, blocking collectives, advance(): stats = lax.all_gather(stats, 'sub', axis=0)  17.8 us
    all_to_all x2, starting transfers between devices, exchange(): lax.all_to_all(blocks, ('sub', 'mem'), split_axis=0, concat_axis=0, tiled...  10.3 us
    pallas_call x1, Pallas kernels, pack_state(): pl.pallas_call(pack_state_kernel, grid=(slabs, local // block), in_specs=...  4.84 us
    pallas_call x1, Pallas kernels, forecasts(): pl.pallas_call(forecast_kernel, in_specs=[WHOLE] * 4, out_specs=WHOLE, ou...  4.48 us
    pallas_call x1, Pallas kernels, pack_obs(): pl.pallas_call(pack_obs_kernel, in_specs=[ANY], out_specs=ANY, out_shape=...  3.69 us
  transfers between devices with their start and end apart: 2, of which 2 were waited for; matrix products, arithmetic and copies ran while one was open for 1% of the time, Pallas kernels for 14%

profile of v17, /device:TPU:0, one launch (start us, length us, event | category | flops | bytes accessed | tf_op | source)
XLA Modules:
  0.0 174.6 jit_solution(17731968274524484076)
XLA Ops:
  0.0 3.7 %pack_obs.1 = bf16[2,2,8,64,512]{4,3,2,1,0:T(8,128)(2,1)} custom-call(bf16[2,64,16,512]{3,2,1,0:T(8,128)(2,1)} %bitcast.25), custom_call_target="tpu_custom_call" | custom-call | tf_op jit(solution)/shard_map/pack_obs/pallas_call | solution.py:86
  3.7 7.4 %all-to-all-start.1 = ((bf16[32,64,512]{2,1,0:T(8,128)(2,1)}), bf16[32,64,512]{2,1,0:T(8,128)(2,1)}, u32[]{:S(2)}, u32[]{:S(2)}) async-start(bf16[32,64,512]{2,1,0:T(8,128)(2,1)} %bitcast.24), calls=%async_computation.1 | async-start | bytes 4194304 | tf_op jit(solution)/shard_map/all_to_all | solution.py:456
  11.2 4.8 %pack_state.1 = bf16[2,2,8,64,512]{4,3,2,1,0:T(8,128)(2,1)} custom-call(bf16[2,64,8,1024]{3,2,1,0:T(8,128)(2,1)} %cells.1), custom_call_target="tpu_custom_call" | custom-call | tf_op jit(solution)/shard_map/pack_state/pallas_call | solution.py:153
  16.0 45.2 %all-to-all-done.1 = bf16[32,64,512]{2,1,0:T(8,128)(2,1)} async-done(((bf16[32,64,512]{2,1,0:T(8,128)(2,1)}), bf16[32,64,512]{2,1,0:T(8,128)(2,1)}, u32[]{:S(2)}, u32[]{:S(2)}) %all-to-all-start.1) | async-done | bytes 2097184 | tf_op jit(solution)/shard_map/all_to_all | solution.py:456
  61.2 0.0 copy-start.2
  61.2 0.0 copy-start.3
  61.2 2.9 %all-to-all-start = ((bf16[32,64,512]{2,1,0:T(8,128)(2,1)}), bf16[32,64,512]{2,1,0:T(8,128)(2,1)S(1)}, u32[]{:S(2)}, u32[]{:S(2)}) async-start(bf16[32,64,512]{2,1,0:T(8,128)(2,1)} %bitcast.23), calls=%async_computation | async-start | bytes 4194304 | tf_op jit(solution)/shard_map/all_to_all | solution.py:456
  64.2 0.0 copy-done.2
  64.2 0.0 copy-done.3
  64.2 17.8 %all-gather = bf16[8,2,2,512]{3,1,0,2:T(2,128)(2,1)S(1)} all-gather(bf16[2,2,2,512]{3,1,0,2:T(2,128)(2,1)S(1)} %pad_maximum_fusion.2), channel_id=2, replica_groups=mesh['sub'=4,'mem'=8] {'sub'}, dimensions={0}, use_global_device_ids=true | all-gather | bytes 40960 | tf_op jit(solution)/shard_map/all_gather | solution.py:469
  82.0 0.1 reverse.4
  82.1 0.8 dynamic_slice.7
  82.9 0.1 pad_maximum_fusion.4.speed
  83.1 20.5 %transform.1 = (bf16[4,512,512]{2,1,0:T(8,128)(2,1)S(1)}, f32[4,512,128]{2,1,0:T(8,128)S(1)}) custom-call(bf16[4,512,512]{2,1,0:T(8,128)(2,1)} %bitcast.4.before.middle.after, bf16[4,512,512]{2,1,0:T(8,128)(2,1)} %bitcast.4.before.middle.after, bf16[4,512,512]{2,1,0:T(8,128)(2,1)} %bitcast.4.before.middle.after, f32[4,1,1024]{2,1,0:T(1,128)S(1)} %get-tuple-element.10.obs, ...), custom_call_target="tpu_custom_call" | custom-call | flops 11811160064 | bytes 8388608 | tf_op jit(solution)/shard_map/transform/pallas_call | solution.py:283
  103.5 0.0 copy-start
  103.6 1.3 copy-done
  104.9 9.3 %all-to-all-done = bf16[32,64,512]{2,1,0:T(8,128)(2,1)S(1)} async-done(((bf16[32,64,512]{2,1,0:T(8,128)(2,1)}), bf16[32,64,512]{2,1,0:T(8,128)(2,1)S(1)}, u32[]{:S(2)}, u32[]{:S(2)}) %all-to-all-start) | async-done | bytes 2097184 | tf_op jit(solution)/shard_map/all_to_all | solution.py:456
  114.2 0.0 copy-start.1
  114.2 1.6 copy-done.1
  115.8 4.5 %forecast.1 = bf16[4,512,512]{2,1,0:T(8,128)(2,1)S(1)} custom-call(bf16[4,512,512]{2,1,0:T(8,128)(2,1)S(1)} %bitcast.21, bf16[4,512,512]{2,1,0:T(8,128)(2,1)S(1)} %copy-done.1, f32[4,512,128]{2,1,0:T(8,128)S(1)} %get-tuple-element.8.rest, f32[1,128]{1,0:T(1,128)S(1)} %pad_maximum_fusion.4.speed), custom_call_target="tpu_custom_call" | custom-call | tf_op jit(solution)/shard_map/forecast/pallas_call | solution.py:378
  120.3 52.0 %all_to_all.15 = bf16[32,64,512]{2,1,0:T(8,128)(2,1)S(1)} all-to-all(bf16[32,64,512]{2,1,0:T(8,128)(2,1)S(1)} %bitcast.22), channel_id=1, replica_groups=mesh['sub'=4,'mem'=8] {'sub','mem'}, dimensions={0} | all-to-all | bytes 4194304 | tf_op jit(solution)/shard_map/all_to_all | solution.py:456
  172.3 2.3 %unpack_state.1 = bf16[2,64,8,1024]{3,2,1,0:T(8,128)(2,1)} custom-call(bf16[2,2,8,64,512]{4,3,2,1,0:T(8,128)(2,1)S(1)} %bitcast.20), custom_call_target="tpu_custom_call" | custom-call | tf_op jit(solution)/shard_map/unpack_state/pallas_call | solution.py:219
  (11 shorter events, 0.2 us)
Async XLA Ops:
  3.7 57.5 %all-to-all-start.1 = ((bf16[32,64,512]{2,1,0:T(8,128)(2,1)}), bf16[32,64,512]{2,1,0:T(8,128)(2,1)}, u32[]{:S(2)}, u32[]{:S(2)}) async-start(bf16[32,64,512]{2,1,0:T(8,128)(2,1)} %bitcast.24), calls=%async_computation.1 | async-start | bytes 4194304 | tf_op jit(solution)/shard_map/all_to_all | solution.py:456
  61.2 2.9 %copy-start.2 = (bf16[2,1,2,512]{3,2,1,0:T(2,128)(2,1)S(1)}, bf16[2,1,2,512]{3,2,1,0:T(2,128)(2,1)}, u32[]{:S(2)}) copy-start(bf16[2,1,2,512]{3,2,1,0:T(2,128)(2,1)} %param.8) | copy-start | bytes 12292
  61.2 2.9 %copy-start.3 = (bf16[2,1,2,512]{3,2,1,0:T(2,128)(2,1)S(1)}, bf16[2,1,2,512]{3,2,1,0:T(2,128)(2,1)}, u32[]{:S(2)}) copy-start(bf16[2,1,2,512]{3,2,1,0:T(2,128)(2,1)} %param.7) | copy-start | bytes 12292
  61.2 53.0 %all-to-all-start = ((bf16[32,64,512]{2,1,0:T(8,128)(2,1)}), bf16[32,64,512]{2,1,0:T(8,128)(2,1)S(1)}, u32[]{:S(2)}, u32[]{:S(2)}) async-start(bf16[32,64,512]{2,1,0:T(8,128)(2,1)} %bitcast.23), calls=%async_computation | async-start | bytes 4194304 | tf_op jit(solution)/shard_map/all_to_all | solution.py:456
  103.5 1.3 copy-start
  114.2 1.6 copy-start.1
